TPU v7x, 128 devices: a whole 4x4x4 slice. The times are simulated.
128 devices in a mesh: row: 8 (over z_lo, x), seq: 16 (over y, z_hi, core).
Axes of the slice: x: 4, y: 4, z: 4 (z_hi: 2, z_lo: 2; z = z_hi * 2 + z_lo), core: 2. Of those that a mesh axis runs over, the one named last changes fastest.
Arguments:
- mixer_input: bfloat16 [32768, 4352], P(('row', 'seq')), parts along dimension 0, may hold values from -6 to 6
- gate_input: bfloat16 [32768, 4096], P(('row', 'seq')), parts along dimension 0, may hold values from -6 to 6
- conv_forward: float32 [4, 4352], replicated, may hold values from -3 to 3
- conv_reverse: float32 [4, 4352], replicated, may hold values from -3 to 3
- step_size: float32 [64, 32768], P(None, ('row', 'seq')), parts along dimension 1, may hold values from 0 to 1, as said below
- decay_rate: float32 [512], P('row'), parts along dimension 0, may hold values from 1 to 8, as said below
- skip_scale: float32 [64], replicated, may hold values from 0.5 to 1.5
- norm_gain: float32 [4096], replicated, may hold values from 0.5 to 1.5
Outputs:
- mixer_output: bfloat16 [32768, 4096], P(('row', 'seq')), parts along dimension 0
There are 8 independent parts, one for each index of `row`. A program takes and returns all parts, laid end to end along the dimension named above; an argument that names none is the same for every part. Nothing has to cross between parts.
Inputs may be any that keep to these rules, and one draw needn't show every extreme that they name: `step_size`: positive step sizes. `decay_rate`: positive coefficients.
All inputs are finite; a program needn't handle non-finite values.
Results may differ from a plain program's by a relative error of at most 0.007.
Values may be sent and summed in bfloat16 or wider, within the bound.
No kernel may reach another device: no remote copies, remote signals or barrier semaphores. Data moves between devices by JAX's collectives and lax.ppermute only.
A program may use at most 192 MiB of HBM per device.

v0:
```python
import jax
import jax.numpy as jnp
from jax import lax
from jax.sharding import PartitionSpec as P

HEADS = 64
HEAD_DIM = 64
STATE = 128
WIDTH = 4
GROUP = 256


def with_halo(cells, sides, width):
    for axis, dim in sides:
        count = lax.axis_size(axis)
        ends = count - 1
        head = lax.slice_in_dim(cells, 0, width, axis=dim)
        tail = lax.slice_in_dim(cells, cells.shape[dim] - width, cells.shape[dim], axis=dim)
        cells = jnp.concatenate(
            [
                lax.ppermute(tail, axis, [(i, (i + 1) % count) for i in range(ends)]),
                cells,
                lax.ppermute(head, axis, [((i + 1) % count, i) for i in range(ends)]),
            ],
            axis=dim,
        )
    return cells


def entering(array, axis, combine, identity, reverse):
    devices, mine = (lax.axis_size(axis), lax.axis_index(axis))
    everything = jax.tree.map(lambda part: lax.all_gather(part, axis), array)
    start = jax.tree.map(
        lambda part, zero: jnp.broadcast_to(jnp.asarray(zero, part.dtype), part.shape),
        array,
        identity,
    )

    def lap(k, before):
        at = devices - 1 - k if reverse else k
        reached = at > mine if reverse else at < mine
        new = combine(before, jax.tree.map(lambda part: part[at], everything))
        return jax.tree.map(lambda a, b: jnp.where(reached, a, b), new, before)

    return lax.fori_loop(0, devices, lap, start)


def conv_pair(padded, conv_forward, conv_reverse, length):
    reach = conv_forward.shape[0] - 1
    ahead = jnp.zeros((length, padded.shape[1]), jnp.float32)
    behind = jnp.zeros((length, padded.shape[1]), jnp.float32)
    for kernel_tap in range(reach + 1):
        ahead = ahead + conv_forward[kernel_tap] * padded[kernel_tap : kernel_tap + length]
        start = 2 * reach - kernel_tap
        behind = behind + conv_reverse[kernel_tap] * padded[start : start + length]
    return (jax.nn.silu(ahead).astype(jnp.bfloat16), jax.nn.silu(behind).astype(jnp.bfloat16))


def split_pieces(convolved):
    length = convolved.shape[0]
    inner = HEADS * HEAD_DIM
    values = convolved[:, :inner].reshape(length, HEADS, HEAD_DIM)
    keys = convolved[:, inner : inner + STATE]
    queries = convolved[:, inner + STATE :]
    return (values, keys, queries)


def block_terms(block_values, block_keys, block_queries, block_steps, decay_rate):
    log_steps = -decay_rate[:, None] * block_steps
    cumulative = jnp.cumsum(log_steps, axis=1)
    width = block_steps.shape[1]
    position = jnp.arange(width)
    causal = position[:, None] >= position[None, :]
    segment = jnp.where(causal[None], cumulative[:, :, None] - cumulative[:, None, :], -1e30)
    intersection = jnp.dot(block_queries, block_keys.T, preferred_element_type=jnp.float32)
    scores = (intersection[None] * jnp.exp(segment) * block_steps[:, None, :]).astype(jnp.bfloat16)
    within = jnp.einsum("hts,shp->thp", scores, block_values, preferred_element_type=jnp.float32)
    factors = block_steps * jnp.exp(cumulative[:, -1:] - cumulative)
    weighted = (block_values * factors.T[:, :, None]).astype(jnp.bfloat16)
    state = jnp.einsum("tn,thp->hpn", block_keys, weighted, preferred_element_type=jnp.float32)
    return (within, state, cumulative)


def local_pass(values, keys, queries, steps, decay_rate):
    block_count = values.shape[0] // GROUP
    value_blocks = values.reshape(block_count, GROUP, HEADS, HEAD_DIM)
    key_blocks = keys.reshape(block_count, GROUP, STATE)
    query_blocks = queries.reshape(block_count, GROUP, STATE)
    step_blocks = steps.reshape(HEADS, block_count, GROUP).transpose(1, 0, 2)
    within, states, cumulative = lax.map(
        lambda item: block_terms(item[0], item[1], item[2], item[3], decay_rate),
        (value_blocks, key_blocks, query_blocks, step_blocks),
    )
    ends = cumulative[:, :, -1]

    def advance(carry, item):
        return (jnp.exp(item[1])[:, None, None] * carry + item[0], carry)

    start_state = jnp.zeros((HEADS, HEAD_DIM, STATE), jnp.float32)
    total_state, entries = lax.scan(advance, start_state, (states, ends))
    offsets = jnp.cumsum(ends, axis=0) - ends
    total_decay = jnp.exp(jnp.sum(ends, axis=0))
    return (within, entries, cumulative, offsets, query_blocks, total_decay, total_state)


def finish(local_parts, carried):
    within, entries, cumulative, offsets, query_blocks = local_parts[:5]
    queries_wide = query_blocks.astype(jnp.float32)
    growth = jnp.exp(cumulative).transpose(0, 2, 1)[..., None]
    entries = entries + jnp.exp(offsets)[:, :, None, None] * carried[None]
    carried_term = jnp.einsum(
        "ctn,chpn->cthp", queries_wide, entries, precision=lax.Precision.HIGHEST
    )
    result = within + growth * carried_term
    return result.reshape(-1, HEADS, HEAD_DIM)


def combine(earlier, later):
    return (earlier[0] * later[0], later[0][:, None, None] * earlier[1] + later[1])


def per_device(
    mixer_input,
    gate_input,
    conv_forward,
    conv_reverse,
    step_size,
    decay_rate,
    skip_scale,
    norm_gain,
):
    length = mixer_input.shape[0]
    padded = with_halo(mixer_input, (("seq", 0),), WIDTH - 1)
    ahead, behind = conv_pair(padded, conv_forward, conv_reverse, length)
    values_ahead, keys_ahead, queries_ahead = split_pieces(ahead)
    values_behind, keys_behind, queries_behind = split_pieces(behind)
    forward_parts = local_pass(values_ahead, keys_ahead, queries_ahead, step_size, decay_rate)
    reverse_parts = local_pass(
        values_behind[::-1], keys_behind[::-1], queries_behind[::-1], step_size[:, ::-1], decay_rate
    )
    identity = (jnp.ones((HEADS,), jnp.float32), jnp.zeros((HEADS, HEAD_DIM, STATE), jnp.float32))
    forward_in = entering((forward_parts[5], forward_parts[6]), "seq", combine, identity, False)[1]
    reverse_in = entering((reverse_parts[5], reverse_parts[6]), "seq", combine, identity, True)[1]
    forward = finish(forward_parts, forward_in)
    reverse = finish(reverse_parts, reverse_in)[::-1]
    mixed = forward + reverse + skip_scale[None, :, None] * values_ahead
    gated = mixed.reshape(length, HEADS * HEAD_DIM) * jax.nn.silu(gate_input.astype(jnp.float32))
    scale = lax.rsqrt(jnp.mean(gated * gated, axis=-1, keepdims=True) + 1e-05)
    return (gated * scale * norm_gain).astype(jnp.bfloat16)


def solution(mesh):
    in_specs = (
        P(("row", "seq"), None),
        P(("row", "seq"), None),
        P(),
        P(),
        P(None, ("row", "seq")),
        P("row"),
        P(),
        P(),
    )
    out_specs = P(("row", "seq"), None)
    return jax.shard_map(
        per_device, mesh=mesh, in_specs=in_specs, out_specs=out_specs, check_vma=False
    )
```

profile of v0, /device:TPU:1, one launch (start us, length us, event | category | flops | bytes accessed | tf_op | source)
XLA Modules:
  0.0 483.8 jit_solution(3737897916042205043)
XLA Ops:
  7.6 3.3 collective-permute-start.1
  10.9 5.5 %collective-permute-start = (bf16[3,4352]{1,0:T(4,128)(2,1)S(1)}, bf16[3,4352]{1,0:T(4,128)(2,1)S(1)}, u32[]{:S(2)}, u32[]{:S(2)}) collective-permute-start(bf16[3,4352]{1,0:T(4,128)(2,1)S(1)} %get-tuple-element.390), channel_id=1, source_target_pairs={{0,1},{1,2},{2,3},{3,4},{4,5},{5,6},{6,7},{7,8},{8,9},{9,10},{10,1... | collective-permute-start | bytes 78344 | tf_op jit(solution)/shard_map/ppermute | solution.py:21
  20.6 9.6 %multiply_convert_fusion.4 = (bf16[256,4352]{1,0:T(8,128)(2,1)S(1)}, bf16[256,4352]{1,0:T(8,128)(2,1)}) fusion(bf16[256,4352]{1,0:T(8,128)(2,1)} %param.12, bf16[259,4352]{1,0:T(8,128)(2,1)S(1)} %constant_dynamic-update-slice_fusion, f32[4352]{0:T(1024)S(1)} %get-tuple-element.355, f32[4352]{0:T(1024)S(1)} %get-tuple-element.356, ...), kind=kLoop, calls=%fused_computation.30 | loop fusion | flops 44564480 | bytes 13534720 | tf_op jit(solution)/shard_map/convert_element_type | solution.py:56
  30.4 2.5 copy.39
  32.9 6.1 %rev.15 = bf16[256,64,64]{0,2,1:T(8,128)(2,1)} reverse(bf16[256,64,64]{0,2,1:T(8,128)(2,1)} %bitcast.89), dimensions={0} | reverse | bytes 4194304 | tf_op jit(solution)/shard_map/rev | solution.py:139
  39.0 3.8 fusion.39
  46.1 4.1 copy.34
  50.2 3.6 fusion.36
  54.0 22.2 %all-gather.2 = f32[16,64,1]{1,2,0:T(1,128)S(1)} all-gather(f32[1,64,1]{1,2,0:T(1,128)S(1)} %copy.43), channel_id=4, replica_groups=mesh['row'=8,'seq'=16] {'seq'}, dimensions={0}, use_global_device_ids=true | all-gather | bytes 4352 | tf_op jit(solution)/shard_map/all_gather | solution.py:32
  76.2 20.9 %all-gather = f32[16,64,1]{1,2,0:T(1,128)S(1)} all-gather(f32[1,64,1]{1,2,0:T(1,128)S(1)} %copy.38), channel_id=2, replica_groups=mesh['row'=8,'seq'=16] {'seq'}, dimensions={0}, use_global_device_ids=true | all-gather | bytes 4352 | tf_op jit(solution)/shard_map/all_gather | solution.py:32
  98.5 134.6 %all-gather.9.cloned.1.call-done = f32[1024,64,128]{2,1,0:T(8,128)} async-done(((f32[64,64,128]{2,1,0:T(8,128)}), f32[1024,64,128]{2,1,0:T(8,128)}) %all-gather.9.cloned.1.call-update) | async-done | bytes 33554448 | tf_op jit(solution)/shard_map/all_gather | solution.py:32
  233.1 63.8 %while.21 = (s32[]{:T(128)}, f32[64,64,128]{2,1,0:T(8,128)}, s32[]{:T(128)}, f32[16,64]{1,0:T(8,128)S(1)}, f32[16,64,64,128]{3,2,1,0:T(8,128)}, /*index=5*/s32[]{:T(128)}, s32[]{:T(128)}, s32[]{:T(128)}, s32[]{:T(128)}) while((s32[]{:T(128)}, f32[64,64,128]{2,1,0:T(8,128)}, s32[]{:T(128)}, f32[16,64]{1,0:T(8,128)S(1)}, ...), condition=%wide.region_7.8_spmd.clone, body=%wide.region_6.7_spmd.clone.sunk | while | flops 2097160 | bytes 6292399 | solution.py:45
  233.1 3.2 fusion.69
  236.4 3.9 fusion.69
  240.3 4.2 fusion.69
  244.5 4.4 fusion.69
  248.9 3.9 fusion.69
  252.8 3.9 fusion.69
  256.7 3.9 fusion.69
  260.5 3.9 fusion.69
  264.5 3.9 fusion.69
  268.4 3.9 fusion.69
  272.2 4.2 fusion.69
  276.4 3.9 fusion.69
  280.3 3.9 fusion.69
  284.1 3.9 fusion.69
  288.0 3.9 fusion.69
  291.9 5.0 %fusion.69 = f32[64,64,128]{2,1,0:T(8,128)} fusion(f32[16,64,64,128]{3,2,1,0:T(8,128)} %get-tuple-element.485, s32[]{:T(128)S(6)} %select_n.90, f32[64,64,128]{2,1,0:T(8,128)} %get-tuple-element.473, f32[64]{0:T(128)S(1)} %dynamic-slice_bitcast_fusion.5, pred[]{:T(512)S(6)} %compare.7, pred[]{:T(512)S(6)} %gt.12), kind=kLoop, calls=%fused_computation.4.clone.1 | loop fusion | flops 2097152 | bytes 6291718 | tf_op jit(solution)/shard_map/while/body/eval_jaxpr/jit(_where)/select_n | solution.py:43
  296.9 4.3 fusion.30
  301.2 6.3 %bitcast_add_fusion.2 = f32[256,64,64]{0,2,1:T(8,128)} fusion(f32[256,64,64]{0,2,1:T(8,128)S(1)} %fusion.30, bf16[256,64,64]{0,2,1:T(8,128)(2,1)S(1)} %copy-done.4, f32[64,256]{1,0:T(8,128)S(1)} %rev.18, f32[64,256]{1,0:T(8,128)S(1)} %copy_bitcast_fusion, f32[256,256]{1,0:T(8,128)S(1)} %fusion.55, pred[256,256]{1,0:T(8,128)(4,1)S(1)} %iota_compare_fusion, ...), kind=kOutput, calls=%fused_computation.38 | convolution fusion | flops 559939584 | bytes 11010048 | tf_op jit(solution)/shard_map/while/body/eval_jaxpr/hts,shp->thp/dot_general | solution.py:77
  307.5 7.2 %rev.19 = f32[256,64,64]{0,2,1:T(8,128)} reverse(f32[256,64,64]{0,2,1:T(8,128)} %bitcast_add_fusion.2), dimensions={0} | reverse | bytes 8388608 | tf_op jit(solution)/shard_map/rev | solution.py:145
  314.7 106.0 %all-gather.7.cloned.1.call-done = f32[1024,64,128]{2,1,0:T(8,128)} async-done(((f32[64,64,128]{2,1,0:T(8,128)}), f32[1024,64,128]{2,1,0:T(8,128)}) %all-gather.7.cloned.1.call-update) | async-done | bytes 33554448 | tf_op jit(solution)/shard_map/all_gather | solution.py:32
  420.7 34.0 %while.20 = (s32[]{:T(128)}, f32[64,64,128]{2,1,0:T(8,128)S(1)}, s32[]{:T(128)}, f32[16,64]{1,0:T(8,128)S(1)}, f32[16,64,64,128]{3,2,1,0:T(8,128)}, /*index=5*/s32[]{:T(128)}, s32[]{:T(128)}) while((s32[]{:T(128)}, f32[64,64,128]{2,1,0:T(8,128)S(1)}, s32[]{:T(128)}, f32[16,64]{1,0:T(8,128)S(1)}, f32[16,64,64,128]{3,2,1,0:T(8,128)}, ...), condition=%wide.region_3.4_spmd.clone, body=%wide.region_2.3_spmd.clone.sunk | while | flops 2097156 | bytes 6292337 | solution.py:45
  422.8 2.1 fusion.68
  425.0 2.1 fusion.68
  427.1 2.1 fusion.68
  429.2 2.1 fusion.68
  431.3 2.1 fusion.68
  433.5 2.1 fusion.68
  439.9 2.1 fusion.68
  442.0 2.1 fusion.68
  444.1 2.1 fusion.68
  446.2 2.1 fusion.68
  454.7 2.8 fusion.33
  457.6 6.6 %fusion.19 = f32[256,64,64]{0,2,1:T(8,128)} fusion(bf16[256,64,64]{0,2,1:T(8,128)(2,1)S(1)} %bitcast.88, f32[256,64,64]{0,2,1:T(8,128)S(1)} %copy-done.5, f32[256,64,64]{0,2,1:T(8,128)S(1)} %fusion.33, f32[64,256]{1,0:T(8,128)S(1)} %copy-done.6, f32[64,256]{1,0:T(8,128)S(1)} %copy_bitcast_fusion.1, f32[256,256]{1,0:T(8,128)S(1)} %fusion.47, ...), kind=kOutput, calls=%fused_computation.33 | convolution fusion | flops 564133888 | bytes 15204608 | tf_op jit(solution)/shard_map/while/body/eval_jaxpr/hts,shp->thp/dot_general | solution.py:77
  464.2 5.8 %copy.44 = f32[256,4096]{1,0:T(8,128)} copy(f32[256,4096]{0,1:T(8,128)} %bitcast.90) | data formatting | bytes 8388608 | tf_op jit(solution)/shard_map/reshape | solution.py:147
  470.0 3.9 multiply_reduce_fusion
  473.9 3.1 multiply_convert_fusion.6
  (113 shorter events, 22.9 us)
Async XLA Ops:
  6.5 11.7 %copy-start.10 = (f32[64]{0:T(128)S(1)}, f32[64]{0:T(128)}, u32[]{:S(2)}) copy-start(f32[64]{0:T(128)} %param.17) | copy-start | bytes 772
  6.5 11.7 %copy-start.6 = (f32[64,256]{1,0:T(8,128)S(1)}, f32[64,256]{1,0:T(8,128)}, u32[]{:S(2)}) copy-start(f32[64,256]{1,0:T(8,128)} %param.16) | copy-start | bytes 196612
  6.5 13.6 %copy-start.7 = (f32[4,4352]{1,0:T(4,128)S(1)}, f32[4,4352]{1,0:T(4,128)}, u32[]{:S(2)}) copy-start(f32[4,4352]{1,0:T(4,128)} %param.15) | copy-start | bytes 208900
  6.5 13.6 %copy-start.8 = (f32[4,4352]{1,0:T(4,128)S(1)}, f32[4,4352]{1,0:T(4,128)}, u32[]{:S(2)}) copy-start(f32[4,4352]{1,0:T(4,128)} %param.14) | copy-start | bytes 208900
  6.5 226.6 %all-gather.9.cloned.1.call-start = ((), (), s32[]{:S(2)}) async-start(), calls=%async_computation.1 | async-start | bytes 35651584 | tf_op jit(solution)/shard_map/all_gather | solution.py:32
  7.6 12.9 %collective-permute-start.1 = (bf16[3,4352]{1,0:T(4,128)(2,1)S(1)}, bf16[3,4352]{1,0:T(4,128)(2,1)S(1)}, u32[]{:S(2)}, u32[]{:S(2)}) collective-permute-start(bf16[3,4352]{1,0:T(4,128)(2,1)S(1)} %get-tuple-element.389), channel_id=1, source_target_pairs={{1,0},{2,1},{3,2},{4,3},{5,4},{6,5},{7,6},{8,7},{9,8},{10,9},{11,1... | collective-permute-start | bytes 78344 | tf_op jit(solution)/shard_map/ppermute | solution.py:23
  10.9 9.6 %collective-permute-start = (bf16[3,4352]{1,0:T(4,128)(2,1)S(1)}, bf16[3,4352]{1,0:T(4,128)(2,1)S(1)}, u32[]{:S(2)}, u32[]{:S(2)}) collective-permute-start(bf16[3,4352]{1,0:T(4,128)(2,1)S(1)} %get-tuple-element.390), channel_id=1, source_target_pairs={{0,1},{1,2},{2,3},{3,4},{4,5},{5,6},{6,7},{7,8},{8,9},{9,10},{10,1... | collective-permute-start | bytes 78344 | tf_op jit(solution)/shard_map/ppermute | solution.py:21
  39.0 5.6 %copy-start.1 = (bf16[256,4352]{1,0:T(8,128)(2,1)S(1)}, bf16[256,4352]{1,0:T(8,128)(2,1)}, u32[]{:S(2)}) copy-start(bf16[256,4352]{1,0:T(8,128)(2,1)} %get-tuple-element.388) | copy-start | bytes 6684676
  42.8 377.9 %all-gather.7.cloned.1.call-start = ((), (), s32[]{:S(2)}) async-start(), calls=%async_computation | async-start | bytes 35651584 | tf_op jit(solution)/shard_map/all_gather | solution.py:32
  296.9 4.3 copy-start.4
  454.7 2.9 copy-start.3
  454.7 2.9 copy-start.5
  454.7 2.9 copy-start.11
  464.2 5.8 %copy-start.2 = (bf16[256,4096]{1,0:T(8,128)(2,1)S(1)}, bf16[256,4096]{1,0:T(8,128)(2,1)}, u32[]{:S(2)}) copy-start(bf16[256,4096]{1,0:T(8,128)(2,1)} %param.13) | copy-start | bytes 6291460
  470.0 3.9 copy-start
  470.0 3.9 copy-start.9
Sparse Core Ops, SparseCore 0:
  43.0 190.1 all-gather.8
  235.5 185.1 all-gather.6
where the time goes:
time: 485 us; the launch traced here: 484 us
  waiting for transfers between devices  241 us (50%)
  other arithmetic  116 us (24%)
  blocking collectives  43.1 us (9%)
  local copies, waits for them, and re-layouts  32.4 us (7%)
  matrix products  28.6 us (6%)
  between operations  13.8 us (3%)
  starting transfers between devices  8.89 us (2%)
    all_gather x2, waiting for transfers between devices, entering(): everything = jax.tree.map(lambda part: lax.all_gather(part, axis), array)  241 us
    select_n x32, other arithmetic, lap(): return jax.tree.map(lambda a, b: jnp.where(reached, a, b), new, before)  96.9 us
    all_gather x2, blocking collectives, entering(): everything = jax.tree.map(lambda part: lax.all_gather(part, axis), array)  43.1 us
    dot_general x2, matrix products, block_terms(): jnp.einsum('hts,shp->thp', scores, block_values, preferred_element_type=j...  12.9 us
  transfers between devices with their start and end apart: 4, of which 2 were waited for; matrix products, arithmetic and copies ran while one was open for 20% of the time, Pallas kernels for 0%

commit v1 on v0

v1 whole, which is shorter than its diff:
```python
import functools

import jax
import jax.numpy as jnp
from jax import lax
from jax.experimental import pallas as pl
from jax.experimental.pallas import tpu as pltpu
from jax.sharding import PartitionSpec as P

HEADS = 64
HEAD_DIM = 64
STATE = 128
TOK = 256
SUB = 128
INNER = 4096
E = 4352
QUART = INNER // 4
CW = 512
HC = CW // HEAD_DIM
HALO = 16
MSG = 2 * STATE + 16
YMSG = STATE + 16
PIECES = 2
LOG2E = 1.4426950408889634
F32 = jnp.float32
BF16 = jnp.bfloat16
WF, WR, GF, GR, WV, GT = range(6)
MIB = 2**20


def dot(a, b, **kw):
    return jnp.dot(a, b, preferred_element_type=F32, **kw)


def shape(dtype, *dims):
    return jax.ShapeDtypeStruct(dims, dtype)


VMEM = pl.BlockSpec(memory_space=pltpu.VMEM)
HBM = pl.BlockSpec(memory_space=pltpu.HBM)


def vmem(dtype, *dims):
    return pltpu.VMEM(dims, dtype)


def call(kernel, name, outs, operands, params=(), scratch=(), limit=12, flops=10**8, moved=10**6, aliases=None):
    operands = [pltpu.with_memory_space_constraint(v, pltpu.VMEM) for v in operands]
    params = [pltpu.with_memory_space_constraint(v, pltpu.HBM) for v in params]
    return pl.pallas_call(
        kernel,
        name=name,
        in_specs=[VMEM] * len(operands) + [HBM] * len(params),
        out_specs=[HBM if isinstance(o, jax.ShapeDtypeStruct) else VMEM for o in outs],
        out_shape=outs,
        scratch_shapes=list(scratch),
        input_output_aliases=aliases or {},
        compiler_params=pltpu.CompilerParams(vmem_limit_bytes=limit * MIB),
        cost_estimate=pl.CostEstimate(flops=flops, bytes_accessed=moved, transcendentals=0),
    )(*operands, *params)


def place():
    at = lax.axis_index("seq")
    return at & 1, (at >> 1) & 1, at >> 2


def columns(start, width):
    return pl.ds(pl.multiple_of(start, 128), width)


def split2(x):
    hi = x.astype(BF16)
    lo = (x - hi.astype(F32)).astype(BF16)
    return hi, lo


def spread_matrix(start, width=CW):
    k = lax.broadcasted_iota(jnp.int32, (2 * HEADS, width), 0)
    col = lax.broadcasted_iota(jnp.int32, (2 * HEADS, width), 1)
    low = (k & (HEADS - 1)) * HEAD_DIM - start
    return jnp.where((col >= low) & (col < low + HEAD_DIM), 1.0, 0.0).astype(BF16)


def read_decay(rows):
    rows = rows.astype(F32)
    return rows[0:1] + rows[1:2]


def decay_rows(d):
    hi, lo = split2(d)
    none = jnp.zeros((14, d.shape[1]), F32)
    return jnp.concatenate([hi.astype(F32), lo.astype(F32), none], axis=0).astype(BF16)


def make_tables(step_t, decay, skip, table_ref, mcol_ref, mrow_ref, drow_ref):
    step = jnp.transpose(step_t)
    a = -decay * step
    row = lax.broadcasted_iota(jnp.int32, (TOK, TOK), 0)
    col = lax.broadcasted_iota(jnp.int32, (TOK, TOK), 1)
    tri = jnp.where((row >= col) & ((row >= SUB) == (col >= SUB)), 1.0, 0.0)
    cum = dot(tri, a, precision=lax.Precision.HIGHEST)
    excl = cum - a
    e0 = cum[SUB - 1 : SUB]
    e1 = cum[TOK - 1 : TOK]
    ends = jnp.concatenate([jnp.broadcast_to(e0, (SUB, HEADS)), jnp.broadcast_to(e1, (SUB, HEADS))], axis=0)
    zero = jnp.zeros_like(cum)

    def put(at, value):
        hi, lo = split2(value)
        table_ref[at] = jnp.concatenate([hi, lo], axis=1)

    put(WF, step * jnp.exp(jnp.minimum(ends - cum, zero)))
    put(WR, step * jnp.exp(excl))
    put(GF, jnp.exp(cum))
    put(GR, jnp.exp(jnp.minimum(ends - excl, zero)))
    put(WV, step * jnp.exp(-0.5 * a))
    put(GT, jnp.exp(0.5 * a))
    m = (cum - 0.5 * a) * LOG2E
    mcol_ref[...] = jnp.concatenate([m, zero], axis=1)
    mrow_ref[...] = jnp.transpose(m)
    h0, l0 = split2(jnp.exp(e0))
    h1, l1 = split2(jnp.exp(e1))
    hd, ld = split2(jnp.exp(e0 + e1))
    hs, ls = split2(skip)
    no = jnp.zeros_like(h0)
    wide = [
        jnp.concatenate([hd, no], axis=1).astype(F32),
        jnp.concatenate([no, ld], axis=1).astype(F32),
        jnp.zeros((6, 2 * HEADS), F32),
        jnp.concatenate([h0, l0], axis=1).astype(F32),
        jnp.concatenate([h1, l1], axis=1).astype(F32),
        jnp.concatenate([hs, ls], axis=1).astype(F32),
        jnp.zeros((5, 2 * HEADS), F32),
    ]
    drow_ref[...] = jnp.concatenate(wide, axis=0).astype(BF16)


def conv(x, cf, cr):
    rows = x.shape[0]
    back = pltpu.roll(x, 1, 0)
    fore = pltpu.roll(x, rows - 1, 0)
    h = cf[3:4] * x + cf[2:3] * back + pltpu.roll(cf[1:2] * x + cf[0:1] * back, 2, 0)
    g = cr[3:4] * x + cr[2:3] * fore + pltpu.roll(cr[1:2] * x + cr[0:1] * fore, rows - 2, 0)
    return h, g


def silu_of_half(h):
    return (h + h * jnp.tanh(h)).astype(BF16)


def copy_all(pairs, sems):
    copies = [pltpu.make_async_copy(src, dst, sems.at[k]) for k, (src, dst) in enumerate(pairs)]
    for copy in copies:
        copy.start()
    return copies


def quarter(k):
    c, z, y = place()
    return (c if k >= 2 else 1 - c) * 2 + (z if k & 1 else 1 - z)


def front_kernel(
    x_hbm, step_hbm, decay_hbm, skip_hbm, cf_hbm, cr_hbm,
    table_ref, mcol_ref, mrow_ref, drow_ref, x_ref, taps_ref, kq_ref, u0_ref, u2_ref,
    step_ref, decay_ref, skip_ref, cf_ref, cr_ref, sems,
):
    copies = copy_all(
        [
            (step_hbm, step_ref),
            (decay_hbm, decay_ref),
            (skip_hbm, skip_ref),
            (cf_hbm, cf_ref),
            (cr_hbm, cr_ref),
            (x_hbm, x_ref),
        ],
        sems,
    )
    for copy in copies[:3]:
        copy.wait()
    make_tables(step_ref[...], decay_ref[...], skip_ref[...], table_ref, mcol_ref, mrow_ref, drow_ref)
    for copy in copies[3:]:
        copy.wait()
    taps_ref[0:4] = cf_ref[...] * 0.5
    taps_ref[4:8] = cr_ref[...] * 0.5
    for ref, start in ((kq_ref, INNER), (u0_ref, quarter(0) * QUART), (u2_ref, quarter(2) * QUART)):

        def body(i, _):
            at = columns(start + i * 128, 128)
            cols = columns(i * 128, 128)
            h, g = conv(x_ref[:, at].astype(F32), taps_ref[0:4, at], taps_ref[4:8, at])
            ref[0, :, cols] = silu_of_half(h)
            ref[1, :, cols] = silu_of_half(g)
            return _

        lax.fori_loop(0, ref.shape[2] // 128, body, 0)


def make_front(x, step_size, decay_rate, skip_scale, cf, cr):
    return call(
        front_kernel,
        "front",
        [
            vmem(BF16, 6, TOK, 2 * HEADS),
            vmem(F32, TOK, 2 * HEADS),
            vmem(F32, HEADS, TOK),
            vmem(BF16, 16, 2 * HEADS),
            vmem(BF16, TOK, E),
            vmem(F32, 8, E),
            vmem(BF16, 2, TOK, 2 * STATE),
            vmem(BF16, 2, TOK, QUART),
            vmem(BF16, 2, TOK, QUART),
        ],
        (),
        (x, step_size, decay_rate.reshape(1, HEADS), skip_scale.reshape(1, HEADS), cf, cr),
        [
            pltpu.VMEM((HEADS, TOK), F32),
            pltpu.VMEM((1, HEADS), F32),
            pltpu.VMEM((1, HEADS), F32),
            pltpu.VMEM((4, E), F32),
            pltpu.VMEM((4, E), F32),
            pltpu.SemaphoreType.DMA((6,)),
        ],
    )


def edges(x_ref, core_ref, chip_ref, at):
    c, z, y = place()
    core, chip = core_ref[:, at].astype(F32), chip_ref[:, at].astype(F32)
    return jnp.where(c == 0, chip, core), jnp.where(c == 0, core, chip)


def repair(u_ref, x_ref, taps_ref, core_ref, chip_ref, start):
    def body(i, _):
        at = columns(start + i * 256, 256)
        cols = columns(i * 256, 256)
        prev, nxt = edges(x_ref, core_ref, chip_ref, at)
        cf, cr = taps_ref[0:4, at], taps_ref[4:8, at]
        h, _g = conv(jnp.concatenate([prev, x_ref[0:HALO, at].astype(F32)], axis=0), cf, cr)
        u_ref[0, 0:HALO, cols] = silu_of_half(h[HALO:])
        _h, g = conv(jnp.concatenate([x_ref[TOK - HALO : TOK, at].astype(F32), nxt], axis=0), cf, cr)
        u_ref[1, TOK - HALO : TOK, cols] = silu_of_half(g[:HALO])
        return _

    lax.fori_loop(0, u_ref.shape[2] // 256, body, 0)


def local_states(u_ref, kt_ref, table_ref, drow_ref, sub_ref, msg_ref, which, piece):
    spread = spread_matrix(quarter(which) * QUART + piece * CW)
    drow = dot(drow_ref[...], spread)
    d0, d1 = drow[8:9], drow[9:10]
    cols = slice(piece * CW, (piece + 1) * CW)

    def weighted(d, row, r):
        w = dot(table_ref[row, r : r + SUB], spread)
        return (u_ref[d, r : r + SUB, cols].astype(F32) * w).astype(BF16)

    f0 = dot(kt_ref[0, :, 0:SUB], weighted(0, WF, 0))
    f1 = dot(kt_ref[0, :, SUB:TOK], weighted(0, WF, SUB))
    r0 = dot(kt_ref[1, :, 0:SUB], weighted(1, WR, 0))
    r1 = dot(kt_ref[1, :, SUB:TOK], weighted(1, WR, SUB))
    fwd, rev = d1 * f0 + f1, r0 + d0 * r1
    sub_ref[0, :, cols] = f0.astype(BF16)
    sub_ref[1, :, cols] = r1.astype(BF16)
    msg_ref[0:STATE, cols] = fwd.astype(BF16)
    msg_ref[STATE : 2 * STATE, cols] = rev.astype(BF16)
    msg_ref[2 * STATE : MSG, cols] = drow.astype(BF16)
    return fwd, rev, drow


def joined(fwd, rev, drow, far_ref, chip_ref, piece):
    c, z, y = place()
    core0 = c == 0
    cols = slice(piece * CW, (piece + 1) * CW)
    dm = drow[0:1] + drow[1:2]
    do = read_decay(far_ref[2 * STATE : MSG, cols])
    one = jnp.ones_like(dm)
    am, ao = jnp.where(core0, do, one), jnp.where(core0, one, dm)
    chip_ref[0:STATE] = (am * fwd + ao * far_ref[0:STATE, cols].astype(F32)).astype(BF16)
    am, ao = jnp.where(core0, one, do), jnp.where(core0, dm, one)
    chip_ref[STATE : 2 * STATE] = (am * rev + ao * far_ref[STATE : 2 * STATE, cols].astype(F32)).astype(BF16)
    chip_ref[2 * STATE : MSG] = decay_rows(dm * do)


def first_kernel(
    kq_in, u_in, x_ref, taps_ref, core_ref, chip_ref, table_ref, drow_ref, kq_ref, u_ref, kt_ref, sub_ref, msg_ref
):
    repair(kq_ref, x_ref, taps_ref, core_ref, chip_ref, INNER)
    for d in range(2):
        kt_ref[d] = jnp.transpose(kq_ref[d, :, 0:STATE].astype(F32)).astype(BF16)
    repair(u_ref, x_ref, taps_ref, core_ref, chip_ref, quarter(0) * QUART)
    for piece in range(PIECES):
        local_states(u_ref, kt_ref, table_ref, drow_ref, sub_ref, msg_ref, 0, piece)


def partner_kernel(
    u_in, x_ref, taps_ref, core_ref, chip_ref, table_ref, drow_ref, kt_ref, far_ref, u_ref, sub_ref, msg_ref, *chip_refs
):
    repair(u_ref, x_ref, taps_ref, core_ref, chip_ref, quarter(2) * QUART)
    for piece in range(PIECES):
        state = local_states(u_ref, kt_ref, table_ref, drow_ref, sub_ref, msg_ref, 2, piece)
        joined(*state, far_ref, chip_refs[piece], piece)


def rest_kernel(
    x_ref, taps_ref, core_ref, chip_ref, table_ref, drow_ref, kt_ref, u1_ref, u3_ref, sub_ref, msg_ref
):
    for which, ref in ((1, u1_ref), (3, u3_ref)):

        def body(i, _):
            at = columns(quarter(which) * QUART + i * 128, 128)
            cols = columns(i * 128, 128)
            prev, nxt = edges(x_ref, core_ref, chip_ref, at)
            x = jnp.concatenate([prev[HALO - 8 :], x_ref[:, at].astype(F32), nxt[:8]], axis=0)
            h, g = conv(x, taps_ref[0:4, at], taps_ref[4:8, at])
            ref[0, :, cols] = silu_of_half(h[8 : TOK + 8])
            ref[1, :, cols] = silu_of_half(g[8 : TOK + 8])
            return _

        lax.fori_loop(0, QUART // 128, body, 0)
    for piece in range(PIECES):
        local_states(u1_ref, kt_ref, table_ref, drow_ref, sub_ref, msg_ref, 1, piece)


def own_kernel(u_ref, table_ref, drow_ref, kt_ref, far_ref, sub_ref, msg_ref, *chip_refs):
    for piece in range(PIECES):
        state = local_states(u_ref, kt_ref, table_ref, drow_ref, sub_ref, msg_ref, 3, piece)
        joined(*state, far_ref, chip_refs[piece], piece)


U = vmem(BF16, 2, TOK, QUART)
SUBSTATE = vmem(BF16, 2, STATE, QUART)
MESSAGE = vmem(BF16, MSG, QUART)
CHIP = [vmem(BF16, MSG, CW)] * PIECES


def group_kernel(keep_ref, got_ref, *outs):
    c, z, y = place()
    z0 = z == 0
    dm, do = read_decay(keep_ref[2 * STATE : MSG]), read_decay(got_ref[2 * STATE : MSG])
    one = jnp.ones_like(dm)
    am, ao = jnp.where(z0, do, one), jnp.where(z0, one, dm)
    fwd = (am * keep_ref[0:STATE].astype(F32) + ao * got_ref[0:STATE].astype(F32)).astype(BF16)
    am, ao = jnp.where(z0, one, do), jnp.where(z0, dm, one)
    rows = slice(STATE, 2 * STATE)
    rev = (am * keep_ref[rows].astype(F32) + ao * got_ref[rows].astype(F32)).astype(BF16)
    decay = decay_rows(dm * do)
    for k in range(1, 4):
        outs[k - 1][0:STATE] = jnp.where(y + k < 4, fwd, rev)
        outs[k - 1][STATE:YMSG] = decay


def make_group(keep, got):
    return call(group_kernel, "group", [vmem(BF16, YMSG, keep.shape[1])] * 3, (keep, got))


def entries_kernel(keep_ref, got_ref, r1_ref, r2_ref, r3_ref, mine_ref, back_ref):
    c, z, y = place()
    z0 = z == 0
    r = [ref[0:STATE].astype(F32) for ref in (r1_ref, r2_ref, r3_ref)]
    d = [read_decay(ref[STATE:YMSG]) for ref in (r1_ref, r2_ref, r3_ref)]
    zero = jnp.zeros_like(r[0])
    ef = jnp.where(y >= 3, r[2], zero)
    ef = jnp.where(y >= 2, r[1] + d[1] * ef, zero)
    ef = jnp.where(y >= 1, r[0] + d[0] * ef, zero)
    er = jnp.where(y <= 0, r[0], zero)
    er = jnp.where(y <= 1, r[1] + d[1] * er, zero)
    er = jnp.where(y <= 2, r[2] + d[2] * er, zero)
    dm, do = read_decay(keep_ref[2 * STATE : MSG]), read_decay(got_ref[2 * STATE : MSG])
    df = jnp.where(z0, dm, do)
    tf = jnp.where(z0, keep_ref[0:STATE].astype(F32), got_ref[0:STATE].astype(F32))
    second_f = df * ef + tf
    dr = jnp.where(z0, do, dm)
    rows = slice(STATE, 2 * STATE)
    tr = jnp.where(z0, got_ref[rows].astype(F32), keep_ref[rows].astype(F32))
    first_r = dr * er + tr
    mine_ref[0] = jnp.where(z0, ef, second_f).astype(BF16)
    mine_ref[1] = jnp.where(z0, first_r, er).astype(BF16)
    back_ref[0] = jnp.where(z0, second_f, ef).astype(BF16)
    back_ref[1] = jnp.where(z0, er, first_r).astype(BF16)


def make_entries(keep, got, arrived):
    return call(entries_kernel, "entries", [vmem(BF16, 2, STATE, keep.shape[1])] * 2, (keep, got, *arrived))


def within_kernel(pair, ua_ref, ub_ref, kq_ref, table_ref, mcol_ref, mrow_ref, drow_ref, gate_hbm, gain_hbm, *refs):
    if pair == 0:
        outa_ref, outb_ref, gate_ref, gain_ref, qk_ref, sems = refs
        copies = copy_all([(gate_hbm, gate_ref), (gain_hbm, gain_ref)], sems)
    else:
        outa_ref, outb_ref, qk_ref = refs
    row = lax.broadcasted_iota(jnp.int32, (SUB, SUB), 0)
    col = lax.broadcasted_iota(jnp.int32, (SUB, SUB), 1)
    low = lax.broadcasted_iota(jnp.int32, (SUB, 2 * HEAD_DIM), 1) < HEAD_DIM
    for b in range(2):
        rows = slice(b * SUB, (b + 1) * SUB)
        for d in range(2):
            keys = kq_ref[d, rows, 0:STATE]
            queries = kq_ref[d, rows, STATE : 2 * STATE]
            prod = lax.dot_general(queries, keys, (((1,), (1,)), ((), ())), preferred_element_type=F32)
            qk_ref[d, b] = jnp.where((row >= col) if d == 0 else (row <= col), prod, 0.0)

    for u_ref, out_ref, which in ((ua_ref, outa_ref, pair), (ub_ref, outb_ref, pair + 2)):

        def body(i, _):
            chunk = quarter(which) * (QUART // CW) + i
            spread = spread_matrix(chunk * CW)
            skip = dot(drow_ref[...], spread)[10:11]
            mcol = pltpu.roll(mcol_ref[...], 2 * HEADS - HC * chunk, 1)
            mrow = mrow_ref[pl.ds(pl.multiple_of(chunk * HC, HC), HC), :]
            for b in range(2):
                rows = slice(b * SUB, (b + 1) * SUB)
                wv = dot(table_ref[WV, rows], spread)
                gt = dot(table_ref[GT, rows], spread)
                for two in range(HC // 2):
                    cols = slice(two * 128, (two + 1) * 128)
                    at = columns(i * CW + two * 128, 128)
                    up = u_ref[0, rows, at].astype(F32)
                    xf = (up * wv[:, cols]).astype(BF16)
                    xb = (u_ref[1, rows, at].astype(F32) * wv[:, cols]).astype(BF16)
                    none = jnp.zeros_like(xf)
                    left, right = [], []
                    for h in range(2):
                        k = two * 2 + h
                        diff = mcol[rows, k : k + 1] - mrow[k : k + 1, rows]
                        decay = jnp.exp2(-jnp.abs(diff))
                        left += [(decay * qk_ref[0, b]).astype(BF16), (decay * qk_ref[1, b]).astype(BF16)]
                        keep = low if h == 0 else ~low
                        right += [jnp.where(keep, xf, none), jnp.where(keep, xb, none)]
                    res = dot(jnp.concatenate(left, axis=1), jnp.concatenate(right, axis=0))
                    out_ref[rows, at] = (res * gt[:, cols] + up * skip[:, cols]).astype(BF16)
            return _

        lax.fori_loop(0, QUART // CW, body, 0)
    if pair == 0:
        for copy in copies:
            copy.wait()


def make_within(pair, ua, ub, kq, table, mcol, mrow, drow, gate, gain):
    outs = [vmem(BF16, TOK, QUART)] * 2
    scratch = [pltpu.VMEM((2, 2, SUB, SUB), F32)]
    if pair == 0:
        outs += [vmem(BF16, TOK, INNER), vmem(F32, 1, INNER)]
        scratch += [pltpu.SemaphoreType.DMA((2,))]
    return call(
        functools.partial(within_kernel, pair),
        "within_a" if pair == 0 else "within_b",
        outs,
        (ua, ub, kq, table, mcol, mrow, drow),
        (gate, gain),
        scratch,
    )


def finish_part(which, piece, entry_ref, far_ref, sub_ref, within_ref, shared, gated_ref, start, square):
    kq_ref, table_ref, drow_ref, gate_ref = shared
    c, z, y = place()
    core0 = c == 0
    at = columns(quarter(which) * QUART + piece * CW, CW)
    cols = slice(piece * CW, (piece + 1) * CW)
    spread = spread_matrix(quarter(which) * QUART + piece * CW)
    drow = dot(drow_ref[...], spread)
    d0, d1 = drow[8:9], drow[9:10]
    moved = read_decay(far_ref[2 * STATE : MSG, cols])
    state = far_ref[pl.ds(pl.multiple_of((1 - c) * STATE, STATE), STATE), cols].astype(F32)
    one = jnp.ones_like(moved)
    none = jnp.zeros_like(state)
    ef = jnp.where(core0, one, moved) * entry_ref[0].astype(F32) + jnp.where(core0, none, state)
    er = jnp.where(core0, moved, one) * entry_ref[1].astype(F32) + jnp.where(core0, state, none)
    inside = [
        (ef.astype(BF16), (er * d1 + sub_ref[1, :, cols].astype(F32)).astype(BF16)),
        ((ef * d0 + sub_ref[0, :, cols].astype(F32)).astype(BF16), er.astype(BF16)),
    ]
    for b in range(2):
        rows = slice(b * SUB, (b + 1) * SUB)
        cf = dot(kq_ref[0, rows, STATE : 2 * STATE], inside[b][0])
        cr = dot(kq_ref[1, rows, STATE : 2 * STATE], inside[b][1])
        gf = dot(table_ref[GF, rows], spread)
        gr = dot(table_ref[GR, rows], spread)
        mixed = within_ref[rows, cols].astype(F32) + gf * cf + gr * cr
        half = gate_ref[rows, at].astype(F32) * 0.5
        gated = mixed * (half + half * jnp.tanh(half))
        gated_ref[rows, start : start + CW] = gated
        sq = gated * gated
        for k in range(0, CW, 128):
            part = sq[:, k : k + 128]
            square[b] = part if square[b] is None else square[b] + part


def finish_kernel(whiches, piece, last, before, *refs):
    refs = list(refs)
    parts = [[refs.pop(0) for _ in range(4)] for _ in whiches]
    shared = [refs.pop(0) for _ in range(4)]
    square = [None, None]
    if last:
        gain_ref = refs.pop(0)
        earlier = [(refs.pop(0), list(done)) for done in before]
        squares = [refs.pop(0) for _ in before]
        out_hbm, gated_ref, out_ref, sems = refs
    else:
        gated_ref, square_ref = refs
    for k, (which, part) in enumerate(zip(whiches, parts)):
        finish_part(which, piece, *part, shared, gated_ref, k * CW, square)
    if not last:
        square_ref[0:SUB] = square[0]
        square_ref[SUB:TOK] = square[1]
        return
    pieces = [(gated_ref, 0, whiches[0], piece)]
    for ref, done in earlier:
        pieces += [(ref, k * CW, which, p) for k, (which, p) in enumerate(done)]
    step = 64
    copies = []
    for b in range(2):
        total = square[b]
        for ref in squares:
            total = total + ref[b * SUB : (b + 1) * SUB]
        mean = jnp.sum(total, axis=1, keepdims=True) * (1.0 / INNER)
        scale = lax.rsqrt(mean + 1e-05)
        for r in range(0, SUB, step):
            rows = slice(b * SUB + r, b * SUB + r + step)
            for ref, start, which, p in pieces:
                at = columns(quarter(which) * QUART + p * CW, CW)
                out_ref[rows, at] = (
                    ref[rows, start : start + CW] * scale[r : r + step] * gain_ref[:, at]
                ).astype(BF16)
            copies.append(pltpu.make_async_copy(out_ref.at[rows], out_hbm.at[rows], sems.at[len(copies)]))
            copies[-1].start()
    for copy in copies:
        copy.wait()


def make_finish(whiches, piece, parts, shared, gain=None, before=()):
    last = gain is not None
    operands = [v for part in parts for v in part] + list(shared)
    scratch = []
    if last:
        operands += [gain] + [done[1][0] for done in before] + [done[1][1] for done in before]
        outs = [shape(BF16, TOK, INNER)]
        scratch = [pltpu.VMEM((TOK, CW), F32), pltpu.VMEM((TOK, INNER), BF16), pltpu.SemaphoreType.DMA((4,))]
    else:
        outs = [vmem(F32, TOK, CW * len(whiches)), vmem(F32, TOK, 128)]
    kernel = functools.partial(finish_kernel, whiches, piece, last, [done[0] for done in before])
    name = "finish_" + "".join(map(str, whiches)) + "ab"[piece]
    return call(kernel, name, outs, operands, (), scratch)


def per_device(mixer_input, gate_input, conv_forward, conv_reverse, step_size, decay_rate, skip_scale, norm_gain):
    n = lax.axis_size("seq")
    barrier = lax.optimization_barrier
    c = lax.axis_index("seq") & 1

    def send(v, perm):
        return lax.ppermute(v, "seq", perm)

    core = [(i, i ^ 1) for i in range(n)]
    zswap = [(i, i ^ 2) for i in range(n)]
    chips = [(i, i + 1) for i in range(1, n - 1, 2)] + [(i + 1, i) for i in range(1, n - 1, 2)]

    head, tail = mixer_input[:HALO], mixer_input[TOK - HALO :]
    halo_core = send(jnp.where(c == 0, tail, head), core)
    halo_chip = send(jnp.where(c == 0, head, tail), chips)
    table, mcol, mrow, drow, x, taps, kq, u0, u2 = make_front(
        mixer_input, step_size, decay_rate, skip_scale, conv_forward, conv_reverse
    )
    halo = (x, taps, halo_core, halo_chip)
    kq, u0, kt, sub0, msg0 = call(
        first_kernel,
        "states_0",
        [vmem(BF16, 2, TOK, 2 * STATE), U, vmem(BF16, 2, STATE, TOK), SUBSTATE, MESSAGE],
        (kq, u0, *halo, table, drow),
        aliases={0: 0, 1: 1},
    )
    far2 = send(msg0, core)
    u2, sub2, msg2, *zsend = call(
        partner_kernel,
        "states_2",
        [U, SUBSTATE, MESSAGE, *CHIP],
        (u2, *halo, table, drow, kt, far2),
        aliases={0: 0},
    )
    got = [send(m, zswap) for m in zsend]
    x, zsend = barrier((x, zsend))
    halo = (x, taps, halo_core, halo_chip)
    u1, u3, sub1, msg1 = call(rest_kernel, "states_1", [U, U, SUBSTATE, MESSAGE], (*halo, table, drow, kt))
    far3 = send(msg1, core)
    sub3, msg3, *keep = call(own_kernel, "states_3", [SUBSTATE, MESSAGE, *CHIP], (u3, table, drow, kt, far3))
    far0 = send(msg2, core)
    far1 = send(msg3, core)

    arrived, mine, back = [], [], []
    for p in range(PIECES):
        msgs = make_group(keep[p], got[p])
        arrived.append([send(m, [(i, (i + 4 * k) % n) for i in range(n)]) for k, m in enumerate(msgs, 1)])
    gate, gain = gate_input, norm_gain.reshape(1, INNER)
    tables = (kq, table, mcol, mrow, drow)
    u0, u2, msgs = barrier((u0, u2, msgs))
    w0, w2, gate, gain = make_within(0, u0, u2, *tables, gate, gain)
    arrived[0], w0, w2 = barrier((arrived[0], w0, w2))
    for p in range(PIECES):
        m, b = make_entries(keep[p], got[p], arrived[p])
        mine.append(m)
        back.append(b)
    entry2 = [send(b, zswap) for b in back]
    entry1 = [send(m, core) for m in mine]
    u1, u3, back = barrier((u1, u3, back))
    w1, w3 = make_within(1, u1, u3, *tables, gate_input, norm_gain.reshape(1, INNER))
    shared = (kq, table, drow, gate)
    done = []
    for p in range(PIECES):
        parts = [(mine[p], far3, sub3, w3), (entry1[p], far1, sub1, w1)]
        done.append(([(3, p), (1, p)], make_finish((3, 1), p, parts, shared)))
    entry2[0], *rest = barrier((entry2[0], *[v for d in done for v in d[1]]))
    done = [(d[0], rest[2 * k : 2 * k + 2]) for k, d in enumerate(done)]
    entry0 = [send(e, core) for e in entry2]
    parts = [(entry2[0], far2, sub2, w2), (entry0[0], far0, sub0, w0)]
    done.append(([(2, 0), (0, 0)], make_finish((2, 0), 0, parts, shared)))
    done.append(([(2, 1)], make_finish((2,), 1, [(entry2[1], far2, sub2, w2)], shared)))
    (out,) = make_finish((0,), 1, [(entry0[1], far0, sub0, w0)], shared, gain, done)
    return out


def solution(mesh):
    in_specs = (
        P(("row", "seq"), None),
        P(("row", "seq"), None),
        P(),
        P(),
        P(None, ("row", "seq")),
        P("row"),
        P(),
        P(),
    )
    out_specs = P(("row", "seq"), None)
    return jax.shard_map(per_device, mesh=mesh, in_specs=in_specs, out_specs=out_specs, check_vma=False)
```

time: 485 us -> 77.5 us (0.16)
  waiting for transfers between devices: 241 us -> 15.6 us
  other arithmetic: 116 us -> 1 us
  blocking collectives: 43.1 us -> 0 us
  local copies, waits for them, and re-layouts: 32.4 us -> 0 us
  Pallas kernels: 0 us -> 28.9 us
  matrix products: 28.6 us -> 0 us
  starting transfers between devices: 8.89 us -> 31.4 us
  between operations: 13.8 us -> 0.38 us
    all_gather x2 -> x0, waiting for transfers between devices: 241 us -> none  [entering(): everything = jax.tree.map(lambda part: lax.all_gather(part, axis), array)]
    select_n x32 -> x1, other arithmetic: 96.9 us -> 1 us  [per_device(): halo_chip = send(jnp.where(c == 0, head, tail), chips)]
    all_gather x2 -> x0, blocking collectives: 43.1 us -> none  [entering(): everything = jax.tree.map(lambda part: lax.all_gather(part, axis), array)]
    pallas_call x0 -> x16, Pallas kernels: none -> 28.9 us  [call(): pl.pallas_call(kernel, name=name, in_specs=[VMEM] * len(operands) + [HBM]...]
    dot_general x8 -> x0, matrix products: 28.6 us -> none  [the longest x2 12.9 us: block_terms(): jnp.einsum('hts,shp->thp', scores, block_values, preferred_element_type=j...]
    ppermute x2 -> x20, starting transfers between devices: 8.82 us -> 31.4 us  [send(): return lax.ppermute(v, 'seq', perm)]
    ppermute x2 -> x20, waiting for transfers between devices: 0.01 us -> 15.6 us  [send(): return lax.ppermute(v, 'seq', perm)]
    rev x5 -> x0, local copies, waits for them, and re-layouts: 13.6 us -> none  [the longest x1 7.24 us: per_device(): reverse = finish(reverse_parts, reverse_in)[::-1]]
  transfers between devices with their start and end apart: 4 -> 20, of which waited for: 2 -> 6; matrix products, arithmetic and copies ran while one was open for 20% -> 0% of each run, Pallas kernels for 0% -> 25%
where the time goes in v1:
time: 77.5 us; the launch traced here: 77.3 us
  starting transfers between devices  31.4 us (41%)
  Pallas kernels  28.9 us (37%)
  waiting for transfers between devices  15.6 us (20%)
  other arithmetic  1 us (1%)
    ppermute x20, starting transfers between devices, send(): return lax.ppermute(v, 'seq', perm)  31.4 us
    pallas_call x16, Pallas kernels, call(): pl.pallas_call(kernel, name=name, in_specs=[VMEM] * len(operands) + [HBM]...  28.9 us
    ppermute x20, waiting for transfers between devices, send(): return lax.ppermute(v, 'seq', perm)  15.6 us
  transfers between devices with their start and end apart: 20, of which 6 were waited for; matrix products, arithmetic and copies ran while one was open for 0% of the time, Pallas kernels for 25%

profile of v1, /device:TPU:1, one launch (start us, length us, event | category | flops | bytes accessed | tf_op | source)
XLA Modules:
  0.0 77.3 jit_solution(16130399892463720300)
XLA Ops:
  0.0 1.0 %broadcast_select_fusion = (bf16[16,4352]{1,0:T(8,128)(2,1)S(1)}, bf16[16,4352]{1,0:T(8,128)(2,1)S(1)}) fusion(pred[]{:T(512)S(6)} %eq.4, bf16[256,4352]{1,0:T(8,128)(2,1)} %x_hbm.1), kind=kLoop, calls=%fused_computation | loop fusion | flops 139264 | bytes 557057 | tf_op jit(solution)/shard_map/jit(_where)/select_n | solution.py:564
  1.0 1.5 %collective-permute-start = (bf16[16,4352]{1,0:T(8,128)(2,1)S(1)}, bf16[16,4352]{1,0:T(8,128)(2,1)S(1)}, u32[]{:S(2)}, u32[]{:S(2)}) collective-permute-start(bf16[16,4352]{1,0:T(8,128)(2,1)S(1)} %get-tuple-element.138), channel_id=1, source_target_pairs={{0,1},{1,0},{2,3},{3,2},{4,5},{5,4},{6,7},{7,6},{8,9},{9,8},{10,11... | collective-permute-start | bytes 417800 | tf_op jit(solution)/shard_map/ppermute | solution.py:556
  2.5 5.5 %collective-permute-start.1 = (bf16[16,4352]{1,0:T(8,128)(2,1)S(1)}, bf16[16,4352]{1,0:T(8,128)(2,1)S(1)}, u32[]{:S(2)}, u32[]{:S(2)}) collective-permute-start(bf16[16,4352]{1,0:T(8,128)(2,1)S(1)} %get-tuple-element.137), channel_id=1, source_target_pairs={{1,2},{3,4},{5,6},{7,8},{9,10},{11,12},{13,14},{2,1},{4,3},{6,5},{... | collective-permute-start | bytes 417800 | tf_op jit(solution)/shard_map/ppermute | solution.py:556
  8.0 4.4 %front.1 = (bf16[6,256,128]{2,1,0:T(8,128)(2,1)S(1)}, f32[256,128]{1,0:T(8,128)S(1)}, f32[64,256]{1,0:T(8,128)S(1)}, bf16[16,128]{1,0:T(8,128)(2,1)S(1)}, bf16[2...) custom-call(bf16[256,4352]{1,0:T(8,128)(2,1)} %x_hbm.1, ...), custom_call_target="tpu_custom_call" | custom-call | flops 100000000 | bytes 1000000 | tf_op jit(solution)/shard_map/front/pallas_call | solution.py:50
  12.5 1.9 %states_0.1 = (bf16[2,256,256]{2,1,0:T(8,128)(2,1)S(1)}, bf16[2,256,1024]{2,1,0:T(8,128)(2,1)S(1)}, bf16[2,128,256]{2,1,0:T(8,128)(2,1)S(1)}, bf16[2,128,1024]{2,1,0:T(8,128)(2,1)S(1)}, bf16[272,1024]{1,0:T(8,128)(2,1)S(1)}) custom-call(bf16[2,256,256]{2,1,0:T(8,128)(2,1)S(1)} %get-tuple-element.76.kq_in, ...), custom_call_target="tpu_custom_call", output_to_operand_aliasing={{0}: (0, {}), {1}: (1, {})} | custom-call | flops 100000000 | bytes 1000000 | tf_op jit(solution)/shard_map/states_0/pallas_call | solution.py:50
  14.3 0.1 collective-permute-start.2
  14.4 1.9 %collective-permute-done.2.far_ref.refs_1_ = bf16[272,1024]{1,0:T(8,128)(2,1)S(1)} collective-permute-done((bf16[272,1024]{1,0:T(8,128)(2,1)S(1)}, bf16[272,1024]{1,0:T(8,128)(2,1)S(1)}, u32[]{:S(2)}, u32[]{:S(2)}) %collective-permute-start.2) | collective-permute-done | bytes 557088 | tf_op jit(solution)/shard_map/ppermute | solution.py:556
  16.4 1.7 %states_2.1 = (bf16[2,256,1024]{2,1,0:T(8,128)(2,1)S(1)}, bf16[2,128,1024]{2,1,0:T(8,128)(2,1)S(1)}, bf16[272,1024]{1,0:T(8,128)(2,1)S(1)}, bf16[272,512]{1,0:T(8,128)(2,1)S(1)}, bf16[272,512]{1,0:T(8,128)(2,1)S(1)}) custom-call(bf16[2,256,1024]{2,1,0:T(8,128)(2,1)S(1)} %get-tuple-element.72.u_in, ...), custom_call_target="tpu_custom_call", output_to_operand_aliasing={{0}: (0, {})} | custom-call | flops 100000000 | bytes 1000000 | tf_op jit(solution)/shard_map/states_2/pallas_call | solution.py:50
  18.1 4.1 %states_1.1 = (bf16[2,256,1024]{2,1,0:T(8,128)(2,1)S(1)}, bf16[2,256,1024]{2,1,0:T(8,128)(2,1)S(1)}, bf16[2,128,1024]{2,1,0:T(8,128)(2,1)S(1)}, bf16[272,1024]{1,0:T(8,128)(2,1)S(1)}) custom-call(bf16[256,4352]{1,0:T(8,128)(2,1)S(1)} %get-tuple-element.82.x_ref, f32[8,4352]{1,0:T(8,128)S(1)} %get-tuple-element.73.taps_ref, ...), custom_call_target="tpu_custom_call" | custom-call | flops 100000000 | bytes 1000000 | tf_op jit(solution)/shard_map/states_1/pallas_call | solution.py:50
  22.2 0.2 collective-permute-start.3
  22.4 2.5 %collective-permute-start.4 = (bf16[272,512]{1,0:T(8,128)(2,1)S(1)}, bf16[272,512]{1,0:T(8,128)(2,1)S(1)}, u32[]{:S(2)}, u32[]{:S(2)}) collective-permute-start(bf16[272,512]{1,0:T(8,128)(2,1)S(1)} %get-tuple-element.81), channel_id=1, source_target_pairs={{0,2},{1,3},{2,0},{3,1},{4,6},{5,7},{6,4},{7,5},{8,10},{9,11},{10,... | collective-permute-start | bytes 835592 | tf_op jit(solution)/shard_map/ppermute | solution.py:556
  24.9 0.5 collective-permute-start.11
  25.4 0.0 collective-permute-done.3.far_ref.refs_1_
  25.4 1.6 %states_3.1 = (bf16[2,128,1024]{2,1,0:T(8,128)(2,1)S(1)}, bf16[272,1024]{1,0:T(8,128)(2,1)S(1)}, bf16[272,512]{1,0:T(8,128)(2,1)S(1)}, bf16[272,512]{1,0:T(8,128)(2,1)S(1)}) custom-call(bf16[2,256,1024]{2,1,0:T(8,128)(2,1)S(1)} %get-tuple-element.116.u_ref.ub_ref, bf16[6,256,128]{2,1,0:T(8,128)(2,1)S(1)} %get-tuple-element.74.table_ref.refs_9_.refs_5_, ...), custom_call_target="tpu_custom_call" | custom-call | flops 100000000 | bytes 1000000 | tf_op jit(solution)/shard_map/states_3/pallas_call | solution.py:50
  27.0 4.8 %collective-permute-done.4.got_ref = bf16[272,512]{1,0:T(8,128)(2,1)S(1)} collective-permute-done((bf16[272,512]{1,0:T(8,128)(2,1)S(1)}, bf16[272,512]{1,0:T(8,128)(2,1)S(1)}, u32[]{:S(2)}, u32[]{:S(2)}) %collective-permute-start.4) | collective-permute-done | bytes 278560 | tf_op jit(solution)/shard_map/ppermute | solution.py:556
  31.8 0.1 group.2
  32.0 1.8 %collective-permute-start.5 = (bf16[144,512]{1,0:T(8,128)(2,1)S(1)}, bf16[144,512]{1,0:T(8,128)(2,1)S(1)}, u32[]{:S(2)}, u32[]{:S(2)}) collective-permute-start(bf16[144,512]{1,0:T(8,128)(2,1)S(1)} %get-tuple-element.86), channel_id=1, source_target_pairs={{0,4},{1,5},{2,6},{3,7},{4,8},{5,9},{6,10},{7,11},{8,12},{9,13},{1... | collective-permute-start | bytes 442376 | tf_op jit(solution)/shard_map/ppermute | solution.py:556
  33.8 2.9 %collective-permute-start.6 = (bf16[144,512]{1,0:T(8,128)(2,1)S(1)}, bf16[144,512]{1,0:T(8,128)(2,1)S(1)}, u32[]{:S(2)}, u32[]{:S(2)}) collective-permute-start(bf16[144,512]{1,0:T(8,128)(2,1)S(1)} %get-tuple-element.87), channel_id=1, source_target_pairs={{0,8},{1,9},{2,10},{3,11},{4,12},{5,13},{6,14},{7,15},{8,0},{9,1},... | collective-permute-start | bytes 442376 | tf_op jit(solution)/shard_map/ppermute | solution.py:556
  36.7 0.8 %collective-permute-start.7 = (bf16[144,512]{1,0:T(8,128)(2,1)S(1)}, bf16[144,512]{1,0:T(8,128)(2,1)S(1)}, u32[]{:S(2)}, u32[]{:S(2)}) collective-permute-start(bf16[144,512]{1,0:T(8,128)(2,1)S(1)} %get-tuple-element.88), channel_id=1, source_target_pairs={{0,12},{1,13},{2,14},{3,15},{4,0},{5,1},{6,2},{7,3},{8,4},{9,5},{1... | collective-permute-start | bytes 442376 | tf_op jit(solution)/shard_map/ppermute | solution.py:556
  37.5 2.3 %collective-permute-start.17 = (bf16[272,1024]{1,0:T(8,128)(2,1)S(1)}, bf16[272,1024]{1,0:T(8,128)(2,1)S(1)}, u32[]{:S(2)}, u32[]{:S(2)}) collective-permute-start(bf16[272,1024]{1,0:T(8,128)(2,1)S(1)} %get-tuple-element.118), channel_id=1, source_target_pairs={{0,1},{1,0},{2,3},{3,2},{4,5},{5,4},{6,7},{7,6},{8,9},{9,8},{10,11... | collective-permute-start | bytes 1671176 | tf_op jit(solution)/shard_map/ppermute | solution.py:556
  39.8 0.0 collective-permute-done.5.r1_ref
  39.8 2.1 %collective-permute-done.6.r2_ref = bf16[144,512]{1,0:T(8,128)(2,1)S(1)} collective-permute-done((bf16[144,512]{1,0:T(8,128)(2,1)S(1)}, bf16[144,512]{1,0:T(8,128)(2,1)S(1)}, u32[]{:S(2)}, u32[]{:S(2)}) %collective-permute-start.6) | collective-permute-done | bytes 147488 | tf_op jit(solution)/shard_map/ppermute | solution.py:556
  42.0 0.6 collective-permute-done.7.r3_ref
  42.6 0.3 entries.2
  42.9 2.2 %collective-permute-start.18 = (bf16[2,128,512]{2,1,0:T(8,128)(2,1)S(1)}, bf16[2,128,512]{2,1,0:T(8,128)(2,1)S(1)}, u32[]{:S(2)}, u32[]{:S(2)}) collective-permute-start(bf16[2,128,512]{2,1,0:T(8,128)(2,1)S(1)} %get-tuple-element.123.refs_0_), channel_id=1, source_target_pairs={{0,1},{1,0},{2,3},{3,2},{4,5},{5,4},{6,7},{7,6},{8,9},{9,8},{10,11... | collective-permute-start | bytes 786440 | tf_op jit(solution)/shard_map/ppermute | solution.py:556
  45.1 0.0 collective-permute-done.11.got_ref
  45.1 0.1 group.3
  45.2 1.0 %collective-permute-start.12 = (bf16[144,512]{1,0:T(8,128)(2,1)S(1)}, bf16[144,512]{1,0:T(8,128)(2,1)S(1)}, u32[]{:S(2)}, u32[]{:S(2)}) collective-permute-start(bf16[144,512]{1,0:T(8,128)(2,1)S(1)} %get-tuple-element.93), channel_id=1, source_target_pairs={{0,4},{1,5},{2,6},{3,7},{4,8},{5,9},{6,10},{7,11},{8,12},{9,13},{1... | collective-permute-start | bytes 442376 | tf_op jit(solution)/shard_map/ppermute | solution.py:556
  46.3 2.1 %collective-permute-start.13 = (bf16[144,512]{1,0:T(8,128)(2,1)S(1)}, bf16[144,512]{1,0:T(8,128)(2,1)S(1)}, u32[]{:S(2)}, u32[]{:S(2)}) collective-permute-start(bf16[144,512]{1,0:T(8,128)(2,1)S(1)} %get-tuple-element.94), channel_id=1, source_target_pairs={{0,8},{1,9},{2,10},{3,11},{4,12},{5,13},{6,14},{7,15},{8,0},{9,1},... | collective-permute-start | bytes 442376 | tf_op jit(solution)/shard_map/ppermute | solution.py:556
  48.4 1.0 %collective-permute-start.14 = (bf16[144,512]{1,0:T(8,128)(2,1)S(1)}, bf16[144,512]{1,0:T(8,128)(2,1)S(1)}, u32[]{:S(2)}, u32[]{:S(2)}) collective-permute-start(bf16[144,512]{1,0:T(8,128)(2,1)S(1)} %get-tuple-element.95), channel_id=1, source_target_pairs={{0,12},{1,13},{2,14},{3,15},{4,0},{5,1},{6,2},{7,3},{8,4},{9,5},{1... | collective-permute-start | bytes 442376 | tf_op jit(solution)/shard_map/ppermute | solution.py:556
  49.4 2.6 %collective-permute-done.12.r1_ref = bf16[144,512]{1,0:T(8,128)(2,1)S(1)} collective-permute-done((bf16[144,512]{1,0:T(8,128)(2,1)S(1)}, bf16[144,512]{1,0:T(8,128)(2,1)S(1)}, u32[]{:S(2)}, u32[]{:S(2)}) %collective-permute-start.12) | collective-permute-done | bytes 147488 | tf_op jit(solution)/shard_map/ppermute | solution.py:556
  52.0 0.8 %collective-permute-start.10 = (bf16[272,1024]{1,0:T(8,128)(2,1)S(1)}, bf16[272,1024]{1,0:T(8,128)(2,1)S(1)}, u32[]{:S(2)}, u32[]{:S(2)}) collective-permute-start(bf16[272,1024]{1,0:T(8,128)(2,1)S(1)} %get-tuple-element.90), channel_id=1, source_target_pairs={{0,1},{1,0},{2,3},{3,2},{4,5},{5,4},{6,7},{7,6},{8,9},{9,8},{10,11... | collective-permute-start | bytes 1671176 | tf_op jit(solution)/shard_map/ppermute | solution.py:556
  52.8 3.8 %within_a.1 = (bf16[256,1024]{1,0:T(8,128)(2,1)S(1)}, bf16[256,1024]{1,0:T(8,128)(2,1)S(1)}, bf16[256,4096]{1,0:T(8,128)(2,1)S(1)}, f32[1,4096]{1,0:T(1,128)S(1)}) custom-call(bf16[2,256,1024]{2,1,0:T(8,128)(2,1)S(1)} %get-tuple-element.98.ua_ref, bf16[2,256,1024]{2,1,0:T(8,128)(2,1)S(1)} %get-tuple-element.99.ub_ref, ...), custom_call_target="tpu_custom_call" | custom-call | flops 100000000 | bytes 1000000 | tf_op jit(solution)/shard_map/within_a/pallas_call | solution.py:50
  56.6 0.0 collective-permute-done.13.r2_ref
  56.6 0.0 collective-permute-done.14.r3_ref
  56.7 0.3 entries.3
  57.0 0.1 collective-permute-start.16
  57.1 1.7 %collective-permute-start.15 = (bf16[2,128,512]{2,1,0:T(8,128)(2,1)S(1)}, bf16[2,128,512]{2,1,0:T(8,128)(2,1)S(1)}, u32[]{:S(2)}, u32[]{:S(2)}) collective-permute-start(bf16[2,128,512]{2,1,0:T(8,128)(2,1)S(1)} %get-tuple-element.111), channel_id=1, source_target_pairs={{0,2},{1,3},{2,0},{3,1},{4,6},{5,7},{6,4},{7,5},{8,10},{9,11},{10,... | collective-permute-start | bytes 786440 | tf_op jit(solution)/shard_map/ppermute | solution.py:556
  58.8 1.4 %collective-permute-start.8 = (bf16[2,128,512]{2,1,0:T(8,128)(2,1)S(1)}, bf16[2,128,512]{2,1,0:T(8,128)(2,1)S(1)}, u32[]{:S(2)}, u32[]{:S(2)}) collective-permute-start(bf16[2,128,512]{2,1,0:T(8,128)(2,1)S(1)} %get-tuple-element.89), channel_id=1, source_target_pairs={{0,2},{1,3},{2,0},{3,1},{4,6},{5,7},{6,4},{7,5},{8,10},{9,11},{10,... | collective-permute-start | bytes 786440 | tf_op jit(solution)/shard_map/ppermute | solution.py:556
  60.1 3.8 %within_b.1 = (bf16[256,1024]{1,0:T(8,128)(2,1)S(1)}, bf16[256,1024]{1,0:T(8,128)(2,1)S(1)}) custom-call(bf16[2,256,1024]{2,1,0:T(8,128)(2,1)S(1)} %get-tuple-element.115.ua_ref, bf16[2,256,1024]{2,1,0:T(8,128)(2,1)S(1)} %get-tuple-element.116.u_ref.ub_ref, bf16[2,256,256]{2,1,0:T(8,128)(2,1)S(1)} %get-tuple-element.100.kq_ref.refs_8_.refs_4_, ...), custom_call_target="tpu_custom_call" | custom-call | flops 100000000 | bytes 1000000 | tf_op jit(solution)/shard_map/within_b/pallas_call | solution.py:50
  63.9 1.3 %finish_31b.1 = (f32[256,1024]{1,0:T(8,128)S(1)}, f32[256,128]{1,0:T(8,128)S(1)}) custom-call(bf16[2,128,512]{2,1,0:T(8,128)(2,1)S(1)} %get-tuple-element.123.refs_0_, bf16[272,1024]{1,0:T(8,128)(2,1)S(1)} %collective-permute-done.3.far_ref.refs_1_, bf16[2,128,1024]{2,1,0:T(8,128)(2,1)S(1)} %get-tuple-element.113.refs_2_, ...), custom_call_target="tpu_custom_call" | custom-call | flops 100000000 | bytes 1000000 | tf_op jit(solution)/shard_map/finish_31b/pallas_call | solution.py:50
  65.2 1.3 %finish_31a.1 = (f32[256,1024]{1,0:T(8,128)S(1)}, f32[256,128]{1,0:T(8,128)S(1)}) custom-call(bf16[2,128,512]{2,1,0:T(8,128)(2,1)S(1)} %get-tuple-element.112.refs_0_, bf16[272,1024]{1,0:T(8,128)(2,1)S(1)} %collective-permute-done.3.far_ref.refs_1_, bf16[2,128,1024]{2,1,0:T(8,128)(2,1)S(1)} %get-tuple-element.113.refs_2_, ...), custom_call_target="tpu_custom_call" | custom-call | flops 100000000 | bytes 1000000 | tf_op jit(solution)/shard_map/finish_31a/pallas_call | solution.py:50
  66.5 1.7 %collective-permute-start.19 = (bf16[2,128,512]{2,1,0:T(8,128)(2,1)S(1)}, bf16[2,128,512]{2,1,0:T(8,128)(2,1)S(1)}, u32[]{:S(2)}, u32[]{:S(2)}) collective-permute-start(bf16[2,128,512]{2,1,0:T(8,128)(2,1)S(1)} %collective-permute-done.15.refs_0_), channel_id=1, source_target_pairs={{0,1},{1,0},{2,3},{3,2},{4,5},{5,4},{6,7},{7,6},{8,9},{9,8},{10,11... | collective-permute-start | bytes 786440 | tf_op jit(solution)/shard_map/ppermute | solution.py:556
  68.2 3.5 %collective-permute-done.8.refs_0_ = bf16[2,128,512]{2,1,0:T(8,128)(2,1)S(1)} collective-permute-done((bf16[2,128,512]{2,1,0:T(8,128)(2,1)S(1)}, bf16[2,128,512]{2,1,0:T(8,128)(2,1)S(1)}, u32[]{:S(2)}, u32[]{:S(2)}) %collective-permute-start.8) | collective-permute-done | bytes 262176 | tf_op jit(solution)/shard_map/ppermute | solution.py:556
  71.8 1.3 %collective-permute-start.9 = (bf16[2,128,512]{2,1,0:T(8,128)(2,1)S(1)}, bf16[2,128,512]{2,1,0:T(8,128)(2,1)S(1)}, u32[]{:S(2)}, u32[]{:S(2)}) collective-permute-start(bf16[2,128,512]{2,1,0:T(8,128)(2,1)S(1)} %collective-permute-done.8.refs_0_), channel_id=1, source_target_pairs={{0,1},{1,0},{2,3},{3,2},{4,5},{5,4},{6,7},{7,6},{8,9},{9,8},{10,11... | collective-permute-start | bytes 786440 | tf_op jit(solution)/shard_map/ppermute | solution.py:556
  73.0 0.7 finish_2b.1
  73.7 1.3 %finish_20a.1 = (f32[256,1024]{1,0:T(8,128)S(1)}, f32[256,128]{1,0:T(8,128)S(1)}) custom-call(bf16[2,128,512]{2,1,0:T(8,128)(2,1)S(1)} %collective-permute-done.15.refs_0_, bf16[272,1024]{1,0:T(8,128)(2,1)S(1)} %collective-permute-done.2.far_ref.refs_1_, bf16[2,128,1024]{2,1,0:T(8,128)(2,1)S(1)} %get-tuple-element.129.refs_2_, ...), custom_call_target="tpu_custom_call" | custom-call | flops 100000000 | bytes 1000000 | tf_op jit(solution)/shard_map/finish_20a/pallas_call | solution.py:50
  75.0 2.2 %finish_0b.1 = bf16[256,4096]{1,0:T(8,128)(2,1)} custom-call(bf16[2,128,512]{2,1,0:T(8,128)(2,1)S(1)} %collective-permute-done.9.refs_0_, bf16[272,1024]{1,0:T(8,128)(2,1)S(1)} %collective-permute-done.10.refs_5_.refs_1_, bf16[2,128,1024]{2,1,0:T(8,128)(2,1)S(1)} %get-tuple-element.91.refs_6_.refs_2_, ...), custom_call_target="tpu_custom_call" | custom-call | flops 100000000 | bytes 1000000 | tf_op jit(solution)/shard_map/finish_0b/pallas_call | solution.py:50
  (9 shorter events, 0.0 us)
Async XLA Ops:
  1.0 11.4 %collective-permute-start = (bf16[16,4352]{1,0:T(8,128)(2,1)S(1)}, bf16[16,4352]{1,0:T(8,128)(2,1)S(1)}, u32[]{:S(2)}, u32[]{:S(2)}) collective-permute-start(bf16[16,4352]{1,0:T(8,128)(2,1)S(1)} %get-tuple-element.138), channel_id=1, source_target_pairs={{0,1},{1,0},{2,3},{3,2},{4,5},{5,4},{6,7},{7,6},{8,9},{9,8},{10,11... | collective-permute-start | bytes 417800 | tf_op jit(solution)/shard_map/ppermute | solution.py:556
  2.5 10.0 %collective-permute-start.1 = (bf16[16,4352]{1,0:T(8,128)(2,1)S(1)}, bf16[16,4352]{1,0:T(8,128)(2,1)S(1)}, u32[]{:S(2)}, u32[]{:S(2)}) collective-permute-start(bf16[16,4352]{1,0:T(8,128)(2,1)S(1)} %get-tuple-element.137), channel_id=1, source_target_pairs={{1,2},{3,4},{5,6},{7,8},{9,10},{11,12},{13,14},{2,1},{4,3},{6,5},{... | collective-permute-start | bytes 417800 | tf_op jit(solution)/shard_map/ppermute | solution.py:556
  14.3 2.0 %collective-permute-start.2 = (bf16[272,1024]{1,0:T(8,128)(2,1)S(1)}, bf16[272,1024]{1,0:T(8,128)(2,1)S(1)}, u32[]{:S(2)}, u32[]{:S(2)}) collective-permute-start(bf16[272,1024]{1,0:T(8,128)(2,1)S(1)} %get-tuple-element.79), channel_id=1, source_target_pairs={{0,1},{1,0},{2,3},{3,2},{4,5},{5,4},{6,7},{7,6},{8,9},{9,8},{10,11... | collective-permute-start | bytes 1671176 | tf_op jit(solution)/shard_map/ppermute | solution.py:556
  22.2 3.2 %collective-permute-start.3 = (bf16[272,1024]{1,0:T(8,128)(2,1)S(1)}, bf16[272,1024]{1,0:T(8,128)(2,1)S(1)}, u32[]{:S(2)}, u32[]{:S(2)}) collective-permute-start(bf16[272,1024]{1,0:T(8,128)(2,1)S(1)} %get-tuple-element.84), channel_id=1, source_target_pairs={{0,1},{1,0},{2,3},{3,2},{4,5},{5,4},{6,7},{7,6},{8,9},{9,8},{10,11... | collective-permute-start | bytes 1671176 | tf_op jit(solution)/shard_map/ppermute | solution.py:556
  22.4 9.4 %collective-permute-start.4 = (bf16[272,512]{1,0:T(8,128)(2,1)S(1)}, bf16[272,512]{1,0:T(8,128)(2,1)S(1)}, u32[]{:S(2)}, u32[]{:S(2)}) collective-permute-start(bf16[272,512]{1,0:T(8,128)(2,1)S(1)} %get-tuple-element.81), channel_id=1, source_target_pairs={{0,2},{1,3},{2,0},{3,1},{4,6},{5,7},{6,4},{7,5},{8,10},{9,11},{10,... | collective-permute-start | bytes 835592 | tf_op jit(solution)/shard_map/ppermute | solution.py:556
  24.9 20.2 %collective-permute-start.11 = (bf16[272,512]{1,0:T(8,128)(2,1)S(1)}, bf16[272,512]{1,0:T(8,128)(2,1)S(1)}, u32[]{:S(2)}, u32[]{:S(2)}) collective-permute-start(bf16[272,512]{1,0:T(8,128)(2,1)S(1)} %get-tuple-element.80), channel_id=1, source_target_pairs={{0,2},{1,3},{2,0},{3,1},{4,6},{5,7},{6,4},{7,5},{8,10},{9,11},{10,... | collective-permute-start | bytes 835592 | tf_op jit(solution)/shard_map/ppermute | solution.py:556
  32.0 7.9 %collective-permute-start.5 = (bf16[144,512]{1,0:T(8,128)(2,1)S(1)}, bf16[144,512]{1,0:T(8,128)(2,1)S(1)}, u32[]{:S(2)}, u32[]{:S(2)}) collective-permute-start(bf16[144,512]{1,0:T(8,128)(2,1)S(1)} %get-tuple-element.86), channel_id=1, source_target_pairs={{0,4},{1,5},{2,6},{3,7},{4,8},{5,9},{6,10},{7,11},{8,12},{9,13},{1... | collective-permute-start | bytes 442376 | tf_op jit(solution)/shard_map/ppermute | solution.py:556
  33.8 8.1 %collective-permute-start.6 = (bf16[144,512]{1,0:T(8,128)(2,1)S(1)}, bf16[144,512]{1,0:T(8,128)(2,1)S(1)}, u32[]{:S(2)}, u32[]{:S(2)}) collective-permute-start(bf16[144,512]{1,0:T(8,128)(2,1)S(1)} %get-tuple-element.87), channel_id=1, source_target_pairs={{0,8},{1,9},{2,10},{3,11},{4,12},{5,13},{6,14},{7,15},{8,0},{9,1},... | collective-permute-start | bytes 442376 | tf_op jit(solution)/shard_map/ppermute | solution.py:556
  36.7 5.9 %collective-permute-start.7 = (bf16[144,512]{1,0:T(8,128)(2,1)S(1)}, bf16[144,512]{1,0:T(8,128)(2,1)S(1)}, u32[]{:S(2)}, u32[]{:S(2)}) collective-permute-start(bf16[144,512]{1,0:T(8,128)(2,1)S(1)} %get-tuple-element.88), channel_id=1, source_target_pairs={{0,12},{1,13},{2,14},{3,15},{4,0},{5,1},{6,2},{7,3},{8,4},{9,5},{1... | collective-permute-start | bytes 442376 | tf_op jit(solution)/shard_map/ppermute | solution.py:556
  37.5 26.4 %collective-permute-start.17 = (bf16[272,1024]{1,0:T(8,128)(2,1)S(1)}, bf16[272,1024]{1,0:T(8,128)(2,1)S(1)}, u32[]{:S(2)}, u32[]{:S(2)}) collective-permute-start(bf16[272,1024]{1,0:T(8,128)(2,1)S(1)} %get-tuple-element.118), channel_id=1, source_target_pairs={{0,1},{1,0},{2,3},{3,2},{4,5},{5,4},{6,7},{7,6},{8,9},{9,8},{10,11... | collective-permute-start | bytes 1671176 | tf_op jit(solution)/shard_map/ppermute | solution.py:556
  42.9 15.8 %collective-permute-start.18 = (bf16[2,128,512]{2,1,0:T(8,128)(2,1)S(1)}, bf16[2,128,512]{2,1,0:T(8,128)(2,1)S(1)}, u32[]{:S(2)}, u32[]{:S(2)}) collective-permute-start(bf16[2,128,512]{2,1,0:T(8,128)(2,1)S(1)} %get-tuple-element.123.refs_0_), channel_id=1, source_target_pairs={{0,1},{1,0},{2,3},{3,2},{4,5},{5,4},{6,7},{7,6},{8,9},{9,8},{10,11... | collective-permute-start | bytes 786440 | tf_op jit(solution)/shard_map/ppermute | solution.py:556
  45.2 6.7 %collective-permute-start.12 = (bf16[144,512]{1,0:T(8,128)(2,1)S(1)}, bf16[144,512]{1,0:T(8,128)(2,1)S(1)}, u32[]{:S(2)}, u32[]{:S(2)}) collective-permute-start(bf16[144,512]{1,0:T(8,128)(2,1)S(1)} %get-tuple-element.93), channel_id=1, source_target_pairs={{0,4},{1,5},{2,6},{3,7},{4,8},{5,9},{6,10},{7,11},{8,12},{9,13},{1... | collective-permute-start | bytes 442376 | tf_op jit(solution)/shard_map/ppermute | solution.py:556
  46.3 10.4 %collective-permute-start.13 = (bf16[144,512]{1,0:T(8,128)(2,1)S(1)}, bf16[144,512]{1,0:T(8,128)(2,1)S(1)}, u32[]{:S(2)}, u32[]{:S(2)}) collective-permute-start(bf16[144,512]{1,0:T(8,128)(2,1)S(1)} %get-tuple-element.94), channel_id=1, source_target_pairs={{0,8},{1,9},{2,10},{3,11},{4,12},{5,13},{6,14},{7,15},{8,0},{9,1},... | collective-permute-start | bytes 442376 | tf_op jit(solution)/shard_map/ppermute | solution.py:556
  48.4 8.3 %collective-permute-start.14 = (bf16[144,512]{1,0:T(8,128)(2,1)S(1)}, bf16[144,512]{1,0:T(8,128)(2,1)S(1)}, u32[]{:S(2)}, u32[]{:S(2)}) collective-permute-start(bf16[144,512]{1,0:T(8,128)(2,1)S(1)} %get-tuple-element.95), channel_id=1, source_target_pairs={{0,12},{1,13},{2,14},{3,15},{4,0},{5,1},{6,2},{7,3},{8,4},{9,5},{1... | collective-permute-start | bytes 442376 | tf_op jit(solution)/shard_map/ppermute | solution.py:556
  52.0 21.7 %collective-permute-start.10 = (bf16[272,1024]{1,0:T(8,128)(2,1)S(1)}, bf16[272,1024]{1,0:T(8,128)(2,1)S(1)}, u32[]{:S(2)}, u32[]{:S(2)}) collective-permute-start(bf16[272,1024]{1,0:T(8,128)(2,1)S(1)} %get-tuple-element.90), channel_id=1, source_target_pairs={{0,1},{1,0},{2,3},{3,2},{4,5},{5,4},{6,7},{7,6},{8,9},{9,8},{10,11... | collective-permute-start | bytes 1671176 | tf_op jit(solution)/shard_map/ppermute | solution.py:556
  57.0 8.2 %collective-permute-start.16 = (bf16[2,128,512]{2,1,0:T(8,128)(2,1)S(1)}, bf16[2,128,512]{2,1,0:T(8,128)(2,1)S(1)}, u32[]{:S(2)}, u32[]{:S(2)}) collective-permute-start(bf16[2,128,512]{2,1,0:T(8,128)(2,1)S(1)} %get-tuple-element.112.refs_0_), channel_id=1, source_target_pairs={{0,1},{1,0},{2,3},{3,2},{4,5},{5,4},{6,7},{7,6},{8,9},{9,8},{10,11... | collective-permute-start | bytes 786440 | tf_op jit(solution)/shard_map/ppermute | solution.py:556
  57.1 9.4 %collective-permute-start.15 = (bf16[2,128,512]{2,1,0:T(8,128)(2,1)S(1)}, bf16[2,128,512]{2,1,0:T(8,128)(2,1)S(1)}, u32[]{:S(2)}, u32[]{:S(2)}) collective-permute-start(bf16[2,128,512]{2,1,0:T(8,128)(2,1)S(1)} %get-tuple-element.111), channel_id=1, source_target_pairs={{0,2},{1,3},{2,0},{3,1},{4,6},{5,7},{6,4},{7,5},{8,10},{9,11},{10,... | collective-permute-start | bytes 786440 | tf_op jit(solution)/shard_map/ppermute | solution.py:556
  58.8 13.0 %collective-permute-start.8 = (bf16[2,128,512]{2,1,0:T(8,128)(2,1)S(1)}, bf16[2,128,512]{2,1,0:T(8,128)(2,1)S(1)}, u32[]{:S(2)}, u32[]{:S(2)}) collective-permute-start(bf16[2,128,512]{2,1,0:T(8,128)(2,1)S(1)} %get-tuple-element.89), channel_id=1, source_target_pairs={{0,2},{1,3},{2,0},{3,1},{4,6},{5,7},{6,4},{7,5},{8,10},{9,11},{10,... | collective-permute-start | bytes 786440 | tf_op jit(solution)/shard_map/ppermute | solution.py:556
  66.5 7.1 %collective-permute-start.19 = (bf16[2,128,512]{2,1,0:T(8,128)(2,1)S(1)}, bf16[2,128,512]{2,1,0:T(8,128)(2,1)S(1)}, u32[]{:S(2)}, u32[]{:S(2)}) collective-permute-start(bf16[2,128,512]{2,1,0:T(8,128)(2,1)S(1)} %collective-permute-done.15.refs_0_), channel_id=1, source_target_pairs={{0,1},{1,0},{2,3},{3,2},{4,5},{5,4},{6,7},{7,6},{8,9},{9,8},{10,11... | collective-permute-start | bytes 786440 | tf_op jit(solution)/shard_map/ppermute | solution.py:556
  71.8 3.2 %collective-permute-start.9 = (bf16[2,128,512]{2,1,0:T(8,128)(2,1)S(1)}, bf16[2,128,512]{2,1,0:T(8,128)(2,1)S(1)}, u32[]{:S(2)}, u32[]{:S(2)}) collective-permute-start(bf16[2,128,512]{2,1,0:T(8,128)(2,1)S(1)} %collective-permute-done.8.refs_0_), channel_id=1, source_target_pairs={{0,1},{1,0},{2,3},{3,2},{4,5},{5,4},{6,7},{7,6},{8,9},{9,8},{10,11... | collective-permute-start | bytes 786440 | tf_op jit(solution)/shard_map/ppermute | solution.py:556

commit v2 on v1

--- a/solution.py
+++ b/solution.py
@@ -44,7 +44,7 @@
     return pltpu.VMEM(dims, dtype)
 
 
-def call(kernel, name, outs, operands, params=(), scratch=(), limit=12, flops=10**8, moved=10**6, aliases=None):
+def call(kernel, name, outs, operands, params=(), scratch=(), limit=12, us=1.0, aliases=None):
     operands = [pltpu.with_memory_space_constraint(v, pltpu.VMEM) for v in operands]
     params = [pltpu.with_memory_space_constraint(v, pltpu.HBM) for v in params]
     return pl.pallas_call(
@@ -56,7 +56,7 @@
         scratch_shapes=list(scratch),
         input_output_aliases=aliases or {},
         compiler_params=pltpu.CompilerParams(vmem_limit_bytes=limit * MIB),
-        cost_estimate=pl.CostEstimate(flops=flops, bytes_accessed=moved, transcendentals=0),
+        cost_estimate=pl.CostEstimate(flops=int(us * 1e8), bytes_accessed=int(us * 3e5), transcendentals=0),
     )(*operands, *params)
 
 
@@ -161,9 +161,21 @@
     return (c if k >= 2 else 1 - c) * 2 + (z if k & 1 else 1 - z)
 
 
+def conv_inside(x_ref, taps_ref, u_ref, start):
+    def body(i, _):
+        at = columns(start + i * 128, 128)
+        cols = columns(i * 128, 128)
+        h, g = conv(x_ref[:, at].astype(F32), taps_ref[0:4, at], taps_ref[4:8, at])
+        u_ref[0, :, cols] = silu_of_half(h)
+        u_ref[1, :, cols] = silu_of_half(g)
+        return _
+
+    lax.fori_loop(0, u_ref.shape[2] // 128, body, 0)
+
+
 def front_kernel(
-    x_hbm, step_hbm, decay_hbm, skip_hbm, cf_hbm, cr_hbm,
-    table_ref, mcol_ref, mrow_ref, drow_ref, x_ref, taps_ref, kq_ref, u0_ref, u2_ref,
+    after_ref, x_hbm, step_hbm, decay_hbm, skip_hbm, cf_hbm, cr_hbm,
+    x_ref, table_ref, mcol_ref, mrow_ref, drow_ref, taps_ref, kq_ref, u0_ref,
     step_ref, decay_ref, skip_ref, cf_ref, cr_ref, sems,
 ):
     copies = copy_all(
@@ -171,9 +183,9 @@
             (step_hbm, step_ref),
             (decay_hbm, decay_ref),
             (skip_hbm, skip_ref),
+            (x_hbm, x_ref),
             (cf_hbm, cf_ref),
             (cr_hbm, cr_ref),
-            (x_hbm, x_ref),
         ],
         sems,
     )
@@ -184,35 +196,40 @@
         copy.wait()
     taps_ref[0:4] = cf_ref[...] * 0.5
     taps_ref[4:8] = cr_ref[...] * 0.5
-    for ref, start in ((kq_ref, INNER), (u0_ref, quarter(0) * QUART), (u2_ref, quarter(2) * QUART)):
-
-        def body(i, _):
-            at = columns(start + i * 128, 128)
-            cols = columns(i * 128, 128)
-            h, g = conv(x_ref[:, at].astype(F32), taps_ref[0:4, at], taps_ref[4:8, at])
-            ref[0, :, cols] = silu_of_half(h)
-            ref[1, :, cols] = silu_of_half(g)
-            return _
-
-        lax.fori_loop(0, ref.shape[2] // 128, body, 0)
-
-
-def make_front(x, step_size, decay_rate, skip_scale, cf, cr):
+    conv_inside(x_ref, taps_ref, kq_ref, INNER)
+    conv_inside(x_ref, taps_ref, u0_ref, quarter(0) * QUART)
+
+
+def edge_kernel(x_hbm, to_core_ref, to_chip_ref, sems):
+    c, z, y = place()
+    first, end = x_hbm.at[0:HALO], x_hbm.at[TOK - HALO : TOK]
+
+    @pl.when(c == 0)
+    def _():
+        for copy in copy_all([(end, to_core_ref), (first, to_chip_ref)], sems):
+            copy.wait()
+
+    @pl.when(c == 1)
+    def _():
+        for copy in copy_all([(first, to_core_ref), (end, to_chip_ref)], sems):
+            copy.wait()
+
+
+def make_front(after, x, step_size, decay_rate, skip_scale, cf, cr):
     return call(
         front_kernel,
         "front",
         [
+            vmem(BF16, TOK, E),
             vmem(BF16, 6, TOK, 2 * HEADS),
             vmem(F32, TOK, 2 * HEADS),
             vmem(F32, HEADS, TOK),
             vmem(BF16, 16, 2 * HEADS),
-            vmem(BF16, TOK, E),
             vmem(F32, 8, E),
             vmem(BF16, 2, TOK, 2 * STATE),
             vmem(BF16, 2, TOK, QUART),
-            vmem(BF16, 2, TOK, QUART),
         ],
-        (),
+        (after,),
         (x, step_size, decay_rate.reshape(1, HEADS), skip_scale.reshape(1, HEADS), cf, cr),
         [
             pltpu.VMEM((HEADS, TOK), F32),
@@ -223,6 +240,10 @@
             pltpu.SemaphoreType.DMA((6,)),
         ],
     )
+
+
+def conv_kernel(x_ref, taps_ref, u1_ref):
+    conv_inside(x_ref, taps_ref, u1_ref, quarter(1) * QUART)
 
 
 def edges(x_ref, core_ref, chip_ref, at):
@@ -246,7 +267,10 @@
     lax.fori_loop(0, u_ref.shape[2] // 256, body, 0)
 
 
-def local_states(u_ref, kt_ref, table_ref, drow_ref, sub_ref, msg_ref, which, piece):
+BASE = {(which, piece): (which % 2) * QUART + piece * CW for which in range(4) for piece in range(PIECES)}
+
+
+def local_states(u_ref, kt_ref, table_ref, drow_ref, sub_ref, msg_ref, which, piece, base):
     spread = spread_matrix(quarter(which) * QUART + piece * CW)
     drow = dot(drow_ref[...], spread)
     d0, d1 = drow[8:9], drow[9:10]
@@ -261,6 +285,7 @@
     r0 = dot(kt_ref[1, :, 0:SUB], weighted(1, WR, 0))
     r1 = dot(kt_ref[1, :, SUB:TOK], weighted(1, WR, SUB))
     fwd, rev = d1 * f0 + f1, r0 + d0 * r1
+    cols = slice(base, base + CW)
     sub_ref[0, :, cols] = f0.astype(BF16)
     sub_ref[1, :, cols] = r1.astype(BF16)
     msg_ref[0:STATE, cols] = fwd.astype(BF16)
@@ -269,10 +294,10 @@
     return fwd, rev, drow
 
 
-def joined(fwd, rev, drow, far_ref, chip_ref, piece):
+def joined(fwd, rev, drow, far_ref, chip_ref, base):
     c, z, y = place()
     core0 = c == 0
-    cols = slice(piece * CW, (piece + 1) * CW)
+    cols = slice(base, base + CW)
     dm = drow[0:1] + drow[1:2]
     do = read_decay(far_ref[2 * STATE : MSG, cols])
     one = jnp.ones_like(dm)
@@ -283,59 +308,61 @@
     chip_ref[2 * STATE : MSG] = decay_rows(dm * do)
 
 
-def first_kernel(
-    kq_in, u_in, x_ref, taps_ref, core_ref, chip_ref, table_ref, drow_ref, kq_ref, u_ref, kt_ref, sub_ref, msg_ref
+def far_kernel(
+    kq_in, u0_in, u1_in, x_ref, taps_ref, core_ref, chip_ref, table_ref, drow_ref,
+    kq_ref, u0_ref, u1_ref, kt_ref, sub_ref, msg_ref,
 ):
     repair(kq_ref, x_ref, taps_ref, core_ref, chip_ref, INNER)
     for d in range(2):
         kt_ref[d] = jnp.transpose(kq_ref[d, :, 0:STATE].astype(F32)).astype(BF16)
-    repair(u_ref, x_ref, taps_ref, core_ref, chip_ref, quarter(0) * QUART)
-    for piece in range(PIECES):
-        local_states(u_ref, kt_ref, table_ref, drow_ref, sub_ref, msg_ref, 0, piece)
-
-
-def partner_kernel(
-    u_in, x_ref, taps_ref, core_ref, chip_ref, table_ref, drow_ref, kt_ref, far_ref, u_ref, sub_ref, msg_ref, *chip_refs
+    for which, u_ref in ((0, u0_ref), (1, u1_ref)):
+        repair(u_ref, x_ref, taps_ref, core_ref, chip_ref, quarter(which) * QUART)
+        for piece in range(PIECES):
+            local_states(u_ref, kt_ref, table_ref, drow_ref, sub_ref, msg_ref, which, piece, BASE[which, piece])
+
+
+def partner_kernel(u_ref, table_ref, drow_ref, kt_ref, far_ref, sub_ref, msg_ref, zsend_ref):
+    state = local_states(u_ref, kt_ref, table_ref, drow_ref, sub_ref, msg_ref, 2, 0, 0)
+    joined(*state, far_ref, zsend_ref, BASE[2, 0])
+
+
+def conv_own_kernel(which, x_ref, taps_ref, core_ref, chip_ref, after_ref, u_ref):
+    def body(i, _):
+        at = columns(quarter(which) * QUART + i * 128, 128)
+        cols = columns(i * 128, 128)
+        prev, nxt = edges(x_ref, core_ref, chip_ref, at)
+        x = jnp.concatenate([prev[HALO - 8 :], x_ref[:, at].astype(F32), nxt[:8]], axis=0)
+        h, g = conv(x, taps_ref[0:4, at], taps_ref[4:8, at])
+        u_ref[0, :, cols] = silu_of_half(h[8 : TOK + 8])
+        u_ref[1, :, cols] = silu_of_half(g[8 : TOK + 8])
+        return _
+
+    lax.fori_loop(0, QUART // 128, body, 0)
+
+
+def own_kernel(
+    u2_ref, u3_ref, table_ref, drow_ref, kt_ref, far_ref, sub_in, msg_in,
+    sub_ref, msg_ref, zsend_ref, keep0_ref, keep1_ref,
 ):
-    repair(u_ref, x_ref, taps_ref, core_ref, chip_ref, quarter(2) * QUART)
-    for piece in range(PIECES):
-        state = local_states(u_ref, kt_ref, table_ref, drow_ref, sub_ref, msg_ref, 2, piece)
-        joined(*state, far_ref, chip_refs[piece], piece)
-
-
-def rest_kernel(
-    x_ref, taps_ref, core_ref, chip_ref, table_ref, drow_ref, kt_ref, u1_ref, u3_ref, sub_ref, msg_ref
-):
-    for which, ref in ((1, u1_ref), (3, u3_ref)):
-
-        def body(i, _):
-            at = columns(quarter(which) * QUART + i * 128, 128)
-            cols = columns(i * 128, 128)
-            prev, nxt = edges(x_ref, core_ref, chip_ref, at)
-            x = jnp.concatenate([prev[HALO - 8 :], x_ref[:, at].astype(F32), nxt[:8]], axis=0)
-            h, g = conv(x, taps_ref[0:4, at], taps_ref[4:8, at])
-            ref[0, :, cols] = silu_of_half(h[8 : TOK + 8])
-            ref[1, :, cols] = silu_of_half(g[8 : TOK + 8])
-            return _
-
-        lax.fori_loop(0, QUART // 128, body, 0)
-    for piece in range(PIECES):
-        local_states(u1_ref, kt_ref, table_ref, drow_ref, sub_ref, msg_ref, 1, piece)
-
-
-def own_kernel(u_ref, table_ref, drow_ref, kt_ref, far_ref, sub_ref, msg_ref, *chip_refs):
-    for piece in range(PIECES):
-        state = local_states(u_ref, kt_ref, table_ref, drow_ref, sub_ref, msg_ref, 3, piece)
-        joined(*state, far_ref, chip_refs[piece], piece)
+    sub_ref[:, :, 0:CW] = sub_in[...]
+    msg_ref[:, 0:CW] = msg_in[...]
+    todo = [(u2_ref, 2, 1, zsend_ref), (u3_ref, 3, 0, keep0_ref), (u3_ref, 3, 1, keep1_ref)]
+    for u_ref, which, piece, chip_ref in todo:
+        base = BASE[which, piece]
+        state = local_states(u_ref, kt_ref, table_ref, drow_ref, sub_ref, msg_ref, which, piece, base)
+        joined(*state, far_ref, chip_ref, base)
 
 
 U = vmem(BF16, 2, TOK, QUART)
-SUBSTATE = vmem(BF16, 2, STATE, QUART)
-MESSAGE = vmem(BF16, MSG, QUART)
-CHIP = [vmem(BF16, MSG, CW)] * PIECES
-
-
-def group_kernel(keep_ref, got_ref, *outs):
+KEYS = vmem(BF16, 2, TOK, 2 * STATE)
+CHIP = vmem(BF16, MSG, CW)
+
+
+def states_out(pieces):
+    return [vmem(BF16, 2, STATE, pieces * CW), vmem(BF16, MSG, pieces * CW)]
+
+
+def group(keep_ref, got_ref, outs):
     c, z, y = place()
     z0 = z == 0
     dm, do = read_decay(keep_ref[2 * STATE : MSG]), read_decay(got_ref[2 * STATE : MSG])
@@ -351,11 +378,7 @@
         outs[k - 1][STATE:YMSG] = decay
 
 
-def make_group(keep, got):
-    return call(group_kernel, "group", [vmem(BF16, YMSG, keep.shape[1])] * 3, (keep, got))
-
-
-def entries_kernel(keep_ref, got_ref, r1_ref, r2_ref, r3_ref, mine_ref, back_ref):
+def entries(keep_ref, got_ref, r1_ref, r2_ref, r3_ref, mine_ref, back_ref):
     c, z, y = place()
     z0 = z == 0
     r = [ref[0:STATE].astype(F32) for ref in (r1_ref, r2_ref, r3_ref)]
@@ -381,16 +404,38 @@
     back_ref[1] = jnp.where(z0, er, first_r).astype(BF16)
 
 
-def make_entries(keep, got, arrived):
-    return call(entries_kernel, "entries", [vmem(BF16, 2, STATE, keep.shape[1])] * 2, (keep, got, *arrived))
-
-
-def within_kernel(pair, ua_ref, ub_ref, kq_ref, table_ref, mcol_ref, mrow_ref, drow_ref, gate_hbm, gain_hbm, *refs):
-    if pair == 0:
-        outa_ref, outb_ref, gate_ref, gain_ref, qk_ref, sems = refs
+def second_phase_kernel(keep_ref, got_ref, zsend_ref, after_ref, zsend_out, *outs):
+    group(keep_ref, got_ref, outs)
+    zsend_out[...] = zsend_ref[...]
+
+
+def third_phase_kernel(
+    keep0_ref, got0_ref, r1_ref, r2_ref, r3_ref, keep1_ref, got1_ref, after_ref, mine_ref, back_ref, *outs
+):
+    entries(keep0_ref, got0_ref, r1_ref, r2_ref, r3_ref, mine_ref, back_ref)
+    group(keep1_ref, got1_ref, outs)
+
+
+def fourth_phase_kernel(
+    keep_ref, got_ref, r1_ref, r2_ref, r3_ref, mine0_ref, back0_ref, after_ref, mine_ref, back_ref, near_ref
+):
+    entries(keep_ref, got_ref, r1_ref, r2_ref, r3_ref, mine_ref, back_ref)
+    near_ref[0] = mine0_ref[...]
+    near_ref[1] = mine_ref[...]
+    near_ref[2] = back0_ref[...]
+
+
+def fifth_phase_kernel(back_ref, after0_ref, after1_ref, after2_ref, out_ref):
+    out_ref[...] = back_ref[...]
+
+
+def within_kernel(which, u_ref, kq_ref, table_ref, mcol_ref, mrow_ref, drow_ref, after_ref, *refs):
+    copies = []
+    if which == 0:
+        gate_hbm, gain_hbm, out_ref, gate_ref, gain_ref, qk_ref, sems = refs
         copies = copy_all([(gate_hbm, gate_ref), (gain_hbm, gain_ref)], sems)
     else:
-        outa_ref, outb_ref, qk_ref = refs
+        out_ref, qk_ref = refs
     row = lax.broadcasted_iota(jnp.int32, (SUB, SUB), 0)
     col = lax.broadcasted_iota(jnp.int32, (SUB, SUB), 1)
     low = lax.broadcasted_iota(jnp.int32, (SUB, 2 * HEAD_DIM), 1) < HEAD_DIM
@@ -402,60 +447,51 @@
             prod = lax.dot_general(queries, keys, (((1,), (1,)), ((), ())), preferred_element_type=F32)
             qk_ref[d, b] = jnp.where((row >= col) if d == 0 else (row <= col), prod, 0.0)
 
-    for u_ref, out_ref, which in ((ua_ref, outa_ref, pair), (ub_ref, outb_ref, pair + 2)):
-
-        def body(i, _):
-            chunk = quarter(which) * (QUART // CW) + i
-            spread = spread_matrix(chunk * CW)
-            skip = dot(drow_ref[...], spread)[10:11]
-            mcol = pltpu.roll(mcol_ref[...], 2 * HEADS - HC * chunk, 1)
-            mrow = mrow_ref[pl.ds(pl.multiple_of(chunk * HC, HC), HC), :]
-            for b in range(2):
-                rows = slice(b * SUB, (b + 1) * SUB)
-                wv = dot(table_ref[WV, rows], spread)
-                gt = dot(table_ref[GT, rows], spread)
-                for two in range(HC // 2):
-                    cols = slice(two * 128, (two + 1) * 128)
-                    at = columns(i * CW + two * 128, 128)
-                    up = u_ref[0, rows, at].astype(F32)
-                    xf = (up * wv[:, cols]).astype(BF16)
-                    xb = (u_ref[1, rows, at].astype(F32) * wv[:, cols]).astype(BF16)
-                    none = jnp.zeros_like(xf)
-                    left, right = [], []
-                    for h in range(2):
-                        k = two * 2 + h
-                        diff = mcol[rows, k : k + 1] - mrow[k : k + 1, rows]
-                        decay = jnp.exp2(-jnp.abs(diff))
-                        left += [(decay * qk_ref[0, b]).astype(BF16), (decay * qk_ref[1, b]).astype(BF16)]
-                        keep = low if h == 0 else ~low
-                        right += [jnp.where(keep, xf, none), jnp.where(keep, xb, none)]
-                    res = dot(jnp.concatenate(left, axis=1), jnp.concatenate(right, axis=0))
-                    out_ref[rows, at] = (res * gt[:, cols] + up * skip[:, cols]).astype(BF16)
-            return _
-
-        lax.fori_loop(0, QUART // CW, body, 0)
-    if pair == 0:
-        for copy in copies:
-            copy.wait()
-
-
-def make_within(pair, ua, ub, kq, table, mcol, mrow, drow, gate, gain):
-    outs = [vmem(BF16, TOK, QUART)] * 2
+    def body(i, _):
+        chunk = quarter(which) * (QUART // CW) + i
+        spread = spread_matrix(chunk * CW)
+        skip = dot(drow_ref[...], spread)[10:11]
+        mcol = pltpu.roll(mcol_ref[...], 2 * HEADS - HC * chunk, 1)
+        mrow = mrow_ref[pl.ds(pl.multiple_of(chunk * HC, HC), HC), :]
+        for b in range(2):
+            rows = slice(b * SUB, (b + 1) * SUB)
+            wv = dot(table_ref[WV, rows], spread)
+            gt = dot(table_ref[GT, rows], spread)
+            for two in range(HC // 2):
+                cols = slice(two * 128, (two + 1) * 128)
+                at = columns(i * CW + two * 128, 128)
+                up = u_ref[0, rows, at].astype(F32)
+                xf = (up * wv[:, cols]).astype(BF16)
+                xb = (u_ref[1, rows, at].astype(F32) * wv[:, cols]).astype(BF16)
+                none = jnp.zeros_like(xf)
+                left, right = [], []
+                for h in range(2):
+                    k = two * 2 + h
+                    diff = mcol[rows, k : k + 1] - mrow[k : k + 1, rows]
+                    decay = jnp.exp2(-jnp.abs(diff))
+                    left += [(decay * qk_ref[0, b]).astype(BF16), (decay * qk_ref[1, b]).astype(BF16)]
+                    keep = low if h == 0 else ~low
+                    right += [jnp.where(keep, xf, none), jnp.where(keep, xb, none)]
+                res = dot(jnp.concatenate(left, axis=1), jnp.concatenate(right, axis=0))
+                out_ref[rows, at] = (res * gt[:, cols] + up * skip[:, cols]).astype(BF16)
+        return _
+
+    lax.fori_loop(0, QUART // CW, body, 0)
+    for copy in copies:
+        copy.wait()
+
+
+def make_within(which, u, kq, table, mcol, mrow, drow, after, params=()):
+    outs = [vmem(BF16, TOK, QUART)]
     scratch = [pltpu.VMEM((2, 2, SUB, SUB), F32)]
-    if pair == 0:
+    if params:
         outs += [vmem(BF16, TOK, INNER), vmem(F32, 1, INNER)]
         scratch += [pltpu.SemaphoreType.DMA((2,))]
-    return call(
-        functools.partial(within_kernel, pair),
-        "within_a" if pair == 0 else "within_b",
-        outs,
-        (ua, ub, kq, table, mcol, mrow, drow),
-        (gate, gain),
-        scratch,
-    )
-
-
-def finish_part(which, piece, entry_ref, far_ref, sub_ref, within_ref, shared, gated_ref, start, square):
+    operands = (u, kq, table, mcol, mrow, drow, after)
+    return call(functools.partial(within_kernel, which), f"within_{which}", outs, operands, params, scratch)
+
+
+def finish_part(which, piece, entry, far_ref, sub_ref, within_ref, shared, gated_ref, start, square):
     kq_ref, table_ref, drow_ref, gate_ref = shared
     c, z, y = place()
     core0 = c == 0
@@ -464,15 +500,16 @@
     spread = spread_matrix(quarter(which) * QUART + piece * CW)
     drow = dot(drow_ref[...], spread)
     d0, d1 = drow[8:9], drow[9:10]
-    moved = read_decay(far_ref[2 * STATE : MSG, cols])
-    state = far_ref[pl.ds(pl.multiple_of((1 - c) * STATE, STATE), STATE), cols].astype(F32)
+    there = slice(BASE[which, piece], BASE[which, piece] + CW)
+    moved = read_decay(far_ref[2 * STATE : MSG, there])
+    state = far_ref[pl.ds(pl.multiple_of((1 - c) * STATE, STATE), STATE), there].astype(F32)
     one = jnp.ones_like(moved)
     none = jnp.zeros_like(state)
-    ef = jnp.where(core0, one, moved) * entry_ref[0].astype(F32) + jnp.where(core0, none, state)
-    er = jnp.where(core0, moved, one) * entry_ref[1].astype(F32) + jnp.where(core0, state, none)
+    ef = jnp.where(core0, one, moved) * entry[0].astype(F32) + jnp.where(core0, none, state)
+    er = jnp.where(core0, moved, one) * entry[1].astype(F32) + jnp.where(core0, state, none)
     inside = [
-        (ef.astype(BF16), (er * d1 + sub_ref[1, :, cols].astype(F32)).astype(BF16)),
-        ((ef * d0 + sub_ref[0, :, cols].astype(F32)).astype(BF16), er.astype(BF16)),
+        (ef.astype(BF16), (er * d1 + sub_ref[1, :, there].astype(F32)).astype(BF16)),
+        ((ef * d0 + sub_ref[0, :, there].astype(F32)).astype(BF16), er.astype(BF16)),
     ]
     for b in range(2):
         rows = slice(b * SUB, (b + 1) * SUB)
@@ -490,6 +527,9 @@
             square[b] = part if square[b] is None else square[b] + part
 
 
+NEAR = {(1, 0): 0, (1, 1): 1, (0, 0): 2}
+
+
 def finish_kernel(whiches, piece, last, before, *refs):
     refs = list(refs)
     parts = [[refs.pop(0) for _ in range(4)] for _ in whiches]
@@ -503,7 +543,9 @@
     else:
         gated_ref, square_ref = refs
     for k, (which, part) in enumerate(zip(whiches, parts)):
-        finish_part(which, piece, *part, shared, gated_ref, k * CW, square)
+        entry_ref, *part = part
+        entry = entry_ref if len(entry_ref.shape) == 3 else entry_ref.at[NEAR[which, piece]]
+        finish_part(which, piece, entry, *part, shared, gated_ref, k * CW, square)
     if not last:
         square_ref[0:SUB] = square[0]
         square_ref[SUB:TOK] = square[1]
@@ -549,8 +591,6 @@
 
 def per_device(mixer_input, gate_input, conv_forward, conv_reverse, step_size, decay_rate, skip_scale, norm_gain):
     n = lax.axis_size("seq")
-    barrier = lax.optimization_barrier
-    c = lax.axis_index("seq") & 1
 
     def send(v, perm):
         return lax.ppermute(v, "seq", perm)
@@ -559,66 +599,83 @@
     zswap = [(i, i ^ 2) for i in range(n)]
     chips = [(i, i + 1) for i in range(1, n - 1, 2)] + [(i + 1, i) for i in range(1, n - 1, 2)]
 
-    head, tail = mixer_input[:HALO], mixer_input[TOK - HALO :]
-    halo_core = send(jnp.where(c == 0, tail, head), core)
-    halo_chip = send(jnp.where(c == 0, head, tail), chips)
-    table, mcol, mrow, drow, x, taps, kq, u0, u2 = make_front(
-        mixer_input, step_size, decay_rate, skip_scale, conv_forward, conv_reverse
-    )
-    halo = (x, taps, halo_core, halo_chip)
-    kq, u0, kt, sub0, msg0 = call(
-        first_kernel,
-        "states_0",
-        [vmem(BF16, 2, TOK, 2 * STATE), U, vmem(BF16, 2, STATE, TOK), SUBSTATE, MESSAGE],
-        (kq, u0, *halo, table, drow),
-        aliases={0: 0, 1: 1},
-    )
-    far2 = send(msg0, core)
-    u2, sub2, msg2, *zsend = call(
-        partner_kernel,
-        "states_2",
-        [U, SUBSTATE, MESSAGE, *CHIP],
-        (u2, *halo, table, drow, kt, far2),
-        aliases={0: 0},
-    )
-    got = [send(m, zswap) for m in zsend]
-    x, zsend = barrier((x, zsend))
-    halo = (x, taps, halo_core, halo_chip)
-    u1, u3, sub1, msg1 = call(rest_kernel, "states_1", [U, U, SUBSTATE, MESSAGE], (*halo, table, drow, kt))
-    far3 = send(msg1, core)
-    sub3, msg3, *keep = call(own_kernel, "states_3", [SUBSTATE, MESSAGE, *CHIP], (u3, table, drow, kt, far3))
-    far0 = send(msg2, core)
-    far1 = send(msg3, core)
-
-    arrived, mine, back = [], [], []
-    for p in range(PIECES):
-        msgs = make_group(keep[p], got[p])
-        arrived.append([send(m, [(i, (i + 4 * k) % n) for i in range(n)]) for k, m in enumerate(msgs, 1)])
-    gate, gain = gate_input, norm_gain.reshape(1, INNER)
+    def along_y(msgs):
+        return [send(m, [(i, (i + 4 * k) % n) for i in range(n)]) for k, m in enumerate(msgs, 1)]
+
+    edge = vmem(BF16, HALO, E)
+    to_core, to_chip = call(
+        edge_kernel, "edges", [edge, edge], (), (mixer_input,), [pltpu.SemaphoreType.DMA((2,))]
+    )
+    x, table, mcol, mrow, drow, taps, kq, u0 = make_front(
+        to_core, mixer_input, step_size, decay_rate, skip_scale, conv_forward, conv_reverse
+    )
+    halo = (x, taps, send(to_core, core), send(to_chip, chips))
+    (u1,) = call(conv_kernel, "conv", [U], (x, taps))
+    kq, u0, u1, kt, sub_far, msg = call(
+        far_kernel,
+        "states_far",
+        [KEYS, U, U, vmem(BF16, 2, STATE, TOK), *states_out(4)],
+        (kq, u0, u1, *halo, table, drow),
+        aliases={0: 0, 1: 1, 2: 2},
+    )
+    far = send(msg, core)
+    (u2,) = call(functools.partial(conv_own_kernel, 2), "conv_2", [U], (*halo, msg))
+    sub_own, msg, zsend0 = call(
+        partner_kernel, "states_partner", [*states_out(1), CHIP], (u2, table, drow, kt, far)
+    )
+    got0 = send(zsend0, zswap)
+    (u3,) = call(functools.partial(conv_own_kernel, 3), "conv_3", [U], (*halo, zsend0))
+    sub_own, msg, zsend1, keep0, keep1 = call(
+        own_kernel,
+        "states_own",
+        [*states_out(4), CHIP, CHIP, CHIP],
+        (u2, u3, table, drow, kt, far, sub_own, msg),
+    )
+    near = send(msg, core)
     tables = (kq, table, mcol, mrow, drow)
-    u0, u2, msgs = barrier((u0, u2, msgs))
-    w0, w2, gate, gain = make_within(0, u0, u2, *tables, gate, gain)
-    arrived[0], w0, w2 = barrier((arrived[0], w0, w2))
-    for p in range(PIECES):
-        m, b = make_entries(keep[p], got[p], arrived[p])
-        mine.append(m)
-        back.append(b)
-    entry2 = [send(b, zswap) for b in back]
-    entry1 = [send(m, core) for m in mine]
-    u1, u3, back = barrier((u1, u3, back))
-    w1, w3 = make_within(1, u1, u3, *tables, gate_input, norm_gain.reshape(1, INNER))
+    w0, gate, gain = make_within(0, u0, *tables, zsend0, (gate_input, norm_gain.reshape(1, INNER)))
     shared = (kq, table, drow, gate)
+
+    yout = [vmem(BF16, YMSG, CW)] * 3
+    entry = vmem(BF16, 2, STATE, CW)
+    zsend1, *msgs = call(second_phase_kernel, "second_phase", [CHIP, *yout], (keep0, got0, zsend1, w0))
+    got1 = send(zsend1, zswap)
+    arrived = along_y(msgs)
+    (w2,) = make_within(2, u2, *tables, msgs[0])
+
+    mine0, back0, *msgs = call(
+        third_phase_kernel, "third_phase", [entry, entry, *yout], (keep0, got0, *arrived, keep1, got1, w2)
+    )
+    back0 = send(back0, zswap)
+    arrived = along_y(msgs)
+    (w3,) = make_within(3, u3, *tables, msgs[0])
+
+    mine1, back1, entries = call(
+        fourth_phase_kernel,
+        "fourth_phase",
+        [entry, entry, vmem(BF16, 3, 2, STATE, CW)],
+        (keep1, got1, *arrived, mine0, back0, w3),
+    )
+    back1 = send(back1, zswap)
+    entries = send(entries, core)
+    (w1,) = make_within(1, u1, *tables, mine1)
+    inside = (w0, w1, w2, w3)
     done = []
-    for p in range(PIECES):
-        parts = [(mine[p], far3, sub3, w3), (entry1[p], far1, sub1, w1)]
-        done.append(([(3, p), (1, p)], make_finish((3, 1), p, parts, shared)))
-    entry2[0], *rest = barrier((entry2[0], *[v for d in done for v in d[1]]))
-    done = [(d[0], rest[2 * k : 2 * k + 2]) for k, d in enumerate(done)]
-    entry0 = [send(e, core) for e in entry2]
-    parts = [(entry2[0], far2, sub2, w2), (entry0[0], far0, sub0, w0)]
-    done.append(([(2, 0), (0, 0)], make_finish((2, 0), 0, parts, shared)))
-    done.append(([(2, 1)], make_finish((2,), 1, [(entry2[1], far2, sub2, w2)], shared)))
-    (out,) = make_finish((0,), 1, [(entry0[1], far0, sub0, w0)], shared, gain, done)
+
+    def finish(p, *todo, **kw):
+        whiches = tuple(q for q, e in todo)
+        parts = [(e, far if q >= 2 else near, sub_own if q >= 2 else sub_far, inside[q]) for q, e in todo]
+        out = make_finish(whiches, p, parts, shared, **kw)
+        done.append(([(q, p) for q in whiches], out))
+        return out
+
+    finish(0, (2, back0), (0, entries))
+    finish(0, (3, mine0), (1, entries))
+    finish(1, (3, mine1), (1, entries))
+    (back1,) = call(fifth_phase_kernel, "fifth_phase", [entry], (back1, *[d[1][1] for d in done]))
+    entry0 = send(back1, core)
+    finish(1, (2, back1))
+    (out,) = finish(1, (0, entry0), gain=gain, before=tuple(done))
     return out
 
 

time: 77.5 us -> 70 us (0.903)
  waiting for transfers between devices: 15.6 us -> 9.96 us
  starting transfers between devices: 31.4 us -> 29.1 us
  Pallas kernels: 28.9 us -> 30.4 us
  other arithmetic: 1 us -> 0 us
    ppermute x20 -> x16, waiting for transfers between devices: 15.6 us -> 9.96 us  [send(): return lax.ppermute(v, 'seq', perm)]
    ppermute x20 -> x16, starting transfers between devices: 31.4 us -> 29.1 us  [send(): return lax.ppermute(v, 'seq', perm)]
    pallas_call x16 -> x21, Pallas kernels: 28.9 us -> 30.4 us  [call(): pl.pallas_call(kernel, name=name, in_specs=[VMEM] * len(operands) + [HBM]...]
    select_n x1 -> x0, other arithmetic: 1 us -> none  [per_device(): halo_chip = send(jnp.where(c == 0, head, tail), chips)]
  transfers between devices with their start and end apart: 20 -> 16, of which waited for: 6 -> 7; matrix products, arithmetic and copies ran while one was open for 0% -> 0% of each run, Pallas kernels for 25% -> 32%
where the time goes in v2:
time: 70 us; the launch traced here: 69.8 us
  Pallas kernels  30.4 us (43%)
  starting transfers between devices  29.1 us (42%)
  waiting for transfers between devices  9.96 us (14%)
    pallas_call x21, Pallas kernels, call(): pl.pallas_call(kernel, name=name, in_specs=[VMEM] * len(operands) + [HBM]...  30.4 us
    ppermute x16, starting transfers between devices, send(): return lax.ppermute(v, 'seq', perm)  29.1 us
    ppermute x16, waiting for transfers between devices, send(): return lax.ppermute(v, 'seq', perm)  9.96 us
  transfers between devices with their start and end apart: 16, of which 7 were waited for; matrix products, arithmetic and copies ran while one was open for 0% of the time, Pallas kernels for 32%

profile of v2, /device:TPU:1, one launch (start us, length us, event | category | flops | bytes accessed | tf_op | source)
XLA Modules:
  0.0 69.8 jit_solution(8709028163797892256)
XLA Ops:
  0.0 1.0 %edges.1 = (bf16[16,4352]{1,0:T(8,128)(2,1)S(1)}, bf16[16,4352]{1,0:T(8,128)(2,1)S(1)}) custom-call(bf16[256,4352]{1,0:T(8,128)(2,1)} %x_hbm.3), custom_call_target="tpu_custom_call" | custom-call | flops 100000000 | bytes 300000 | tf_op jit(solution)/shard_map/edges/pallas_call | solution.py:50
  1.0 6.9 %collective-permute-start.1 = (bf16[16,4352]{1,0:T(8,128)(2,1)S(1)}, bf16[16,4352]{1,0:T(8,128)(2,1)S(1)}, u32[]{:S(2)}, u32[]{:S(2)}) collective-permute-start(bf16[16,4352]{1,0:T(8,128)(2,1)S(1)} %get-tuple-element.55), channel_id=1, source_target_pairs={{1,2},{3,4},{5,6},{7,8},{9,10},{11,12},{13,14},{2,1},{4,3},{6,5},{... | collective-permute-start | bytes 417800 | tf_op jit(solution)/shard_map/ppermute | solution.py:596
  7.9 0.1 collective-permute-start
  8.0 3.2 %front.1 = (bf16[256,4352]{1,0:T(8,128)(2,1)S(1)}, bf16[6,256,128]{2,1,0:T(8,128)(2,1)S(1)}, f32[256,128]{1,0:T(8,128)S(1)}, f32[64,256]{1,0:T(8,128)S(1)}, bf16...) custom-call(bf16[16,4352]{1,0:T(8,128)(2,1)S(1)} %get-tuple-element., ...), custom_call_target="tpu_custom_call" | custom-call | flops 100000000 | bytes 300000 | tf_op jit(solution)/shard_map/front/pallas_call | solution.py:50
  11.2 1.1 %conv.1.u1_in = bf16[2,256,1024]{2,1,0:T(8,128)(2,1)S(1)} custom-call(bf16[256,4352]{1,0:T(8,128)(2,1)S(1)} %get-tuple-element.53.x_ref, f32[8,4352]{1,0:T(8,128)S(1)} %get-tuple-element.54.taps_ref), custom_call_target="tpu_custom_call" | custom-call | flops 100000000 | bytes 300000 | tf_op jit(solution)/shard_map/conv/pallas_call | solution.py:50
  12.4 0.0 collective-permute-done.core_ref
  12.4 3.6 %states_far.1 = (bf16[2,256,256]{2,1,0:T(8,128)(2,1)S(1)}, bf16[2,256,1024]{2,1,0:T(8,128)(2,1)S(1)}, bf16[2,256,1024]{2,1,0:T(8,128)(2,1)S(1)}, bf16[2,128,256]...) custom-call(bf16[2,256,256]{2,1,0:T(8,128)(2,1)S(1)} %get-tuple-elem, ...), custom_call_target="tpu_custom_call", output_to_operand_aliasing={{0}: (0, {}), {1}: (1, {}), {2}: (2, {})} | custom-call | flops 100000000 | bytes 300000 | tf_op jit(solution)/shard_map/states_far/pallas_call | solution.py:50
  16.0 0.6 collective-permute-start.2
  16.6 1.2 %conv_2.1.u_ref.u2_ref = bf16[2,256,1024]{2,1,0:T(8,128)(2,1)S(1)} custom-call(bf16[256,4352]{1,0:T(8,128)(2,1)S(1)} %get-tuple-element.53.x_ref, f32[8,4352]{1,0:T(8,128)S(1)} %get-tuple-element.54.taps_ref, bf16[16,4352]{1,0:T(8,128)(2,1)S(1)} %collective-permute-done.core_ref, bf16[16,4352]{1,0:T(8,128)(2,1)S(1)} %collective-permute-done.1.chip_ref, ...), custom_call_target="tpu_custom_call" | custom-call | flops 100000000 | bytes 300000 | tf_op jit(solution)/shard_map/conv_2/pallas_call | solution.py:50
  17.8 1.1 %collective-permute-done.2.far_ref.refs_1_ = bf16[272,2048]{1,0:T(8,128)(2,1)S(1)} collective-permute-done((bf16[272,2048]{1,0:T(8,128)(2,1)S(1)}, bf16[272,2048]{1,0:T(8,128)(2,1)S(1)}, u32[]{:S(2)}, u32[]{:S(2)}) %collective-permute-start.2) | collective-permute-done | bytes 1114144 | tf_op jit(solution)/shard_map/ppermute | solution.py:596
  19.0 0.9 %states_partner.1 = (bf16[2,128,512]{2,1,0:T(8,128)(2,1)S(1)}, bf16[272,512]{1,0:T(8,128)(2,1)S(1)}, bf16[272,512]{1,0:T(8,128)(2,1)S(1)}) custom-call(bf16[2,256,1024]{2,1,0:T(8,128)(2,1)S(1)} %conv_2.1.u_ref.u2_ref, bf16[6,256,128]{2,1,0:T(8,128)(2,1)S(1)} %get-tuple-element.58.table_ref.refs_9_.refs_5_, ...), custom_call_target="tpu_custom_call" | custom-call | flops 100000000 | bytes 300000 | tf_op jit(solution)/shard_map/states_partner/pallas_call | solution.py:50
  19.8 2.7 %collective-permute-start.3 = (bf16[272,512]{1,0:T(8,128)(2,1)S(1)}, bf16[272,512]{1,0:T(8,128)(2,1)S(1)}, u32[]{:S(2)}, u32[]{:S(2)}) collective-permute-start(bf16[272,512]{1,0:T(8,128)(2,1)S(1)} %get-tuple-element.62.after_ref), channel_id=1, source_target_pairs={{0,2},{1,3},{2,0},{3,1},{4,6},{5,7},{6,4},{7,5},{8,10},{9,11},{10,... | collective-permute-start | bytes 835592 | tf_op jit(solution)/shard_map/ppermute | solution.py:596
  22.5 2.0 %within_0.1 = (bf16[256,1024]{1,0:T(8,128)(2,1)S(1)}, bf16[256,4096]{1,0:T(8,128)(2,1)S(1)}, f32[1,4096]{1,0:T(1,128)S(1)}) custom-call(bf16[2,256,1024]{2,1,0:T(8,128)(2,1)S(1)} %get-tuple-element.68.u_ref, bf16[2,256,256]{2,1,0:T(8,128)(2,1)S(1)} %get-tuple-element.69.kq_ref.refs_8_.refs_4_, ...), custom_call_target="tpu_custom_call" | custom-call | flops 100000000 | bytes 300000 | tf_op jit(solution)/shard_map/within_0/pallas_call | solution.py:50
  24.5 1.2 %conv_3.1.u3_ref.u_ref = bf16[2,256,1024]{2,1,0:T(8,128)(2,1)S(1)} custom-call(bf16[256,4352]{1,0:T(8,128)(2,1)S(1)} %get-tuple-element.53.x_ref, f32[8,4352]{1,0:T(8,128)S(1)} %get-tuple-element.54.taps_ref, bf16[16,4352]{1,0:T(8,128)(2,1)S(1)} %collective-permute-done.core_ref, bf16[16,4352]{1,0:T(8,128)(2,1)S(1)} %collective-permute-done.1.chip_ref, ...), custom_call_target="tpu_custom_call" | custom-call | flops 100000000 | bytes 300000 | tf_op jit(solution)/shard_map/conv_3/pallas_call | solution.py:50
  25.8 2.4 %states_own.1 = (bf16[2,128,2048]{2,1,0:T(8,128)(2,1)S(1)}, bf16[272,2048]{1,0:T(8,128)(2,1)S(1)}, bf16[272,512]{1,0:T(8,128)(2,1)S(1)}, bf16[272,512]{1,0:T(8,128)(2,1)S(1)}, bf16[272,512]{1,0:T(8,128)(2,1)S(1)}) custom-call(bf16[2,256,1024]{2,1,0:T(8,128)(2,1)S(1)} %conv_2.1.u_ref.u2_ref, bf16[2,256,1024]{2,1,0:T(8,128)(2,1)S(1)} %conv_3.1.u3_ref.u_ref, ...), custom_call_target="tpu_custom_call" | custom-call | flops 100000000 | bytes 300000 | tf_op jit(solution)/shard_map/states_own/pallas_call | solution.py:50
  28.1 1.1 %collective-permute-done.3.got_ref.got0_ref = bf16[272,512]{1,0:T(8,128)(2,1)S(1)} collective-permute-done((bf16[272,512]{1,0:T(8,128)(2,1)S(1)}, bf16[272,512]{1,0:T(8,128)(2,1)S(1)}, u32[]{:S(2)}, u32[]{:S(2)}) %collective-permute-start.3) | collective-permute-done | bytes 278560 | tf_op jit(solution)/shard_map/ppermute | solution.py:596
  29.3 0.2 second_phase.1
  29.4 2.7 %collective-permute-start.4 = (bf16[272,512]{1,0:T(8,128)(2,1)S(1)}, bf16[272,512]{1,0:T(8,128)(2,1)S(1)}, u32[]{:S(2)}, u32[]{:S(2)}) collective-permute-start(bf16[272,512]{1,0:T(8,128)(2,1)S(1)} %get-tuple-element.73), channel_id=1, source_target_pairs={{0,2},{1,3},{2,0},{3,1},{4,6},{5,7},{6,4},{7,5},{8,10},{9,11},{10,... | collective-permute-start | bytes 835592 | tf_op jit(solution)/shard_map/ppermute | solution.py:596
  32.1 2.9 %collective-permute-start.6 = (bf16[144,512]{1,0:T(8,128)(2,1)S(1)}, bf16[144,512]{1,0:T(8,128)(2,1)S(1)}, u32[]{:S(2)}, u32[]{:S(2)}) collective-permute-start(bf16[144,512]{1,0:T(8,128)(2,1)S(1)} %get-tuple-element.75), channel_id=1, source_target_pairs={{0,8},{1,9},{2,10},{3,11},{4,12},{5,13},{6,14},{7,15},{8,0},{9,1},... | collective-permute-start | bytes 442376 | tf_op jit(solution)/shard_map/ppermute | solution.py:596
  35.0 0.8 %collective-permute-start.7 = (bf16[144,512]{1,0:T(8,128)(2,1)S(1)}, bf16[144,512]{1,0:T(8,128)(2,1)S(1)}, u32[]{:S(2)}, u32[]{:S(2)}) collective-permute-start(bf16[144,512]{1,0:T(8,128)(2,1)S(1)} %get-tuple-element.76), channel_id=1, source_target_pairs={{0,12},{1,13},{2,14},{3,15},{4,0},{5,1},{6,2},{7,3},{8,4},{9,5},{1... | collective-permute-start | bytes 442376 | tf_op jit(solution)/shard_map/ppermute | solution.py:596
  35.8 0.7 collective-permute-start.5
  36.5 2.3 %collective-permute-start.14 = (bf16[272,2048]{1,0:T(8,128)(2,1)S(1)}, bf16[272,2048]{1,0:T(8,128)(2,1)S(1)}, u32[]{:S(2)}, u32[]{:S(2)}) collective-permute-start(bf16[272,2048]{1,0:T(8,128)(2,1)S(1)} %get-tuple-element.85), channel_id=1, source_target_pairs={{0,1},{1,0},{2,3},{3,2},{4,5},{5,4},{6,7},{7,6},{8,9},{9,8},{10,11... | collective-permute-start | bytes 3342344 | tf_op jit(solution)/shard_map/ppermute | solution.py:596
  38.8 2.0 %within_2.1.after_ref.refs_3_ = bf16[256,1024]{1,0:T(8,128)(2,1)S(1)} custom-call(bf16[2,256,1024]{2,1,0:T(8,128)(2,1)S(1)} %conv_2.1.u_ref.u2_ref, bf16[2,256,256]{2,1,0:T(8,128)(2,1)S(1)} %get-tuple-element.69.kq_ref.refs_8_.refs_4_, bf16[6,256,128]{2,1,0:T(8,128)(2,1)S(1)} %get-tuple-element.58.table_ref.refs_9_.refs_5_, ...), custom_call_target="tpu_custom_call" | custom-call | flops 100000000 | bytes 300000 | tf_op jit(solution)/shard_map/within_2/pallas_call | solution.py:50
  40.8 0.0 collective-permute-done.6.r2_ref
  40.8 0.0 collective-permute-done.7.r3_ref
  40.8 1.0 %collective-permute-done.5.r1_ref = bf16[144,512]{1,0:T(8,128)(2,1)S(1)} collective-permute-done((bf16[144,512]{1,0:T(8,128)(2,1)S(1)}, bf16[144,512]{1,0:T(8,128)(2,1)S(1)}, u32[]{:S(2)}, u32[]{:S(2)}) %collective-permute-start.5) | collective-permute-done | bytes 147488 | tf_op jit(solution)/shard_map/ppermute | solution.py:596
  41.9 0.0 collective-permute-done.4.got1_ref.got_ref
  41.9 0.5 third_phase.1
  42.3 0.5 collective-permute-start.11
  42.9 2.6 %collective-permute-start.9 = (bf16[144,512]{1,0:T(8,128)(2,1)S(1)}, bf16[144,512]{1,0:T(8,128)(2,1)S(1)}, u32[]{:S(2)}, u32[]{:S(2)}) collective-permute-start(bf16[144,512]{1,0:T(8,128)(2,1)S(1)} %get-tuple-element.78), channel_id=1, source_target_pairs={{0,8},{1,9},{2,10},{3,11},{4,12},{5,13},{6,14},{7,15},{8,0},{9,1},... | collective-permute-start | bytes 442376 | tf_op jit(solution)/shard_map/ppermute | solution.py:596
  45.5 1.0 %collective-permute-start.10 = (bf16[144,512]{1,0:T(8,128)(2,1)S(1)}, bf16[144,512]{1,0:T(8,128)(2,1)S(1)}, u32[]{:S(2)}, u32[]{:S(2)}) collective-permute-start(bf16[144,512]{1,0:T(8,128)(2,1)S(1)} %get-tuple-element.79), channel_id=1, source_target_pairs={{0,12},{1,13},{2,14},{3,15},{4,0},{5,1},{6,2},{7,3},{8,4},{9,5},{1... | collective-permute-start | bytes 442376 | tf_op jit(solution)/shard_map/ppermute | solution.py:596
  46.4 0.5 collective-permute-start.8
  46.9 2.0 %within_3.1.after_ref.refs_3_ = bf16[256,1024]{1,0:T(8,128)(2,1)S(1)} custom-call(bf16[2,256,1024]{2,1,0:T(8,128)(2,1)S(1)} %conv_3.1.u3_ref.u_ref, bf16[2,256,256]{2,1,0:T(8,128)(2,1)S(1)} %get-tuple-element.69.kq_ref.refs_8_.refs_4_, bf16[6,256,128]{2,1,0:T(8,128)(2,1)S(1)} %get-tuple-element.58.table_ref.refs_9_.refs_5_, ...), custom_call_target="tpu_custom_call" | custom-call | flops 100000000 | bytes 300000 | tf_op jit(solution)/shard_map/within_3/pallas_call | solution.py:50
  48.9 0.0 collective-permute-done.9.r2_ref
  48.9 2.5 %collective-permute-done.10.r3_ref = bf16[144,512]{1,0:T(8,128)(2,1)S(1)} collective-permute-done((bf16[144,512]{1,0:T(8,128)(2,1)S(1)}, bf16[144,512]{1,0:T(8,128)(2,1)S(1)}, u32[]{:S(2)}, u32[]{:S(2)}) %collective-permute-start.10) | collective-permute-done | bytes 147488 | tf_op jit(solution)/shard_map/ppermute | solution.py:596
  51.4 2.3 %collective-permute-done.8.r1_ref = bf16[144,512]{1,0:T(8,128)(2,1)S(1)} collective-permute-done((bf16[144,512]{1,0:T(8,128)(2,1)S(1)}, bf16[144,512]{1,0:T(8,128)(2,1)S(1)}, u32[]{:S(2)}, u32[]{:S(2)}) %collective-permute-start.8) | collective-permute-done | bytes 147488 | tf_op jit(solution)/shard_map/ppermute | solution.py:596
  53.7 0.6 fourth_phase.1
  54.3 1.7 %collective-permute-start.13 = (bf16[3,2,128,512]{3,2,1,0:T(8,128)(2,1)S(1)}, bf16[3,2,128,512]{3,2,1,0:T(8,128)(2,1)S(1)}, u32[]{:S(2)}, u32[]{:S(2)}) collective-permute-start(bf16[3,2,128,512]{3,2,1,0:T(8,128)(2,1)S(1)} %get-tuple-element.84), channel_id=1, source_target_pairs={{0,1},{1,0},{2,3},{3,2},{4,5},{5,4},{6,7},{7,6},{8,9},{9,8},{10,11... | collective-permute-start | bytes 2359304 | tf_op jit(solution)/shard_map/ppermute | solution.py:596
  56.0 2.2 %collective-permute-start.12 = (bf16[2,128,512]{2,1,0:T(8,128)(2,1)S(1)}, bf16[2,128,512]{2,1,0:T(8,128)(2,1)S(1)}, u32[]{:S(2)}, u32[]{:S(2)}) collective-permute-start(bf16[2,128,512]{2,1,0:T(8,128)(2,1)S(1)} %get-tuple-element.82), channel_id=1, source_target_pairs={{0,2},{1,3},{2,0},{3,1},{4,6},{5,7},{6,4},{7,5},{8,10},{9,11},{10,... | collective-permute-start | bytes 786440 | tf_op jit(solution)/shard_map/ppermute | solution.py:596
  58.2 2.0 %within_1.1.refs_7_ = bf16[256,1024]{1,0:T(8,128)(2,1)S(1)} custom-call(bf16[2,256,1024]{2,1,0:T(8,128)(2,1)S(1)} %get-tuple-element.89.u_ref, bf16[2,256,256]{2,1,0:T(8,128)(2,1)S(1)} %get-tuple-element.69.kq_ref.refs_8_.refs_4_, bf16[6,256,128]{2,1,0:T(8,128)(2,1)S(1)} %get-tuple-element.58.table_ref.refs_9_.refs_5_, ...), custom_call_target="tpu_custom_call" | custom-call | flops 100000000 | bytes 300000 | tf_op jit(solution)/shard_map/within_1/pallas_call | solution.py:50
  60.2 1.3 %finish_31b.1 = (f32[256,1024]{1,0:T(8,128)S(1)}, f32[256,128]{1,0:T(8,128)S(1)}) custom-call(bf16[2,128,512]{2,1,0:T(8,128)(2,1)S(1)} %get-tuple-element.90.after_ref.refs_0_, bf16[272,2048]{1,0:T(8,128)(2,1)S(1)} %collective-permute-done.2.far_ref.refs_1_, bf16[2,128,2048]{2,1,0:T(8,128)(2,1)S(1)} %get-tuple-element.83.refs_2_, ...), custom_call_target="tpu_custom_call" | custom-call | flops 100000000 | bytes 300000 | tf_op jit(solution)/shard_map/finish_31b/pallas_call | solution.py:50
  61.5 1.3 %finish_31a.1 = (f32[256,1024]{1,0:T(8,128)S(1)}, f32[256,128]{1,0:T(8,128)S(1)}) custom-call(bf16[2,128,512]{2,1,0:T(8,128)(2,1)S(1)} %get-tuple-element.80.mine0_ref.refs_0_, bf16[272,2048]{1,0:T(8,128)(2,1)S(1)} %collective-permute-done.2.far_ref.refs_1_, bf16[2,128,2048]{2,1,0:T(8,128)(2,1)S(1)} %get-tuple-element.83.refs_2_, ...), custom_call_target="tpu_custom_call" | custom-call | flops 100000000 | bytes 300000 | tf_op jit(solution)/shard_map/finish_31a/pallas_call | solution.py:50
  62.8 1.3 %finish_20a.1 = (f32[256,1024]{1,0:T(8,128)S(1)}, f32[256,128]{1,0:T(8,128)S(1)}) custom-call(bf16[2,128,512]{2,1,0:T(8,128)(2,1)S(1)} %collective-permute-done.11.back0_ref.refs_0_, bf16[272,2048]{1,0:T(8,128)(2,1)S(1)} %collective-permute-done.2.far_ref.refs_1_, bf16[2,128,2048]{2,1,0:T(8,128)(2,1)S(1)} %get-tuple-element.83.refs_2_, ...), custom_call_target="tpu_custom_call" | custom-call | flops 100000000 | bytes 300000 | tf_op jit(solution)/shard_map/finish_20a/pallas_call | solution.py:50
  64.1 1.3 %collective-permute-done.12.back_ref = bf16[2,128,512]{2,1,0:T(8,128)(2,1)S(1)} collective-permute-done((bf16[2,128,512]{2,1,0:T(8,128)(2,1)S(1)}, bf16[2,128,512]{2,1,0:T(8,128)(2,1)S(1)}, u32[]{:S(2)}, u32[]{:S(2)}) %collective-permute-start.12) | collective-permute-done | bytes 262176 | tf_op jit(solution)/shard_map/ppermute | solution.py:596
  65.4 1.0 %collective-permute-start.15 = (bf16[2,128,512]{2,1,0:T(8,128)(2,1)S(1)}, bf16[2,128,512]{2,1,0:T(8,128)(2,1)S(1)}, u32[]{:S(2)}, u32[]{:S(2)}) collective-permute-start(bf16[2,128,512]{2,1,0:T(8,128)(2,1)S(1)} %fifth_phase.1.refs_0_), channel_id=1, source_target_pairs={{0,1},{1,0},{2,3},{3,2},{4,5},{5,4},{6,7},{7,6},{8,9},{9,8},{10,11... | collective-permute-start | bytes 786440 | tf_op jit(solution)/shard_map/ppermute | solution.py:596
  66.4 0.6 finish_2b.1
  67.0 0.5 collective-permute-done.15.refs_0_
  67.5 2.2 %finish_0b.1 = bf16[256,4096]{1,0:T(8,128)(2,1)} custom-call(bf16[2,128,512]{2,1,0:T(8,128)(2,1)S(1)} %collective-permute-done.15.refs_0_, bf16[272,2048]{1,0:T(8,128)(2,1)S(1)} %collective-permute-done.14.refs_5_.refs_1_, bf16[2,128,2048]{2,1,0:T(8,128)(2,1)S(1)} %get-tuple-element.86.refs_6_.refs_2_, ...), custom_call_target="tpu_custom_call" | custom-call | flops 100000000 | bytes 300000 | tf_op jit(solution)/shard_map/finish_0b/pallas_call | solution.py:50
  (5 shorter events, 0.0 us)
Async XLA Ops:
  1.0 11.4 %collective-permute-start.1 = (bf16[16,4352]{1,0:T(8,128)(2,1)S(1)}, bf16[16,4352]{1,0:T(8,128)(2,1)S(1)}, u32[]{:S(2)}, u32[]{:S(2)}) collective-permute-start(bf16[16,4352]{1,0:T(8,128)(2,1)S(1)} %get-tuple-element.55), channel_id=1, source_target_pairs={{1,2},{3,4},{5,6},{7,8},{9,10},{11,12},{13,14},{2,1},{4,3},{6,5},{... | collective-permute-start | bytes 417800 | tf_op jit(solution)/shard_map/ppermute | solution.py:596
  7.9 4.5 %collective-permute-start = (bf16[16,4352]{1,0:T(8,128)(2,1)S(1)}, bf16[16,4352]{1,0:T(8,128)(2,1)S(1)}, u32[]{:S(2)}, u32[]{:S(2)}) collective-permute-start(bf16[16,4352]{1,0:T(8,128)(2,1)S(1)} %get-tuple-element.52.after_ref), channel_id=1, source_target_pairs={{0,1},{1,0},{2,3},{3,2},{4,5},{5,4},{6,7},{7,6},{8,9},{9,8},{10,11... | collective-permute-start | bytes 417800 | tf_op jit(solution)/shard_map/ppermute | solution.py:596
  16.0 3.0 %collective-permute-start.2 = (bf16[272,2048]{1,0:T(8,128)(2,1)S(1)}, bf16[272,2048]{1,0:T(8,128)(2,1)S(1)}, u32[]{:S(2)}, u32[]{:S(2)}) collective-permute-start(bf16[272,2048]{1,0:T(8,128)(2,1)S(1)} %get-tuple-element.60.after_ref), channel_id=1, source_target_pairs={{0,1},{1,0},{2,3},{3,2},{4,5},{5,4},{6,7},{7,6},{8,9},{9,8},{10,11... | collective-permute-start | bytes 3342344 | tf_op jit(solution)/shard_map/ppermute | solution.py:596
  19.8 9.4 %collective-permute-start.3 = (bf16[272,512]{1,0:T(8,128)(2,1)S(1)}, bf16[272,512]{1,0:T(8,128)(2,1)S(1)}, u32[]{:S(2)}, u32[]{:S(2)}) collective-permute-start(bf16[272,512]{1,0:T(8,128)(2,1)S(1)} %get-tuple-element.62.after_ref), channel_id=1, source_target_pairs={{0,2},{1,3},{2,0},{3,1},{4,6},{5,7},{6,4},{7,5},{8,10},{9,11},{10,... | collective-permute-start | bytes 835592 | tf_op jit(solution)/shard_map/ppermute | solution.py:596
  29.4 12.4 %collective-permute-start.4 = (bf16[272,512]{1,0:T(8,128)(2,1)S(1)}, bf16[272,512]{1,0:T(8,128)(2,1)S(1)}, u32[]{:S(2)}, u32[]{:S(2)}) collective-permute-start(bf16[272,512]{1,0:T(8,128)(2,1)S(1)} %get-tuple-element.73), channel_id=1, source_target_pairs={{0,2},{1,3},{2,0},{3,1},{4,6},{5,7},{6,4},{7,5},{8,10},{9,11},{10,... | collective-permute-start | bytes 835592 | tf_op jit(solution)/shard_map/ppermute | solution.py:596
  32.1 8.7 %collective-permute-start.6 = (bf16[144,512]{1,0:T(8,128)(2,1)S(1)}, bf16[144,512]{1,0:T(8,128)(2,1)S(1)}, u32[]{:S(2)}, u32[]{:S(2)}) collective-permute-start(bf16[144,512]{1,0:T(8,128)(2,1)S(1)} %get-tuple-element.75), channel_id=1, source_target_pairs={{0,8},{1,9},{2,10},{3,11},{4,12},{5,13},{6,14},{7,15},{8,0},{9,1},... | collective-permute-start | bytes 442376 | tf_op jit(solution)/shard_map/ppermute | solution.py:596
  35.0 5.8 %collective-permute-start.7 = (bf16[144,512]{1,0:T(8,128)(2,1)S(1)}, bf16[144,512]{1,0:T(8,128)(2,1)S(1)}, u32[]{:S(2)}, u32[]{:S(2)}) collective-permute-start(bf16[144,512]{1,0:T(8,128)(2,1)S(1)} %get-tuple-element.76), channel_id=1, source_target_pairs={{0,12},{1,13},{2,14},{3,15},{4,0},{5,1},{6,2},{7,3},{8,4},{9,5},{1... | collective-permute-start | bytes 442376 | tf_op jit(solution)/shard_map/ppermute | solution.py:596
  35.8 6.1 %collective-permute-start.5 = (bf16[144,512]{1,0:T(8,128)(2,1)S(1)}, bf16[144,512]{1,0:T(8,128)(2,1)S(1)}, u32[]{:S(2)}, u32[]{:S(2)}) collective-permute-start(bf16[144,512]{1,0:T(8,128)(2,1)S(1)} %get-tuple-element.74.after_ref), channel_id=1, source_target_pairs={{0,4},{1,5},{2,6},{3,7},{4,8},{5,9},{6,10},{7,11},{8,12},{9,13},{1... | collective-permute-start | bytes 442376 | tf_op jit(solution)/shard_map/ppermute | solution.py:596
  36.5 23.7 %collective-permute-start.14 = (bf16[272,2048]{1,0:T(8,128)(2,1)S(1)}, bf16[272,2048]{1,0:T(8,128)(2,1)S(1)}, u32[]{:S(2)}, u32[]{:S(2)}) collective-permute-start(bf16[272,2048]{1,0:T(8,128)(2,1)S(1)} %get-tuple-element.85), channel_id=1, source_target_pairs={{0,1},{1,0},{2,3},{3,2},{4,5},{5,4},{6,7},{7,6},{8,9},{9,8},{10,11... | collective-permute-start | bytes 3342344 | tf_op jit(solution)/shard_map/ppermute | solution.py:596
  42.3 11.4 %collective-permute-start.11 = (bf16[2,128,512]{2,1,0:T(8,128)(2,1)S(1)}, bf16[2,128,512]{2,1,0:T(8,128)(2,1)S(1)}, u32[]{:S(2)}, u32[]{:S(2)}) collective-permute-start(bf16[2,128,512]{2,1,0:T(8,128)(2,1)S(1)} %get-tuple-element.81), channel_id=1, source_target_pairs={{0,2},{1,3},{2,0},{3,1},{4,6},{5,7},{6,4},{7,5},{8,10},{9,11},{10,... | collective-permute-start | bytes 786440 | tf_op jit(solution)/shard_map/ppermute | solution.py:596
  42.9 6.1 %collective-permute-start.9 = (bf16[144,512]{1,0:T(8,128)(2,1)S(1)}, bf16[144,512]{1,0:T(8,128)(2,1)S(1)}, u32[]{:S(2)}, u32[]{:S(2)}) collective-permute-start(bf16[144,512]{1,0:T(8,128)(2,1)S(1)} %get-tuple-element.78), channel_id=1, source_target_pairs={{0,8},{1,9},{2,10},{3,11},{4,12},{5,13},{6,14},{7,15},{8,0},{9,1},... | collective-permute-start | bytes 442376 | tf_op jit(solution)/shard_map/ppermute | solution.py:596
  45.5 5.9 %collective-permute-start.10 = (bf16[144,512]{1,0:T(8,128)(2,1)S(1)}, bf16[144,512]{1,0:T(8,128)(2,1)S(1)}, u32[]{:S(2)}, u32[]{:S(2)}) collective-permute-start(bf16[144,512]{1,0:T(8,128)(2,1)S(1)} %get-tuple-element.79), channel_id=1, source_target_pairs={{0,12},{1,13},{2,14},{3,15},{4,0},{5,1},{6,2},{7,3},{8,4},{9,5},{1... | collective-permute-start | bytes 442376 | tf_op jit(solution)/shard_map/ppermute | solution.py:596
  46.4 7.3 %collective-permute-start.8 = (bf16[144,512]{1,0:T(8,128)(2,1)S(1)}, bf16[144,512]{1,0:T(8,128)(2,1)S(1)}, u32[]{:S(2)}, u32[]{:S(2)}) collective-permute-start(bf16[144,512]{1,0:T(8,128)(2,1)S(1)} %get-tuple-element.77.after_ref), channel_id=1, source_target_pairs={{0,4},{1,5},{2,6},{3,7},{4,8},{5,9},{6,10},{7,11},{8,12},{9,13},{1... | collective-permute-start | bytes 442376 | tf_op jit(solution)/shard_map/ppermute | solution.py:596
  54.3 5.9 %collective-permute-start.13 = (bf16[3,2,128,512]{3,2,1,0:T(8,128)(2,1)S(1)}, bf16[3,2,128,512]{3,2,1,0:T(8,128)(2,1)S(1)}, u32[]{:S(2)}, u32[]{:S(2)}) collective-permute-start(bf16[3,2,128,512]{3,2,1,0:T(8,128)(2,1)S(1)} %get-tuple-element.84), channel_id=1, source_target_pairs={{0,1},{1,0},{2,3},{3,2},{4,5},{5,4},{6,7},{7,6},{8,9},{9,8},{10,11... | collective-permute-start | bytes 2359304 | tf_op jit(solution)/shard_map/ppermute | solution.py:596
  56.0 9.4 %collective-permute-start.12 = (bf16[2,128,512]{2,1,0:T(8,128)(2,1)S(1)}, bf16[2,128,512]{2,1,0:T(8,128)(2,1)S(1)}, u32[]{:S(2)}, u32[]{:S(2)}) collective-permute-start(bf16[2,128,512]{2,1,0:T(8,128)(2,1)S(1)} %get-tuple-element.82), channel_id=1, source_target_pairs={{0,2},{1,3},{2,0},{3,1},{4,6},{5,7},{6,4},{7,5},{8,10},{9,11},{10,... | collective-permute-start | bytes 786440 | tf_op jit(solution)/shard_map/ppermute | solution.py:596
  65.4 2.1 %collective-permute-start.15 = (bf16[2,128,512]{2,1,0:T(8,128)(2,1)S(1)}, bf16[2,128,512]{2,1,0:T(8,128)(2,1)S(1)}, u32[]{:S(2)}, u32[]{:S(2)}) collective-permute-start(bf16[2,128,512]{2,1,0:T(8,128)(2,1)S(1)} %fifth_phase.1.refs_0_), channel_id=1, source_target_pairs={{0,1},{1,0},{2,3},{3,2},{4,5},{5,4},{6,7},{7,6},{8,9},{9,8},{10,11... | collective-permute-start | bytes 786440 | tf_op jit(solution)/shard_map/ppermute | solution.py:596

commit v3 on v2

v3 whole, which is shorter than its diff:
```python
import functools

import jax
import jax.numpy as jnp
from jax import lax
from jax.experimental import pallas as pl
from jax.experimental.pallas import tpu as pltpu
from jax.sharding import PartitionSpec as P

HEADS = 64
HEAD_DIM = 64
STATE = 128
TOK = 256
SUB = 128
INNER = 4096
E = 4352
HALF = INNER // 2
QUART = INNER // 4
WIDE = HALF + 2 * STATE
STEPS = 256
CW = 512
HC = CW // HEAD_DIM
HALO = 16
MSG = 2 * STATE + 16
YMSG = STATE + 16
LOG2E = 1.4426950408889634
F32 = jnp.float32
BF16 = jnp.bfloat16
WF, WR, GF, GR, WV, GT = range(6)
MIB = 2**20


def dot(a, b, **kw):
    return jnp.dot(a, b, preferred_element_type=F32, **kw)


def shape(dtype, *dims):
    return jax.ShapeDtypeStruct(dims, dtype)


VMEM = pl.BlockSpec(memory_space=pltpu.VMEM)
HBM = pl.BlockSpec(memory_space=pltpu.HBM)


def vmem(dtype, *dims):
    return pltpu.VMEM(dims, dtype)


def call(kernel, name, outs, operands, params=(), scratch=(), limit=12, us=1.0, aliases=None):
    operands = [pltpu.with_memory_space_constraint(v, pltpu.VMEM) for v in operands]
    params = [pltpu.with_memory_space_constraint(v, pltpu.HBM) for v in params]
    return pl.pallas_call(
        kernel,
        name=name,
        in_specs=[VMEM] * len(operands) + [HBM] * len(params),
        out_specs=[HBM if isinstance(o, jax.ShapeDtypeStruct) else VMEM for o in outs],
        out_shape=outs,
        scratch_shapes=list(scratch),
        input_output_aliases=aliases or {},
        compiler_params=pltpu.CompilerParams(vmem_limit_bytes=limit * MIB),
        cost_estimate=pl.CostEstimate(flops=int(us * 1e8), bytes_accessed=int(us * 3e5), transcendentals=0),
    )(*operands, *params)


def place():
    at = lax.axis_index("seq")
    return at & 1, (at >> 1) & 1, at >> 2


def columns(start, width):
    return pl.ds(pl.multiple_of(start, 128), width)


def split2(x):
    hi = x.astype(BF16)
    lo = (x - hi.astype(F32)).astype(BF16)
    return hi, lo


def spread_matrix(start, width=CW):
    k = lax.broadcasted_iota(jnp.int32, (2 * HEADS, width), 0)
    col = lax.broadcasted_iota(jnp.int32, (2 * HEADS, width), 1)
    low = (k & (HEADS - 1)) * HEAD_DIM - start
    return jnp.where((col >= low) & (col < low + HEAD_DIM), 1.0, 0.0).astype(BF16)


def read_decay(rows):
    rows = rows.astype(F32)
    return rows[0:1] + rows[1:2]


def decay_rows(d):
    hi, lo = split2(d)
    none = jnp.zeros((14, d.shape[1]), F32)
    return jnp.concatenate([hi.astype(F32), lo.astype(F32), none], axis=0).astype(BF16)


def make_tables(step, decay, skip, table_ref, mcol_ref, mrow_ref, drow_ref):
    a = -decay * step
    row = lax.broadcasted_iota(jnp.int32, (TOK, TOK), 0)
    col = lax.broadcasted_iota(jnp.int32, (TOK, TOK), 1)
    tri = jnp.where((row >= col) & ((row >= SUB) == (col >= SUB)), 1.0, 0.0)
    cum = dot(tri, a, precision=lax.Precision.HIGHEST)
    excl = cum - a
    e0 = cum[SUB - 1 : SUB]
    e1 = cum[TOK - 1 : TOK]
    ends = jnp.concatenate([jnp.broadcast_to(e0, (SUB, HEADS)), jnp.broadcast_to(e1, (SUB, HEADS))], axis=0)
    zero = jnp.zeros_like(cum)

    def put(at, value):
        hi, lo = split2(value)
        table_ref[at] = jnp.concatenate([hi, lo], axis=1)

    put(WF, step * jnp.exp(jnp.minimum(ends - cum, zero)))
    put(WR, step * jnp.exp(excl))
    put(GF, jnp.exp(cum))
    put(GR, jnp.exp(jnp.minimum(ends - excl, zero)))
    put(WV, step * jnp.exp(-0.5 * a))
    put(GT, jnp.exp(0.5 * a))
    m = (cum - 0.5 * a) * LOG2E
    mcol_ref[...] = jnp.concatenate([m, zero], axis=1)
    mrow_ref[...] = jnp.transpose(m)
    h0, l0 = split2(jnp.exp(e0))
    h1, l1 = split2(jnp.exp(e1))
    hd, ld = split2(jnp.exp(e0 + e1))
    hs, ls = split2(skip)
    no = jnp.zeros_like(h0)
    wide = [
        jnp.concatenate([hd, no], axis=1).astype(F32),
        jnp.concatenate([no, ld], axis=1).astype(F32),
        jnp.zeros((6, 2 * HEADS), F32),
        jnp.concatenate([h0, l0], axis=1).astype(F32),
        jnp.concatenate([h1, l1], axis=1).astype(F32),
        jnp.concatenate([hs, ls], axis=1).astype(F32),
        jnp.zeros((5, 2 * HEADS), F32),
    ]
    drow_ref[...] = jnp.concatenate(wide, axis=0).astype(BF16)


def conv(x, cf, cr):
    rows = x.shape[0]
    back = pltpu.roll(x, 1, 0)
    fore = pltpu.roll(x, rows - 1, 0)
    h = cf[3:4] * x + cf[2:3] * back + pltpu.roll(cf[1:2] * x + cf[0:1] * back, 2, 0)
    g = cr[3:4] * x + cr[2:3] * fore + pltpu.roll(cr[1:2] * x + cr[0:1] * fore, rows - 2, 0)
    return h, g


def silu_of_half(h):
    return (h + h * jnp.tanh(h)).astype(BF16)


def copy_all(pairs, sems):
    copies = [pltpu.make_async_copy(src, dst, sems.at[k]) for k, (src, dst) in enumerate(pairs)]
    for copy in copies:
        copy.start()
    return copies


def start_of(k, p):
    c, z, y = place()
    return (z if k == 3 else 1 - z) * QUART + p * CW


def edge_kernel(x_hbm, step_hbm, to_core_ref, to_chip_ref, step_ref, sems):
    c, z, y = place()
    far = columns((1 - c) * HALF, HALF)
    ends = pl.ds(pl.multiple_of(c * (TOK - HALO), HALO), HALO)
    copies = copy_all(
        [
            (step_hbm, step_ref),
            (x_hbm.at[ends], to_chip_ref),
            (x_hbm.at[:, far], to_core_ref.at[:, 0:HALF]),
            (x_hbm.at[:, INNER:E], to_core_ref.at[:, HALF:WIDE]),
        ],
        sems,
    )
    copies[0].wait()
    step = jnp.transpose(step_ref[...])
    p0 = step.astype(BF16).astype(F32)
    p1 = (step - p0).astype(BF16).astype(F32)
    p2 = step - p0 - p1
    to_core_ref[:, WIDE : WIDE + STEPS] = jnp.concatenate([p0, p1, p2, jnp.zeros_like(p0)], axis=1).astype(BF16)
    for copy in copies[1:]:
        copy.wait()


def halo_kernel(halo_ref, after_ref, mine_ref, to_core_ref):
    c, z, y = place()
    for ref, half in ((mine_ref, c), (to_core_ref, 1 - c)):
        ref[:, 0:HALF] = halo_ref[:, columns(half * HALF, HALF)]
        ref[:, HALF:WIDE] = halo_ref[:, INNER:E]


def conv_piece(x_ref, taps_ref, u_ref, start, halo=None):
    def body(i, _):
        at = columns(start + i * 128, 128)
        cols = columns(i * 128, 128)
        cf, cr = taps_ref[0:4, at], taps_ref[4:8, at]
        x0, x1 = x_ref[0, :, at].astype(F32), x_ref[1, :, at].astype(F32)
        before, after = halo(at) if halo else (x0[0:8], x1[TOK - 8 :])
        for b, rows in enumerate(((before, x0, x1[0:8]), (x0[TOK - 8 :], x1, after))):
            h, g = conv(jnp.concatenate(rows, axis=0), cf, cr)
            u_ref[b, 0, :, cols] = silu_of_half(h[8 : TOK + 8])
            u_ref[b, 1, :, cols] = silu_of_half(g[8 : TOK + 8])
        return _

    lax.fori_loop(0, u_ref.shape[3] // 128, body, 0)


def halo_of(chip_ref, core_ref):
    def rows(at):
        c, z, y = place()
        chip, core = chip_ref[:, at].astype(F32), core_ref[:, at].astype(F32)
        before, after = jnp.where(c == 0, chip, core), jnp.where(c == 0, core, chip)
        return before[HALO - 8 :], after[:8]

    return rows


def repair(x_ref, taps_ref, u_ref, start, halo):
    def body(i, _):
        at = columns(start + i * 256, 256)
        cols = columns(i * 256, 256)
        cf, cr = taps_ref[0:4, at], taps_ref[4:8, at]
        before, after = halo(at)
        h, _g = conv(jnp.concatenate([before, x_ref[0, 0:HALO, at].astype(F32)], axis=0), cf, cr)
        u_ref[0, 0, 0:HALO, cols] = silu_of_half(h[8:])
        _h, g = conv(jnp.concatenate([x_ref[1, TOK - HALO : TOK, at].astype(F32), after], axis=0), cf, cr)
        u_ref[1, 1, TOK - HALO : TOK, cols] = silu_of_half(g[:HALO])
        return _

    lax.fori_loop(0, u_ref.shape[3] // 256, body, 0)


def front_kernel(
    other_ref, x_hbm, step_hbm, decay_hbm, skip_hbm, cf_hbm, cr_hbm, gate_hbm,
    x_ref, table_ref, mcol_ref, mrow_ref, drow_ref, taps_ref, kq_ref, u_ref, gate_ref, gate_to_core_ref,
    step_ref, decay_ref, skip_ref, cf_ref, cr_ref, sems,
):
    c, z, y = place()
    half = columns(c * HALF, HALF)
    copies = copy_all(
        [
            (step_hbm, step_ref),
            (decay_hbm, decay_ref),
            (skip_hbm, skip_ref),
            (x_hbm.at[:, half], x_ref.at[c, :, 0:HALF]),
            (x_hbm.at[:, INNER:E], x_ref.at[c, :, HALF:WIDE]),
            (cf_hbm.at[:, half], cf_ref.at[:, 0:HALF]),
            (cf_hbm.at[:, INNER:E], cf_ref.at[:, HALF:WIDE]),
            (cr_hbm.at[:, half], cr_ref.at[:, 0:HALF]),
            (cr_hbm.at[:, INNER:E], cr_ref.at[:, HALF:WIDE]),
            (other_ref.at[:, 0:WIDE], x_ref.at[1 - c]),
            (gate_hbm.at[:, half], gate_ref),
            (gate_hbm.at[:, columns((1 - c) * HALF, HALF)], gate_to_core_ref),
        ],
        sems,
    )
    for copy in copies[:3]:
        copy.wait()
    def half_of(values):
        return jnp.where(c == 0, values[:, 0 : HEADS // 2], values[:, HEADS // 2 : HEADS])

    parts = other_ref[:, WIDE : WIDE + STEPS].astype(F32)
    other = half_of(parts[:, 0:HEADS] + parts[:, HEADS : 2 * HEADS] + parts[:, 2 * HEADS : 3 * HEADS])
    mine = half_of(jnp.transpose(step_ref[...]))
    step = jnp.concatenate([jnp.where(c == 0, mine, other), jnp.where(c == 0, other, mine)], axis=1)
    decay, skip = half_of(decay_ref[...]), half_of(skip_ref[...])
    decay, skip = jnp.concatenate([decay, decay], axis=1), jnp.concatenate([skip, skip], axis=1)
    make_tables(step, decay, skip, table_ref, mcol_ref, mrow_ref, drow_ref)
    for copy in copies[3:10]:
        copy.wait()
    taps_ref[0:4] = cf_ref[...] * 0.5
    taps_ref[4:8] = cr_ref[...] * 0.5
    conv_piece(x_ref, taps_ref, kq_ref, HALF)
    conv_piece(x_ref, taps_ref, u_ref, start_of(2, 0))
    for copy in copies[10:]:
        copy.wait()


def piece_states(u_ref, kt_ref, table_ref, drow_ref, start, saved_ref, chip_ref):
    blocks = []
    for b in range(2):
        spread = spread_matrix(b * HALF + start)
        drow = dot(drow_ref[...], spread)
        d0, d1 = drow[8:9], drow[9:10]

        def weighted(d, row, r):
            w = dot(table_ref[row, r : r + SUB], spread)
            return (u_ref[b, d, r : r + SUB].astype(F32) * w).astype(BF16)

        f0 = dot(kt_ref[b, 0, :, 0:SUB], weighted(0, WF, 0))
        f1 = dot(kt_ref[b, 0, :, SUB:TOK], weighted(0, WF, SUB))
        r0 = dot(kt_ref[b, 1, :, 0:SUB], weighted(1, WR, 0))
        r1 = dot(kt_ref[b, 1, :, SUB:TOK], weighted(1, WR, SUB))
        saved_ref[2 * b] = f0.astype(BF16)
        saved_ref[2 * b + 1] = r1.astype(BF16)
        blocks.append((d1 * f0 + f1, r0 + d0 * r1, drow[0:1] + drow[1:2]))
    (f0, r0, d0), (f1, r1, d1) = blocks
    saved_ref[4] = f0.astype(BF16)
    saved_ref[5] = r1.astype(BF16)
    chip_ref[0:STATE] = (d1 * f0 + f1).astype(BF16)
    chip_ref[STATE : 2 * STATE] = (r0 + d0 * r1).astype(BF16)
    chip_ref[2 * STATE : MSG] = decay_rows(d0 * d1)


def first_states_kernel(
    kq_in, u_in, x_ref, taps_ref, chip_halo_ref, core_halo_ref, table_ref, drow_ref,
    kq_ref, u_ref, kt_ref, saved_ref, chip_ref,
):
    halo = halo_of(chip_halo_ref, core_halo_ref)
    repair(x_ref, taps_ref, kq_ref, HALF, halo)
    for b in range(2):
        for d in range(2):
            kt_ref[b, d] = jnp.transpose(kq_ref[b, d, :, 0:STATE].astype(F32)).astype(BF16)
    start = start_of(2, 0)
    repair(x_ref, taps_ref, u_ref, start, halo)
    piece_states(u_ref, kt_ref, table_ref, drow_ref, start, saved_ref, chip_ref)


def rest_kernel(todo, x_ref, taps_ref, chip_halo_ref, core_halo_ref, table_ref, drow_ref, kt_ref, after_ref, *outs):
    for n, piece in enumerate(todo):
        u_ref, saved_ref, chip_ref = outs[3 * n : 3 * n + 3]
        conv_piece(x_ref, taps_ref, u_ref, start_of(*piece), halo_of(chip_halo_ref, core_halo_ref))
        piece_states(u_ref, kt_ref, table_ref, drow_ref, start_of(*piece), saved_ref, chip_ref)


KEYS = vmem(BF16, 2, 2, TOK, 2 * STATE)
U = vmem(BF16, 2, 2, TOK, CW)
SAVED = vmem(BF16, 6, STATE, CW)
CHIP = vmem(BF16, MSG, CW)


def group(keep_ref, got_ref, outs):
    c, z, y = place()
    z0 = z == 0
    dm, do = read_decay(keep_ref[2 * STATE : MSG]), read_decay(got_ref[2 * STATE : MSG])
    one = jnp.ones_like(dm)
    am, ao = jnp.where(z0, do, one), jnp.where(z0, one, dm)
    fwd = (am * keep_ref[0:STATE].astype(F32) + ao * got_ref[0:STATE].astype(F32)).astype(BF16)
    am, ao = jnp.where(z0, one, do), jnp.where(z0, dm, one)
    rows = slice(STATE, 2 * STATE)
    rev = (am * keep_ref[rows].astype(F32) + ao * got_ref[rows].astype(F32)).astype(BF16)
    decay = decay_rows(dm * do)
    for k in range(1, 4):
        outs[k - 1][0:STATE] = jnp.where(y + k < 4, fwd, rev)
        outs[k - 1][STATE:YMSG] = decay


def entries(keep_ref, got_ref, r1_ref, r2_ref, r3_ref, mine_ref, back_ref):
    c, z, y = place()
    z0 = z == 0
    r = [ref[0:STATE].astype(F32) for ref in (r1_ref, r2_ref, r3_ref)]
    d = [read_decay(ref[STATE:YMSG]) for ref in (r1_ref, r2_ref, r3_ref)]
    zero = jnp.zeros_like(r[0])
    ef = jnp.where(y >= 3, r[2], zero)
    ef = jnp.where(y >= 2, r[1] + d[1] * ef, zero)
    ef = jnp.where(y >= 1, r[0] + d[0] * ef, zero)
    er = jnp.where(y <= 0, r[0], zero)
    er = jnp.where(y <= 1, r[1] + d[1] * er, zero)
    er = jnp.where(y <= 2, r[2] + d[2] * er, zero)
    dm, do = read_decay(keep_ref[2 * STATE : MSG]), read_decay(got_ref[2 * STATE : MSG])
    df = jnp.where(z0, dm, do)
    tf = jnp.where(z0, keep_ref[0:STATE].astype(F32), got_ref[0:STATE].astype(F32))
    second_f = df * ef + tf
    dr = jnp.where(z0, do, dm)
    rows = slice(STATE, 2 * STATE)
    tr = jnp.where(z0, got_ref[rows].astype(F32), keep_ref[rows].astype(F32))
    first_r = dr * er + tr
    mine_ref[0] = jnp.where(z0, ef, second_f).astype(BF16)
    mine_ref[1] = jnp.where(z0, first_r, er).astype(BF16)
    back_ref[0] = jnp.where(z0, second_f, ef).astype(BF16)
    back_ref[1] = jnp.where(z0, er, first_r).astype(BF16)


def second_phase_kernel(keep_ref, got_ref, zsend_ref, after_ref, zsend_out, *outs):
    group(keep_ref, got_ref, outs)
    zsend_out[...] = zsend_ref[...]


def third_phase_kernel(
    keep0_ref, got0_ref, r1_ref, r2_ref, r3_ref, keep1_ref, got1_ref, after_ref, mine_ref, back_ref, *outs
):
    entries(keep0_ref, got0_ref, r1_ref, r2_ref, r3_ref, mine_ref, back_ref)
    group(keep1_ref, got1_ref, outs)


def fourth_phase_kernel(
    keep_ref, got_ref, r1_ref, r2_ref, r3_ref, after0_ref, after1_ref, mine_ref, back_ref
):
    entries(keep_ref, got_ref, r1_ref, r2_ref, r3_ref, mine_ref, back_ref)


def within_kernel(k, p, u_ref, kq_ref, table_ref, mcol_ref, mrow_ref, drow_ref, after_ref, out_ref, qk_ref):
    row = lax.broadcasted_iota(jnp.int32, (SUB, SUB), 0)
    col = lax.broadcasted_iota(jnp.int32, (SUB, SUB), 1)
    low = lax.broadcasted_iota(jnp.int32, (SUB, 2 * HEAD_DIM), 1) < HEAD_DIM

    def block(b, _):
        for s in range(2):
            rows = slice(s * SUB, (s + 1) * SUB)
            for d in range(2):
                keys = kq_ref[b, d, rows, 0:STATE]
                queries = kq_ref[b, d, rows, STATE : 2 * STATE]
                prod = lax.dot_general(queries, keys, (((1,), (1,)), ((), ())), preferred_element_type=F32)
                qk_ref[d, s] = jnp.where((row >= col) if d == 0 else (row <= col), prod, 0.0)
        start = b * HALF + start_of(k, p)
        first = start // HEAD_DIM
        spread = spread_matrix(start)
        skip = dot(drow_ref[...], spread)[10:11]
        mcol = pltpu.roll(mcol_ref[...], 2 * HEADS - first, 1)
        mrow = mrow_ref[pl.ds(pl.multiple_of(first, HC), HC), :]
        for s in range(2):
            rows = slice(s * SUB, (s + 1) * SUB)
            wv = dot(table_ref[WV, rows], spread)
            gt = dot(table_ref[GT, rows], spread)
            for two in range(HC // 2):
                cols = slice(two * 128, (two + 1) * 128)
                up = u_ref[b, 0, rows, cols].astype(F32)
                xf = (up * wv[:, cols]).astype(BF16)
                xb = (u_ref[b, 1, rows, cols].astype(F32) * wv[:, cols]).astype(BF16)
                none = jnp.zeros_like(xf)
                left, right = [], []
                for h in range(2):
                    at = two * 2 + h
                    diff = mcol[rows, at : at + 1] - mrow[at : at + 1, rows]
                    decay = jnp.exp2(-jnp.abs(diff))
                    left += [(decay * qk_ref[0, s]).astype(BF16), (decay * qk_ref[1, s]).astype(BF16)]
                    keep = low if h == 0 else ~low
                    right += [jnp.where(keep, xf, none), jnp.where(keep, xb, none)]
                res = dot(jnp.concatenate(left, axis=1), jnp.concatenate(right, axis=0))
                out_ref[b, rows, cols] = (res * gt[:, cols] + up * skip[:, cols]).astype(BF16)
        return _

    lax.fori_loop(0, 2, block, 0)


def make_within(k, p, u, kq, table, mcol, mrow, drow, after):
    scratch = [pltpu.VMEM((2, 2, SUB, SUB), F32)]
    operands = (u, kq, table, mcol, mrow, drow, after)
    kernel = functools.partial(within_kernel, k, p)
    return call(kernel, f"within_{k}{p}", [vmem(BF16, 2, TOK, CW)], operands, (), scratch)[0]


def finish_part(k, p, other, entry_ref, saved_ref, within_ref, gate_ref, kq_ref, table_ref, drow_ref, put, square):
    c, z, y = place()
    b = 1 - c if other else c
    start = start_of(k, p)
    at = columns(start, CW)
    spread = spread_matrix(b * HALF + start)
    drow = dot(drow_ref[...], spread)
    d0, d1 = drow[8:9], drow[9:10]
    far = dot(drow_ref[...], spread_matrix((1 - b) * HALF + start))
    far = far[0:1] + far[1:2]
    one = jnp.ones_like(far)
    none = jnp.zeros((STATE, CW), F32)
    first = b == 0
    ef = jnp.where(first, one, far) * entry_ref[0].astype(F32) + jnp.where(first, none, saved_ref[4].astype(F32))
    er = jnp.where(first, far, one) * entry_ref[1].astype(F32) + jnp.where(first, saved_ref[5].astype(F32), none)
    inside = [
        (ef.astype(BF16), (er * d1 + saved_ref[2 * b + 1].astype(F32)).astype(BF16)),
        ((ef * d0 + saved_ref[2 * b].astype(F32)).astype(BF16), er.astype(BF16)),
    ]
    for s in range(2):
        rows = slice(s * SUB, (s + 1) * SUB)
        cf = dot(kq_ref[b, 0, rows, STATE : 2 * STATE], inside[s][0])
        cr = dot(kq_ref[b, 1, rows, STATE : 2 * STATE], inside[s][1])
        gf = dot(table_ref[GF, rows], spread)
        gr = dot(table_ref[GR, rows], spread)
        mixed = within_ref[b, rows].astype(F32) + gf * cf + gr * cr
        half = gate_ref[rows, at].astype(F32) * 0.5
        gated = mixed * (half + half * jnp.tanh(half))
        put(rows, gated)
        sq = gated * gated
        for j in range(0, CW, 128):
            part = sq[:, j : j + 128]
            square[s] = part if square[s] is None else square[s] + part


def finish_piece(k, p, entry_ref, saved_ref, within_ref, gate_refs, shared, own_ref, msg_refs, squares):
    def put_own(rows, gated):
        own_ref[rows] = gated

    def put_other(rows, gated):
        msg_refs[rows.start // SUB][:, 0:CW] = gated.astype(BF16)

    for other, put in ((1, put_other), (0, put_own)):
        finish_part(k, p, other, entry_ref, saved_ref, within_ref, gate_refs[other], *shared, put, squares[other])


NEAR = ((3, 0), (3, 1), (2, 0))
BACK = (2, 1)


def finish_near_kernel(k, p, entry_ref, saved_ref, within_ref, gate_ref, gate_other_ref, *refs):
    shared, (square_in, own_ref, *msg_refs, square_ref) = refs[:3], refs[3:]
    squares = [[None, None], [None, None]]
    finish_piece(k, p, entry_ref, saved_ref, within_ref, (gate_ref, gate_other_ref), shared, own_ref, msg_refs, squares)
    for other in range(2):
        for s in range(2):
            rows = slice(s * SUB, (s + 1) * SUB)
            if (k, p) == NEAR[0]:
                square_ref[other, rows] = squares[other][s]
            else:
                square_ref[other, rows] = square_in[other, rows] + squares[other][s]


def finish_other_kernel(entry_ref, saved_ref, within_ref, gate_ref, *refs):
    shared, square_in, msg_refs = refs[:3], refs[3], refs[-2:]
    square = [square_in[1, s * SUB : (s + 1) * SUB] for s in range(2)]

    def put(rows, gated):
        msg_refs[rows.start // SUB][:, 0:CW] = gated.astype(BF16)

    finish_part(*BACK, 1, entry_ref, saved_ref, within_ref, gate_ref, *shared, put, square)
    lane = lax.broadcasted_iota(jnp.int32, (SUB, 128), 1)
    for s in range(2):
        total = jnp.sum(square[s], axis=1, keepdims=True)
        hi = total.astype(BF16).astype(F32)
        sums = jnp.where(lane == 0, hi, jnp.where(lane == 1, total - hi, 0.0))
        msg_refs[s][:, CW : CW + 128] = sums.astype(BF16)


def finish_own_kernel(entry_ref, saved_ref, within_ref, gate_ref, *refs):
    shared, (square_in, after_ref, gain_hbm, own_ref, square_ref, gain_ref, sem) = refs[:3], refs[3:]
    copy = pltpu.make_async_copy(gain_hbm, gain_ref, sem)
    copy.start()
    square = [square_in[0, s * SUB : (s + 1) * SUB] for s in range(2)]

    def put(rows, gated):
        own_ref[rows] = gated

    finish_part(*BACK, 0, entry_ref, saved_ref, within_ref, gate_ref, *shared, put, square)
    for s in range(2):
        square_ref[s * SUB : (s + 1) * SUB] = square[s]
    copy.wait()


def norm_kernel(*refs):
    own_refs, other_refs, (square_ref, gain_ref, out_hbm, out_ref, sems) = refs[:4], refs[4:12], refs[12:]
    c, z, y = place()
    pieces = []
    for n, piece in enumerate((*NEAR, BACK)):
        pieces.append(((own_refs[n], own_refs[n].at[SUB:TOK]), c * HALF + start_of(*piece)))
        pieces.append((other_refs[2 * n : 2 * n + 2], (1 - c) * HALF + start_of(*piece)))
    step = 32
    copies = []
    for r in range(0, TOK, step):
        rows, inside = slice(r, r + step), slice(r % SUB, r % SUB + step)
        total = square_ref[rows] + other_refs[6 + r // SUB][inside, CW : CW + 128].astype(F32)
        scale = lax.rsqrt(jnp.sum(total, axis=1, keepdims=True) * (1.0 / INNER) + 1e-05)
        for refs, start in pieces:
            at = columns(start, CW)
            out_ref[rows, at] = (refs[r // SUB][inside, 0:CW].astype(F32) * scale * gain_ref[:, at]).astype(BF16)
        copies.append(pltpu.make_async_copy(out_ref.at[rows], out_hbm.at[rows], sems.at[len(copies)]))
        copies[-1].start()
    for copy in copies:
        copy.wait()


def per_device(mixer_input, gate_input, conv_forward, conv_reverse, step_size, decay_rate, skip_scale, norm_gain):
    n = lax.axis_size("seq")

    def send(v, perm):
        return lax.ppermute(v, "seq", perm)

    core = [(i, i ^ 1) for i in range(n)]
    zswap = [(i, i ^ 2) for i in range(n)]
    chips = [(i, i + 1) for i in range(1, n - 1, 2)] + [(i + 1, i) for i in range(1, n - 1, 2)]

    def along_y(msgs):
        return [send(m, [(i, (i + 4 * k) % n) for i in range(n)]) for k, m in enumerate(msgs, 1)]

    to_core, to_chip = call(
        edge_kernel,
        "edges",
        [vmem(BF16, TOK, WIDE + STEPS), vmem(BF16, HALO, E)],
        (),
        (mixer_input, step_size),
        [pltpu.VMEM((HEADS, TOK), F32), pltpu.SemaphoreType.DMA((4,))],
    )
    x, table, mcol, mrow, drow, taps, kq, u2a, gate, gate_to_core = call(
        front_kernel,
        "front",
        [
            vmem(BF16, 2, TOK, WIDE),
            vmem(BF16, 6, TOK, 2 * HEADS),
            vmem(F32, TOK, 2 * HEADS),
            vmem(F32, HEADS, TOK),
            vmem(BF16, 16, 2 * HEADS),
            vmem(F32, 8, WIDE),
            KEYS,
            U,
            vmem(BF16, TOK, HALF),
            vmem(BF16, TOK, HALF),
        ],
        (send(to_core, core),),
        (
            mixer_input,
            step_size,
            decay_rate.reshape(1, HEADS),
            skip_scale.reshape(1, HEADS),
            conv_forward,
            conv_reverse,
            gate_input,
        ),
        [
            pltpu.VMEM((HEADS, TOK), F32),
            pltpu.VMEM((1, HEADS), F32),
            pltpu.VMEM((1, HEADS), F32),
            pltpu.VMEM((4, WIDE), F32),
            pltpu.VMEM((4, WIDE), F32),
            pltpu.SemaphoreType.DMA((12,)),
        ],
    )
    chip_halo, to_core = call(
        halo_kernel, "halo", [vmem(BF16, HALO, WIDE)] * 2, (send(to_chip, chips), kq)
    )
    halo = (x, taps, chip_halo, send(to_core, core))
    kq, u2a, kt, saved2a, zsend0 = call(
        first_states_kernel,
        "states_first",
        [KEYS, U, vmem(BF16, 2, 2, STATE, TOK), SAVED, CHIP],
        (kq, u2a, *halo, table, drow),
        aliases={0: 0, 1: 1},
    )
    got0 = send(zsend0, zswap)

    def make_rest(name, todo, after):
        kernel = functools.partial(rest_kernel, todo)
        return call(kernel, name, [U, SAVED, CHIP] * len(todo), (*halo, table, drow, kt, after))

    u2b, saved2b, zsend1, u3a, saved3a, keep0 = make_rest("states_a", ((2, 1), (3, 0)), zsend0)
    tables = (kq, table, mcol, mrow, drow)

    w2a = make_within(2, 0, u2a, *tables, zsend0)
    yout = [vmem(BF16, YMSG, CW)] * 3
    entry = vmem(BF16, 2, STATE, CW)
    zsend1, *msgs = call(second_phase_kernel, "second_phase", [CHIP, *yout], (keep0, got0, zsend1, w2a))
    got1 = send(zsend1, zswap)
    arrived = along_y(msgs)
    u3b, saved3b, keep1 = make_rest("states_b", ((3, 1),), msgs[0])
    w2b = make_within(2, 1, u2b, *tables, msgs[0])

    mine0, back0, *msgs = call(
        third_phase_kernel, "third_phase", [entry, entry, *yout], (keep0, got0, *arrived, keep1, got1, w2b)
    )
    back0 = send(back0, zswap)
    arrived = along_y(msgs)
    w3a = make_within(3, 0, u3a, *tables, msgs[0])
    w3b = make_within(3, 1, u3b, *tables, w3a)

    mine1, back1 = call(fourth_phase_kernel, "fourth_phase", [entry, entry], (keep1, got1, *arrived, w3b, back0))
    back1 = send(back1, zswap)
    gates = (gate, send(gate_to_core, core))
    shared = (kq, table, drow)
    square = kt
    own, other = [], []
    for (k, p), *part in zip(NEAR, (mine0, mine1, back0), (saved3a, saved3b, saved2a), (w3a, w3b, w2a)):
        gated, *msg, square = call(
            functools.partial(finish_near_kernel, k, p),
            f"finish_{k}{p}",
            [vmem(F32, TOK, CW), vmem(BF16, SUB, CW), vmem(BF16, SUB, CW), vmem(F32, 2, TOK, 128)],
            (*part, *gates, *shared, square),
        )
        own.append(gated)
        other += [send(m, core) for m in msg]
    msg = call(
        finish_other_kernel,
        "finish_other",
        [vmem(BF16, SUB, CW + 128)] * 2,
        (back1, saved2b, w2b, gates[1], *shared, square, *other[:4]),
    )
    other += [send(m, core) for m in msg]
    gated, square, gain = call(
        finish_own_kernel,
        "finish_own",
        [vmem(F32, TOK, CW), vmem(F32, TOK, 128), vmem(F32, 1, INNER)],
        (back1, saved2b, w2b, gates[0], *shared, square, msg[0]),
        (norm_gain.reshape(1, INNER),),
        [pltpu.SemaphoreType.DMA(())],
    )
    own.append(gated)
    (out,) = call(
        norm_kernel,
        "norm",
        [shape(BF16, TOK, INNER)],
        (*own, *other, square, gain),
        (),
        [pltpu.VMEM((TOK, INNER), BF16), pltpu.SemaphoreType.DMA((8,))],
    )
    return out


def solution(mesh):
    in_specs = (
        P(("row", "seq"), None),
        P(("row", "seq"), None),
        P(),
        P(),
        P(None, ("row", "seq")),
        P("row"),
        P(),
        P(),
    )
    out_specs = P(("row", "seq"), None)
    return jax.shard_map(per_device, mesh=mesh, in_specs=in_specs, out_specs=out_specs, check_vma=False)
```

time: 70 us -> 65.7 us (0.939)
  waiting for transfers between devices: 9.96 us -> 6.46 us
  starting transfers between devices: 29.1 us -> 28.2 us
    ppermute x16 -> x22, waiting for transfers between devices: 9.96 us -> 6.46 us  [send(): return lax.ppermute(v, 'seq', perm)]
    ppermute x16 -> x22, starting transfers between devices: 29.1 us -> 28.2 us  [send(): return lax.ppermute(v, 'seq', perm)]
    pallas_call x21 -> x19, Pallas kernels: 30.4 us -> 30.5 us  [call(): pl.pallas_call(kernel, name=name, in_specs=[VMEM] * len(operands) + [HBM]...]
  transfers between devices with their start and end apart: 16 -> 22, of which waited for: 7 -> 7; matrix products, arithmetic and copies ran while one was open for 0% -> 0% of each run, Pallas kernels for 32% -> 41%
where the time goes in v3:
time: 65.7 us; the launch traced here: 65.5 us
  Pallas kernels  30.5 us (46%)
  starting transfers between devices  28.2 us (43%)
  waiting for transfers between devices  6.46 us (10%)
    pallas_call x19, Pallas kernels, call(): pl.pallas_call(kernel, name=name, in_specs=[VMEM] * len(operands) + [HBM]...  30.5 us
    ppermute x22, starting transfers between devices, send(): return lax.ppermute(v, 'seq', perm)  28.2 us
    ppermute x22, waiting for transfers between devices, send(): return lax.ppermute(v, 'seq', perm)  6.46 us
  transfers between devices with their start and end apart: 22, of which 7 were waited for; matrix products, arithmetic and copies ran while one was open for 0% of the time, Pallas kernels for 41%

profile of v3, /device:TPU:1, one launch (start us, length us, event | category | flops | bytes accessed | tf_op | source)
XLA Modules:
  0.0 65.5 jit_solution(1486682889050078515)
XLA Ops:
  0.0 1.4 %edges.1 = (bf16[256,2560]{1,0:T(8,128)(2,1)S(1)}, bf16[16,4352]{1,0:T(8,128)(2,1)S(1)}) custom-call(bf16[256,4352]{1,0:T(8,128)(2,1)} %x_hbm.3, f32[64,256]{1,0:T(8,128)} %step_hbm.3), custom_call_target="tpu_custom_call" | custom-call | flops 100000000 | bytes 300000 | tf_op jit(solution)/shard_map/edges/pallas_call | solution.py:52
  1.4 1.5 %collective-permute-start = (bf16[256,2560]{1,0:T(8,128)(2,1)S(1)}, bf16[256,2560]{1,0:T(8,128)(2,1)S(1)}, u32[]{:S(2)}, u32[]{:S(2)}) collective-permute-start(bf16[256,2560]{1,0:T(8,128)(2,1)S(1)} %get-tuple-element.61), channel_id=1, source_target_pairs={{0,1},{1,0},{2,3},{3,2},{4,5},{5,4},{6,7},{7,6},{8,9},{9,8},{10,11... | collective-permute-start | bytes 3932168 | tf_op jit(solution)/shard_map/ppermute | solution.py:566
  2.9 5.5 %collective-permute-start.1 = (bf16[16,4352]{1,0:T(8,128)(2,1)S(1)}, bf16[16,4352]{1,0:T(8,128)(2,1)S(1)}, u32[]{:S(2)}, u32[]{:S(2)}) collective-permute-start(bf16[16,4352]{1,0:T(8,128)(2,1)S(1)} %get-tuple-element.64), channel_id=1, source_target_pairs={{1,2},{3,4},{5,6},{7,8},{9,10},{11,12},{13,14},{2,1},{4,3},{6,5},{... | collective-permute-start | bytes 417800 | tf_op jit(solution)/shard_map/ppermute | solution.py:566
  8.4 0.0 collective-permute-done.other_ref
  8.4 3.5 %front.1 = (bf16[2,256,2304]{2,1,0:T(8,128)(2,1)S(1)}, bf16[6,256,128]{2,1,0:T(8,128)(2,1)S(1)}, f32[256,128]{1,0:T(8,128)S(1)}, f32[64,256]{1,0:T(8,128)S(1)}, ...) custom-call(bf16[256,2560]{1,0:T(8,128)(2,1)S(1)} %collective-permut, ...), custom_call_target="tpu_custom_call" | custom-call | flops 100000000 | bytes 300000 | tf_op jit(solution)/shard_map/front/pallas_call | solution.py:52
  11.9 0.1 collective-permute-start.8
  12.0 0.6 collective-permute-start.2
  12.6 2.2 %collective-permute-done.2.core_halo_ref = bf16[16,2304]{1,0:T(8,128)(2,1)S(1)} collective-permute-done((bf16[16,2304]{1,0:T(8,128)(2,1)S(1)}, bf16[16,2304]{1,0:T(8,128)(2,1)S(1)}, u32[]{:S(2)}, u32[]{:S(2)}) %collective-permute-start.2) | collective-permute-done | bytes 73760 | tf_op jit(solution)/shard_map/ppermute | solution.py:566
  14.8 1.8 %states_first.1 = (bf16[2,2,256,256]{3,2,1,0:T(8,128)(2,1)S(1)}, bf16[2,2,256,512]{3,2,1,0:T(8,128)(2,1)S(1)}, bf16[2,2,128,256]{3,2,1,0:T(8,128)(2,1)S(1)}, bf1...) custom-call(bf16[2,2,256,256]{3,2,1,0:T(8,128)(2,1)S(1)} %get-tuple-element.65.afte, ...), custom_call_target="tpu_custom_call", output_to_operand_aliasing={{0}: (0, {}), {1}: (1, {})} | custom-call | flops 100000000 | bytes 300000 | tf_op jit(solution)/shard_map/states_first/pallas_call | solution.py:52
  16.6 2.0 %collective-permute-start.3 = (bf16[272,512]{1,0:T(8,128)(2,1)S(1)}, bf16[272,512]{1,0:T(8,128)(2,1)S(1)}, u32[]{:S(2)}, u32[]{:S(2)}) collective-permute-start(bf16[272,512]{1,0:T(8,128)(2,1)S(1)} %get-tuple-element.72.after_ref), channel_id=1, source_target_pairs={{0,2},{1,3},{2,0},{3,1},{4,6},{5,7},{6,4},{7,5},{8,10},{9,11},{10,... | collective-permute-start | bytes 835592 | tf_op jit(solution)/shard_map/ppermute | solution.py:566
  18.6 1.9 %within_20.1.after_ref.within_ref = bf16[2,256,512]{2,1,0:T(8,128)(2,1)S(1)} custom-call(bf16[2,2,256,512]{3,2,1,0:T(8,128)(2,1)S(1)} %get-tuple-element.75.u_ref, bf16[2,2,256,256]{3,2,1,0:T(8,128)(2,1)S(1)} %get-tuple-element.76.kq_ref.refs_0_, bf16[6,256,128]{2,1,0:T(8,128)(2,1)S(1)} %get-tuple-element.68.table_ref.refs_1_, ...), custom_call_target="tpu_custom_call" | custom-call | flops 100000000 | bytes 300000 | tf_op jit(solution)/shard_map/within_20/pallas_call | solution.py:52
  20.5 5.5 %states_a.1 = (bf16[2,2,256,512]{3,2,1,0:T(8,128)(2,1)S(1)}, bf16[6,128,512]{2,1,0:T(8,128)(2,1)S(1)}, bf16[272,512]{1,0:T(8,128)(2,1)S(1)}, bf16[2,2,256,512]{3...) custom-call(bf16[2,256,2304]{2,1,0:T(8,128)(2,1)S(1)} %get-tuple-element.62.x_ref, ...), custom_call_target="tpu_custom_call" | custom-call | flops 100000000 | bytes 300000 | tf_op jit(solution)/shard_map/states_a/pallas_call | solution.py:52
  26.0 0.3 collective-permute-done.3.got_ref.got0_ref
  26.3 0.2 second_phase.1
  26.4 2.0 %collective-permute-start.7 = (bf16[272,512]{1,0:T(8,128)(2,1)S(1)}, bf16[272,512]{1,0:T(8,128)(2,1)S(1)}, u32[]{:S(2)}, u32[]{:S(2)}) collective-permute-start(bf16[272,512]{1,0:T(8,128)(2,1)S(1)} %get-tuple-element.83), channel_id=1, source_target_pairs={{0,2},{1,3},{2,0},{3,1},{4,6},{5,7},{6,4},{7,5},{8,10},{9,11},{10,... | collective-permute-start | bytes 835592 | tf_op jit(solution)/shard_map/ppermute | solution.py:566
  28.5 2.9 %collective-permute-start.5 = (bf16[144,512]{1,0:T(8,128)(2,1)S(1)}, bf16[144,512]{1,0:T(8,128)(2,1)S(1)}, u32[]{:S(2)}, u32[]{:S(2)}) collective-permute-start(bf16[144,512]{1,0:T(8,128)(2,1)S(1)} %get-tuple-element.80), channel_id=1, source_target_pairs={{0,8},{1,9},{2,10},{3,11},{4,12},{5,13},{6,14},{7,15},{8,0},{9,1},... | collective-permute-start | bytes 442376 | tf_op jit(solution)/shard_map/ppermute | solution.py:566
  31.4 0.8 %collective-permute-start.6 = (bf16[144,512]{1,0:T(8,128)(2,1)S(1)}, bf16[144,512]{1,0:T(8,128)(2,1)S(1)}, u32[]{:S(2)}, u32[]{:S(2)}) collective-permute-start(bf16[144,512]{1,0:T(8,128)(2,1)S(1)} %get-tuple-element.81), channel_id=1, source_target_pairs={{0,12},{1,13},{2,14},{3,15},{4,0},{5,1},{6,2},{7,3},{8,4},{9,5},{1... | collective-permute-start | bytes 442376 | tf_op jit(solution)/shard_map/ppermute | solution.py:566
  32.1 0.7 %collective-permute-start.4 = (bf16[144,512]{1,0:T(8,128)(2,1)S(1)}, bf16[144,512]{1,0:T(8,128)(2,1)S(1)}, u32[]{:S(2)}, u32[]{:S(2)}) collective-permute-start(bf16[144,512]{1,0:T(8,128)(2,1)S(1)} %get-tuple-element.79.after_ref), channel_id=1, source_target_pairs={{0,4},{1,5},{2,6},{3,7},{4,8},{5,9},{6,10},{7,11},{8,12},{9,13},{1... | collective-permute-start | bytes 442376 | tf_op jit(solution)/shard_map/ppermute | solution.py:566
  32.8 1.9 %within_21.1.after_ref.within_ref = bf16[2,256,512]{2,1,0:T(8,128)(2,1)S(1)} custom-call(bf16[2,2,256,512]{3,2,1,0:T(8,128)(2,1)S(1)} %get-tuple-element.84.u_ref, bf16[2,2,256,256]{3,2,1,0:T(8,128)(2,1)S(1)} %get-tuple-element.76.kq_ref.refs_0_, bf16[6,256,128]{2,1,0:T(8,128)(2,1)S(1)} %get-tuple-element.68.table_ref.refs_1_, ...), custom_call_target="tpu_custom_call" | custom-call | flops 100000000 | bytes 300000 | tf_op jit(solution)/shard_map/within_21/pallas_call | solution.py:52
  34.7 2.7 %states_b.1 = (bf16[2,2,256,512]{3,2,1,0:T(8,128)(2,1)S(1)}, bf16[6,128,512]{2,1,0:T(8,128)(2,1)S(1)}, bf16[272,512]{1,0:T(8,128)(2,1)S(1)}) custom-call(bf16[2,256,2304]{2,1,0:T(8,128)(2,1)S(1)} %get-tuple-element.62.x_ref, f32[8,2304]{1,0:T(8,128)S(1)} %get-tuple-element.63.taps_ref, bf16[16,2304]{1,0:T(8,128)(2,1)S(1)} %get-tuple-element.66.chip_halo_ref, ...), custom_call_target="tpu_custom_call" | custom-call | flops 100000000 | bytes 300000 | tf_op jit(solution)/shard_map/states_b/pallas_call | solution.py:52
  37.5 0.5 collective-permute-done.4.r1_ref
  38.0 0.5 third_phase.1
  38.5 1.1 %collective-permute-start.12 = (bf16[2,128,512]{2,1,0:T(8,128)(2,1)S(1)}, bf16[2,128,512]{2,1,0:T(8,128)(2,1)S(1)}, u32[]{:S(2)}, u32[]{:S(2)}) collective-permute-start(bf16[2,128,512]{2,1,0:T(8,128)(2,1)S(1)} %get-tuple-element.95), channel_id=1, source_target_pairs={{0,2},{1,3},{2,0},{3,1},{4,6},{5,7},{6,4},{7,5},{8,10},{9,11},{10,... | collective-permute-start | bytes 786440 | tf_op jit(solution)/shard_map/ppermute | solution.py:566
  39.5 2.7 %collective-permute-start.10 = (bf16[144,512]{1,0:T(8,128)(2,1)S(1)}, bf16[144,512]{1,0:T(8,128)(2,1)S(1)}, u32[]{:S(2)}, u32[]{:S(2)}) collective-permute-start(bf16[144,512]{1,0:T(8,128)(2,1)S(1)} %get-tuple-element.92), channel_id=1, source_target_pairs={{0,8},{1,9},{2,10},{3,11},{4,12},{5,13},{6,14},{7,15},{8,0},{9,1},... | collective-permute-start | bytes 442376 | tf_op jit(solution)/shard_map/ppermute | solution.py:566
  42.2 1.0 %collective-permute-start.11 = (bf16[144,512]{1,0:T(8,128)(2,1)S(1)}, bf16[144,512]{1,0:T(8,128)(2,1)S(1)}, u32[]{:S(2)}, u32[]{:S(2)}) collective-permute-start(bf16[144,512]{1,0:T(8,128)(2,1)S(1)} %get-tuple-element.93), channel_id=1, source_target_pairs={{0,12},{1,13},{2,14},{3,15},{4,0},{5,1},{6,2},{7,3},{8,4},{9,5},{1... | collective-permute-start | bytes 442376 | tf_op jit(solution)/shard_map/ppermute | solution.py:566
  43.2 0.5 collective-permute-start.9
  43.7 1.9 %within_30.1.within_ref.after_ref = bf16[2,256,512]{2,1,0:T(8,128)(2,1)S(1)} custom-call(bf16[2,2,256,512]{3,2,1,0:T(8,128)(2,1)S(1)} %get-tuple-element.87.u_ref, bf16[2,2,256,256]{3,2,1,0:T(8,128)(2,1)S(1)} %get-tuple-element.76.kq_ref.refs_0_, bf16[6,256,128]{2,1,0:T(8,128)(2,1)S(1)} %get-tuple-element.68.table_ref.refs_1_, ...), custom_call_target="tpu_custom_call" | custom-call | flops 100000000 | bytes 300000 | tf_op jit(solution)/shard_map/within_30/pallas_call | solution.py:52
  45.6 1.9 %within_31.1.after0_ref.within_ref = bf16[2,256,512]{2,1,0:T(8,128)(2,1)S(1)} custom-call(bf16[2,2,256,512]{3,2,1,0:T(8,128)(2,1)S(1)} %get-tuple-element.94.u_ref, bf16[2,2,256,256]{3,2,1,0:T(8,128)(2,1)S(1)} %get-tuple-element.76.kq_ref.refs_0_, bf16[6,256,128]{2,1,0:T(8,128)(2,1)S(1)} %get-tuple-element.68.table_ref.refs_1_, ...), custom_call_target="tpu_custom_call" | custom-call | flops 100000000 | bytes 300000 | tf_op jit(solution)/shard_map/within_31/pallas_call | solution.py:52
  47.5 1.5 %collective-permute-done.11.r3_ref = bf16[144,512]{1,0:T(8,128)(2,1)S(1)} collective-permute-done((bf16[144,512]{1,0:T(8,128)(2,1)S(1)}, bf16[144,512]{1,0:T(8,128)(2,1)S(1)}, u32[]{:S(2)}, u32[]{:S(2)}) %collective-permute-start.11) | collective-permute-done | bytes 147488 | tf_op jit(solution)/shard_map/ppermute | solution.py:566
  48.9 1.5 %collective-permute-done.9.r1_ref = bf16[144,512]{1,0:T(8,128)(2,1)S(1)} collective-permute-done((bf16[144,512]{1,0:T(8,128)(2,1)S(1)}, bf16[144,512]{1,0:T(8,128)(2,1)S(1)}, u32[]{:S(2)}, u32[]{:S(2)}) %collective-permute-start.9) | collective-permute-done | bytes 147488 | tf_op jit(solution)/shard_map/ppermute | solution.py:566
  50.4 0.3 fourth_phase.1
  50.7 2.1 %collective-permute-start.13 = (bf16[2,128,512]{2,1,0:T(8,128)(2,1)S(1)}, bf16[2,128,512]{2,1,0:T(8,128)(2,1)S(1)}, u32[]{:S(2)}, u32[]{:S(2)}) collective-permute-start(bf16[2,128,512]{2,1,0:T(8,128)(2,1)S(1)} %get-tuple-element.103), channel_id=1, source_target_pairs={{0,2},{1,3},{2,0},{3,1},{4,6},{5,7},{6,4},{7,5},{8,10},{9,11},{10,... | collective-permute-start | bytes 786440 | tf_op jit(solution)/shard_map/ppermute | solution.py:566
  52.9 1.3 %finish_30.1 = (f32[256,512]{1,0:T(8,128)S(1)}, bf16[128,512]{1,0:T(8,128)(2,1)S(1)}, bf16[128,512]{1,0:T(8,128)(2,1)S(1)}, f32[2,256,128]{2,1,0:T(8,128)S(1)}) custom-call(bf16[2,128,512]{2,1,0:T(8,128)(2,1)S(1)} %get-tuple-element.85.entry_ref, bf16[6,128,512]{2,1,0:T(8,128)(2,1)S(1)} %get-tuple-element.86.saved_ref, ...), custom_call_target="tpu_custom_call" | custom-call | flops 100000000 | bytes 300000 | tf_op jit(solution)/shard_map/finish_30/pallas_call | solution.py:52
  54.2 2.2 %collective-permute-start.14 = (bf16[128,512]{1,0:T(8,128)(2,1)S(1)}, bf16[128,512]{1,0:T(8,128)(2,1)S(1)}, u32[]{:S(2)}, u32[]{:S(2)}) collective-permute-start(bf16[128,512]{1,0:T(8,128)(2,1)S(1)} %get-tuple-element.106), channel_id=1, source_target_pairs={{0,1},{1,0},{2,3},{3,2},{4,5},{5,4},{6,7},{7,6},{8,9},{9,8},{10,11... | collective-permute-start | bytes 393224 | tf_op jit(solution)/shard_map/ppermute | solution.py:566
  56.4 0.1 collective-permute-start.15
  56.5 1.3 %finish_31.1 = (f32[256,512]{1,0:T(8,128)S(1)}, bf16[128,512]{1,0:T(8,128)(2,1)S(1)}, bf16[128,512]{1,0:T(8,128)(2,1)S(1)}, f32[2,256,128]{2,1,0:T(8,128)S(1)}) custom-call(bf16[2,128,512]{2,1,0:T(8,128)(2,1)S(1)} %get-tuple-element.96.entry_ref, bf16[6,128,512]{2,1,0:T(8,128)(2,1)S(1)} %get-tuple-element.97.saved_ref, ...), custom_call_target="tpu_custom_call" | custom-call | flops 100000000 | bytes 300000 | tf_op jit(solution)/shard_map/finish_31/pallas_call | solution.py:52
  57.9 0.5 collective-permute-start.16
  58.4 0.1 collective-permute-start.17
  58.4 1.4 %finish_20.1 = (f32[256,512]{1,0:T(8,128)S(1)}, bf16[128,512]{1,0:T(8,128)(2,1)S(1)}, bf16[128,512]{1,0:T(8,128)(2,1)S(1)}, f32[2,256,128]{2,1,0:T(8,128)S(1)}) custom-call(bf16[2,128,512]{2,1,0:T(8,128)(2,1)S(1)} %collective-permute-done.12.after1_ref.entry_ref, bf16[6,128,512]{2,1,0:T(8,128)(2,1)S(1)} %get-tuple-element.100.saved_ref, ...), custom_call_target="tpu_custom_call" | custom-call | flops 100000000 | bytes 300000 | tf_op jit(solution)/shard_map/finish_20/pallas_call | solution.py:52
  59.9 0.8 %finish_other.1 = (bf16[128,640]{1,0:T(8,128)(2,1)S(1)}, bf16[128,640]{1,0:T(8,128)(2,1)S(1)}) custom-call(bf16[2,128,512]{2,1,0:T(8,128)(2,1)S(1)} %collective-permute-done.13.entry_ref, bf16[6,128,512]{2,1,0:T(8,128)(2,1)S(1)} %get-tuple-element.104.saved_ref, bf16[2,256,512]{2,1,0:T(8,128)(2,1)S(1)} %within_21.1.after_ref.within_ref, ...), custom_call_target="tpu_custom_call" | custom-call | flops 100000000 | bytes 300000 | tf_op jit(solution)/shard_map/finish_other/pallas_call | solution.py:52
  60.7 1.3 %collective-permute-start.21 = (bf16[128,640]{1,0:T(8,128)(2,1)S(1)}, bf16[128,640]{1,0:T(8,128)(2,1)S(1)}, u32[]{:S(2)}, u32[]{:S(2)}) collective-permute-start(bf16[128,640]{1,0:T(8,128)(2,1)S(1)} %get-tuple-element.114), channel_id=1, source_target_pairs={{0,1},{1,0},{2,3},{3,2},{4,5},{5,4},{6,7},{7,6},{8,9},{9,8},{10,11... | collective-permute-start | bytes 491528 | tf_op jit(solution)/shard_map/ppermute | solution.py:566
  62.0 0.1 collective-permute-start.20
  62.1 0.4 collective-permute-start.18
  62.5 0.1 collective-permute-start.19
  62.6 0.8 %finish_own.1 = (f32[256,512]{1,0:T(8,128)S(1)}, f32[256,128]{1,0:T(8,128)S(1)}, f32[1,4096]{1,0:T(1,128)S(1)}) custom-call(bf16[2,128,512]{2,1,0:T(8,128)(2,1)S(1)} %collective-permute-done.13.entry_ref, bf16[6,128,512]{2,1,0:T(8,128)(2,1)S(1)} %get-tuple-element.104.saved_ref, bf16[2,256,512]{2,1,0:T(8,128)(2,1)S(1)} %within_21.1.after_ref.within_ref, ...), custom_call_target="tpu_custom_call" | custom-call | flops 100000000 | bytes 300000 | tf_op jit(solution)/shard_map/finish_own/pallas_call | solution.py:52
  63.4 0.2 collective-permute-done.18.refs_8_
  63.6 0.3 collective-permute-done.19.refs_9_
  63.9 1.5 %norm.1 = bf16[256,4096]{1,0:T(8,128)(2,1)} custom-call(f32[256,512]{1,0:T(8,128)S(1)} %get-tuple-element.91.refs_0_, f32[256,512]{1,0:T(8,128)S(1)} %get-tuple-element.99.refs_1_, f32[256,512]{1,0:T(8,128)S(1)} %get-tuple-element.102.refs_2_, f32[256,512]{1,0:T(8,128)S(1)} %get-tuple-element.111.refs_3_, ...), custom_call_target="tpu_custom_call" | custom-call | flops 100000000 | bytes 300000 | tf_op jit(solution)/shard_map/norm/pallas_call | solution.py:52
  (15 shorter events, 0.1 us)
Async XLA Ops:
  1.4 7.0 %collective-permute-start = (bf16[256,2560]{1,0:T(8,128)(2,1)S(1)}, bf16[256,2560]{1,0:T(8,128)(2,1)S(1)}, u32[]{:S(2)}, u32[]{:S(2)}) collective-permute-start(bf16[256,2560]{1,0:T(8,128)(2,1)S(1)} %get-tuple-element.61), channel_id=1, source_target_pairs={{0,1},{1,0},{2,3},{3,2},{4,5},{5,4},{6,7},{7,6},{8,9},{9,8},{10,11... | collective-permute-start | bytes 3932168 | tf_op jit(solution)/shard_map/ppermute | solution.py:566
  2.9 9.1 %collective-permute-start.1 = (bf16[16,4352]{1,0:T(8,128)(2,1)S(1)}, bf16[16,4352]{1,0:T(8,128)(2,1)S(1)}, u32[]{:S(2)}, u32[]{:S(2)}) collective-permute-start(bf16[16,4352]{1,0:T(8,128)(2,1)S(1)} %get-tuple-element.64), channel_id=1, source_target_pairs={{1,2},{3,4},{5,6},{7,8},{9,10},{11,12},{13,14},{2,1},{4,3},{6,5},{... | collective-permute-start | bytes 417800 | tf_op jit(solution)/shard_map/ppermute | solution.py:566
  11.9 41.0 %collective-permute-start.8 = (bf16[256,2048]{1,0:T(8,128)(2,1)S(1)}, bf16[256,2048]{1,0:T(8,128)(2,1)S(1)}, u32[]{:S(2)}, u32[]{:S(2)}) collective-permute-start(bf16[256,2048]{1,0:T(8,128)(2,1)S(1)} %get-tuple-element.90), channel_id=1, source_target_pairs={{0,1},{1,0},{2,3},{3,2},{4,5},{5,4},{6,7},{7,6},{8,9},{9,8},{10,11... | collective-permute-start | bytes 3145736 | tf_op jit(solution)/shard_map/ppermute | solution.py:566
  12.0 2.7 %collective-permute-start.2 = (bf16[16,2304]{1,0:T(8,128)(2,1)S(1)}, bf16[16,2304]{1,0:T(8,128)(2,1)S(1)}, u32[]{:S(2)}, u32[]{:S(2)}) collective-permute-start(bf16[16,2304]{1,0:T(8,128)(2,1)S(1)} %get-tuple-element.67), channel_id=1, source_target_pairs={{0,1},{1,0},{2,3},{3,2},{4,5},{5,4},{6,7},{7,6},{8,9},{9,8},{10,11... | collective-permute-start | bytes 221192 | tf_op jit(solution)/shard_map/ppermute | solution.py:566
  16.6 9.7 %collective-permute-start.3 = (bf16[272,512]{1,0:T(8,128)(2,1)S(1)}, bf16[272,512]{1,0:T(8,128)(2,1)S(1)}, u32[]{:S(2)}, u32[]{:S(2)}) collective-permute-start(bf16[272,512]{1,0:T(8,128)(2,1)S(1)} %get-tuple-element.72.after_ref), channel_id=1, source_target_pairs={{0,2},{1,3},{2,0},{3,1},{4,6},{5,7},{6,4},{7,5},{8,10},{9,11},{10,... | collective-permute-start | bytes 835592 | tf_op jit(solution)/shard_map/ppermute | solution.py:566
  26.4 11.5 %collective-permute-start.7 = (bf16[272,512]{1,0:T(8,128)(2,1)S(1)}, bf16[272,512]{1,0:T(8,128)(2,1)S(1)}, u32[]{:S(2)}, u32[]{:S(2)}) collective-permute-start(bf16[272,512]{1,0:T(8,128)(2,1)S(1)} %get-tuple-element.83), channel_id=1, source_target_pairs={{0,2},{1,3},{2,0},{3,1},{4,6},{5,7},{6,4},{7,5},{8,10},{9,11},{10,... | collective-permute-start | bytes 835592 | tf_op jit(solution)/shard_map/ppermute | solution.py:566
  28.5 9.0 %collective-permute-start.5 = (bf16[144,512]{1,0:T(8,128)(2,1)S(1)}, bf16[144,512]{1,0:T(8,128)(2,1)S(1)}, u32[]{:S(2)}, u32[]{:S(2)}) collective-permute-start(bf16[144,512]{1,0:T(8,128)(2,1)S(1)} %get-tuple-element.80), channel_id=1, source_target_pairs={{0,8},{1,9},{2,10},{3,11},{4,12},{5,13},{6,14},{7,15},{8,0},{9,1},... | collective-permute-start | bytes 442376 | tf_op jit(solution)/shard_map/ppermute | solution.py:566
  31.4 6.1 %collective-permute-start.6 = (bf16[144,512]{1,0:T(8,128)(2,1)S(1)}, bf16[144,512]{1,0:T(8,128)(2,1)S(1)}, u32[]{:S(2)}, u32[]{:S(2)}) collective-permute-start(bf16[144,512]{1,0:T(8,128)(2,1)S(1)} %get-tuple-element.81), channel_id=1, source_target_pairs={{0,12},{1,13},{2,14},{3,15},{4,0},{5,1},{6,2},{7,3},{8,4},{9,5},{1... | collective-permute-start | bytes 442376 | tf_op jit(solution)/shard_map/ppermute | solution.py:566
  32.1 5.8 %collective-permute-start.4 = (bf16[144,512]{1,0:T(8,128)(2,1)S(1)}, bf16[144,512]{1,0:T(8,128)(2,1)S(1)}, u32[]{:S(2)}, u32[]{:S(2)}) collective-permute-start(bf16[144,512]{1,0:T(8,128)(2,1)S(1)} %get-tuple-element.79.after_ref), channel_id=1, source_target_pairs={{0,4},{1,5},{2,6},{3,7},{4,8},{5,9},{6,10},{7,11},{8,12},{9,13},{1... | collective-permute-start | bytes 442376 | tf_op jit(solution)/shard_map/ppermute | solution.py:566
  38.5 12.0 %collective-permute-start.12 = (bf16[2,128,512]{2,1,0:T(8,128)(2,1)S(1)}, bf16[2,128,512]{2,1,0:T(8,128)(2,1)S(1)}, u32[]{:S(2)}, u32[]{:S(2)}) collective-permute-start(bf16[2,128,512]{2,1,0:T(8,128)(2,1)S(1)} %get-tuple-element.95), channel_id=1, source_target_pairs={{0,2},{1,3},{2,0},{3,1},{4,6},{5,7},{6,4},{7,5},{8,10},{9,11},{10,... | collective-permute-start | bytes 786440 | tf_op jit(solution)/shard_map/ppermute | solution.py:566
  39.5 7.9 %collective-permute-start.10 = (bf16[144,512]{1,0:T(8,128)(2,1)S(1)}, bf16[144,512]{1,0:T(8,128)(2,1)S(1)}, u32[]{:S(2)}, u32[]{:S(2)}) collective-permute-start(bf16[144,512]{1,0:T(8,128)(2,1)S(1)} %get-tuple-element.92), channel_id=1, source_target_pairs={{0,8},{1,9},{2,10},{3,11},{4,12},{5,13},{6,14},{7,15},{8,0},{9,1},... | collective-permute-start | bytes 442376 | tf_op jit(solution)/shard_map/ppermute | solution.py:566
  42.2 6.7 %collective-permute-start.11 = (bf16[144,512]{1,0:T(8,128)(2,1)S(1)}, bf16[144,512]{1,0:T(8,128)(2,1)S(1)}, u32[]{:S(2)}, u32[]{:S(2)}) collective-permute-start(bf16[144,512]{1,0:T(8,128)(2,1)S(1)} %get-tuple-element.93), channel_id=1, source_target_pairs={{0,12},{1,13},{2,14},{3,15},{4,0},{5,1},{6,2},{7,3},{8,4},{9,5},{1... | collective-permute-start | bytes 442376 | tf_op jit(solution)/shard_map/ppermute | solution.py:566
  43.2 7.2 %collective-permute-start.9 = (bf16[144,512]{1,0:T(8,128)(2,1)S(1)}, bf16[144,512]{1,0:T(8,128)(2,1)S(1)}, u32[]{:S(2)}, u32[]{:S(2)}) collective-permute-start(bf16[144,512]{1,0:T(8,128)(2,1)S(1)} %get-tuple-element.88.after_ref), channel_id=1, source_target_pairs={{0,4},{1,5},{2,6},{3,7},{4,8},{5,9},{6,10},{7,11},{8,12},{9,13},{1... | collective-permute-start | bytes 442376 | tf_op jit(solution)/shard_map/ppermute | solution.py:566
  50.7 9.1 %collective-permute-start.13 = (bf16[2,128,512]{2,1,0:T(8,128)(2,1)S(1)}, bf16[2,128,512]{2,1,0:T(8,128)(2,1)S(1)}, u32[]{:S(2)}, u32[]{:S(2)}) collective-permute-start(bf16[2,128,512]{2,1,0:T(8,128)(2,1)S(1)} %get-tuple-element.103), channel_id=1, source_target_pairs={{0,2},{1,3},{2,0},{3,1},{4,6},{5,7},{6,4},{7,5},{8,10},{9,11},{10,... | collective-permute-start | bytes 786440 | tf_op jit(solution)/shard_map/ppermute | solution.py:566
  54.2 5.6 %collective-permute-start.14 = (bf16[128,512]{1,0:T(8,128)(2,1)S(1)}, bf16[128,512]{1,0:T(8,128)(2,1)S(1)}, u32[]{:S(2)}, u32[]{:S(2)}) collective-permute-start(bf16[128,512]{1,0:T(8,128)(2,1)S(1)} %get-tuple-element.106), channel_id=1, source_target_pairs={{0,1},{1,0},{2,3},{3,2},{4,5},{5,4},{6,7},{7,6},{8,9},{9,8},{10,11... | collective-permute-start | bytes 393224 | tf_op jit(solution)/shard_map/ppermute | solution.py:566
  56.4 3.4 %collective-permute-start.15 = (bf16[128,512]{1,0:T(8,128)(2,1)S(1)}, bf16[128,512]{1,0:T(8,128)(2,1)S(1)}, u32[]{:S(2)}, u32[]{:S(2)}) collective-permute-start(bf16[128,512]{1,0:T(8,128)(2,1)S(1)} %get-tuple-element.107), channel_id=1, source_target_pairs={{0,1},{1,0},{2,3},{3,2},{4,5},{5,4},{6,7},{7,6},{8,9},{9,8},{10,11... | collective-permute-start | bytes 393224 | tf_op jit(solution)/shard_map/ppermute | solution.py:566
  57.9 2.0 %collective-permute-start.16 = (bf16[128,512]{1,0:T(8,128)(2,1)S(1)}, bf16[128,512]{1,0:T(8,128)(2,1)S(1)}, u32[]{:S(2)}, u32[]{:S(2)}) collective-permute-start(bf16[128,512]{1,0:T(8,128)(2,1)S(1)} %get-tuple-element.108), channel_id=1, source_target_pairs={{0,1},{1,0},{2,3},{3,2},{4,5},{5,4},{6,7},{7,6},{8,9},{9,8},{10,11... | collective-permute-start | bytes 393224 | tf_op jit(solution)/shard_map/ppermute | solution.py:566
  58.4 1.5 %collective-permute-start.17 = (bf16[128,512]{1,0:T(8,128)(2,1)S(1)}, bf16[128,512]{1,0:T(8,128)(2,1)S(1)}, u32[]{:S(2)}, u32[]{:S(2)}) collective-permute-start(bf16[128,512]{1,0:T(8,128)(2,1)S(1)} %get-tuple-element.109), channel_id=1, source_target_pairs={{0,1},{1,0},{2,3},{3,2},{4,5},{5,4},{6,7},{7,6},{8,9},{9,8},{10,11... | collective-permute-start | bytes 393224 | tf_op jit(solution)/shard_map/ppermute | solution.py:566
  60.7 3.2 %collective-permute-start.21 = (bf16[128,640]{1,0:T(8,128)(2,1)S(1)}, bf16[128,640]{1,0:T(8,128)(2,1)S(1)}, u32[]{:S(2)}, u32[]{:S(2)}) collective-permute-start(bf16[128,640]{1,0:T(8,128)(2,1)S(1)} %get-tuple-element.114), channel_id=1, source_target_pairs={{0,1},{1,0},{2,3},{3,2},{4,5},{5,4},{6,7},{7,6},{8,9},{9,8},{10,11... | collective-permute-start | bytes 491528 | tf_op jit(solution)/shard_map/ppermute | solution.py:566
  62.0 1.9 %collective-permute-start.20 = (bf16[128,640]{1,0:T(8,128)(2,1)S(1)}, bf16[128,640]{1,0:T(8,128)(2,1)S(1)}, u32[]{:S(2)}, u32[]{:S(2)}) collective-permute-start(bf16[128,640]{1,0:T(8,128)(2,1)S(1)} %get-tuple-element.110.refs_4_), channel_id=1, source_target_pairs={{0,1},{1,0},{2,3},{3,2},{4,5},{5,4},{6,7},{7,6},{8,9},{9,8},{10,11... | collective-permute-start | bytes 491528 | tf_op jit(solution)/shard_map/ppermute | solution.py:566
  62.1 1.5 %collective-permute-start.18 = (bf16[128,512]{1,0:T(8,128)(2,1)S(1)}, bf16[128,512]{1,0:T(8,128)(2,1)S(1)}, u32[]{:S(2)}, u32[]{:S(2)}) collective-permute-start(bf16[128,512]{1,0:T(8,128)(2,1)S(1)} %get-tuple-element.112), channel_id=1, source_target_pairs={{0,1},{1,0},{2,3},{3,2},{4,5},{5,4},{6,7},{7,6},{8,9},{9,8},{10,11... | collective-permute-start | bytes 393224 | tf_op jit(solution)/shard_map/ppermute | solution.py:566
  62.5 1.3 %collective-permute-start.19 = (bf16[128,512]{1,0:T(8,128)(2,1)S(1)}, bf16[128,512]{1,0:T(8,128)(2,1)S(1)}, u32[]{:S(2)}, u32[]{:S(2)}) collective-permute-start(bf16[128,512]{1,0:T(8,128)(2,1)S(1)} %get-tuple-element.113), channel_id=1, source_target_pairs={{0,1},{1,0},{2,3},{3,2},{4,5},{5,4},{6,7},{7,6},{8,9},{9,8},{10,11... | collective-permute-start | bytes 393224 | tf_op jit(solution)/shard_map/ppermute | solution.py:566

commit v4 on v3

--- a/solution.py
+++ b/solution.py
@@ -82,6 +82,11 @@
     col = lax.broadcasted_iota(jnp.int32, (2 * HEADS, width), 1)
     low = (k & (HEADS - 1)) * HEAD_DIM - start
     return jnp.where((col >= low) & (col < low + HEAD_DIM), 1.0, 0.0).astype(BF16)
+
+
+def expand(table_ref, first, spread):
+    both = dot(table_ref[first : first + 2].reshape(2 * TOK, 2 * HEADS), spread)
+    return both[0:TOK], both[TOK:]
 
 
 def read_decay(rows):
@@ -234,8 +239,8 @@
 
 
 def front_kernel(
-    other_ref, x_hbm, step_hbm, decay_hbm, skip_hbm, cf_hbm, cr_hbm, gate_hbm,
-    x_ref, table_ref, mcol_ref, mrow_ref, drow_ref, taps_ref, kq_ref, u_ref, gate_ref, gate_to_core_ref,
+    other_ref, x_hbm, step_hbm, decay_hbm, skip_hbm, cf_hbm, cr_hbm,
+    x_ref, table_ref, mcol_ref, mrow_ref, drow_ref, taps_ref, kq_ref, u_ref,
     step_ref, decay_ref, skip_ref, cf_ref, cr_ref, sems,
 ):
     c, z, y = place()
@@ -252,8 +257,6 @@
             (cr_hbm.at[:, half], cr_ref.at[:, 0:HALF]),
             (cr_hbm.at[:, INNER:E], cr_ref.at[:, HALF:WIDE]),
             (other_ref.at[:, 0:WIDE], x_ref.at[1 - c]),
-            (gate_hbm.at[:, half], gate_ref),
-            (gate_hbm.at[:, columns((1 - c) * HALF, HALF)], gate_to_core_ref),
         ],
         sems,
     )
@@ -269,31 +272,31 @@
     decay, skip = half_of(decay_ref[...]), half_of(skip_ref[...])
     decay, skip = jnp.concatenate([decay, decay], axis=1), jnp.concatenate([skip, skip], axis=1)
     make_tables(step, decay, skip, table_ref, mcol_ref, mrow_ref, drow_ref)
-    for copy in copies[3:10]:
+    for copy in copies[3:]:
         copy.wait()
     taps_ref[0:4] = cf_ref[...] * 0.5
     taps_ref[4:8] = cr_ref[...] * 0.5
     conv_piece(x_ref, taps_ref, kq_ref, HALF)
     conv_piece(x_ref, taps_ref, u_ref, start_of(2, 0))
-    for copy in copies[10:]:
-        copy.wait()
-
-
-def piece_states(u_ref, kt_ref, table_ref, drow_ref, start, saved_ref, chip_ref):
+
+
+def piece_states(u_ref, kt_ref, table_ref, drow_ref, start, saved_ref, spread_ref, chip_ref):
     blocks = []
     for b in range(2):
         spread = spread_matrix(b * HALF + start)
+        spread_ref[b] = spread
         drow = dot(drow_ref[...], spread)
         d0, d1 = drow[8:9], drow[9:10]
 
-        def weighted(d, row, r):
-            w = dot(table_ref[row, r : r + SUB], spread)
-            return (u_ref[b, d, r : r + SUB].astype(F32) * w).astype(BF16)
-
-        f0 = dot(kt_ref[b, 0, :, 0:SUB], weighted(0, WF, 0))
-        f1 = dot(kt_ref[b, 0, :, SUB:TOK], weighted(0, WF, SUB))
-        r0 = dot(kt_ref[b, 1, :, 0:SUB], weighted(1, WR, 0))
-        r1 = dot(kt_ref[b, 1, :, SUB:TOK], weighted(1, WR, SUB))
+        weights = expand(table_ref, WF, spread)
+
+        def weighted(d, r):
+            return (u_ref[b, d, r : r + SUB].astype(F32) * weights[d][r : r + SUB]).astype(BF16)
+
+        f0 = dot(kt_ref[b, 0, :, 0:SUB], weighted(0, 0))
+        f1 = dot(kt_ref[b, 0, :, SUB:TOK], weighted(0, SUB))
+        r0 = dot(kt_ref[b, 1, :, 0:SUB], weighted(1, 0))
+        r1 = dot(kt_ref[b, 1, :, SUB:TOK], weighted(1, SUB))
         saved_ref[2 * b] = f0.astype(BF16)
         saved_ref[2 * b + 1] = r1.astype(BF16)
         blocks.append((d1 * f0 + f1, r0 + d0 * r1, drow[0:1] + drow[1:2]))
@@ -306,9 +309,12 @@
 
 
 def first_states_kernel(
-    kq_in, u_in, x_ref, taps_ref, chip_halo_ref, core_halo_ref, table_ref, drow_ref,
-    kq_ref, u_ref, kt_ref, saved_ref, chip_ref,
+    kq_in, u_in, x_ref, taps_ref, chip_halo_ref, core_halo_ref, table_ref, drow_ref, gate_hbm,
+    kq_ref, u_ref, kt_ref, saved_ref, spread_ref, chip_ref, gate_to_core_ref, sem,
 ):
+    c, z, y = place()
+    copy = pltpu.make_async_copy(gate_hbm.at[:, columns((1 - c) * HALF, HALF)], gate_to_core_ref, sem)
+    copy.start()
     halo = halo_of(chip_halo_ref, core_halo_ref)
     repair(x_ref, taps_ref, kq_ref, HALF, halo)
     for b in range(2):
@@ -316,19 +322,28 @@
             kt_ref[b, d] = jnp.transpose(kq_ref[b, d, :, 0:STATE].astype(F32)).astype(BF16)
     start = start_of(2, 0)
     repair(x_ref, taps_ref, u_ref, start, halo)
-    piece_states(u_ref, kt_ref, table_ref, drow_ref, start, saved_ref, chip_ref)
+    piece_states(u_ref, kt_ref, table_ref, drow_ref, start, saved_ref, spread_ref, chip_ref)
+    copy.wait()
 
 
 def rest_kernel(todo, x_ref, taps_ref, chip_halo_ref, core_halo_ref, table_ref, drow_ref, kt_ref, after_ref, *outs):
+    c, z, y = place()
+    copies = []
+    if len(todo) == 2:
+        gate_hbm, gain_hbm, *outs, gate_ref, gain_ref, sems = outs
+        copies = copy_all([(gate_hbm.at[:, columns(c * HALF, HALF)], gate_ref), (gain_hbm, gain_ref)], sems)
     for n, piece in enumerate(todo):
-        u_ref, saved_ref, chip_ref = outs[3 * n : 3 * n + 3]
+        u_ref, saved_ref, spread_ref, chip_ref = outs[4 * n : 4 * n + 4]
         conv_piece(x_ref, taps_ref, u_ref, start_of(*piece), halo_of(chip_halo_ref, core_halo_ref))
-        piece_states(u_ref, kt_ref, table_ref, drow_ref, start_of(*piece), saved_ref, chip_ref)
+        piece_states(u_ref, kt_ref, table_ref, drow_ref, start_of(*piece), saved_ref, spread_ref, chip_ref)
+    for copy in copies:
+        copy.wait()
 
 
 KEYS = vmem(BF16, 2, 2, TOK, 2 * STATE)
 U = vmem(BF16, 2, 2, TOK, CW)
 SAVED = vmem(BF16, 6, STATE, CW)
+SPREAD = vmem(BF16, 2, 2 * HEADS, CW)
 CHIP = vmem(BF16, MSG, CW)
 
 
@@ -374,84 +389,81 @@
     back_ref[1] = jnp.where(z0, er, first_r).astype(BF16)
 
 
-def second_phase_kernel(keep_ref, got_ref, zsend_ref, after_ref, zsend_out, *outs):
-    group(keep_ref, got_ref, outs)
-    zsend_out[...] = zsend_ref[...]
-
-
-def third_phase_kernel(
-    keep0_ref, got0_ref, r1_ref, r2_ref, r3_ref, keep1_ref, got1_ref, after_ref, mine_ref, back_ref, *outs
-):
-    entries(keep0_ref, got0_ref, r1_ref, r2_ref, r3_ref, mine_ref, back_ref)
-    group(keep1_ref, got1_ref, outs)
-
-
-def fourth_phase_kernel(
-    keep_ref, got_ref, r1_ref, r2_ref, r3_ref, after0_ref, after1_ref, mine_ref, back_ref
-):
-    entries(keep_ref, got_ref, r1_ref, r2_ref, r3_ref, mine_ref, back_ref)
-
-
-def within_kernel(k, p, u_ref, kq_ref, table_ref, mcol_ref, mrow_ref, drow_ref, after_ref, out_ref, qk_ref):
+def group_kernel(keep_ref, got_ref, *refs):
+    group(keep_ref, got_ref, refs[-3:])
+
+
+def entries_kernel(keep_ref, got_ref, r1_ref, r2_ref, r3_ref, *refs):
+    entries(keep_ref, got_ref, r1_ref, r2_ref, r3_ref, *refs[-2:])
+
+
+def within_kernel(k, p, u_ref, spread_ref, kq_ref, table_ref, mcol_ref, mrow_ref, drow_ref, after_ref, *refs):
+    make_qk = len(refs) == 2 and refs[1].shape[0] == 2 and len(refs[1].shape) == 5
+    qk_ref, out_ref = (refs[1], refs[0]) if make_qk else refs
     row = lax.broadcasted_iota(jnp.int32, (SUB, SUB), 0)
     col = lax.broadcasted_iota(jnp.int32, (SUB, SUB), 1)
     low = lax.broadcasted_iota(jnp.int32, (SUB, 2 * HEAD_DIM), 1) < HEAD_DIM
 
     def block(b, _):
-        for s in range(2):
-            rows = slice(s * SUB, (s + 1) * SUB)
-            for d in range(2):
-                keys = kq_ref[b, d, rows, 0:STATE]
-                queries = kq_ref[b, d, rows, STATE : 2 * STATE]
-                prod = lax.dot_general(queries, keys, (((1,), (1,)), ((), ())), preferred_element_type=F32)
-                qk_ref[d, s] = jnp.where((row >= col) if d == 0 else (row <= col), prod, 0.0)
+        if make_qk:
+            for s in range(2):
+                rows = slice(s * SUB, (s + 1) * SUB)
+                for d in range(2):
+                    keys = kq_ref[b, d, rows, 0:STATE]
+                    queries = kq_ref[b, d, rows, STATE : 2 * STATE]
+                    prod = lax.dot_general(queries, keys, (((1,), (1,)), ((), ())), preferred_element_type=F32)
+                    qk_ref[b, d, s] = jnp.where((row >= col) if d == 0 else (row <= col), prod, 0.0)
         start = b * HALF + start_of(k, p)
         first = start // HEAD_DIM
-        spread = spread_matrix(start)
+        spread = spread_ref[b]
         skip = dot(drow_ref[...], spread)[10:11]
         mcol = pltpu.roll(mcol_ref[...], 2 * HEADS - first, 1)
         mrow = mrow_ref[pl.ds(pl.multiple_of(first, HC), HC), :]
+        wv, gt = expand(table_ref, WV, spread)
         for s in range(2):
             rows = slice(s * SUB, (s + 1) * SUB)
-            wv = dot(table_ref[WV, rows], spread)
-            gt = dot(table_ref[GT, rows], spread)
             for two in range(HC // 2):
                 cols = slice(two * 128, (two + 1) * 128)
                 up = u_ref[b, 0, rows, cols].astype(F32)
-                xf = (up * wv[:, cols]).astype(BF16)
-                xb = (u_ref[b, 1, rows, cols].astype(F32) * wv[:, cols]).astype(BF16)
+                xf = (up * wv[rows, cols]).astype(BF16)
+                xb = (u_ref[b, 1, rows, cols].astype(F32) * wv[rows, cols]).astype(BF16)
                 none = jnp.zeros_like(xf)
                 left, right = [], []
                 for h in range(2):
                     at = two * 2 + h
                     diff = mcol[rows, at : at + 1] - mrow[at : at + 1, rows]
                     decay = jnp.exp2(-jnp.abs(diff))
-                    left += [(decay * qk_ref[0, s]).astype(BF16), (decay * qk_ref[1, s]).astype(BF16)]
+                    left += [(decay * qk_ref[b, 0, s]).astype(BF16), (decay * qk_ref[b, 1, s]).astype(BF16)]
                     keep = low if h == 0 else ~low
                     right += [jnp.where(keep, xf, none), jnp.where(keep, xb, none)]
                 res = dot(jnp.concatenate(left, axis=1), jnp.concatenate(right, axis=0))
-                out_ref[b, rows, cols] = (res * gt[:, cols] + up * skip[:, cols]).astype(BF16)
+                out_ref[b, rows, cols] = (res * gt[rows, cols] + up * skip[:, cols]).astype(BF16)
         return _
 
     lax.fori_loop(0, 2, block, 0)
 
 
-def make_within(k, p, u, kq, table, mcol, mrow, drow, after):
-    scratch = [pltpu.VMEM((2, 2, SUB, SUB), F32)]
-    operands = (u, kq, table, mcol, mrow, drow, after)
+QK = vmem(F32, 2, 2, 2, SUB, SUB)
+
+
+def make_within(k, p, u, spread, kq, table, mcol, mrow, drow, after, qk=None):
+    outs = [vmem(BF16, 2, TOK, CW)]
+    operands = (u, spread, kq, table, mcol, mrow, drow, after)
     kernel = functools.partial(within_kernel, k, p)
-    return call(kernel, f"within_{k}{p}", [vmem(BF16, 2, TOK, CW)], operands, (), scratch)[0]
-
-
-def finish_part(k, p, other, entry_ref, saved_ref, within_ref, gate_ref, kq_ref, table_ref, drow_ref, put, square):
+    if qk is None:
+        return call(kernel, f"within_{k}{p}", [*outs, QK], operands)
+    return call(kernel, f"within_{k}{p}", outs, (*operands, qk))[0]
+
+
+def finish_part(k, p, other, entry_ref, saved_ref, spread_ref, within_ref, gate_ref, kq_ref, table_ref, drow_ref, put, square):
     c, z, y = place()
     b = 1 - c if other else c
     start = start_of(k, p)
     at = columns(start, CW)
-    spread = spread_matrix(b * HALF + start)
+    spread = spread_ref[b]
     drow = dot(drow_ref[...], spread)
     d0, d1 = drow[8:9], drow[9:10]
-    far = dot(drow_ref[...], spread_matrix((1 - b) * HALF + start))
+    far = dot(drow_ref[...], spread_ref[1 - b])
     far = far[0:1] + far[1:2]
     one = jnp.ones_like(far)
     none = jnp.zeros((STATE, CW), F32)
@@ -462,13 +474,12 @@
         (ef.astype(BF16), (er * d1 + saved_ref[2 * b + 1].astype(F32)).astype(BF16)),
         ((ef * d0 + saved_ref[2 * b].astype(F32)).astype(BF16), er.astype(BF16)),
     ]
+    gf, gr = expand(table_ref, GF, spread)
     for s in range(2):
         rows = slice(s * SUB, (s + 1) * SUB)
         cf = dot(kq_ref[b, 0, rows, STATE : 2 * STATE], inside[s][0])
         cr = dot(kq_ref[b, 1, rows, STATE : 2 * STATE], inside[s][1])
-        gf = dot(table_ref[GF, rows], spread)
-        gr = dot(table_ref[GR, rows], spread)
-        mixed = within_ref[b, rows].astype(F32) + gf * cf + gr * cr
+        mixed = within_ref[b, rows].astype(F32) + gf[rows] * cf + gr[rows] * cr
         half = gate_ref[rows, at].astype(F32) * 0.5
         gated = mixed * (half + half * jnp.tanh(half))
         put(rows, gated)
@@ -478,7 +489,7 @@
             square[s] = part if square[s] is None else square[s] + part
 
 
-def finish_piece(k, p, entry_ref, saved_ref, within_ref, gate_refs, shared, own_ref, msg_refs, squares):
+def finish_piece(k, p, entry_ref, saved_ref, spread_ref, within_ref, gates, shared, own_ref, msg_refs, squares):
     def put_own(rows, gated):
         own_ref[rows] = gated
 
@@ -486,17 +497,18 @@
         msg_refs[rows.start // SUB][:, 0:CW] = gated.astype(BF16)
 
     for other, put in ((1, put_other), (0, put_own)):
-        finish_part(k, p, other, entry_ref, saved_ref, within_ref, gate_refs[other], *shared, put, squares[other])
+        finish_part(k, p, other, entry_ref, saved_ref, spread_ref, within_ref, gates[other], *shared, put, squares[other])
 
 
 NEAR = ((3, 0), (3, 1), (2, 0))
 BACK = (2, 1)
 
 
-def finish_near_kernel(k, p, entry_ref, saved_ref, within_ref, gate_ref, gate_other_ref, *refs):
+def finish_near_kernel(k, p, entry_ref, saved_ref, spread_ref, within_ref, gate_ref, gate_other_ref, *refs):
     shared, (square_in, own_ref, *msg_refs, square_ref) = refs[:3], refs[3:]
     squares = [[None, None], [None, None]]
-    finish_piece(k, p, entry_ref, saved_ref, within_ref, (gate_ref, gate_other_ref), shared, own_ref, msg_refs, squares)
+    gates = (gate_ref, gate_other_ref)
+    finish_piece(k, p, entry_ref, saved_ref, spread_ref, within_ref, gates, shared, own_ref, msg_refs, squares)
     for other in range(2):
         for s in range(2):
             rows = slice(s * SUB, (s + 1) * SUB)
@@ -506,14 +518,14 @@
                 square_ref[other, rows] = square_in[other, rows] + squares[other][s]
 
 
-def finish_other_kernel(entry_ref, saved_ref, within_ref, gate_ref, *refs):
+def finish_other_kernel(entry_ref, saved_ref, spread_ref, within_ref, gate_ref, *refs):
     shared, square_in, msg_refs = refs[:3], refs[3], refs[-2:]
     square = [square_in[1, s * SUB : (s + 1) * SUB] for s in range(2)]
 
     def put(rows, gated):
         msg_refs[rows.start // SUB][:, 0:CW] = gated.astype(BF16)
 
-    finish_part(*BACK, 1, entry_ref, saved_ref, within_ref, gate_ref, *shared, put, square)
+    finish_part(*BACK, 1, entry_ref, saved_ref, spread_ref, within_ref, gate_ref, *shared, put, square)
     lane = lax.broadcasted_iota(jnp.int32, (SUB, 128), 1)
     for s in range(2):
         total = jnp.sum(square[s], axis=1, keepdims=True)
@@ -522,19 +534,16 @@
         msg_refs[s][:, CW : CW + 128] = sums.astype(BF16)
 
 
-def finish_own_kernel(entry_ref, saved_ref, within_ref, gate_ref, *refs):
-    shared, (square_in, after_ref, gain_hbm, own_ref, square_ref, gain_ref, sem) = refs[:3], refs[3:]
-    copy = pltpu.make_async_copy(gain_hbm, gain_ref, sem)
-    copy.start()
+def finish_own_kernel(entry_ref, saved_ref, spread_ref, within_ref, gate_ref, *refs):
+    shared, (square_in, after_ref, own_ref, square_ref) = refs[:3], refs[3:]
     square = [square_in[0, s * SUB : (s + 1) * SUB] for s in range(2)]
 
     def put(rows, gated):
         own_ref[rows] = gated
 
-    finish_part(*BACK, 0, entry_ref, saved_ref, within_ref, gate_ref, *shared, put, square)
+    finish_part(*BACK, 0, entry_ref, saved_ref, spread_ref, within_ref, gate_ref, *shared, put, square)
     for s in range(2):
         square_ref[s * SUB : (s + 1) * SUB] = square[s]
-    copy.wait()
 
 
 def norm_kernel(*refs):
@@ -580,7 +589,7 @@
         (mixer_input, step_size),
         [pltpu.VMEM((HEADS, TOK), F32), pltpu.SemaphoreType.DMA((4,))],
     )
-    x, table, mcol, mrow, drow, taps, kq, u2a, gate, gate_to_core = call(
+    x, table, mcol, mrow, drow, taps, kq, u2a = call(
         front_kernel,
         "front",
         [
@@ -592,8 +601,6 @@
             vmem(F32, 8, WIDE),
             KEYS,
             U,
-            vmem(BF16, TOK, HALF),
-            vmem(BF16, TOK, HALF),
         ],
         (send(to_core, core),),
         (
@@ -603,7 +610,6 @@
             skip_scale.reshape(1, HEADS),
             conv_forward,
             conv_reverse,
-            gate_input,
         ),
         [
             pltpu.VMEM((HEADS, TOK), F32),
@@ -611,53 +617,65 @@
             pltpu.VMEM((1, HEADS), F32),
             pltpu.VMEM((4, WIDE), F32),
             pltpu.VMEM((4, WIDE), F32),
-            pltpu.SemaphoreType.DMA((12,)),
+            pltpu.SemaphoreType.DMA((10,)),
         ],
     )
     chip_halo, to_core = call(
         halo_kernel, "halo", [vmem(BF16, HALO, WIDE)] * 2, (send(to_chip, chips), kq)
     )
     halo = (x, taps, chip_halo, send(to_core, core))
-    kq, u2a, kt, saved2a, zsend0 = call(
+    kq, u2a, kt, saved2a, spread2a, zsend0, gate_to_core = call(
         first_states_kernel,
         "states_first",
-        [KEYS, U, vmem(BF16, 2, 2, STATE, TOK), SAVED, CHIP],
+        [KEYS, U, vmem(BF16, 2, 2, STATE, TOK), SAVED, SPREAD, CHIP, vmem(BF16, TOK, HALF)],
         (kq, u2a, *halo, table, drow),
+        (gate_input,),
+        [pltpu.SemaphoreType.DMA(())],
         aliases={0: 0, 1: 1},
     )
     got0 = send(zsend0, zswap)
 
     def make_rest(name, todo, after):
         kernel = functools.partial(rest_kernel, todo)
-        return call(kernel, name, [U, SAVED, CHIP] * len(todo), (*halo, table, drow, kt, after))
-
-    u2b, saved2b, zsend1, u3a, saved3a, keep0 = make_rest("states_a", ((2, 1), (3, 0)), zsend0)
+        outs = [U, SAVED, SPREAD, CHIP] * len(todo)
+        if len(todo) == 1:
+            return call(kernel, name, outs, (*halo, table, drow, kt, after))
+        outs += [vmem(BF16, TOK, HALF), vmem(F32, 1, INNER)]
+        sems = [pltpu.SemaphoreType.DMA((2,))]
+        params = (gate_input, norm_gain.reshape(1, INNER))
+        return call(kernel, name, outs, (*halo, table, drow, kt, after), params, sems)
+
+    u2b, saved2b, spread2b, zsend1, u3a, saved3a, spread3a, keep0, gate, gain = make_rest(
+        "states_a", ((2, 1), (3, 0)), zsend0
+    )
+    got1 = send(zsend1, zswap)
+    u3b, saved3b, spread3b, keep1 = make_rest("states_b", ((3, 1),), zsend1)
+    gates = (gate, send(gate_to_core, core))
     tables = (kq, table, mcol, mrow, drow)
-
-    w2a = make_within(2, 0, u2a, *tables, zsend0)
     yout = [vmem(BF16, YMSG, CW)] * 3
     entry = vmem(BF16, 2, STATE, CW)
-    zsend1, *msgs = call(second_phase_kernel, "second_phase", [CHIP, *yout], (keep0, got0, zsend1, w2a))
-    got1 = send(zsend1, zswap)
-    arrived = along_y(msgs)
-    u3b, saved3b, keep1 = make_rest("states_b", ((3, 1),), msgs[0])
-    w2b = make_within(2, 1, u2b, *tables, msgs[0])
-
-    mine0, back0, *msgs = call(
-        third_phase_kernel, "third_phase", [entry, entry, *yout], (keep0, got0, *arrived, keep1, got1, w2b)
-    )
+
+    msgs = call(group_kernel, "group_a", yout, (keep0, got0, keep1, gates[1]))
+    arrived0 = along_y(msgs)
+    w2a, qk = make_within(2, 0, u2a, spread2a, *tables, msgs[0])
+    msgs = call(group_kernel, "group_b", yout, (keep1, got1, w2a))
+    arrived1 = along_y(msgs)
+    mine0, back0 = call(entries_kernel, "entries_a", [entry, entry], (keep0, got0, *arrived0, msgs[0]))
     back0 = send(back0, zswap)
-    arrived = along_y(msgs)
-    w3a = make_within(3, 0, u3a, *tables, msgs[0])
-    w3b = make_within(3, 1, u3b, *tables, w3a)
-
-    mine1, back1 = call(fourth_phase_kernel, "fourth_phase", [entry, entry], (keep1, got1, *arrived, w3b, back0))
+    w3a = make_within(3, 0, u3a, spread3a, *tables, mine0, qk)
+    mine1, back1 = call(entries_kernel, "entries_b", [entry, entry], (keep1, got1, *arrived1, w3a))
     back1 = send(back1, zswap)
-    gates = (gate, send(gate_to_core, core))
+    w3b = make_within(3, 1, u3b, spread3b, *tables, mine1, qk)
+    w2b = make_within(2, 1, u2b, spread2b, *tables, mine1, qk)
     shared = (kq, table, drow)
     square = kt
     own, other = [], []
-    for (k, p), *part in zip(NEAR, (mine0, mine1, back0), (saved3a, saved3b, saved2a), (w3a, w3b, w2a)):
+    parts = (
+        (mine0, saved3a, spread3a, w3a),
+        (mine1, saved3b, spread3b, w3b),
+        (back0, saved2a, spread2a, w2a),
+    )
+    for (k, p), part in zip(NEAR, parts):
         gated, *msg, square = call(
             functools.partial(finish_near_kernel, k, p),
             f"finish_{k}{p}",
@@ -670,16 +688,14 @@
         finish_other_kernel,
         "finish_other",
         [vmem(BF16, SUB, CW + 128)] * 2,
-        (back1, saved2b, w2b, gates[1], *shared, square, *other[:4]),
+        (back1, saved2b, spread2b, w2b, *gates[1:], *shared, square, *other[:4]),
     )
     other += [send(m, core) for m in msg]
-    gated, square, gain = call(
+    gated, square = call(
         finish_own_kernel,
         "finish_own",
-        [vmem(F32, TOK, CW), vmem(F32, TOK, 128), vmem(F32, 1, INNER)],
-        (back1, saved2b, w2b, gates[0], *shared, square, msg[0]),
-        (norm_gain.reshape(1, INNER),),
-        [pltpu.SemaphoreType.DMA(())],
+        [vmem(F32, TOK, CW), vmem(F32, TOK, 128)],
+        (back1, saved2b, spread2b, w2b, gates[0], *shared, square, msg[0]),
     )
     own.append(gated)
     (out,) = call(

time: 65.7 us -> 59.8 us (0.910)
  Pallas kernels: 30.5 us -> 26.5 us
  waiting for transfers between devices: 6.46 us -> 3.65 us
  starting transfers between devices: 28.2 us -> 29.2 us
    pallas_call x19 -> x20, Pallas kernels: 30.5 us -> 26.5 us  [call(): pl.pallas_call(kernel, name=name, in_specs=[VMEM] * len(operands) + [HBM]...]
    ppermute x22, waiting for transfers between devices: 6.46 us -> 3.65 us  [send(): return lax.ppermute(v, 'seq', perm)]
    ppermute x22, starting transfers between devices: 28.2 us -> 29.2 us  [send(): return lax.ppermute(v, 'seq', perm)]
  transfers between devices with their start and end apart: 22 -> 22, of which waited for: 7 -> 7; matrix products, arithmetic and copies ran while one was open for 0% -> 0% of each run, Pallas kernels for 41% -> 36%
where the time goes in v4:
time: 59.8 us; the launch traced here: 59.7 us
  starting transfers between devices  29.2 us (49%)
  Pallas kernels  26.5 us (44%)
  waiting for transfers between devices  3.65 us (6%)
    ppermute x22, starting transfers between devices, send(): return lax.ppermute(v, 'seq', perm)  29.2 us
    pallas_call x20, Pallas kernels, call(): pl.pallas_call(kernel, name=name, in_specs=[VMEM] * len(operands) + [HBM]...  26.5 us
    ppermute x22, waiting for transfers between devices, send(): return lax.ppermute(v, 'seq', perm)  3.65 us
  transfers between devices with their start and end apart: 22, of which 7 were waited for; matrix products, arithmetic and copies ran while one was open for 0% of the time, Pallas kernels for 36%

profile of v4, /device:TPU:1, one launch (start us, length us, event | category | flops | bytes accessed | tf_op | source)
XLA Modules:
  0.0 59.7 jit_solution(10165375143646542687)
XLA Ops:
  0.0 1.4 %edges.1 = (bf16[256,2560]{1,0:T(8,128)(2,1)S(1)}, bf16[16,4352]{1,0:T(8,128)(2,1)S(1)}) custom-call(bf16[256,4352]{1,0:T(8,128)(2,1)} %x_hbm.3, f32[64,256]{1,0:T(8,128)} %step_hbm.3), custom_call_target="tpu_custom_call" | custom-call | flops 100000000 | bytes 300000 | tf_op jit(solution)/shard_map/edges/pallas_call | solution.py:52
  1.4 1.5 %collective-permute-start = (bf16[256,2560]{1,0:T(8,128)(2,1)S(1)}, bf16[256,2560]{1,0:T(8,128)(2,1)S(1)}, u32[]{:S(2)}, u32[]{:S(2)}) collective-permute-start(bf16[256,2560]{1,0:T(8,128)(2,1)S(1)} %get-tuple-element.66), channel_id=1, source_target_pairs={{0,1},{1,0},{2,3},{3,2},{4,5},{5,4},{6,7},{7,6},{8,9},{9,8},{10,11... | collective-permute-start | bytes 3932168 | tf_op jit(solution)/shard_map/ppermute | solution.py:575
  2.9 5.5 %collective-permute-start.1 = (bf16[16,4352]{1,0:T(8,128)(2,1)S(1)}, bf16[16,4352]{1,0:T(8,128)(2,1)S(1)}, u32[]{:S(2)}, u32[]{:S(2)}) collective-permute-start(bf16[16,4352]{1,0:T(8,128)(2,1)S(1)} %get-tuple-element.69), channel_id=1, source_target_pairs={{1,2},{3,4},{5,6},{7,8},{9,10},{11,12},{13,14},{2,1},{4,3},{6,5},{... | collective-permute-start | bytes 417800 | tf_op jit(solution)/shard_map/ppermute | solution.py:575
  8.4 3.5 %front.1 = (bf16[2,256,2304]{2,1,0:T(8,128)(2,1)S(1)}, bf16[6,256,128]{2,1,0:T(8,128)(2,1)S(1)}, f32[256,128]{1,0:T(8,128)S(1)}, f32[64,256]{1,0:T(8,128)S(1)}, ...) custom-call(bf16[256,2560]{1,0:T(8,128)(2,1)S(1)} %collective-permut, ...), custom_call_target="tpu_custom_call" | custom-call | flops 100000000 | bytes 300000 | tf_op jit(solution)/shard_map/front/pallas_call | solution.py:52
  11.9 0.1 collective-permute-start.2
  12.0 1.3 %collective-permute-done.2.core_halo_ref = bf16[16,2304]{1,0:T(8,128)(2,1)S(1)} collective-permute-done((bf16[16,2304]{1,0:T(8,128)(2,1)S(1)}, bf16[16,2304]{1,0:T(8,128)(2,1)S(1)}, u32[]{:S(2)}, u32[]{:S(2)}) %collective-permute-start.2) | collective-permute-done | bytes 73760 | tf_op jit(solution)/shard_map/ppermute | solution.py:575
  13.3 1.3 %states_first.1 = (bf16[2,2,256,256]{3,2,1,0:T(8,128)(2,1)S(1)}, bf16[2,2,256,512]{3,2,1,0:T(8,128)(2,1)S(1)}, bf16[2,2,128,256]{3,2,1,0:T(8,128)(2,1)S(1)}, bf1...) custom-call(bf16[2,2,256,256]{3,2,1,0:T(8,128)(2,1)S(1)} %get-tuple-, ...), custom_call_target="tpu_custom_call", output_to_operand_aliasing={{0}: (0, {}), {1}: (1, {})} | custom-call | flops 100000000 | bytes 300000 | tf_op jit(solution)/shard_map/states_first/pallas_call | solution.py:52
  14.5 0.3 collective-permute-start.4
  14.8 3.4 %collective-permute-start.3 = (bf16[272,512]{1,0:T(8,128)(2,1)S(1)}, bf16[272,512]{1,0:T(8,128)(2,1)S(1)}, u32[]{:S(2)}, u32[]{:S(2)}) collective-permute-start(bf16[272,512]{1,0:T(8,128)(2,1)S(1)} %get-tuple-element.77.after_ref), channel_id=1, source_target_pairs={{0,2},{1,3},{2,0},{3,1},{4,6},{5,7},{6,4},{7,5},{8,10},{9,11},{10,... | collective-permute-start | bytes 835592 | tf_op jit(solution)/shard_map/ppermute | solution.py:575
  18.2 4.3 %states_a.1 = (bf16[2,2,256,512]{3,2,1,0:T(8,128)(2,1)S(1)}, bf16[6,128,512]{2,1,0:T(8,128)(2,1)S(1)}, bf16[2,128,512]{2,1,0:T(8,128)(2,1)S(1)}, bf16[272,512]{1...) custom-call(bf16[2,256,2304]{2,1,0:T(8,128)(2,1)S(1)} %get-tuple-ele, ...), custom_call_target="tpu_custom_call" | custom-call | flops 100000000 | bytes 300000 | tf_op jit(solution)/shard_map/states_a/pallas_call | solution.py:52
  22.5 0.1 collective-permute-start.8
  22.6 2.2 %states_b.1 = (bf16[2,2,256,512]{3,2,1,0:T(8,128)(2,1)S(1)}, bf16[6,128,512]{2,1,0:T(8,128)(2,1)S(1)}, bf16[2,128,512]{2,1,0:T(8,128)(2,1)S(1)}, bf16[272,512]{1,0:T(8,128)(2,1)S(1)}) custom-call(bf16[2,256,2304]{2,1,0:T(8,128)(2,1)S(1)} %get-tuple-element.67.x_ref, f32[8,2304]{1,0:T(8,128)S(1)} %get-tuple-element.68.taps_ref, ...), custom_call_target="tpu_custom_call" | custom-call | flops 100000000 | bytes 300000 | tf_op jit(solution)/shard_map/states_b/pallas_call | solution.py:52
  24.8 0.1 collective-permute-done.3.got_ref
  24.9 0.1 group_a.1
  25.1 3.0 %collective-permute-start.6 = (bf16[144,512]{1,0:T(8,128)(2,1)S(1)}, bf16[144,512]{1,0:T(8,128)(2,1)S(1)}, u32[]{:S(2)}, u32[]{:S(2)}) collective-permute-start(bf16[144,512]{1,0:T(8,128)(2,1)S(1)} %get-tuple-element.83), channel_id=1, source_target_pairs={{0,8},{1,9},{2,10},{3,11},{4,12},{5,13},{6,14},{7,15},{8,0},{9,1},... | collective-permute-start | bytes 442376 | tf_op jit(solution)/shard_map/ppermute | solution.py:575
  28.1 0.8 %collective-permute-start.7 = (bf16[144,512]{1,0:T(8,128)(2,1)S(1)}, bf16[144,512]{1,0:T(8,128)(2,1)S(1)}, u32[]{:S(2)}, u32[]{:S(2)}) collective-permute-start(bf16[144,512]{1,0:T(8,128)(2,1)S(1)} %get-tuple-element.84), channel_id=1, source_target_pairs={{0,12},{1,13},{2,14},{3,15},{4,0},{5,1},{6,2},{7,3},{8,4},{9,5},{1... | collective-permute-start | bytes 442376 | tf_op jit(solution)/shard_map/ppermute | solution.py:575
  28.9 0.7 %collective-permute-start.5 = (bf16[144,512]{1,0:T(8,128)(2,1)S(1)}, bf16[144,512]{1,0:T(8,128)(2,1)S(1)}, u32[]{:S(2)}, u32[]{:S(2)}) collective-permute-start(bf16[144,512]{1,0:T(8,128)(2,1)S(1)} %get-tuple-element.82.after_ref), channel_id=1, source_target_pairs={{0,4},{1,5},{2,6},{3,7},{4,8},{5,9},{6,10},{7,11},{8,12},{9,13},{1... | collective-permute-start | bytes 442376 | tf_op jit(solution)/shard_map/ppermute | solution.py:575
  29.6 1.8 %within_20.1 = (bf16[2,256,512]{2,1,0:T(8,128)(2,1)S(1)}, f32[2,2,2,128,128]{4,3,2,1,0:T(8,128)S(1)}) custom-call(bf16[2,2,256,512]{3,2,1,0:T(8,128)(2,1)S(1)} %get-tuple-element.85.u_ref, bf16[2,128,512]{2,1,0:T(8,128)(2,1)S(1)} %get-tuple-element.86.spread_ref, bf16[2,2,256,256]{3,2,1,0:T(8,128)(2,1)S(1)} %get-tuple-element.87.kq_ref.refs_0_, ...), custom_call_target="tpu_custom_call" | custom-call | flops 100000000 | bytes 300000 | tf_op jit(solution)/shard_map/within_20/pallas_call | solution.py:52
  31.4 0.3 collective-permute-done.8.got_ref
  31.7 0.1 group_b.1
  31.8 3.0 %collective-permute-start.10 = (bf16[144,512]{1,0:T(8,128)(2,1)S(1)}, bf16[144,512]{1,0:T(8,128)(2,1)S(1)}, u32[]{:S(2)}, u32[]{:S(2)}) collective-permute-start(bf16[144,512]{1,0:T(8,128)(2,1)S(1)} %get-tuple-element.99), channel_id=1, source_target_pairs={{0,8},{1,9},{2,10},{3,11},{4,12},{5,13},{6,14},{7,15},{8,0},{9,1},... | collective-permute-start | bytes 442376 | tf_op jit(solution)/shard_map/ppermute | solution.py:575
  34.8 0.8 %collective-permute-start.11 = (bf16[144,512]{1,0:T(8,128)(2,1)S(1)}, bf16[144,512]{1,0:T(8,128)(2,1)S(1)}, u32[]{:S(2)}, u32[]{:S(2)}) collective-permute-start(bf16[144,512]{1,0:T(8,128)(2,1)S(1)} %get-tuple-element.100), channel_id=1, source_target_pairs={{0,12},{1,13},{2,14},{3,15},{4,0},{5,1},{6,2},{7,3},{8,4},{9,5},{1... | collective-permute-start | bytes 442376 | tf_op jit(solution)/shard_map/ppermute | solution.py:575
  35.6 0.7 %collective-permute-start.9 = (bf16[144,512]{1,0:T(8,128)(2,1)S(1)}, bf16[144,512]{1,0:T(8,128)(2,1)S(1)}, u32[]{:S(2)}, u32[]{:S(2)}) collective-permute-start(bf16[144,512]{1,0:T(8,128)(2,1)S(1)} %get-tuple-element.91.refs_0_), channel_id=1, source_target_pairs={{0,4},{1,5},{2,6},{3,7},{4,8},{5,9},{6,10},{7,11},{8,12},{9,13},{1... | collective-permute-start | bytes 442376 | tf_op jit(solution)/shard_map/ppermute | solution.py:575
  36.3 0.3 entries_a.1
  36.7 2.1 %collective-permute-start.12 = (bf16[2,128,512]{2,1,0:T(8,128)(2,1)S(1)}, bf16[2,128,512]{2,1,0:T(8,128)(2,1)S(1)}, u32[]{:S(2)}, u32[]{:S(2)}) collective-permute-start(bf16[2,128,512]{2,1,0:T(8,128)(2,1)S(1)} %get-tuple-element.107), channel_id=1, source_target_pairs={{0,2},{1,3},{2,0},{3,1},{4,6},{5,7},{6,4},{7,5},{8,10},{9,11},{10,... | collective-permute-start | bytes 786440 | tf_op jit(solution)/shard_map/ppermute | solution.py:575
  38.8 1.7 %within_30.1.within_ref.refs_0_ = bf16[2,256,512]{2,1,0:T(8,128)(2,1)S(1)} custom-call(bf16[2,2,256,512]{3,2,1,0:T(8,128)(2,1)S(1)} %get-tuple-element.95.u_ref, bf16[2,128,512]{2,1,0:T(8,128)(2,1)S(1)} %get-tuple-element.94.spread_ref, bf16[2,2,256,256]{3,2,1,0:T(8,128)(2,1)S(1)} %get-tuple-element.87.kq_ref.refs_0_, ...), custom_call_target="tpu_custom_call" | custom-call | flops 100000000 | bytes 300000 | tf_op jit(solution)/shard_map/within_30/pallas_call | solution.py:52
  40.5 0.2 collective-permute-done.11.r3_ref
  40.7 1.1 %collective-permute-done.9.r1_ref = bf16[144,512]{1,0:T(8,128)(2,1)S(1)} collective-permute-done((bf16[144,512]{1,0:T(8,128)(2,1)S(1)}, bf16[144,512]{1,0:T(8,128)(2,1)S(1)}, u32[]{:S(2)}, u32[]{:S(2)}) %collective-permute-start.9) | collective-permute-done | bytes 147488 | tf_op jit(solution)/shard_map/ppermute | solution.py:575
  41.7 0.3 entries_b.1
  42.1 3.7 %collective-permute-start.13 = (bf16[2,128,512]{2,1,0:T(8,128)(2,1)S(1)}, bf16[2,128,512]{2,1,0:T(8,128)(2,1)S(1)}, u32[]{:S(2)}, u32[]{:S(2)}) collective-permute-start(bf16[2,128,512]{2,1,0:T(8,128)(2,1)S(1)} %get-tuple-element.111), channel_id=1, source_target_pairs={{0,2},{1,3},{2,0},{3,1},{4,6},{5,7},{6,4},{7,5},{8,10},{9,11},{10,... | collective-permute-start | bytes 786440 | tf_op jit(solution)/shard_map/ppermute | solution.py:575
  45.7 1.1 %finish_30.1 = (f32[256,512]{1,0:T(8,128)S(1)}, bf16[128,512]{1,0:T(8,128)(2,1)S(1)}, bf16[128,512]{1,0:T(8,128)(2,1)S(1)}, f32[2,256,128]{2,1,0:T(8,128)S(1)}) custom-call(bf16[2,128,512]{2,1,0:T(8,128)(2,1)S(1)} %get-tuple-element.92.after_ref.entry_ref, bf16[6,128,512]{2,1,0:T(8,128)(2,1)S(1)} %get-tuple-element.93.saved_ref, ...), custom_call_target="tpu_custom_call" | custom-call | flops 100000000 | bytes 300000 | tf_op jit(solution)/shard_map/finish_30/pallas_call | solution.py:52
  46.8 1.8 %collective-permute-start.14 = (bf16[128,512]{1,0:T(8,128)(2,1)S(1)}, bf16[128,512]{1,0:T(8,128)(2,1)S(1)}, u32[]{:S(2)}, u32[]{:S(2)}) collective-permute-start(bf16[128,512]{1,0:T(8,128)(2,1)S(1)} %get-tuple-element.116), channel_id=1, source_target_pairs={{0,1},{1,0},{2,3},{3,2},{4,5},{5,4},{6,7},{7,6},{8,9},{9,8},{10,11... | collective-permute-start | bytes 393224 | tf_op jit(solution)/shard_map/ppermute | solution.py:575
  48.6 0.1 collective-permute-start.15
  48.7 1.6 %within_31.1.within_ref = bf16[2,256,512]{2,1,0:T(8,128)(2,1)S(1)} custom-call(bf16[2,2,256,512]{3,2,1,0:T(8,128)(2,1)S(1)} %get-tuple-element.104.u_ref, bf16[2,128,512]{2,1,0:T(8,128)(2,1)S(1)} %get-tuple-element.103.spread_ref, bf16[2,2,256,256]{3,2,1,0:T(8,128)(2,1)S(1)} %get-tuple-element.87.kq_ref.refs_0_, ...), custom_call_target="tpu_custom_call" | custom-call | flops 100000000 | bytes 300000 | tf_op jit(solution)/shard_map/within_31/pallas_call | solution.py:52
  50.4 1.1 %finish_31.1 = (f32[256,512]{1,0:T(8,128)S(1)}, bf16[128,512]{1,0:T(8,128)(2,1)S(1)}, bf16[128,512]{1,0:T(8,128)(2,1)S(1)}, f32[2,256,128]{2,1,0:T(8,128)S(1)}) custom-call(bf16[2,128,512]{2,1,0:T(8,128)(2,1)S(1)} %get-tuple-element.101.after_ref.entry_ref, bf16[6,128,512]{2,1,0:T(8,128)(2,1)S(1)} %get-tuple-element.102.saved_ref, ...), custom_call_target="tpu_custom_call" | custom-call | flops 100000000 | bytes 300000 | tf_op jit(solution)/shard_map/finish_31/pallas_call | solution.py:52
  51.5 0.5 collective-permute-start.16
  52.0 0.1 collective-permute-start.17
  52.1 1.6 %within_21.1.within_ref = bf16[2,256,512]{2,1,0:T(8,128)(2,1)S(1)} custom-call(bf16[2,2,256,512]{3,2,1,0:T(8,128)(2,1)S(1)} %get-tuple-element.114.u_ref, bf16[2,128,512]{2,1,0:T(8,128)(2,1)S(1)} %get-tuple-element.113.spread_ref, bf16[2,2,256,256]{3,2,1,0:T(8,128)(2,1)S(1)} %get-tuple-element.87.kq_ref.refs_0_, ...), custom_call_target="tpu_custom_call" | custom-call | flops 100000000 | bytes 300000 | tf_op jit(solution)/shard_map/within_21/pallas_call | solution.py:52
  53.8 1.1 %finish_20.1 = (f32[256,512]{1,0:T(8,128)S(1)}, bf16[128,512]{1,0:T(8,128)(2,1)S(1)}, bf16[128,512]{1,0:T(8,128)(2,1)S(1)}, f32[2,256,128]{2,1,0:T(8,128)S(1)}) custom-call(bf16[2,128,512]{2,1,0:T(8,128)(2,1)S(1)} %collective-permute-done.12.entry_ref, bf16[6,128,512]{2,1,0:T(8,128)(2,1)S(1)} %get-tuple-element.108.saved_ref, ...), custom_call_target="tpu_custom_call" | custom-call | flops 100000000 | bytes 300000 | tf_op jit(solution)/shard_map/finish_20/pallas_call | solution.py:52
  54.9 0.7 %finish_other.1 = (bf16[128,640]{1,0:T(8,128)(2,1)S(1)}, bf16[128,640]{1,0:T(8,128)(2,1)S(1)}) custom-call(bf16[2,128,512]{2,1,0:T(8,128)(2,1)S(1)} %collective-permute-done.13.entry_ref, bf16[6,128,512]{2,1,0:T(8,128)(2,1)S(1)} %get-tuple-element.112.saved_ref, bf16[2,128,512]{2,1,0:T(8,128)(2,1)S(1)} %get-tuple-element.113.spread_ref, ...), custom_call_target="tpu_custom_call" | custom-call | flops 100000000 | bytes 300000 | tf_op jit(solution)/shard_map/finish_other/pallas_call | solution.py:52
  55.6 0.5 collective-permute-start.21
  56.1 0.1 collective-permute-start.20
  56.2 0.4 collective-permute-start.18
  56.6 0.1 collective-permute-start.19
  56.7 0.6 finish_own.1
  57.3 0.4 collective-permute-done.18.refs_8_
  57.7 0.3 collective-permute-done.19.refs_9_
  58.0 1.5 %norm.1 = bf16[256,4096]{1,0:T(8,128)(2,1)} custom-call(f32[256,512]{1,0:T(8,128)S(1)} %get-tuple-element.98.refs_0_, f32[256,512]{1,0:T(8,128)S(1)} %get-tuple-element.106.refs_1_, f32[256,512]{1,0:T(8,128)S(1)} %get-tuple-element.110.refs_2_, f32[256,512]{1,0:T(8,128)S(1)} %get-tuple-element.121.refs_3_, ...), custom_call_target="tpu_custom_call" | custom-call | flops 100000000 | bytes 300000 | tf_op jit(solution)/shard_map/norm/pallas_call | solution.py:52
  (16 shorter events, 0.1 us)
Async XLA Ops:
  1.4 7.0 %collective-permute-start = (bf16[256,2560]{1,0:T(8,128)(2,1)S(1)}, bf16[256,2560]{1,0:T(8,128)(2,1)S(1)}, u32[]{:S(2)}, u32[]{:S(2)}) collective-permute-start(bf16[256,2560]{1,0:T(8,128)(2,1)S(1)} %get-tuple-element.66), channel_id=1, source_target_pairs={{0,1},{1,0},{2,3},{3,2},{4,5},{5,4},{6,7},{7,6},{8,9},{9,8},{10,11... | collective-permute-start | bytes 3932168 | tf_op jit(solution)/shard_map/ppermute | solution.py:575
  2.9 9.0 %collective-permute-start.1 = (bf16[16,4352]{1,0:T(8,128)(2,1)S(1)}, bf16[16,4352]{1,0:T(8,128)(2,1)S(1)}, u32[]{:S(2)}, u32[]{:S(2)}) collective-permute-start(bf16[16,4352]{1,0:T(8,128)(2,1)S(1)} %get-tuple-element.69), channel_id=1, source_target_pairs={{1,2},{3,4},{5,6},{7,8},{9,10},{11,12},{13,14},{2,1},{4,3},{6,5},{... | collective-permute-start | bytes 417800 | tf_op jit(solution)/shard_map/ppermute | solution.py:575
  11.9 1.3 %collective-permute-start.2 = (bf16[16,2304]{1,0:T(8,128)(2,1)S(1)}, bf16[16,2304]{1,0:T(8,128)(2,1)S(1)}, u32[]{:S(2)}, u32[]{:S(2)}) collective-permute-start(bf16[16,2304]{1,0:T(8,128)(2,1)S(1)} %get-tuple-element.72), channel_id=1, source_target_pairs={{0,1},{1,0},{2,3},{3,2},{4,5},{5,4},{6,7},{7,6},{8,9},{9,8},{10,11... | collective-permute-start | bytes 221192 | tf_op jit(solution)/shard_map/ppermute | solution.py:575
  14.5 10.4 %collective-permute-start.4 = (bf16[256,2048]{1,0:T(8,128)(2,1)S(1)}, bf16[256,2048]{1,0:T(8,128)(2,1)S(1)}, u32[]{:S(2)}, u32[]{:S(2)}) collective-permute-start(bf16[256,2048]{1,0:T(8,128)(2,1)S(1)} %get-tuple-element.81), channel_id=1, source_target_pairs={{0,1},{1,0},{2,3},{3,2},{4,5},{5,4},{6,7},{7,6},{8,9},{9,8},{10,11... | collective-permute-start | bytes 3145736 | tf_op jit(solution)/shard_map/ppermute | solution.py:575
  14.8 10.1 %collective-permute-start.3 = (bf16[272,512]{1,0:T(8,128)(2,1)S(1)}, bf16[272,512]{1,0:T(8,128)(2,1)S(1)}, u32[]{:S(2)}, u32[]{:S(2)}) collective-permute-start(bf16[272,512]{1,0:T(8,128)(2,1)S(1)} %get-tuple-element.77.after_ref), channel_id=1, source_target_pairs={{0,2},{1,3},{2,0},{3,1},{4,6},{5,7},{6,4},{7,5},{8,10},{9,11},{10,... | collective-permute-start | bytes 835592 | tf_op jit(solution)/shard_map/ppermute | solution.py:575
  22.5 9.2 %collective-permute-start.8 = (bf16[272,512]{1,0:T(8,128)(2,1)S(1)}, bf16[272,512]{1,0:T(8,128)(2,1)S(1)}, u32[]{:S(2)}, u32[]{:S(2)}) collective-permute-start(bf16[272,512]{1,0:T(8,128)(2,1)S(1)} %get-tuple-element.79.after_ref), channel_id=1, source_target_pairs={{0,2},{1,3},{2,0},{3,1},{4,6},{5,7},{6,4},{7,5},{8,10},{9,11},{10,... | collective-permute-start | bytes 835592 | tf_op jit(solution)/shard_map/ppermute | solution.py:575
  25.1 10.5 %collective-permute-start.6 = (bf16[144,512]{1,0:T(8,128)(2,1)S(1)}, bf16[144,512]{1,0:T(8,128)(2,1)S(1)}, u32[]{:S(2)}, u32[]{:S(2)}) collective-permute-start(bf16[144,512]{1,0:T(8,128)(2,1)S(1)} %get-tuple-element.83), channel_id=1, source_target_pairs={{0,8},{1,9},{2,10},{3,11},{4,12},{5,13},{6,14},{7,15},{8,0},{9,1},... | collective-permute-start | bytes 442376 | tf_op jit(solution)/shard_map/ppermute | solution.py:575
  28.1 8.2 %collective-permute-start.7 = (bf16[144,512]{1,0:T(8,128)(2,1)S(1)}, bf16[144,512]{1,0:T(8,128)(2,1)S(1)}, u32[]{:S(2)}, u32[]{:S(2)}) collective-permute-start(bf16[144,512]{1,0:T(8,128)(2,1)S(1)} %get-tuple-element.84), channel_id=1, source_target_pairs={{0,12},{1,13},{2,14},{3,15},{4,0},{5,1},{6,2},{7,3},{8,4},{9,5},{1... | collective-permute-start | bytes 442376 | tf_op jit(solution)/shard_map/ppermute | solution.py:575
  28.9 7.4 %collective-permute-start.5 = (bf16[144,512]{1,0:T(8,128)(2,1)S(1)}, bf16[144,512]{1,0:T(8,128)(2,1)S(1)}, u32[]{:S(2)}, u32[]{:S(2)}) collective-permute-start(bf16[144,512]{1,0:T(8,128)(2,1)S(1)} %get-tuple-element.82.after_ref), channel_id=1, source_target_pairs={{0,4},{1,5},{2,6},{3,7},{4,8},{5,9},{6,10},{7,11},{8,12},{9,13},{1... | collective-permute-start | bytes 442376 | tf_op jit(solution)/shard_map/ppermute | solution.py:575
  31.8 8.6 %collective-permute-start.10 = (bf16[144,512]{1,0:T(8,128)(2,1)S(1)}, bf16[144,512]{1,0:T(8,128)(2,1)S(1)}, u32[]{:S(2)}, u32[]{:S(2)}) collective-permute-start(bf16[144,512]{1,0:T(8,128)(2,1)S(1)} %get-tuple-element.99), channel_id=1, source_target_pairs={{0,8},{1,9},{2,10},{3,11},{4,12},{5,13},{6,14},{7,15},{8,0},{9,1},... | collective-permute-start | bytes 442376 | tf_op jit(solution)/shard_map/ppermute | solution.py:575
  34.8 5.8 %collective-permute-start.11 = (bf16[144,512]{1,0:T(8,128)(2,1)S(1)}, bf16[144,512]{1,0:T(8,128)(2,1)S(1)}, u32[]{:S(2)}, u32[]{:S(2)}) collective-permute-start(bf16[144,512]{1,0:T(8,128)(2,1)S(1)} %get-tuple-element.100), channel_id=1, source_target_pairs={{0,12},{1,13},{2,14},{3,15},{4,0},{5,1},{6,2},{7,3},{8,4},{9,5},{1... | collective-permute-start | bytes 442376 | tf_op jit(solution)/shard_map/ppermute | solution.py:575
  35.6 6.1 %collective-permute-start.9 = (bf16[144,512]{1,0:T(8,128)(2,1)S(1)}, bf16[144,512]{1,0:T(8,128)(2,1)S(1)}, u32[]{:S(2)}, u32[]{:S(2)}) collective-permute-start(bf16[144,512]{1,0:T(8,128)(2,1)S(1)} %get-tuple-element.91.refs_0_), channel_id=1, source_target_pairs={{0,4},{1,5},{2,6},{3,7},{4,8},{5,9},{6,10},{7,11},{8,12},{9,13},{1... | collective-permute-start | bytes 442376 | tf_op jit(solution)/shard_map/ppermute | solution.py:575
  36.7 15.3 %collective-permute-start.12 = (bf16[2,128,512]{2,1,0:T(8,128)(2,1)S(1)}, bf16[2,128,512]{2,1,0:T(8,128)(2,1)S(1)}, u32[]{:S(2)}, u32[]{:S(2)}) collective-permute-start(bf16[2,128,512]{2,1,0:T(8,128)(2,1)S(1)} %get-tuple-element.107), channel_id=1, source_target_pairs={{0,2},{1,3},{2,0},{3,1},{4,6},{5,7},{6,4},{7,5},{8,10},{9,11},{10,... | collective-permute-start | bytes 786440 | tf_op jit(solution)/shard_map/ppermute | solution.py:575
  42.1 12.9 %collective-permute-start.13 = (bf16[2,128,512]{2,1,0:T(8,128)(2,1)S(1)}, bf16[2,128,512]{2,1,0:T(8,128)(2,1)S(1)}, u32[]{:S(2)}, u32[]{:S(2)}) collective-permute-start(bf16[2,128,512]{2,1,0:T(8,128)(2,1)S(1)} %get-tuple-element.111), channel_id=1, source_target_pairs={{0,2},{1,3},{2,0},{3,1},{4,6},{5,7},{6,4},{7,5},{8,10},{9,11},{10,... | collective-permute-start | bytes 786440 | tf_op jit(solution)/shard_map/ppermute | solution.py:575
  46.8 8.0 %collective-permute-start.14 = (bf16[128,512]{1,0:T(8,128)(2,1)S(1)}, bf16[128,512]{1,0:T(8,128)(2,1)S(1)}, u32[]{:S(2)}, u32[]{:S(2)}) collective-permute-start(bf16[128,512]{1,0:T(8,128)(2,1)S(1)} %get-tuple-element.116), channel_id=1, source_target_pairs={{0,1},{1,0},{2,3},{3,2},{4,5},{5,4},{6,7},{7,6},{8,9},{9,8},{10,11... | collective-permute-start | bytes 393224 | tf_op jit(solution)/shard_map/ppermute | solution.py:575
  48.6 6.3 %collective-permute-start.15 = (bf16[128,512]{1,0:T(8,128)(2,1)S(1)}, bf16[128,512]{1,0:T(8,128)(2,1)S(1)}, u32[]{:S(2)}, u32[]{:S(2)}) collective-permute-start(bf16[128,512]{1,0:T(8,128)(2,1)S(1)} %get-tuple-element.117), channel_id=1, source_target_pairs={{0,1},{1,0},{2,3},{3,2},{4,5},{5,4},{6,7},{7,6},{8,9},{9,8},{10,11... | collective-permute-start | bytes 393224 | tf_op jit(solution)/shard_map/ppermute | solution.py:575
  51.5 3.4 %collective-permute-start.16 = (bf16[128,512]{1,0:T(8,128)(2,1)S(1)}, bf16[128,512]{1,0:T(8,128)(2,1)S(1)}, u32[]{:S(2)}, u32[]{:S(2)}) collective-permute-start(bf16[128,512]{1,0:T(8,128)(2,1)S(1)} %get-tuple-element.118), channel_id=1, source_target_pairs={{0,1},{1,0},{2,3},{3,2},{4,5},{5,4},{6,7},{7,6},{8,9},{9,8},{10,11... | collective-permute-start | bytes 393224 | tf_op jit(solution)/shard_map/ppermute | solution.py:575
  52.0 2.9 %collective-permute-start.17 = (bf16[128,512]{1,0:T(8,128)(2,1)S(1)}, bf16[128,512]{1,0:T(8,128)(2,1)S(1)}, u32[]{:S(2)}, u32[]{:S(2)}) collective-permute-start(bf16[128,512]{1,0:T(8,128)(2,1)S(1)} %get-tuple-element.119), channel_id=1, source_target_pairs={{0,1},{1,0},{2,3},{3,2},{4,5},{5,4},{6,7},{7,6},{8,9},{9,8},{10,11... | collective-permute-start | bytes 393224 | tf_op jit(solution)/shard_map/ppermute | solution.py:575
  55.6 2.4 %collective-permute-start.21 = (bf16[128,640]{1,0:T(8,128)(2,1)S(1)}, bf16[128,640]{1,0:T(8,128)(2,1)S(1)}, u32[]{:S(2)}, u32[]{:S(2)}) collective-permute-start(bf16[128,640]{1,0:T(8,128)(2,1)S(1)} %get-tuple-element.124), channel_id=1, source_target_pairs={{0,1},{1,0},{2,3},{3,2},{4,5},{5,4},{6,7},{7,6},{8,9},{9,8},{10,11... | collective-permute-start | bytes 491528 | tf_op jit(solution)/shard_map/ppermute | solution.py:575
  56.1 1.9 %collective-permute-start.20 = (bf16[128,640]{1,0:T(8,128)(2,1)S(1)}, bf16[128,640]{1,0:T(8,128)(2,1)S(1)}, u32[]{:S(2)}, u32[]{:S(2)}) collective-permute-start(bf16[128,640]{1,0:T(8,128)(2,1)S(1)} %get-tuple-element.120.refs_4_), channel_id=1, source_target_pairs={{0,1},{1,0},{2,3},{3,2},{4,5},{5,4},{6,7},{7,6},{8,9},{9,8},{10,11... | collective-permute-start | bytes 491528 | tf_op jit(solution)/shard_map/ppermute | solution.py:575
  56.2 1.5 %collective-permute-start.18 = (bf16[128,512]{1,0:T(8,128)(2,1)S(1)}, bf16[128,512]{1,0:T(8,128)(2,1)S(1)}, u32[]{:S(2)}, u32[]{:S(2)}) collective-permute-start(bf16[128,512]{1,0:T(8,128)(2,1)S(1)} %get-tuple-element.122), channel_id=1, source_target_pairs={{0,1},{1,0},{2,3},{3,2},{4,5},{5,4},{6,7},{7,6},{8,9},{9,8},{10,11... | collective-permute-start | bytes 393224 | tf_op jit(solution)/shard_map/ppermute | solution.py:575
  56.6 1.3 %collective-permute-start.19 = (bf16[128,512]{1,0:T(8,128)(2,1)S(1)}, bf16[128,512]{1,0:T(8,128)(2,1)S(1)}, u32[]{:S(2)}, u32[]{:S(2)}) collective-permute-start(bf16[128,512]{1,0:T(8,128)(2,1)S(1)} %get-tuple-element.123), channel_id=1, source_target_pairs={{0,1},{1,0},{2,3},{3,2},{4,5},{5,4},{6,7},{7,6},{8,9},{9,8},{10,11... | collective-permute-start | bytes 393224 | tf_op jit(solution)/shard_map/ppermute | solution.py:575

commit v5 on v4

--- a/solution.py
+++ b/solution.py
@@ -104,8 +104,12 @@
     a = -decay * step
     row = lax.broadcasted_iota(jnp.int32, (TOK, TOK), 0)
     col = lax.broadcasted_iota(jnp.int32, (TOK, TOK), 1)
-    tri = jnp.where((row >= col) & ((row >= SUB) == (col >= SUB)), 1.0, 0.0)
-    cum = dot(tri, a, precision=lax.Precision.HIGHEST)
+    tri = jnp.where((row >= col) & ((row >= SUB) == (col >= SUB)), 1.0, 0.0).astype(BF16)
+    p0 = a.astype(BF16)
+    p1 = (a - p0.astype(F32)).astype(BF16)
+    p2 = (a - p0.astype(F32) - p1.astype(F32)).astype(BF16)
+    sums = dot(tri, jnp.concatenate([p0, p1, p2, jnp.zeros_like(p0)], axis=1))
+    cum = sums[:, 0:HEADS] + sums[:, HEADS : 2 * HEADS] + sums[:, 2 * HEADS : 3 * HEADS]
     excl = cum - a
     e0 = cum[SUB - 1 : SUB]
     e1 = cum[TOK - 1 : TOK]
@@ -309,7 +313,7 @@
 
 
 def first_states_kernel(
-    kq_in, u_in, x_ref, taps_ref, chip_halo_ref, core_halo_ref, table_ref, drow_ref, gate_hbm,
+    kq_in, u_in, x_ref, taps_ref, chip_halo_ref, core_halo_ref, table_ref, drow_ref, after_ref, gate_hbm,
     kq_ref, u_ref, kt_ref, saved_ref, spread_ref, chip_ref, gate_to_core_ref, sem,
 ):
     c, z, y = place()
@@ -326,15 +330,23 @@
     copy.wait()
 
 
+def conv_kernel(x_ref, taps_ref, u_ref):
+    conv_piece(x_ref, taps_ref, u_ref, start_of(2, 1))
+
+
 def rest_kernel(todo, x_ref, taps_ref, chip_halo_ref, core_halo_ref, table_ref, drow_ref, kt_ref, after_ref, *outs):
     c, z, y = place()
     copies = []
     if len(todo) == 2:
-        gate_hbm, gain_hbm, *outs, gate_ref, gain_ref, sems = outs
+        _u_in, gate_hbm, gain_hbm, *outs, gate_ref, gain_ref, sems = outs
         copies = copy_all([(gate_hbm.at[:, columns(c * HALF, HALF)], gate_ref), (gain_hbm, gain_ref)], sems)
     for n, piece in enumerate(todo):
         u_ref, saved_ref, spread_ref, chip_ref = outs[4 * n : 4 * n + 4]
-        conv_piece(x_ref, taps_ref, u_ref, start_of(*piece), halo_of(chip_halo_ref, core_halo_ref))
+        halo = halo_of(chip_halo_ref, core_halo_ref)
+        if piece == (2, 1):
+            repair(x_ref, taps_ref, u_ref, start_of(*piece), halo)
+        else:
+            conv_piece(x_ref, taps_ref, u_ref, start_of(*piece), halo)
         piece_states(u_ref, kt_ref, table_ref, drow_ref, start_of(*piece), saved_ref, spread_ref, chip_ref)
     for copy in copies:
         copy.wait()
@@ -489,6 +501,10 @@
             square[s] = part if square[s] is None else square[s] + part
 
 
+def halves(refs):
+    return refs if len(refs) == 2 else (refs[0].at[0:SUB], refs[0].at[SUB:TOK])
+
+
 def finish_piece(k, p, entry_ref, saved_ref, spread_ref, within_ref, gates, shared, own_ref, msg_refs, squares):
     def put_own(rows, gated):
         own_ref[rows] = gated
@@ -506,6 +522,7 @@
 
 def finish_near_kernel(k, p, entry_ref, saved_ref, spread_ref, within_ref, gate_ref, gate_other_ref, *refs):
     shared, (square_in, own_ref, *msg_refs, square_ref) = refs[:3], refs[3:]
+    msg_refs = halves(msg_refs)
     squares = [[None, None], [None, None]]
     gates = (gate_ref, gate_other_ref)
     finish_piece(k, p, entry_ref, saved_ref, spread_ref, within_ref, gates, shared, own_ref, msg_refs, squares)
@@ -519,7 +536,7 @@
 
 
 def finish_other_kernel(entry_ref, saved_ref, spread_ref, within_ref, gate_ref, *refs):
-    shared, square_in, msg_refs = refs[:3], refs[3], refs[-2:]
+    shared, square_in, msg_refs = refs[:3], refs[3], halves(refs[-1:])
     square = [square_in[1, s * SUB : (s + 1) * SUB] for s in range(2)]
 
     def put(rows, gated):
@@ -547,17 +564,18 @@
 
 
 def norm_kernel(*refs):
-    own_refs, other_refs, (square_ref, gain_ref, out_hbm, out_ref, sems) = refs[:4], refs[4:12], refs[12:]
+    own_refs, other_refs, (square_ref, gain_ref, out_hbm, out_ref, sems) = refs[:4], refs[4:10], refs[10:]
+    other_refs = (other_refs[0:2], other_refs[2:4], halves(other_refs[4:5]), halves(other_refs[5:6]))
     c, z, y = place()
     pieces = []
     for n, piece in enumerate((*NEAR, BACK)):
         pieces.append(((own_refs[n], own_refs[n].at[SUB:TOK]), c * HALF + start_of(*piece)))
-        pieces.append((other_refs[2 * n : 2 * n + 2], (1 - c) * HALF + start_of(*piece)))
+        pieces.append((other_refs[n], (1 - c) * HALF + start_of(*piece)))
     step = 32
     copies = []
     for r in range(0, TOK, step):
         rows, inside = slice(r, r + step), slice(r % SUB, r % SUB + step)
-        total = square_ref[rows] + other_refs[6 + r // SUB][inside, CW : CW + 128].astype(F32)
+        total = square_ref[rows] + other_refs[3][r // SUB][inside, CW : CW + 128].astype(F32)
         scale = lax.rsqrt(jnp.sum(total, axis=1, keepdims=True) * (1.0 / INNER) + 1e-05)
         for refs, start in pieces:
             at = columns(start, CW)
@@ -624,11 +642,12 @@
         halo_kernel, "halo", [vmem(BF16, HALO, WIDE)] * 2, (send(to_chip, chips), kq)
     )
     halo = (x, taps, chip_halo, send(to_core, core))
+    (u2b,) = call(conv_kernel, "conv_21", [U], (x, taps))
     kq, u2a, kt, saved2a, spread2a, zsend0, gate_to_core = call(
         first_states_kernel,
         "states_first",
         [KEYS, U, vmem(BF16, 2, 2, STATE, TOK), SAVED, SPREAD, CHIP, vmem(BF16, TOK, HALF)],
-        (kq, u2a, *halo, table, drow),
+        (kq, u2a, *halo, table, drow, u2b),
         (gate_input,),
         [pltpu.SemaphoreType.DMA(())],
         aliases={0: 0, 1: 1},
@@ -643,22 +662,23 @@
         outs += [vmem(BF16, TOK, HALF), vmem(F32, 1, INNER)]
         sems = [pltpu.SemaphoreType.DMA((2,))]
         params = (gate_input, norm_gain.reshape(1, INNER))
-        return call(kernel, name, outs, (*halo, table, drow, kt, after), params, sems)
-
-    u2b, saved2b, spread2b, zsend1, u3a, saved3a, spread3a, keep0, gate, gain = make_rest(
-        "states_a", ((2, 1), (3, 0)), zsend0
+        return call(kernel, name, outs, (*halo, table, drow, kt, after, u2b), params, sems, aliases={8: 0})
+
+    u3a, saved3a, spread3a, keep0 = make_rest("states_a", ((3, 0),), zsend0)
+    u2b, saved2b, spread2b, zsend1, u3b, saved3b, spread3b, keep1, gate, gain = make_rest(
+        "states_b", ((2, 1), (3, 1)), keep0
     )
     got1 = send(zsend1, zswap)
-    u3b, saved3b, spread3b, keep1 = make_rest("states_b", ((3, 1),), zsend1)
     gates = (gate, send(gate_to_core, core))
     tables = (kq, table, mcol, mrow, drow)
     yout = [vmem(BF16, YMSG, CW)] * 3
     entry = vmem(BF16, 2, STATE, CW)
 
-    msgs = call(group_kernel, "group_a", yout, (keep0, got0, keep1, gates[1]))
+    w2a, qk = make_within(2, 0, u2a, spread2a, *tables, keep1)
+    msgs = call(group_kernel, "group_a", yout, (keep0, got0, w2a, gates[1]))
     arrived0 = along_y(msgs)
-    w2a, qk = make_within(2, 0, u2a, spread2a, *tables, msgs[0])
-    msgs = call(group_kernel, "group_b", yout, (keep1, got1, w2a))
+    w2b = make_within(2, 1, u2b, spread2b, *tables, msgs[0], qk)
+    msgs = call(group_kernel, "group_b", yout, (keep1, got1, w2b))
     arrived1 = along_y(msgs)
     mine0, back0 = call(entries_kernel, "entries_a", [entry, entry], (keep0, got0, *arrived0, msgs[0]))
     back0 = send(back0, zswap)
@@ -666,7 +686,6 @@
     mine1, back1 = call(entries_kernel, "entries_b", [entry, entry], (keep1, got1, *arrived1, w3a))
     back1 = send(back1, zswap)
     w3b = make_within(3, 1, u3b, spread3b, *tables, mine1, qk)
-    w2b = make_within(2, 1, u2b, spread2b, *tables, mine1, qk)
     shared = (kq, table, drow)
     square = kt
     own, other = [], []
@@ -675,11 +694,12 @@
         (mine1, saved3b, spread3b, w3b),
         (back0, saved2a, spread2a, w2a),
     )
-    for (k, p), part in zip(NEAR, parts):
+    two, one = [vmem(BF16, SUB, CW)] * 2, [vmem(BF16, TOK, CW)]
+    for (k, p), part, message in zip(NEAR, parts, (two, two, one)):
         gated, *msg, square = call(
             functools.partial(finish_near_kernel, k, p),
             f"finish_{k}{p}",
-            [vmem(F32, TOK, CW), vmem(BF16, SUB, CW), vmem(BF16, SUB, CW), vmem(F32, 2, TOK, 128)],
+            [vmem(F32, TOK, CW), *message, vmem(F32, 2, TOK, 128)],
             (*part, *gates, *shared, square),
         )
         own.append(gated)
@@ -687,7 +707,7 @@
     msg = call(
         finish_other_kernel,
         "finish_other",
-        [vmem(BF16, SUB, CW + 128)] * 2,
+        [vmem(BF16, TOK, CW + 128)],
         (back1, saved2b, spread2b, w2b, *gates[1:], *shared, square, *other[:4]),
     )
     other += [send(m, core) for m in msg]

time: 59.8 us -> 58.5 us (0.978)
  starting transfers between devices: 29.2 us -> 27.4 us
    ppermute x22 -> x20, starting transfers between devices: 29.2 us -> 27.4 us  [send(): return lax.ppermute(v, 'seq', perm)]
    ppermute x22 -> x20, waiting for transfers between devices: 3.65 us -> 4.08 us  [send(): return lax.ppermute(v, 'seq', perm)]
    pallas_call x20 -> x21, Pallas kernels: 26.5 us -> 26.5 us  [call(): pl.pallas_call(kernel, name=name, in_specs=[VMEM] * len(operands) + [HBM]...]
  transfers between devices with their start and end apart: 22 -> 20, of which waited for: 7 -> 6; matrix products, arithmetic and copies ran while one was open for 0% -> 0% of each run, Pallas kernels for 36% -> 37%
where the time goes in v5:
time: 58.5 us; the launch traced here: 58.4 us
  starting transfers between devices  27.4 us (47%)
  Pallas kernels  26.5 us (45%)
  waiting for transfers between devices  4.08 us (7%)
    ppermute x20, starting transfers between devices, send(): return lax.ppermute(v, 'seq', perm)  27.4 us
    pallas_call x21, Pallas kernels, call(): pl.pallas_call(kernel, name=name, in_specs=[VMEM] * len(operands) + [HBM]...  26.5 us
    ppermute x20, waiting for transfers between devices, send(): return lax.ppermute(v, 'seq', perm)  4.08 us
  transfers between devices with their start and end apart: 20, of which 6 were waited for; matrix products, arithmetic and copies ran while one was open for 0% of the time, Pallas kernels for 37%

profile of v5, /device:TPU:1, one launch (start us, length us, event | category | flops | bytes accessed | tf_op | source)
XLA Modules:
  0.0 58.4 jit_solution(14734301931447886536)
XLA Ops:
  0.0 1.4 %edges.1 = (bf16[256,2560]{1,0:T(8,128)(2,1)S(1)}, bf16[16,4352]{1,0:T(8,128)(2,1)S(1)}) custom-call(bf16[256,4352]{1,0:T(8,128)(2,1)} %x_hbm.3, f32[64,256]{1,0:T(8,128)} %step_hbm.3), custom_call_target="tpu_custom_call" | custom-call | flops 100000000 | bytes 300000 | tf_op jit(solution)/shard_map/edges/pallas_call | solution.py:52
  1.4 1.5 %collective-permute-start = (bf16[256,2560]{1,0:T(8,128)(2,1)S(1)}, bf16[256,2560]{1,0:T(8,128)(2,1)S(1)}, u32[]{:S(2)}, u32[]{:S(2)}) collective-permute-start(bf16[256,2560]{1,0:T(8,128)(2,1)S(1)} %get-tuple-element.63), channel_id=1, source_target_pairs={{0,1},{1,0},{2,3},{3,2},{4,5},{5,4},{6,7},{7,6},{8,9},{9,8},{10,11... | collective-permute-start | bytes 3932168 | tf_op jit(solution)/shard_map/ppermute | solution.py:593
  2.9 5.5 %collective-permute-start.1 = (bf16[16,4352]{1,0:T(8,128)(2,1)S(1)}, bf16[16,4352]{1,0:T(8,128)(2,1)S(1)}, u32[]{:S(2)}, u32[]{:S(2)}) collective-permute-start(bf16[16,4352]{1,0:T(8,128)(2,1)S(1)} %get-tuple-element.66), channel_id=1, source_target_pairs={{1,2},{3,4},{5,6},{7,8},{9,10},{11,12},{13,14},{2,1},{4,3},{6,5},{... | collective-permute-start | bytes 417800 | tf_op jit(solution)/shard_map/ppermute | solution.py:593
  8.4 0.0 collective-permute-done.other_ref
  8.4 3.5 %front.1 = (bf16[2,256,2304]{2,1,0:T(8,128)(2,1)S(1)}, bf16[6,256,128]{2,1,0:T(8,128)(2,1)S(1)}, f32[256,128]{1,0:T(8,128)S(1)}, f32[64,256]{1,0:T(8,128)S(1)}, ...) custom-call(bf16[256,2560]{1,0:T(8,128)(2,1)S(1)} %collective-permut, ...), custom_call_target="tpu_custom_call" | custom-call | flops 100000000 | bytes 300000 | tf_op jit(solution)/shard_map/front/pallas_call | solution.py:52
  11.9 0.1 collective-permute-start.2
  12.0 1.1 %conv_21.1.after_ref.outs_0_ = bf16[2,2,256,512]{3,2,1,0:T(8,128)(2,1)S(1)} custom-call(bf16[2,256,2304]{2,1,0:T(8,128)(2,1)S(1)} %get-tuple-element.64.x_ref, f32[8,2304]{1,0:T(8,128)S(1)} %get-tuple-element.65.taps_ref), custom_call_target="tpu_custom_call" | custom-call | flops 100000000 | bytes 300000 | tf_op jit(solution)/shard_map/conv_21/pallas_call | solution.py:52
  13.1 0.1 collective-permute-done.2.core_halo_ref
  13.2 1.3 %states_first.1 = (bf16[2,2,256,256]{3,2,1,0:T(8,128)(2,1)S(1)}, bf16[2,2,256,512]{3,2,1,0:T(8,128)(2,1)S(1)}, bf16[2,2,128,256]{3,2,1,0:T(8,128)(2,1)S(1)}, bf1...) custom-call(bf16[2,2,256,256]{3,2,1,0:T(8,128)(2,1)S(1)} %get-tuple-, ...), custom_call_target="tpu_custom_call", output_to_operand_aliasing={{0}: (0, {}), {1}: (1, {})} | custom-call | flops 100000000 | bytes 300000 | tf_op jit(solution)/shard_map/states_first/pallas_call | solution.py:52
  14.5 0.5 collective-permute-start.4
  15.0 3.4 %collective-permute-start.3 = (bf16[272,512]{1,0:T(8,128)(2,1)S(1)}, bf16[272,512]{1,0:T(8,128)(2,1)S(1)}, u32[]{:S(2)}, u32[]{:S(2)}) collective-permute-start(bf16[272,512]{1,0:T(8,128)(2,1)S(1)} %get-tuple-element.74.after_ref), channel_id=1, source_target_pairs={{0,2},{1,3},{2,0},{3,1},{4,6},{5,7},{6,4},{7,5},{8,10},{9,11},{10,... | collective-permute-start | bytes 835592 | tf_op jit(solution)/shard_map/ppermute | solution.py:593
  18.4 2.1 %states_a.1 = (bf16[2,2,256,512]{3,2,1,0:T(8,128)(2,1)S(1)}, bf16[6,128,512]{2,1,0:T(8,128)(2,1)S(1)}, bf16[2,128,512]{2,1,0:T(8,128)(2,1)S(1)}, bf16[272,512]{1,0:T(8,128)(2,1)S(1)}) custom-call(bf16[2,256,2304]{2,1,0:T(8,128)(2,1)S(1)} %get-tuple-element.64.x_ref, f32[8,2304]{1,0:T(8,128)S(1)} %get-tuple-element.65.taps_ref, ...), custom_call_target="tpu_custom_call" | custom-call | flops 100000000 | bytes 300000 | tf_op jit(solution)/shard_map/states_a/pallas_call | solution.py:52
  20.5 3.3 %states_b.1 = (bf16[2,2,256,512]{3,2,1,0:T(8,128)(2,1)S(1)}, bf16[6,128,512]{2,1,0:T(8,128)(2,1)S(1)}, bf16[2,128,512]{2,1,0:T(8,128)(2,1)S(1)}, bf16[272,512]{1...) custom-call(bf16[2,256,2304]{2,1,0:T(8,128)(2,1)S(1)} %get-tuple-ele, ...), custom_call_target="tpu_custom_call", output_to_operand_aliasing={{0}: (8, {})} | custom-call | flops 100000000 | bytes 300000 | tf_op jit(solution)/shard_map/states_b/pallas_call | solution.py:52
  23.8 0.1 collective-permute-start.8
  23.9 1.8 %within_20.1 = (bf16[2,256,512]{2,1,0:T(8,128)(2,1)S(1)}, f32[2,2,2,128,128]{4,3,2,1,0:T(8,128)S(1)}) custom-call(bf16[2,2,256,512]{3,2,1,0:T(8,128)(2,1)S(1)} %get-tuple-element.76.u_ref, bf16[2,128,512]{2,1,0:T(8,128)(2,1)S(1)} %get-tuple-element.77.spread_ref, bf16[2,2,256,256]{3,2,1,0:T(8,128)(2,1)S(1)} %get-tuple-element.78.kq_ref.refs_0_, ...), custom_call_target="tpu_custom_call" | custom-call | flops 100000000 | bytes 300000 | tf_op jit(solution)/shard_map/within_20/pallas_call | solution.py:52
  25.8 0.0 collective-permute-done.4.refs_1_.gate_other_ref.gate_ref
  25.8 0.1 group_a.1
  25.9 3.2 %collective-permute-start.6 = (bf16[144,512]{1,0:T(8,128)(2,1)S(1)}, bf16[144,512]{1,0:T(8,128)(2,1)S(1)}, u32[]{:S(2)}, u32[]{:S(2)}) collective-permute-start(bf16[144,512]{1,0:T(8,128)(2,1)S(1)} %get-tuple-element.85), channel_id=1, source_target_pairs={{0,8},{1,9},{2,10},{3,11},{4,12},{5,13},{6,14},{7,15},{8,0},{9,1},... | collective-permute-start | bytes 442376 | tf_op jit(solution)/shard_map/ppermute | solution.py:593
  29.1 0.8 %collective-permute-start.7 = (bf16[144,512]{1,0:T(8,128)(2,1)S(1)}, bf16[144,512]{1,0:T(8,128)(2,1)S(1)}, u32[]{:S(2)}, u32[]{:S(2)}) collective-permute-start(bf16[144,512]{1,0:T(8,128)(2,1)S(1)} %get-tuple-element.86), channel_id=1, source_target_pairs={{0,12},{1,13},{2,14},{3,15},{4,0},{5,1},{6,2},{7,3},{8,4},{9,5},{1... | collective-permute-start | bytes 442376 | tf_op jit(solution)/shard_map/ppermute | solution.py:593
  29.9 0.7 %collective-permute-start.5 = (bf16[144,512]{1,0:T(8,128)(2,1)S(1)}, bf16[144,512]{1,0:T(8,128)(2,1)S(1)}, u32[]{:S(2)}, u32[]{:S(2)}) collective-permute-start(bf16[144,512]{1,0:T(8,128)(2,1)S(1)} %get-tuple-element.84.after_ref), channel_id=1, source_target_pairs={{0,4},{1,5},{2,6},{3,7},{4,8},{5,9},{6,10},{7,11},{8,12},{9,13},{1... | collective-permute-start | bytes 442376 | tf_op jit(solution)/shard_map/ppermute | solution.py:593
  30.6 1.7 %within_21.1.refs_0_.within_ref = bf16[2,256,512]{2,1,0:T(8,128)(2,1)S(1)} custom-call(bf16[2,2,256,512]{3,2,1,0:T(8,128)(2,1)S(1)} %get-tuple-element.88.u_ref, bf16[2,128,512]{2,1,0:T(8,128)(2,1)S(1)} %get-tuple-element.89.spread_ref, bf16[2,2,256,256]{3,2,1,0:T(8,128)(2,1)S(1)} %get-tuple-element.78.kq_ref.refs_0_, ...), custom_call_target="tpu_custom_call" | custom-call | flops 100000000 | bytes 300000 | tf_op jit(solution)/shard_map/within_21/pallas_call | solution.py:52
  32.2 1.0 %collective-permute-done.8.got_ref = bf16[272,512]{1,0:T(8,128)(2,1)S(1)} collective-permute-done((bf16[272,512]{1,0:T(8,128)(2,1)S(1)}, bf16[272,512]{1,0:T(8,128)(2,1)S(1)}, u32[]{:S(2)}, u32[]{:S(2)}) %collective-permute-start.8) | collective-permute-done | bytes 278560 | tf_op jit(solution)/shard_map/ppermute | solution.py:593
  33.2 0.1 group_b.1
  33.4 3.0 %collective-permute-start.10 = (bf16[144,512]{1,0:T(8,128)(2,1)S(1)}, bf16[144,512]{1,0:T(8,128)(2,1)S(1)}, u32[]{:S(2)}, u32[]{:S(2)}) collective-permute-start(bf16[144,512]{1,0:T(8,128)(2,1)S(1)} %get-tuple-element.98), channel_id=1, source_target_pairs={{0,8},{1,9},{2,10},{3,11},{4,12},{5,13},{6,14},{7,15},{8,0},{9,1},... | collective-permute-start | bytes 442376 | tf_op jit(solution)/shard_map/ppermute | solution.py:593
  36.4 0.8 %collective-permute-start.11 = (bf16[144,512]{1,0:T(8,128)(2,1)S(1)}, bf16[144,512]{1,0:T(8,128)(2,1)S(1)}, u32[]{:S(2)}, u32[]{:S(2)}) collective-permute-start(bf16[144,512]{1,0:T(8,128)(2,1)S(1)} %get-tuple-element.99), channel_id=1, source_target_pairs={{0,12},{1,13},{2,14},{3,15},{4,0},{5,1},{6,2},{7,3},{8,4},{9,5},{1... | collective-permute-start | bytes 442376 | tf_op jit(solution)/shard_map/ppermute | solution.py:593
  37.1 0.7 %collective-permute-start.9 = (bf16[144,512]{1,0:T(8,128)(2,1)S(1)}, bf16[144,512]{1,0:T(8,128)(2,1)S(1)}, u32[]{:S(2)}, u32[]{:S(2)}) collective-permute-start(bf16[144,512]{1,0:T(8,128)(2,1)S(1)} %get-tuple-element.91.refs_0_), channel_id=1, source_target_pairs={{0,4},{1,5},{2,6},{3,7},{4,8},{5,9},{6,10},{7,11},{8,12},{9,13},{1... | collective-permute-start | bytes 442376 | tf_op jit(solution)/shard_map/ppermute | solution.py:593
  37.8 0.3 entries_a.1
  38.2 1.3 %collective-permute-start.12 = (bf16[2,128,512]{2,1,0:T(8,128)(2,1)S(1)}, bf16[2,128,512]{2,1,0:T(8,128)(2,1)S(1)}, u32[]{:S(2)}, u32[]{:S(2)}) collective-permute-start(bf16[2,128,512]{2,1,0:T(8,128)(2,1)S(1)} %get-tuple-element.106), channel_id=1, source_target_pairs={{0,2},{1,3},{2,0},{3,1},{4,6},{5,7},{6,4},{7,5},{8,10},{9,11},{10,... | collective-permute-start | bytes 786440 | tf_op jit(solution)/shard_map/ppermute | solution.py:593
  39.5 1.6 %within_30.1.within_ref.refs_0_ = bf16[2,256,512]{2,1,0:T(8,128)(2,1)S(1)} custom-call(bf16[2,2,256,512]{3,2,1,0:T(8,128)(2,1)S(1)} %get-tuple-element.95.u_ref, bf16[2,128,512]{2,1,0:T(8,128)(2,1)S(1)} %get-tuple-element.94.spread_ref, bf16[2,2,256,256]{3,2,1,0:T(8,128)(2,1)S(1)} %get-tuple-element.78.kq_ref.refs_0_, ...), custom_call_target="tpu_custom_call" | custom-call | flops 100000000 | bytes 300000 | tf_op jit(solution)/shard_map/within_30/pallas_call | solution.py:52
  41.1 1.0 %collective-permute-done.11.r3_ref = bf16[144,512]{1,0:T(8,128)(2,1)S(1)} collective-permute-done((bf16[144,512]{1,0:T(8,128)(2,1)S(1)}, bf16[144,512]{1,0:T(8,128)(2,1)S(1)}, u32[]{:S(2)}, u32[]{:S(2)}) %collective-permute-start.11) | collective-permute-done | bytes 147488 | tf_op jit(solution)/shard_map/ppermute | solution.py:593
  42.2 0.8 %collective-permute-done.9.r1_ref = bf16[144,512]{1,0:T(8,128)(2,1)S(1)} collective-permute-done((bf16[144,512]{1,0:T(8,128)(2,1)S(1)}, bf16[144,512]{1,0:T(8,128)(2,1)S(1)}, u32[]{:S(2)}, u32[]{:S(2)}) %collective-permute-start.9) | collective-permute-done | bytes 147488 | tf_op jit(solution)/shard_map/ppermute | solution.py:593
  43.0 0.3 entries_b.1
  43.3 2.6 %collective-permute-start.13 = (bf16[2,128,512]{2,1,0:T(8,128)(2,1)S(1)}, bf16[2,128,512]{2,1,0:T(8,128)(2,1)S(1)}, u32[]{:S(2)}, u32[]{:S(2)}) collective-permute-start(bf16[2,128,512]{2,1,0:T(8,128)(2,1)S(1)} %get-tuple-element.110), channel_id=1, source_target_pairs={{0,2},{1,3},{2,0},{3,1},{4,6},{5,7},{6,4},{7,5},{8,10},{9,11},{10,... | collective-permute-start | bytes 786440 | tf_op jit(solution)/shard_map/ppermute | solution.py:593
  46.0 1.1 %finish_30.1 = (f32[256,512]{1,0:T(8,128)S(1)}, bf16[128,512]{1,0:T(8,128)(2,1)S(1)}, bf16[128,512]{1,0:T(8,128)(2,1)S(1)}, f32[2,256,128]{2,1,0:T(8,128)S(1)}) custom-call(bf16[2,128,512]{2,1,0:T(8,128)(2,1)S(1)} %get-tuple-element.92.after_ref.entry_ref, bf16[6,128,512]{2,1,0:T(8,128)(2,1)S(1)} %get-tuple-element.93.saved_ref, ...), custom_call_target="tpu_custom_call" | custom-call | flops 100000000 | bytes 300000 | tf_op jit(solution)/shard_map/finish_30/pallas_call | solution.py:52
  47.1 1.7 %collective-permute-start.14 = (bf16[128,512]{1,0:T(8,128)(2,1)S(1)}, bf16[128,512]{1,0:T(8,128)(2,1)S(1)}, u32[]{:S(2)}, u32[]{:S(2)}) collective-permute-start(bf16[128,512]{1,0:T(8,128)(2,1)S(1)} %get-tuple-element.113), channel_id=1, source_target_pairs={{0,1},{1,0},{2,3},{3,2},{4,5},{5,4},{6,7},{7,6},{8,9},{9,8},{10,11... | collective-permute-start | bytes 393224 | tf_op jit(solution)/shard_map/ppermute | solution.py:593
  48.8 0.1 collective-permute-start.15
  48.9 1.7 %within_31.1.within_ref = bf16[2,256,512]{2,1,0:T(8,128)(2,1)S(1)} custom-call(bf16[2,2,256,512]{3,2,1,0:T(8,128)(2,1)S(1)} %get-tuple-element.103.u_ref, bf16[2,128,512]{2,1,0:T(8,128)(2,1)S(1)} %get-tuple-element.102.spread_ref, bf16[2,2,256,256]{3,2,1,0:T(8,128)(2,1)S(1)} %get-tuple-element.78.kq_ref.refs_0_, ...), custom_call_target="tpu_custom_call" | custom-call | flops 100000000 | bytes 300000 | tf_op jit(solution)/shard_map/within_31/pallas_call | solution.py:52
  50.5 1.1 %finish_31.1 = (f32[256,512]{1,0:T(8,128)S(1)}, bf16[128,512]{1,0:T(8,128)(2,1)S(1)}, bf16[128,512]{1,0:T(8,128)(2,1)S(1)}, f32[2,256,128]{2,1,0:T(8,128)S(1)}) custom-call(bf16[2,128,512]{2,1,0:T(8,128)(2,1)S(1)} %get-tuple-element.100.after_ref.entry_ref, bf16[6,128,512]{2,1,0:T(8,128)(2,1)S(1)} %get-tuple-element.101.saved_ref, ...), custom_call_target="tpu_custom_call" | custom-call | flops 100000000 | bytes 300000 | tf_op jit(solution)/shard_map/finish_31/pallas_call | solution.py:52
  51.7 0.5 collective-permute-start.16
  52.2 0.1 collective-permute-start.17
  52.3 1.1 %finish_20.1 = (f32[256,512]{1,0:T(8,128)S(1)}, bf16[256,512]{1,0:T(8,128)(2,1)S(1)}, f32[2,256,128]{2,1,0:T(8,128)S(1)}) custom-call(bf16[2,128,512]{2,1,0:T(8,128)(2,1)S(1)} %collective-permute-done.12.entry_ref, bf16[6,128,512]{2,1,0:T(8,128)(2,1)S(1)} %get-tuple-element.107.saved_ref, bf16[2,128,512]{2,1,0:T(8,128)(2,1)S(1)} %get-tuple-element.77.spread_ref, ...), custom_call_target="tpu_custom_call" | custom-call | flops 100000000 | bytes 300000 | tf_op jit(solution)/shard_map/finish_20/pallas_call | solution.py:52
  53.4 0.1 collective-permute-done.17.refs_7_
  53.5 0.7 %finish_other.1.refs_4_ = bf16[256,640]{1,0:T(8,128)(2,1)S(1)} custom-call(bf16[2,128,512]{2,1,0:T(8,128)(2,1)S(1)} %collective-permute-done.13.entry_ref, bf16[6,128,512]{2,1,0:T(8,128)(2,1)S(1)} %get-tuple-element.111.saved_ref, bf16[2,128,512]{2,1,0:T(8,128)(2,1)S(1)} %get-tuple-element.89.spread_ref, ...), custom_call_target="tpu_custom_call" | custom-call | flops 100000000 | bytes 300000 | tf_op jit(solution)/shard_map/finish_other/pallas_call | solution.py:52
  54.2 0.8 %collective-permute-start.19 = (bf16[256,640]{1,0:T(8,128)(2,1)S(1)}, bf16[256,640]{1,0:T(8,128)(2,1)S(1)}, u32[]{:S(2)}, u32[]{:S(2)}) collective-permute-start(bf16[256,640]{1,0:T(8,128)(2,1)S(1)} %finish_other.1.refs_4_), channel_id=1, source_target_pairs={{0,1},{1,0},{2,3},{3,2},{4,5},{5,4},{6,7},{7,6},{8,9},{9,8},{10,11... | collective-permute-start | bytes 983048 | tf_op jit(solution)/shard_map/ppermute | solution.py:593
  55.0 0.1 collective-permute-start.18
  55.1 0.6 %finish_own.1 = (f32[256,512]{1,0:T(8,128)S(1)}, f32[256,128]{1,0:T(8,128)S(1)}) custom-call(bf16[2,128,512]{2,1,0:T(8,128)(2,1)S(1)} %collective-permute-done.13.entry_ref, bf16[6,128,512]{2,1,0:T(8,128)(2,1)S(1)} %get-tuple-element.111.saved_ref, bf16[2,128,512]{2,1,0:T(8,128)(2,1)S(1)} %get-tuple-element.89.spread_ref, ...), custom_call_target="tpu_custom_call" | custom-call | flops 100000000 | bytes 300000 | tf_op jit(solution)/shard_map/finish_own/pallas_call | solution.py:52
  55.7 0.9 %collective-permute-done.18.refs_8_ = bf16[256,512]{1,0:T(8,128)(2,1)S(1)} collective-permute-done((bf16[256,512]{1,0:T(8,128)(2,1)S(1)}, bf16[256,512]{1,0:T(8,128)(2,1)S(1)}, u32[]{:S(2)}, u32[]{:S(2)}) %collective-permute-start.18) | collective-permute-done | bytes 262176 | tf_op jit(solution)/shard_map/ppermute | solution.py:593
  56.7 1.5 %norm.1 = bf16[256,4096]{1,0:T(8,128)(2,1)} custom-call(f32[256,512]{1,0:T(8,128)S(1)} %get-tuple-element.97.refs_0_, f32[256,512]{1,0:T(8,128)S(1)} %get-tuple-element.105.refs_1_, f32[256,512]{1,0:T(8,128)S(1)} %get-tuple-element.109.refs_2_, f32[256,512]{1,0:T(8,128)S(1)} %get-tuple-element.117.refs_3_, ...), custom_call_target="tpu_custom_call" | custom-call | flops 100000000 | bytes 300000 | tf_op jit(solution)/shard_map/norm/pallas_call | solution.py:52
  (13 shorter events, 0.1 us)
Async XLA Ops:
  1.4 7.0 %collective-permute-start = (bf16[256,2560]{1,0:T(8,128)(2,1)S(1)}, bf16[256,2560]{1,0:T(8,128)(2,1)S(1)}, u32[]{:S(2)}, u32[]{:S(2)}) collective-permute-start(bf16[256,2560]{1,0:T(8,128)(2,1)S(1)} %get-tuple-element.63), channel_id=1, source_target_pairs={{0,1},{1,0},{2,3},{3,2},{4,5},{5,4},{6,7},{7,6},{8,9},{9,8},{10,11... | collective-permute-start | bytes 3932168 | tf_op jit(solution)/shard_map/ppermute | solution.py:593
  2.9 9.0 %collective-permute-start.1 = (bf16[16,4352]{1,0:T(8,128)(2,1)S(1)}, bf16[16,4352]{1,0:T(8,128)(2,1)S(1)}, u32[]{:S(2)}, u32[]{:S(2)}) collective-permute-start(bf16[16,4352]{1,0:T(8,128)(2,1)S(1)} %get-tuple-element.66), channel_id=1, source_target_pairs={{1,2},{3,4},{5,6},{7,8},{9,10},{11,12},{13,14},{2,1},{4,3},{6,5},{... | collective-permute-start | bytes 417800 | tf_op jit(solution)/shard_map/ppermute | solution.py:593
  11.9 1.3 %collective-permute-start.2 = (bf16[16,2304]{1,0:T(8,128)(2,1)S(1)}, bf16[16,2304]{1,0:T(8,128)(2,1)S(1)}, u32[]{:S(2)}, u32[]{:S(2)}) collective-permute-start(bf16[16,2304]{1,0:T(8,128)(2,1)S(1)} %get-tuple-element.69), channel_id=1, source_target_pairs={{0,1},{1,0},{2,3},{3,2},{4,5},{5,4},{6,7},{7,6},{8,9},{9,8},{10,11... | collective-permute-start | bytes 221192 | tf_op jit(solution)/shard_map/ppermute | solution.py:593
  14.5 11.2 %collective-permute-start.4 = (bf16[256,2048]{1,0:T(8,128)(2,1)S(1)}, bf16[256,2048]{1,0:T(8,128)(2,1)S(1)}, u32[]{:S(2)}, u32[]{:S(2)}) collective-permute-start(bf16[256,2048]{1,0:T(8,128)(2,1)S(1)} %get-tuple-element.83), channel_id=1, source_target_pairs={{0,1},{1,0},{2,3},{3,2},{4,5},{5,4},{6,7},{7,6},{8,9},{9,8},{10,11... | collective-permute-start | bytes 3145736 | tf_op jit(solution)/shard_map/ppermute | solution.py:593
  15.0 10.8 %collective-permute-start.3 = (bf16[272,512]{1,0:T(8,128)(2,1)S(1)}, bf16[272,512]{1,0:T(8,128)(2,1)S(1)}, u32[]{:S(2)}, u32[]{:S(2)}) collective-permute-start(bf16[272,512]{1,0:T(8,128)(2,1)S(1)} %get-tuple-element.74.after_ref), channel_id=1, source_target_pairs={{0,2},{1,3},{2,0},{3,1},{4,6},{5,7},{6,4},{7,5},{8,10},{9,11},{10,... | collective-permute-start | bytes 835592 | tf_op jit(solution)/shard_map/ppermute | solution.py:593
  23.8 9.4 %collective-permute-start.8 = (bf16[272,512]{1,0:T(8,128)(2,1)S(1)}, bf16[272,512]{1,0:T(8,128)(2,1)S(1)}, u32[]{:S(2)}, u32[]{:S(2)}) collective-permute-start(bf16[272,512]{1,0:T(8,128)(2,1)S(1)} %get-tuple-element.87), channel_id=1, source_target_pairs={{0,2},{1,3},{2,0},{3,1},{4,6},{5,7},{6,4},{7,5},{8,10},{9,11},{10,... | collective-permute-start | bytes 835592 | tf_op jit(solution)/shard_map/ppermute | solution.py:593
  25.9 11.2 %collective-permute-start.6 = (bf16[144,512]{1,0:T(8,128)(2,1)S(1)}, bf16[144,512]{1,0:T(8,128)(2,1)S(1)}, u32[]{:S(2)}, u32[]{:S(2)}) collective-permute-start(bf16[144,512]{1,0:T(8,128)(2,1)S(1)} %get-tuple-element.85), channel_id=1, source_target_pairs={{0,8},{1,9},{2,10},{3,11},{4,12},{5,13},{6,14},{7,15},{8,0},{9,1},... | collective-permute-start | bytes 442376 | tf_op jit(solution)/shard_map/ppermute | solution.py:593
  29.1 8.7 %collective-permute-start.7 = (bf16[144,512]{1,0:T(8,128)(2,1)S(1)}, bf16[144,512]{1,0:T(8,128)(2,1)S(1)}, u32[]{:S(2)}, u32[]{:S(2)}) collective-permute-start(bf16[144,512]{1,0:T(8,128)(2,1)S(1)} %get-tuple-element.86), channel_id=1, source_target_pairs={{0,12},{1,13},{2,14},{3,15},{4,0},{5,1},{6,2},{7,3},{8,4},{9,5},{1... | collective-permute-start | bytes 442376 | tf_op jit(solution)/shard_map/ppermute | solution.py:593
  29.9 8.0 %collective-permute-start.5 = (bf16[144,512]{1,0:T(8,128)(2,1)S(1)}, bf16[144,512]{1,0:T(8,128)(2,1)S(1)}, u32[]{:S(2)}, u32[]{:S(2)}) collective-permute-start(bf16[144,512]{1,0:T(8,128)(2,1)S(1)} %get-tuple-element.84.after_ref), channel_id=1, source_target_pairs={{0,4},{1,5},{2,6},{3,7},{4,8},{5,9},{6,10},{7,11},{8,12},{9,13},{1... | collective-permute-start | bytes 442376 | tf_op jit(solution)/shard_map/ppermute | solution.py:593
  33.4 7.8 %collective-permute-start.10 = (bf16[144,512]{1,0:T(8,128)(2,1)S(1)}, bf16[144,512]{1,0:T(8,128)(2,1)S(1)}, u32[]{:S(2)}, u32[]{:S(2)}) collective-permute-start(bf16[144,512]{1,0:T(8,128)(2,1)S(1)} %get-tuple-element.98), channel_id=1, source_target_pairs={{0,8},{1,9},{2,10},{3,11},{4,12},{5,13},{6,14},{7,15},{8,0},{9,1},... | collective-permute-start | bytes 442376 | tf_op jit(solution)/shard_map/ppermute | solution.py:593
  36.4 5.8 %collective-permute-start.11 = (bf16[144,512]{1,0:T(8,128)(2,1)S(1)}, bf16[144,512]{1,0:T(8,128)(2,1)S(1)}, u32[]{:S(2)}, u32[]{:S(2)}) collective-permute-start(bf16[144,512]{1,0:T(8,128)(2,1)S(1)} %get-tuple-element.99), channel_id=1, source_target_pairs={{0,12},{1,13},{2,14},{3,15},{4,0},{5,1},{6,2},{7,3},{8,4},{9,5},{1... | collective-permute-start | bytes 442376 | tf_op jit(solution)/shard_map/ppermute | solution.py:593
  37.1 5.9 %collective-permute-start.9 = (bf16[144,512]{1,0:T(8,128)(2,1)S(1)}, bf16[144,512]{1,0:T(8,128)(2,1)S(1)}, u32[]{:S(2)}, u32[]{:S(2)}) collective-permute-start(bf16[144,512]{1,0:T(8,128)(2,1)S(1)} %get-tuple-element.91.refs_0_), channel_id=1, source_target_pairs={{0,4},{1,5},{2,6},{3,7},{4,8},{5,9},{6,10},{7,11},{8,12},{9,13},{1... | collective-permute-start | bytes 442376 | tf_op jit(solution)/shard_map/ppermute | solution.py:593
  38.2 14.0 %collective-permute-start.12 = (bf16[2,128,512]{2,1,0:T(8,128)(2,1)S(1)}, bf16[2,128,512]{2,1,0:T(8,128)(2,1)S(1)}, u32[]{:S(2)}, u32[]{:S(2)}) collective-permute-start(bf16[2,128,512]{2,1,0:T(8,128)(2,1)S(1)} %get-tuple-element.106), channel_id=1, source_target_pairs={{0,2},{1,3},{2,0},{3,1},{4,6},{5,7},{6,4},{7,5},{8,10},{9,11},{10,... | collective-permute-start | bytes 786440 | tf_op jit(solution)/shard_map/ppermute | solution.py:593
  43.3 10.2 %collective-permute-start.13 = (bf16[2,128,512]{2,1,0:T(8,128)(2,1)S(1)}, bf16[2,128,512]{2,1,0:T(8,128)(2,1)S(1)}, u32[]{:S(2)}, u32[]{:S(2)}) collective-permute-start(bf16[2,128,512]{2,1,0:T(8,128)(2,1)S(1)} %get-tuple-element.110), channel_id=1, source_target_pairs={{0,2},{1,3},{2,0},{3,1},{4,6},{5,7},{6,4},{7,5},{8,10},{9,11},{10,... | collective-permute-start | bytes 786440 | tf_op jit(solution)/shard_map/ppermute | solution.py:593
  47.1 6.3 %collective-permute-start.14 = (bf16[128,512]{1,0:T(8,128)(2,1)S(1)}, bf16[128,512]{1,0:T(8,128)(2,1)S(1)}, u32[]{:S(2)}, u32[]{:S(2)}) collective-permute-start(bf16[128,512]{1,0:T(8,128)(2,1)S(1)} %get-tuple-element.113), channel_id=1, source_target_pairs={{0,1},{1,0},{2,3},{3,2},{4,5},{5,4},{6,7},{7,6},{8,9},{9,8},{10,11... | collective-permute-start | bytes 393224 | tf_op jit(solution)/shard_map/ppermute | solution.py:593
  48.8 4.6 %collective-permute-start.15 = (bf16[128,512]{1,0:T(8,128)(2,1)S(1)}, bf16[128,512]{1,0:T(8,128)(2,1)S(1)}, u32[]{:S(2)}, u32[]{:S(2)}) collective-permute-start(bf16[128,512]{1,0:T(8,128)(2,1)S(1)} %get-tuple-element.114), channel_id=1, source_target_pairs={{0,1},{1,0},{2,3},{3,2},{4,5},{5,4},{6,7},{7,6},{8,9},{9,8},{10,11... | collective-permute-start | bytes 393224 | tf_op jit(solution)/shard_map/ppermute | solution.py:593
  51.7 1.7 %collective-permute-start.16 = (bf16[128,512]{1,0:T(8,128)(2,1)S(1)}, bf16[128,512]{1,0:T(8,128)(2,1)S(1)}, u32[]{:S(2)}, u32[]{:S(2)}) collective-permute-start(bf16[128,512]{1,0:T(8,128)(2,1)S(1)} %get-tuple-element.115), channel_id=1, source_target_pairs={{0,1},{1,0},{2,3},{3,2},{4,5},{5,4},{6,7},{7,6},{8,9},{9,8},{10,11... | collective-permute-start | bytes 393224 | tf_op jit(solution)/shard_map/ppermute | solution.py:593
  52.2 1.3 %collective-permute-start.17 = (bf16[128,512]{1,0:T(8,128)(2,1)S(1)}, bf16[128,512]{1,0:T(8,128)(2,1)S(1)}, u32[]{:S(2)}, u32[]{:S(2)}) collective-permute-start(bf16[128,512]{1,0:T(8,128)(2,1)S(1)} %get-tuple-element.116), channel_id=1, source_target_pairs={{0,1},{1,0},{2,3},{3,2},{4,5},{5,4},{6,7},{7,6},{8,9},{9,8},{10,11... | collective-permute-start | bytes 393224 | tf_op jit(solution)/shard_map/ppermute | solution.py:593
  54.2 2.5 %collective-permute-start.19 = (bf16[256,640]{1,0:T(8,128)(2,1)S(1)}, bf16[256,640]{1,0:T(8,128)(2,1)S(1)}, u32[]{:S(2)}, u32[]{:S(2)}) collective-permute-start(bf16[256,640]{1,0:T(8,128)(2,1)S(1)} %finish_other.1.refs_4_), channel_id=1, source_target_pairs={{0,1},{1,0},{2,3},{3,2},{4,5},{5,4},{6,7},{7,6},{8,9},{9,8},{10,11... | collective-permute-start | bytes 983048 | tf_op jit(solution)/shard_map/ppermute | solution.py:593
  55.0 1.6 %collective-permute-start.18 = (bf16[256,512]{1,0:T(8,128)(2,1)S(1)}, bf16[256,512]{1,0:T(8,128)(2,1)S(1)}, u32[]{:S(2)}, u32[]{:S(2)}) collective-permute-start(bf16[256,512]{1,0:T(8,128)(2,1)S(1)} %get-tuple-element.118), channel_id=1, source_target_pairs={{0,1},{1,0},{2,3},{3,2},{4,5},{5,4},{6,7},{7,6},{8,9},{9,8},{10,11... | collective-permute-start | bytes 786440 | tf_op jit(solution)/shard_map/ppermute | solution.py:593

commit v6 on v5

--- a/solution.py
+++ b/solution.py
@@ -337,8 +337,10 @@
 def rest_kernel(todo, x_ref, taps_ref, chip_halo_ref, core_halo_ref, table_ref, drow_ref, kt_ref, after_ref, *outs):
     c, z, y = place()
     copies = []
-    if len(todo) == 2:
-        _u_in, gate_hbm, gain_hbm, *outs, gate_ref, gain_ref, sems = outs
+    if todo == ((2, 1),):
+        _u_in, *outs = outs
+    if todo == ((3, 1),):
+        gate_hbm, gain_hbm, *outs, gate_ref, gain_ref, sems = outs
         copies = copy_all([(gate_hbm.at[:, columns(c * HALF, HALF)], gate_ref), (gain_hbm, gain_ref)], sems)
     for n, piece in enumerate(todo):
         u_ref, saved_ref, spread_ref, chip_ref = outs[4 * n : 4 * n + 4]
@@ -656,19 +658,20 @@
 
     def make_rest(name, todo, after):
         kernel = functools.partial(rest_kernel, todo)
-        outs = [U, SAVED, SPREAD, CHIP] * len(todo)
-        if len(todo) == 1:
-            return call(kernel, name, outs, (*halo, table, drow, kt, after))
-        outs += [vmem(BF16, TOK, HALF), vmem(F32, 1, INNER)]
-        sems = [pltpu.SemaphoreType.DMA((2,))]
-        params = (gate_input, norm_gain.reshape(1, INNER))
-        return call(kernel, name, outs, (*halo, table, drow, kt, after, u2b), params, sems, aliases={8: 0})
-
-    u3a, saved3a, spread3a, keep0 = make_rest("states_a", ((3, 0),), zsend0)
-    u2b, saved2b, spread2b, zsend1, u3b, saved3b, spread3b, keep1, gate, gain = make_rest(
-        "states_b", ((2, 1), (3, 1)), keep0
-    )
+        outs = [U, SAVED, SPREAD, CHIP]
+        operands = (*halo, table, drow, kt, after)
+        if todo == ((2, 1),):
+            return call(kernel, name, outs, (*operands, u2b), aliases={8: 0})
+        if todo == ((3, 1),):
+            outs += [vmem(BF16, TOK, HALF), vmem(F32, 1, INNER)]
+            params = (gate_input, norm_gain.reshape(1, INNER))
+            return call(kernel, name, outs, operands, params, [pltpu.SemaphoreType.DMA((2,))])
+        return call(kernel, name, outs, operands)
+
+    u3a, saved3a, spread3a, keep0 = make_rest("states_30", ((3, 0),), zsend0)
+    u2b, saved2b, spread2b, zsend1 = make_rest("states_21", ((2, 1),), keep0)
     got1 = send(zsend1, zswap)
+    u3b, saved3b, spread3b, keep1, gate, gain = make_rest("states_31", ((3, 1),), zsend1)
     gates = (gate, send(gate_to_core, core))
     tables = (kq, table, mcol, mrow, drow)
     yout = [vmem(BF16, YMSG, CW)] * 3

time: 58.5 us -> 58.3 us (level)
  waiting for transfers between devices: 4.08 us -> 2.76 us
  starting transfers between devices: 27.4 us -> 28.4 us
    ppermute x20, waiting for transfers between devices: 4.08 us -> 2.76 us  [send(): return lax.ppermute(v, 'seq', perm)]
    ppermute x20, starting transfers between devices: 27.4 us -> 28.4 us  [send(): return lax.ppermute(v, 'seq', perm)]
    pallas_call x21 -> x22, Pallas kernels: 26.5 us -> 26.5 us  [call(): pl.pallas_call(kernel, name=name, in_specs=[VMEM] * len(operands) + [HBM]...]
  transfers between devices with their start and end apart: 20 -> 20, of which waited for: 6 -> 5; matrix products, arithmetic and copies ran while one was open for 0% -> 0% of each run, Pallas kernels for 37% -> 37%
where the time goes in v6:
time: 58.3 us; the launch traced here: 58.1 us
  starting transfers between devices  28.4 us (49%)
  Pallas kernels  26.5 us (45%)
  waiting for transfers between devices  2.76 us (5%)
    ppermute x20, starting transfers between devices, send(): return lax.ppermute(v, 'seq', perm)  28.4 us
    pallas_call x22, Pallas kernels, call(): pl.pallas_call(kernel, name=name, in_specs=[VMEM] * len(operands) + [HBM]...  26.5 us
    ppermute x20, waiting for transfers between devices, send(): return lax.ppermute(v, 'seq', perm)  2.76 us
  transfers between devices with their start and end apart: 20, of which 5 were waited for; matrix products, arithmetic and copies ran while one was open for 0% of the time, Pallas kernels for 37%

profile of v6, /device:TPU:1, one launch (start us, length us, event | category | flops | bytes accessed | tf_op | source)
XLA Modules:
  0.0 58.1 jit_solution(9957869709041213896)
XLA Ops:
  0.0 1.4 %edges.1 = (bf16[256,2560]{1,0:T(8,128)(2,1)S(1)}, bf16[16,4352]{1,0:T(8,128)(2,1)S(1)}) custom-call(bf16[256,4352]{1,0:T(8,128)(2,1)} %x_hbm.3, f32[64,256]{1,0:T(8,128)} %step_hbm.3), custom_call_target="tpu_custom_call" | custom-call | flops 100000000 | bytes 300000 | tf_op jit(solution)/shard_map/edges/pallas_call | solution.py:52
  1.4 1.5 %collective-permute-start = (bf16[256,2560]{1,0:T(8,128)(2,1)S(1)}, bf16[256,2560]{1,0:T(8,128)(2,1)S(1)}, u32[]{:S(2)}, u32[]{:S(2)}) collective-permute-start(bf16[256,2560]{1,0:T(8,128)(2,1)S(1)} %get-tuple-element.63), channel_id=1, source_target_pairs={{0,1},{1,0},{2,3},{3,2},{4,5},{5,4},{6,7},{7,6},{8,9},{9,8},{10,11... | collective-permute-start | bytes 3932168 | tf_op jit(solution)/shard_map/ppermute | solution.py:595
  2.9 5.5 %collective-permute-start.1 = (bf16[16,4352]{1,0:T(8,128)(2,1)S(1)}, bf16[16,4352]{1,0:T(8,128)(2,1)S(1)}, u32[]{:S(2)}, u32[]{:S(2)}) collective-permute-start(bf16[16,4352]{1,0:T(8,128)(2,1)S(1)} %get-tuple-element.66), channel_id=1, source_target_pairs={{1,2},{3,4},{5,6},{7,8},{9,10},{11,12},{13,14},{2,1},{4,3},{6,5},{... | collective-permute-start | bytes 417800 | tf_op jit(solution)/shard_map/ppermute | solution.py:595
  8.4 0.0 collective-permute-done.other_ref
  8.4 3.5 %front.1 = (bf16[2,256,2304]{2,1,0:T(8,128)(2,1)S(1)}, bf16[6,256,128]{2,1,0:T(8,128)(2,1)S(1)}, f32[256,128]{1,0:T(8,128)S(1)}, f32[64,256]{1,0:T(8,128)S(1)}, ...) custom-call(bf16[256,2560]{1,0:T(8,128)(2,1)S(1)} %collective-permut, ...), custom_call_target="tpu_custom_call" | custom-call | flops 100000000 | bytes 300000 | tf_op jit(solution)/shard_map/front/pallas_call | solution.py:52
  11.9 0.1 collective-permute-start.2
  12.0 1.1 %conv_21.1.after_ref.outs_0_ = bf16[2,2,256,512]{3,2,1,0:T(8,128)(2,1)S(1)} custom-call(bf16[2,256,2304]{2,1,0:T(8,128)(2,1)S(1)} %get-tuple-element.64.x_ref, f32[8,2304]{1,0:T(8,128)S(1)} %get-tuple-element.65.taps_ref), custom_call_target="tpu_custom_call" | custom-call | flops 100000000 | bytes 300000 | tf_op jit(solution)/shard_map/conv_21/pallas_call | solution.py:52
  13.1 0.1 collective-permute-done.2.core_halo_ref
  13.2 1.3 %states_first.1 = (bf16[2,2,256,256]{3,2,1,0:T(8,128)(2,1)S(1)}, bf16[2,2,256,512]{3,2,1,0:T(8,128)(2,1)S(1)}, bf16[2,2,128,256]{3,2,1,0:T(8,128)(2,1)S(1)}, bf1...) custom-call(bf16[2,2,256,256]{3,2,1,0:T(8,128)(2,1)S(1)} %get-tuple-, ...), custom_call_target="tpu_custom_call", output_to_operand_aliasing={{0}: (0, {}), {1}: (1, {})} | custom-call | flops 100000000 | bytes 300000 | tf_op jit(solution)/shard_map/states_first/pallas_call | solution.py:52
  14.5 0.5 collective-permute-start.4
  15.0 3.4 %collective-permute-start.3 = (bf16[272,512]{1,0:T(8,128)(2,1)S(1)}, bf16[272,512]{1,0:T(8,128)(2,1)S(1)}, u32[]{:S(2)}, u32[]{:S(2)}) collective-permute-start(bf16[272,512]{1,0:T(8,128)(2,1)S(1)} %get-tuple-element.74.after_ref), channel_id=1, source_target_pairs={{0,2},{1,3},{2,0},{3,1},{4,6},{5,7},{6,4},{7,5},{8,10},{9,11},{10,... | collective-permute-start | bytes 835592 | tf_op jit(solution)/shard_map/ppermute | solution.py:595
  18.4 2.1 %states_30.1 = (bf16[2,2,256,512]{3,2,1,0:T(8,128)(2,1)S(1)}, bf16[6,128,512]{2,1,0:T(8,128)(2,1)S(1)}, bf16[2,128,512]{2,1,0:T(8,128)(2,1)S(1)}, bf16[272,512]{1,0:T(8,128)(2,1)S(1)}) custom-call(bf16[2,256,2304]{2,1,0:T(8,128)(2,1)S(1)} %get-tuple-element.64.x_ref, f32[8,2304]{1,0:T(8,128)S(1)} %get-tuple-element.65.taps_ref, ...), custom_call_target="tpu_custom_call" | custom-call | flops 100000000 | bytes 300000 | tf_op jit(solution)/shard_map/states_30/pallas_call | solution.py:52
  20.6 1.1 %states_21.1 = (bf16[2,2,256,512]{3,2,1,0:T(8,128)(2,1)S(1)}, bf16[6,128,512]{2,1,0:T(8,128)(2,1)S(1)}, bf16[2,128,512]{2,1,0:T(8,128)(2,1)S(1)}, bf16[272,512]{1,0:T(8,128)(2,1)S(1)}) custom-call(bf16[2,256,2304]{2,1,0:T(8,128)(2,1)S(1)} %get-tuple-element.64.x_ref, f32[8,2304]{1,0:T(8,128)S(1)} %get-tuple-element.65.taps_ref, ...), custom_call_target="tpu_custom_call", output_to_operand_aliasing={{0}: (8, {})} | custom-call | flops 100000000 | bytes 300000 | tf_op jit(solution)/shard_map/states_21/pallas_call | solution.py:52
  21.7 0.1 collective-permute-start.8
  21.8 2.2 %states_31.1 = (bf16[2,2,256,512]{3,2,1,0:T(8,128)(2,1)S(1)}, bf16[6,128,512]{2,1,0:T(8,128)(2,1)S(1)}, bf16[2,128,512]{2,1,0:T(8,128)(2,1)S(1)}, bf16[272,512]{...) custom-call(bf16[2,256,2304]{2,1,0:T(8,128)(2,1)S(1)} %get-tuple-element.64.x_ref, ...), custom_call_target="tpu_custom_call" | custom-call | flops 100000000 | bytes 300000 | tf_op jit(solution)/shard_map/states_31/pallas_call | solution.py:52
  24.0 1.8 %within_20.1 = (bf16[2,256,512]{2,1,0:T(8,128)(2,1)S(1)}, f32[2,2,2,128,128]{4,3,2,1,0:T(8,128)S(1)}) custom-call(bf16[2,2,256,512]{3,2,1,0:T(8,128)(2,1)S(1)} %get-tuple-element.76.u_ref, bf16[2,128,512]{2,1,0:T(8,128)(2,1)S(1)} %get-tuple-element.77.spread_ref, bf16[2,2,256,256]{3,2,1,0:T(8,128)(2,1)S(1)} %get-tuple-element.78.kq_ref.refs_0_, ...), custom_call_target="tpu_custom_call" | custom-call | flops 100000000 | bytes 300000 | tf_op jit(solution)/shard_map/within_20/pallas_call | solution.py:52
  25.8 0.1 group_a.1
  25.9 1.5 %collective-permute-start.5 = (bf16[144,512]{1,0:T(8,128)(2,1)S(1)}, bf16[144,512]{1,0:T(8,128)(2,1)S(1)}, u32[]{:S(2)}, u32[]{:S(2)}) collective-permute-start(bf16[144,512]{1,0:T(8,128)(2,1)S(1)} %get-tuple-element.85.after_ref), channel_id=1, source_target_pairs={{0,4},{1,5},{2,6},{3,7},{4,8},{5,9},{6,10},{7,11},{8,12},{9,13},{1... | collective-permute-start | bytes 442376 | tf_op jit(solution)/shard_map/ppermute | solution.py:595
  27.5 2.6 %collective-permute-start.6 = (bf16[144,512]{1,0:T(8,128)(2,1)S(1)}, bf16[144,512]{1,0:T(8,128)(2,1)S(1)}, u32[]{:S(2)}, u32[]{:S(2)}) collective-permute-start(bf16[144,512]{1,0:T(8,128)(2,1)S(1)} %get-tuple-element.86), channel_id=1, source_target_pairs={{0,8},{1,9},{2,10},{3,11},{4,12},{5,13},{6,14},{7,15},{8,0},{9,1},... | collective-permute-start | bytes 442376 | tf_op jit(solution)/shard_map/ppermute | solution.py:595
  30.1 1.1 %collective-permute-start.7 = (bf16[144,512]{1,0:T(8,128)(2,1)S(1)}, bf16[144,512]{1,0:T(8,128)(2,1)S(1)}, u32[]{:S(2)}, u32[]{:S(2)}) collective-permute-start(bf16[144,512]{1,0:T(8,128)(2,1)S(1)} %get-tuple-element.87), channel_id=1, source_target_pairs={{0,12},{1,13},{2,14},{3,15},{4,0},{5,1},{6,2},{7,3},{8,4},{9,5},{1... | collective-permute-start | bytes 442376 | tf_op jit(solution)/shard_map/ppermute | solution.py:595
  31.2 1.7 %within_21.1.refs_0_.within_ref = bf16[2,256,512]{2,1,0:T(8,128)(2,1)S(1)} custom-call(bf16[2,2,256,512]{3,2,1,0:T(8,128)(2,1)S(1)} %get-tuple-element.88.u_ref, bf16[2,128,512]{2,1,0:T(8,128)(2,1)S(1)} %get-tuple-element.89.spread_ref, bf16[2,2,256,256]{3,2,1,0:T(8,128)(2,1)S(1)} %get-tuple-element.78.kq_ref.refs_0_, ...), custom_call_target="tpu_custom_call" | custom-call | flops 100000000 | bytes 300000 | tf_op jit(solution)/shard_map/within_21/pallas_call | solution.py:52
  32.8 0.0 collective-permute-done.8.got_ref
  32.8 0.1 group_b.1
  33.0 0.5 collective-permute-start.9
  33.5 1.9 %collective-permute-start.10 = (bf16[144,512]{1,0:T(8,128)(2,1)S(1)}, bf16[144,512]{1,0:T(8,128)(2,1)S(1)}, u32[]{:S(2)}, u32[]{:S(2)}) collective-permute-start(bf16[144,512]{1,0:T(8,128)(2,1)S(1)} %get-tuple-element.98), channel_id=1, source_target_pairs={{0,8},{1,9},{2,10},{3,11},{4,12},{5,13},{6,14},{7,15},{8,0},{9,1},... | collective-permute-start | bytes 442376 | tf_op jit(solution)/shard_map/ppermute | solution.py:595
  35.4 0.9 %collective-permute-start.11 = (bf16[144,512]{1,0:T(8,128)(2,1)S(1)}, bf16[144,512]{1,0:T(8,128)(2,1)S(1)}, u32[]{:S(2)}, u32[]{:S(2)}) collective-permute-start(bf16[144,512]{1,0:T(8,128)(2,1)S(1)} %get-tuple-element.99), channel_id=1, source_target_pairs={{0,12},{1,13},{2,14},{3,15},{4,0},{5,1},{6,2},{7,3},{8,4},{9,5},{1... | collective-permute-start | bytes 442376 | tf_op jit(solution)/shard_map/ppermute | solution.py:595
  36.3 0.1 collective-permute-done.6.r2_ref
  36.3 0.3 entries_a.1
  36.7 3.1 %collective-permute-start.12 = (bf16[2,128,512]{2,1,0:T(8,128)(2,1)S(1)}, bf16[2,128,512]{2,1,0:T(8,128)(2,1)S(1)}, u32[]{:S(2)}, u32[]{:S(2)}) collective-permute-start(bf16[2,128,512]{2,1,0:T(8,128)(2,1)S(1)} %get-tuple-element.106), channel_id=1, source_target_pairs={{0,2},{1,3},{2,0},{3,1},{4,6},{5,7},{6,4},{7,5},{8,10},{9,11},{10,... | collective-permute-start | bytes 786440 | tf_op jit(solution)/shard_map/ppermute | solution.py:595
  39.8 1.7 %within_30.1.within_ref.refs_0_ = bf16[2,256,512]{2,1,0:T(8,128)(2,1)S(1)} custom-call(bf16[2,2,256,512]{3,2,1,0:T(8,128)(2,1)S(1)} %get-tuple-element.95.u_ref, bf16[2,128,512]{2,1,0:T(8,128)(2,1)S(1)} %get-tuple-element.94.spread_ref, bf16[2,2,256,256]{3,2,1,0:T(8,128)(2,1)S(1)} %get-tuple-element.78.kq_ref.refs_0_, ...), custom_call_target="tpu_custom_call" | custom-call | flops 100000000 | bytes 300000 | tf_op jit(solution)/shard_map/within_30/pallas_call | solution.py:52
  41.5 1.5 %collective-permute-done.10.r2_ref = bf16[144,512]{1,0:T(8,128)(2,1)S(1)} collective-permute-done((bf16[144,512]{1,0:T(8,128)(2,1)S(1)}, bf16[144,512]{1,0:T(8,128)(2,1)S(1)}, u32[]{:S(2)}, u32[]{:S(2)}) %collective-permute-start.10) | collective-permute-done | bytes 147488 | tf_op jit(solution)/shard_map/ppermute | solution.py:595
  43.0 0.3 entries_b.1
  43.4 1.9 %collective-permute-start.13 = (bf16[2,128,512]{2,1,0:T(8,128)(2,1)S(1)}, bf16[2,128,512]{2,1,0:T(8,128)(2,1)S(1)}, u32[]{:S(2)}, u32[]{:S(2)}) collective-permute-start(bf16[2,128,512]{2,1,0:T(8,128)(2,1)S(1)} %get-tuple-element.110), channel_id=1, source_target_pairs={{0,2},{1,3},{2,0},{3,1},{4,6},{5,7},{6,4},{7,5},{8,10},{9,11},{10,... | collective-permute-start | bytes 786440 | tf_op jit(solution)/shard_map/ppermute | solution.py:595
  45.2 1.1 %finish_30.1 = (f32[256,512]{1,0:T(8,128)S(1)}, bf16[128,512]{1,0:T(8,128)(2,1)S(1)}, bf16[128,512]{1,0:T(8,128)(2,1)S(1)}, f32[2,256,128]{2,1,0:T(8,128)S(1)}) custom-call(bf16[2,128,512]{2,1,0:T(8,128)(2,1)S(1)} %get-tuple-element.92.after_ref.entry_ref, bf16[6,128,512]{2,1,0:T(8,128)(2,1)S(1)} %get-tuple-element.93.saved_ref, ...), custom_call_target="tpu_custom_call" | custom-call | flops 100000000 | bytes 300000 | tf_op jit(solution)/shard_map/finish_30/pallas_call | solution.py:52
  46.3 2.6 %collective-permute-start.14 = (bf16[128,512]{1,0:T(8,128)(2,1)S(1)}, bf16[128,512]{1,0:T(8,128)(2,1)S(1)}, u32[]{:S(2)}, u32[]{:S(2)}) collective-permute-start(bf16[128,512]{1,0:T(8,128)(2,1)S(1)} %get-tuple-element.113), channel_id=1, source_target_pairs={{0,1},{1,0},{2,3},{3,2},{4,5},{5,4},{6,7},{7,6},{8,9},{9,8},{10,11... | collective-permute-start | bytes 393224 | tf_op jit(solution)/shard_map/ppermute | solution.py:595
  48.9 0.1 collective-permute-start.15
  49.0 1.6 %within_31.1.within_ref = bf16[2,256,512]{2,1,0:T(8,128)(2,1)S(1)} custom-call(bf16[2,2,256,512]{3,2,1,0:T(8,128)(2,1)S(1)} %get-tuple-element.103.u_ref, bf16[2,128,512]{2,1,0:T(8,128)(2,1)S(1)} %get-tuple-element.102.spread_ref, bf16[2,2,256,256]{3,2,1,0:T(8,128)(2,1)S(1)} %get-tuple-element.78.kq_ref.refs_0_, ...), custom_call_target="tpu_custom_call" | custom-call | flops 100000000 | bytes 300000 | tf_op jit(solution)/shard_map/within_31/pallas_call | solution.py:52
  50.7 1.1 %finish_31.1 = (f32[256,512]{1,0:T(8,128)S(1)}, bf16[128,512]{1,0:T(8,128)(2,1)S(1)}, bf16[128,512]{1,0:T(8,128)(2,1)S(1)}, f32[2,256,128]{2,1,0:T(8,128)S(1)}) custom-call(bf16[2,128,512]{2,1,0:T(8,128)(2,1)S(1)} %get-tuple-element.100.after_ref.entry_ref, bf16[6,128,512]{2,1,0:T(8,128)(2,1)S(1)} %get-tuple-element.101.saved_ref, ...), custom_call_target="tpu_custom_call" | custom-call | flops 100000000 | bytes 300000 | tf_op jit(solution)/shard_map/finish_31/pallas_call | solution.py:52
  51.8 0.5 collective-permute-start.16
  52.3 0.1 collective-permute-start.17
  52.4 1.1 %finish_20.1 = (f32[256,512]{1,0:T(8,128)S(1)}, bf16[256,512]{1,0:T(8,128)(2,1)S(1)}, f32[2,256,128]{2,1,0:T(8,128)S(1)}) custom-call(bf16[2,128,512]{2,1,0:T(8,128)(2,1)S(1)} %collective-permute-done.12.entry_ref, bf16[6,128,512]{2,1,0:T(8,128)(2,1)S(1)} %get-tuple-element.107.saved_ref, bf16[2,128,512]{2,1,0:T(8,128)(2,1)S(1)} %get-tuple-element.77.spread_ref, ...), custom_call_target="tpu_custom_call" | custom-call | flops 100000000 | bytes 300000 | tf_op jit(solution)/shard_map/finish_20/pallas_call | solution.py:52
  53.6 0.1 collective-permute-done.17.refs_7_
  53.7 0.7 %finish_other.1.refs_4_ = bf16[256,640]{1,0:T(8,128)(2,1)S(1)} custom-call(bf16[2,128,512]{2,1,0:T(8,128)(2,1)S(1)} %collective-permute-done.13.entry_ref, bf16[6,128,512]{2,1,0:T(8,128)(2,1)S(1)} %get-tuple-element.111.saved_ref, bf16[2,128,512]{2,1,0:T(8,128)(2,1)S(1)} %get-tuple-element.89.spread_ref, ...), custom_call_target="tpu_custom_call" | custom-call | flops 100000000 | bytes 300000 | tf_op jit(solution)/shard_map/finish_other/pallas_call | solution.py:52
  54.3 0.4 collective-permute-start.19
  54.8 0.2 collective-permute-start.18
  54.9 0.6 %finish_own.1 = (f32[256,512]{1,0:T(8,128)S(1)}, f32[256,128]{1,0:T(8,128)S(1)}) custom-call(bf16[2,128,512]{2,1,0:T(8,128)(2,1)S(1)} %collective-permute-done.13.entry_ref, bf16[6,128,512]{2,1,0:T(8,128)(2,1)S(1)} %get-tuple-element.111.saved_ref, bf16[2,128,512]{2,1,0:T(8,128)(2,1)S(1)} %get-tuple-element.89.spread_ref, ...), custom_call_target="tpu_custom_call" | custom-call | flops 100000000 | bytes 300000 | tf_op jit(solution)/shard_map/finish_own/pallas_call | solution.py:52
  55.5 0.9 %collective-permute-done.18.refs_8_ = bf16[256,512]{1,0:T(8,128)(2,1)S(1)} collective-permute-done((bf16[256,512]{1,0:T(8,128)(2,1)S(1)}, bf16[256,512]{1,0:T(8,128)(2,1)S(1)}, u32[]{:S(2)}, u32[]{:S(2)}) %collective-permute-start.18) | collective-permute-done | bytes 262176 | tf_op jit(solution)/shard_map/ppermute | solution.py:595
  56.4 1.5 %norm.1 = bf16[256,4096]{1,0:T(8,128)(2,1)} custom-call(f32[256,512]{1,0:T(8,128)S(1)} %get-tuple-element.97.refs_0_, f32[256,512]{1,0:T(8,128)S(1)} %get-tuple-element.105.refs_1_, f32[256,512]{1,0:T(8,128)S(1)} %get-tuple-element.109.refs_2_, f32[256,512]{1,0:T(8,128)S(1)} %get-tuple-element.117.refs_3_, ...), custom_call_target="tpu_custom_call" | custom-call | flops 100000000 | bytes 300000 | tf_op jit(solution)/shard_map/norm/pallas_call | solution.py:52
  (14 shorter events, 0.1 us)
Async XLA Ops:
  1.4 7.0 %collective-permute-start = (bf16[256,2560]{1,0:T(8,128)(2,1)S(1)}, bf16[256,2560]{1,0:T(8,128)(2,1)S(1)}, u32[]{:S(2)}, u32[]{:S(2)}) collective-permute-start(bf16[256,2560]{1,0:T(8,128)(2,1)S(1)} %get-tuple-element.63), channel_id=1, source_target_pairs={{0,1},{1,0},{2,3},{3,2},{4,5},{5,4},{6,7},{7,6},{8,9},{9,8},{10,11... | collective-permute-start | bytes 3932168 | tf_op jit(solution)/shard_map/ppermute | solution.py:595
  2.9 9.0 %collective-permute-start.1 = (bf16[16,4352]{1,0:T(8,128)(2,1)S(1)}, bf16[16,4352]{1,0:T(8,128)(2,1)S(1)}, u32[]{:S(2)}, u32[]{:S(2)}) collective-permute-start(bf16[16,4352]{1,0:T(8,128)(2,1)S(1)} %get-tuple-element.66), channel_id=1, source_target_pairs={{1,2},{3,4},{5,6},{7,8},{9,10},{11,12},{13,14},{2,1},{4,3},{6,5},{... | collective-permute-start | bytes 417800 | tf_op jit(solution)/shard_map/ppermute | solution.py:595
  11.9 1.3 %collective-permute-start.2 = (bf16[16,2304]{1,0:T(8,128)(2,1)S(1)}, bf16[16,2304]{1,0:T(8,128)(2,1)S(1)}, u32[]{:S(2)}, u32[]{:S(2)}) collective-permute-start(bf16[16,2304]{1,0:T(8,128)(2,1)S(1)} %get-tuple-element.69), channel_id=1, source_target_pairs={{0,1},{1,0},{2,3},{3,2},{4,5},{5,4},{6,7},{7,6},{8,9},{9,8},{10,11... | collective-permute-start | bytes 221192 | tf_op jit(solution)/shard_map/ppermute | solution.py:595
  14.5 11.3 %collective-permute-start.4 = (bf16[256,2048]{1,0:T(8,128)(2,1)S(1)}, bf16[256,2048]{1,0:T(8,128)(2,1)S(1)}, u32[]{:S(2)}, u32[]{:S(2)}) collective-permute-start(bf16[256,2048]{1,0:T(8,128)(2,1)S(1)} %get-tuple-element.84), channel_id=1, source_target_pairs={{0,1},{1,0},{2,3},{3,2},{4,5},{5,4},{6,7},{7,6},{8,9},{9,8},{10,11... | collective-permute-start | bytes 3145736 | tf_op jit(solution)/shard_map/ppermute | solution.py:595
  15.0 10.8 %collective-permute-start.3 = (bf16[272,512]{1,0:T(8,128)(2,1)S(1)}, bf16[272,512]{1,0:T(8,128)(2,1)S(1)}, u32[]{:S(2)}, u32[]{:S(2)}) collective-permute-start(bf16[272,512]{1,0:T(8,128)(2,1)S(1)} %get-tuple-element.74.after_ref), channel_id=1, source_target_pairs={{0,2},{1,3},{2,0},{3,1},{4,6},{5,7},{6,4},{7,5},{8,10},{9,11},{10,... | collective-permute-start | bytes 835592 | tf_op jit(solution)/shard_map/ppermute | solution.py:595
  21.7 11.1 %collective-permute-start.8 = (bf16[272,512]{1,0:T(8,128)(2,1)S(1)}, bf16[272,512]{1,0:T(8,128)(2,1)S(1)}, u32[]{:S(2)}, u32[]{:S(2)}) collective-permute-start(bf16[272,512]{1,0:T(8,128)(2,1)S(1)} %get-tuple-element.81.after_ref), channel_id=1, source_target_pairs={{0,2},{1,3},{2,0},{3,1},{4,6},{5,7},{6,4},{7,5},{8,10},{9,11},{10,... | collective-permute-start | bytes 835592 | tf_op jit(solution)/shard_map/ppermute | solution.py:595
  25.9 9.4 %collective-permute-start.5 = (bf16[144,512]{1,0:T(8,128)(2,1)S(1)}, bf16[144,512]{1,0:T(8,128)(2,1)S(1)}, u32[]{:S(2)}, u32[]{:S(2)}) collective-permute-start(bf16[144,512]{1,0:T(8,128)(2,1)S(1)} %get-tuple-element.85.after_ref), channel_id=1, source_target_pairs={{0,4},{1,5},{2,6},{3,7},{4,8},{5,9},{6,10},{7,11},{8,12},{9,13},{1... | collective-permute-start | bytes 442376 | tf_op jit(solution)/shard_map/ppermute | solution.py:595
  27.5 8.9 %collective-permute-start.6 = (bf16[144,512]{1,0:T(8,128)(2,1)S(1)}, bf16[144,512]{1,0:T(8,128)(2,1)S(1)}, u32[]{:S(2)}, u32[]{:S(2)}) collective-permute-start(bf16[144,512]{1,0:T(8,128)(2,1)S(1)} %get-tuple-element.86), channel_id=1, source_target_pairs={{0,8},{1,9},{2,10},{3,11},{4,12},{5,13},{6,14},{7,15},{8,0},{9,1},... | collective-permute-start | bytes 442376 | tf_op jit(solution)/shard_map/ppermute | solution.py:595
  30.1 6.2 %collective-permute-start.7 = (bf16[144,512]{1,0:T(8,128)(2,1)S(1)}, bf16[144,512]{1,0:T(8,128)(2,1)S(1)}, u32[]{:S(2)}, u32[]{:S(2)}) collective-permute-start(bf16[144,512]{1,0:T(8,128)(2,1)S(1)} %get-tuple-element.87), channel_id=1, source_target_pairs={{0,12},{1,13},{2,14},{3,15},{4,0},{5,1},{6,2},{7,3},{8,4},{9,5},{1... | collective-permute-start | bytes 442376 | tf_op jit(solution)/shard_map/ppermute | solution.py:595
  33.0 8.5 %collective-permute-start.9 = (bf16[144,512]{1,0:T(8,128)(2,1)S(1)}, bf16[144,512]{1,0:T(8,128)(2,1)S(1)}, u32[]{:S(2)}, u32[]{:S(2)}) collective-permute-start(bf16[144,512]{1,0:T(8,128)(2,1)S(1)} %get-tuple-element.91.refs_0_), channel_id=1, source_target_pairs={{0,4},{1,5},{2,6},{3,7},{4,8},{5,9},{6,10},{7,11},{8,12},{9,13},{1... | collective-permute-start | bytes 442376 | tf_op jit(solution)/shard_map/ppermute | solution.py:595
  33.5 9.6 %collective-permute-start.10 = (bf16[144,512]{1,0:T(8,128)(2,1)S(1)}, bf16[144,512]{1,0:T(8,128)(2,1)S(1)}, u32[]{:S(2)}, u32[]{:S(2)}) collective-permute-start(bf16[144,512]{1,0:T(8,128)(2,1)S(1)} %get-tuple-element.98), channel_id=1, source_target_pairs={{0,8},{1,9},{2,10},{3,11},{4,12},{5,13},{6,14},{7,15},{8,0},{9,1},... | collective-permute-start | bytes 442376 | tf_op jit(solution)/shard_map/ppermute | solution.py:595
  35.4 7.7 %collective-permute-start.11 = (bf16[144,512]{1,0:T(8,128)(2,1)S(1)}, bf16[144,512]{1,0:T(8,128)(2,1)S(1)}, u32[]{:S(2)}, u32[]{:S(2)}) collective-permute-start(bf16[144,512]{1,0:T(8,128)(2,1)S(1)} %get-tuple-element.99), channel_id=1, source_target_pairs={{0,12},{1,13},{2,14},{3,15},{4,0},{5,1},{6,2},{7,3},{8,4},{9,5},{1... | collective-permute-start | bytes 442376 | tf_op jit(solution)/shard_map/ppermute | solution.py:595
  36.7 15.6 %collective-permute-start.12 = (bf16[2,128,512]{2,1,0:T(8,128)(2,1)S(1)}, bf16[2,128,512]{2,1,0:T(8,128)(2,1)S(1)}, u32[]{:S(2)}, u32[]{:S(2)}) collective-permute-start(bf16[2,128,512]{2,1,0:T(8,128)(2,1)S(1)} %get-tuple-element.106), channel_id=1, source_target_pairs={{0,2},{1,3},{2,0},{3,1},{4,6},{5,7},{6,4},{7,5},{8,10},{9,11},{10,... | collective-permute-start | bytes 786440 | tf_op jit(solution)/shard_map/ppermute | solution.py:595
  43.4 10.3 %collective-permute-start.13 = (bf16[2,128,512]{2,1,0:T(8,128)(2,1)S(1)}, bf16[2,128,512]{2,1,0:T(8,128)(2,1)S(1)}, u32[]{:S(2)}, u32[]{:S(2)}) collective-permute-start(bf16[2,128,512]{2,1,0:T(8,128)(2,1)S(1)} %get-tuple-element.110), channel_id=1, source_target_pairs={{0,2},{1,3},{2,0},{3,1},{4,6},{5,7},{6,4},{7,5},{8,10},{9,11},{10,... | collective-permute-start | bytes 786440 | tf_op jit(solution)/shard_map/ppermute | solution.py:595
  46.3 7.2 %collective-permute-start.14 = (bf16[128,512]{1,0:T(8,128)(2,1)S(1)}, bf16[128,512]{1,0:T(8,128)(2,1)S(1)}, u32[]{:S(2)}, u32[]{:S(2)}) collective-permute-start(bf16[128,512]{1,0:T(8,128)(2,1)S(1)} %get-tuple-element.113), channel_id=1, source_target_pairs={{0,1},{1,0},{2,3},{3,2},{4,5},{5,4},{6,7},{7,6},{8,9},{9,8},{10,11... | collective-permute-start | bytes 393224 | tf_op jit(solution)/shard_map/ppermute | solution.py:595
  48.9 4.6 %collective-permute-start.15 = (bf16[128,512]{1,0:T(8,128)(2,1)S(1)}, bf16[128,512]{1,0:T(8,128)(2,1)S(1)}, u32[]{:S(2)}, u32[]{:S(2)}) collective-permute-start(bf16[128,512]{1,0:T(8,128)(2,1)S(1)} %get-tuple-element.114), channel_id=1, source_target_pairs={{0,1},{1,0},{2,3},{3,2},{4,5},{5,4},{6,7},{7,6},{8,9},{9,8},{10,11... | collective-permute-start | bytes 393224 | tf_op jit(solution)/shard_map/ppermute | solution.py:595
  51.8 1.8 %collective-permute-start.16 = (bf16[128,512]{1,0:T(8,128)(2,1)S(1)}, bf16[128,512]{1,0:T(8,128)(2,1)S(1)}, u32[]{:S(2)}, u32[]{:S(2)}) collective-permute-start(bf16[128,512]{1,0:T(8,128)(2,1)S(1)} %get-tuple-element.115), channel_id=1, source_target_pairs={{0,1},{1,0},{2,3},{3,2},{4,5},{5,4},{6,7},{7,6},{8,9},{9,8},{10,11... | collective-permute-start | bytes 393224 | tf_op jit(solution)/shard_map/ppermute | solution.py:595
  52.3 1.3 %collective-permute-start.17 = (bf16[128,512]{1,0:T(8,128)(2,1)S(1)}, bf16[128,512]{1,0:T(8,128)(2,1)S(1)}, u32[]{:S(2)}, u32[]{:S(2)}) collective-permute-start(bf16[128,512]{1,0:T(8,128)(2,1)S(1)} %get-tuple-element.116), channel_id=1, source_target_pairs={{0,1},{1,0},{2,3},{3,2},{4,5},{5,4},{6,7},{7,6},{8,9},{9,8},{10,11... | collective-permute-start | bytes 393224 | tf_op jit(solution)/shard_map/ppermute | solution.py:595
  54.3 2.1 %collective-permute-start.19 = (bf16[256,640]{1,0:T(8,128)(2,1)S(1)}, bf16[256,640]{1,0:T(8,128)(2,1)S(1)}, u32[]{:S(2)}, u32[]{:S(2)}) collective-permute-start(bf16[256,640]{1,0:T(8,128)(2,1)S(1)} %finish_other.1.refs_4_), channel_id=1, source_target_pairs={{0,1},{1,0},{2,3},{3,2},{4,5},{5,4},{6,7},{7,6},{8,9},{9,8},{10,11... | collective-permute-start | bytes 983048 | tf_op jit(solution)/shard_map/ppermute | solution.py:595
  54.8 1.7 %collective-permute-start.18 = (bf16[256,512]{1,0:T(8,128)(2,1)S(1)}, bf16[256,512]{1,0:T(8,128)(2,1)S(1)}, u32[]{:S(2)}, u32[]{:S(2)}) collective-permute-start(bf16[256,512]{1,0:T(8,128)(2,1)S(1)} %get-tuple-element.118), channel_id=1, source_target_pairs={{0,1},{1,0},{2,3},{3,2},{4,5},{5,4},{6,7},{7,6},{8,9},{9,8},{10,11... | collective-permute-start | bytes 786440 | tf_op jit(solution)/shard_map/ppermute | solution.py:595

commit v7 on v6

--- a/solution.py
+++ b/solution.py
@@ -566,8 +566,8 @@
 
 
 def norm_kernel(*refs):
-    own_refs, other_refs, (square_ref, gain_ref, out_hbm, out_ref, sems) = refs[:4], refs[4:10], refs[10:]
-    other_refs = (other_refs[0:2], other_refs[2:4], halves(other_refs[4:5]), halves(other_refs[5:6]))
+    own_refs, other_refs, (square_ref, gain_ref, out_hbm, out_ref, sems) = refs[:4], refs[4:8], refs[8:]
+    other_refs = [halves([ref]) for ref in other_refs]
     c, z, y = place()
     pieces = []
     for n, piece in enumerate((*NEAR, BACK)):
@@ -697,8 +697,8 @@
         (mine1, saved3b, spread3b, w3b),
         (back0, saved2a, spread2a, w2a),
     )
-    two, one = [vmem(BF16, SUB, CW)] * 2, [vmem(BF16, TOK, CW)]
-    for (k, p), part, message in zip(NEAR, parts, (two, two, one)):
+    message = [vmem(BF16, TOK, CW)]
+    for (k, p), part in zip(NEAR, parts):
         gated, *msg, square = call(
             functools.partial(finish_near_kernel, k, p),
             f"finish_{k}{p}",
@@ -711,7 +711,7 @@
         finish_other_kernel,
         "finish_other",
         [vmem(BF16, TOK, CW + 128)],
-        (back1, saved2b, spread2b, w2b, *gates[1:], *shared, square, *other[:4]),
+        (back1, saved2b, spread2b, w2b, *gates[1:], *shared, square, *other[:2]),
     )
     other += [send(m, core) for m in msg]
     gated, square = call(

time: 58.3 us -> 57.9 us (level)
    ppermute x20 -> x18, starting transfers between devices: 28.4 us -> 27.9 us  [send(): return lax.ppermute(v, 'seq', perm)]
    ppermute x20 -> x18, waiting for transfers between devices: 2.76 us -> 3.02 us  [send(): return lax.ppermute(v, 'seq', perm)]
  transfers between devices with their start and end apart: 20 -> 18, of which waited for: 5 -> 5; matrix products, arithmetic and copies ran while one was open for 0% -> 0% of each run, Pallas kernels for 37% -> 37%
where the time goes in v7:
time: 57.9 us; the launch traced here: 57.8 us
  starting transfers between devices  27.9 us (48%)
  Pallas kernels  26.5 us (46%)
  waiting for transfers between devices  3.02 us (5%)
    ppermute x18, starting transfers between devices, send(): return lax.ppermute(v, 'seq', perm)  27.9 us
    pallas_call x22, Pallas kernels, call(): pl.pallas_call(kernel, name=name, in_specs=[VMEM] * len(operands) + [HBM]...  26.5 us
    ppermute x18, waiting for transfers between devices, send(): return lax.ppermute(v, 'seq', perm)  3.02 us
  transfers between devices with their start and end apart: 18, of which 5 were waited for; matrix products, arithmetic and copies ran while one was open for 0% of the time, Pallas kernels for 37%

profile of v7, /device:TPU:1, one launch (start us, length us, event | category | flops | bytes accessed | tf_op | source)
XLA Modules:
  0.0 57.8 jit_solution(13888373090446322563)
XLA Ops:
  0.0 1.4 %edges.1 = (bf16[256,2560]{1,0:T(8,128)(2,1)S(1)}, bf16[16,4352]{1,0:T(8,128)(2,1)S(1)}) custom-call(bf16[256,4352]{1,0:T(8,128)(2,1)} %x_hbm.3, f32[64,256]{1,0:T(8,128)} %step_hbm.3), custom_call_target="tpu_custom_call" | custom-call | flops 100000000 | bytes 300000 | tf_op jit(solution)/shard_map/edges/pallas_call | solution.py:52
  1.4 1.5 %collective-permute-start = (bf16[256,2560]{1,0:T(8,128)(2,1)S(1)}, bf16[256,2560]{1,0:T(8,128)(2,1)S(1)}, u32[]{:S(2)}, u32[]{:S(2)}) collective-permute-start(bf16[256,2560]{1,0:T(8,128)(2,1)S(1)} %get-tuple-element.61), channel_id=1, source_target_pairs={{0,1},{1,0},{2,3},{3,2},{4,5},{5,4},{6,7},{7,6},{8,9},{9,8},{10,11... | collective-permute-start | bytes 3932168 | tf_op jit(solution)/shard_map/ppermute | solution.py:595
  2.9 5.5 %collective-permute-start.1 = (bf16[16,4352]{1,0:T(8,128)(2,1)S(1)}, bf16[16,4352]{1,0:T(8,128)(2,1)S(1)}, u32[]{:S(2)}, u32[]{:S(2)}) collective-permute-start(bf16[16,4352]{1,0:T(8,128)(2,1)S(1)} %get-tuple-element.64), channel_id=1, source_target_pairs={{1,2},{3,4},{5,6},{7,8},{9,10},{11,12},{13,14},{2,1},{4,3},{6,5},{... | collective-permute-start | bytes 417800 | tf_op jit(solution)/shard_map/ppermute | solution.py:595
  8.4 3.5 %front.1 = (bf16[2,256,2304]{2,1,0:T(8,128)(2,1)S(1)}, bf16[6,256,128]{2,1,0:T(8,128)(2,1)S(1)}, f32[256,128]{1,0:T(8,128)S(1)}, f32[64,256]{1,0:T(8,128)S(1)}, ...) custom-call(bf16[256,2560]{1,0:T(8,128)(2,1)S(1)} %collective-permut, ...), custom_call_target="tpu_custom_call" | custom-call | flops 100000000 | bytes 300000 | tf_op jit(solution)/shard_map/front/pallas_call | solution.py:52
  11.9 0.1 collective-permute-start.2
  12.0 1.1 %conv_21.1.after_ref.outs_0_ = bf16[2,2,256,512]{3,2,1,0:T(8,128)(2,1)S(1)} custom-call(bf16[2,256,2304]{2,1,0:T(8,128)(2,1)S(1)} %get-tuple-element.62.x_ref, f32[8,2304]{1,0:T(8,128)S(1)} %get-tuple-element.63.taps_ref), custom_call_target="tpu_custom_call" | custom-call | flops 100000000 | bytes 300000 | tf_op jit(solution)/shard_map/conv_21/pallas_call | solution.py:52
  13.1 0.1 collective-permute-done.2.core_halo_ref
  13.2 1.3 %states_first.1 = (bf16[2,2,256,256]{3,2,1,0:T(8,128)(2,1)S(1)}, bf16[2,2,256,512]{3,2,1,0:T(8,128)(2,1)S(1)}, bf16[2,2,128,256]{3,2,1,0:T(8,128)(2,1)S(1)}, bf1...) custom-call(bf16[2,2,256,256]{3,2,1,0:T(8,128)(2,1)S(1)} %get-tuple-, ...), custom_call_target="tpu_custom_call", output_to_operand_aliasing={{0}: (0, {}), {1}: (1, {})} | custom-call | flops 100000000 | bytes 300000 | tf_op jit(solution)/shard_map/states_first/pallas_call | solution.py:52
  14.5 0.5 collective-permute-start.4
  15.0 3.4 %collective-permute-start.3 = (bf16[272,512]{1,0:T(8,128)(2,1)S(1)}, bf16[272,512]{1,0:T(8,128)(2,1)S(1)}, u32[]{:S(2)}, u32[]{:S(2)}) collective-permute-start(bf16[272,512]{1,0:T(8,128)(2,1)S(1)} %get-tuple-element.72.after_ref), channel_id=1, source_target_pairs={{0,2},{1,3},{2,0},{3,1},{4,6},{5,7},{6,4},{7,5},{8,10},{9,11},{10,... | collective-permute-start | bytes 835592 | tf_op jit(solution)/shard_map/ppermute | solution.py:595
  18.4 2.1 %states_30.1 = (bf16[2,2,256,512]{3,2,1,0:T(8,128)(2,1)S(1)}, bf16[6,128,512]{2,1,0:T(8,128)(2,1)S(1)}, bf16[2,128,512]{2,1,0:T(8,128)(2,1)S(1)}, bf16[272,512]{1,0:T(8,128)(2,1)S(1)}) custom-call(bf16[2,256,2304]{2,1,0:T(8,128)(2,1)S(1)} %get-tuple-element.62.x_ref, f32[8,2304]{1,0:T(8,128)S(1)} %get-tuple-element.63.taps_ref, ...), custom_call_target="tpu_custom_call" | custom-call | flops 100000000 | bytes 300000 | tf_op jit(solution)/shard_map/states_30/pallas_call | solution.py:52
  20.6 1.1 %states_21.1 = (bf16[2,2,256,512]{3,2,1,0:T(8,128)(2,1)S(1)}, bf16[6,128,512]{2,1,0:T(8,128)(2,1)S(1)}, bf16[2,128,512]{2,1,0:T(8,128)(2,1)S(1)}, bf16[272,512]{1,0:T(8,128)(2,1)S(1)}) custom-call(bf16[2,256,2304]{2,1,0:T(8,128)(2,1)S(1)} %get-tuple-element.62.x_ref, f32[8,2304]{1,0:T(8,128)S(1)} %get-tuple-element.63.taps_ref, ...), custom_call_target="tpu_custom_call", output_to_operand_aliasing={{0}: (8, {})} | custom-call | flops 100000000 | bytes 300000 | tf_op jit(solution)/shard_map/states_21/pallas_call | solution.py:52
  21.7 0.1 collective-permute-start.8
  21.8 2.2 %states_31.1 = (bf16[2,2,256,512]{3,2,1,0:T(8,128)(2,1)S(1)}, bf16[6,128,512]{2,1,0:T(8,128)(2,1)S(1)}, bf16[2,128,512]{2,1,0:T(8,128)(2,1)S(1)}, bf16[272,512]{...) custom-call(bf16[2,256,2304]{2,1,0:T(8,128)(2,1)S(1)} %get-tuple-element.62.x_ref, ...), custom_call_target="tpu_custom_call" | custom-call | flops 100000000 | bytes 300000 | tf_op jit(solution)/shard_map/states_31/pallas_call | solution.py:52
  24.0 1.8 %within_20.1 = (bf16[2,256,512]{2,1,0:T(8,128)(2,1)S(1)}, f32[2,2,2,128,128]{4,3,2,1,0:T(8,128)S(1)}) custom-call(bf16[2,2,256,512]{3,2,1,0:T(8,128)(2,1)S(1)} %get-tuple-element.74.u_ref, bf16[2,128,512]{2,1,0:T(8,128)(2,1)S(1)} %get-tuple-element.75.spread_ref, bf16[2,2,256,256]{3,2,1,0:T(8,128)(2,1)S(1)} %get-tuple-element.76.kq_ref.refs_0_, ...), custom_call_target="tpu_custom_call" | custom-call | flops 100000000 | bytes 300000 | tf_op jit(solution)/shard_map/within_20/pallas_call | solution.py:52
  25.8 0.0 collective-permute-done.4.refs_1_.gate_other_ref.gate_ref
  25.8 0.1 group_a.1
  25.9 1.5 %collective-permute-start.5 = (bf16[144,512]{1,0:T(8,128)(2,1)S(1)}, bf16[144,512]{1,0:T(8,128)(2,1)S(1)}, u32[]{:S(2)}, u32[]{:S(2)}) collective-permute-start(bf16[144,512]{1,0:T(8,128)(2,1)S(1)} %get-tuple-element.83.after_ref), channel_id=1, source_target_pairs={{0,4},{1,5},{2,6},{3,7},{4,8},{5,9},{6,10},{7,11},{8,12},{9,13},{1... | collective-permute-start | bytes 442376 | tf_op jit(solution)/shard_map/ppermute | solution.py:595
  27.5 2.6 %collective-permute-start.6 = (bf16[144,512]{1,0:T(8,128)(2,1)S(1)}, bf16[144,512]{1,0:T(8,128)(2,1)S(1)}, u32[]{:S(2)}, u32[]{:S(2)}) collective-permute-start(bf16[144,512]{1,0:T(8,128)(2,1)S(1)} %get-tuple-element.84), channel_id=1, source_target_pairs={{0,8},{1,9},{2,10},{3,11},{4,12},{5,13},{6,14},{7,15},{8,0},{9,1},... | collective-permute-start | bytes 442376 | tf_op jit(solution)/shard_map/ppermute | solution.py:595
  30.1 1.1 %collective-permute-start.7 = (bf16[144,512]{1,0:T(8,128)(2,1)S(1)}, bf16[144,512]{1,0:T(8,128)(2,1)S(1)}, u32[]{:S(2)}, u32[]{:S(2)}) collective-permute-start(bf16[144,512]{1,0:T(8,128)(2,1)S(1)} %get-tuple-element.85), channel_id=1, source_target_pairs={{0,12},{1,13},{2,14},{3,15},{4,0},{5,1},{6,2},{7,3},{8,4},{9,5},{1... | collective-permute-start | bytes 442376 | tf_op jit(solution)/shard_map/ppermute | solution.py:595
  31.2 1.7 %within_21.1.refs_0_.within_ref = bf16[2,256,512]{2,1,0:T(8,128)(2,1)S(1)} custom-call(bf16[2,2,256,512]{3,2,1,0:T(8,128)(2,1)S(1)} %get-tuple-element.86.u_ref, bf16[2,128,512]{2,1,0:T(8,128)(2,1)S(1)} %get-tuple-element.87.spread_ref, bf16[2,2,256,256]{3,2,1,0:T(8,128)(2,1)S(1)} %get-tuple-element.76.kq_ref.refs_0_, ...), custom_call_target="tpu_custom_call" | custom-call | flops 100000000 | bytes 300000 | tf_op jit(solution)/shard_map/within_21/pallas_call | solution.py:52
  32.8 0.1 group_b.1
  33.0 0.5 collective-permute-start.9
  33.5 1.9 %collective-permute-start.10 = (bf16[144,512]{1,0:T(8,128)(2,1)S(1)}, bf16[144,512]{1,0:T(8,128)(2,1)S(1)}, u32[]{:S(2)}, u32[]{:S(2)}) collective-permute-start(bf16[144,512]{1,0:T(8,128)(2,1)S(1)} %get-tuple-element.96), channel_id=1, source_target_pairs={{0,8},{1,9},{2,10},{3,11},{4,12},{5,13},{6,14},{7,15},{8,0},{9,1},... | collective-permute-start | bytes 442376 | tf_op jit(solution)/shard_map/ppermute | solution.py:595
  35.4 0.9 %collective-permute-start.11 = (bf16[144,512]{1,0:T(8,128)(2,1)S(1)}, bf16[144,512]{1,0:T(8,128)(2,1)S(1)}, u32[]{:S(2)}, u32[]{:S(2)}) collective-permute-start(bf16[144,512]{1,0:T(8,128)(2,1)S(1)} %get-tuple-element.97), channel_id=1, source_target_pairs={{0,12},{1,13},{2,14},{3,15},{4,0},{5,1},{6,2},{7,3},{8,4},{9,5},{1... | collective-permute-start | bytes 442376 | tf_op jit(solution)/shard_map/ppermute | solution.py:595
  36.3 0.1 collective-permute-done.6.r2_ref
  36.3 0.3 entries_a.1
  36.7 3.1 %collective-permute-start.12 = (bf16[2,128,512]{2,1,0:T(8,128)(2,1)S(1)}, bf16[2,128,512]{2,1,0:T(8,128)(2,1)S(1)}, u32[]{:S(2)}, u32[]{:S(2)}) collective-permute-start(bf16[2,128,512]{2,1,0:T(8,128)(2,1)S(1)} %get-tuple-element.104), channel_id=1, source_target_pairs={{0,2},{1,3},{2,0},{3,1},{4,6},{5,7},{6,4},{7,5},{8,10},{9,11},{10,... | collective-permute-start | bytes 786440 | tf_op jit(solution)/shard_map/ppermute | solution.py:595
  39.8 1.7 %within_30.1.within_ref.refs_0_ = bf16[2,256,512]{2,1,0:T(8,128)(2,1)S(1)} custom-call(bf16[2,2,256,512]{3,2,1,0:T(8,128)(2,1)S(1)} %get-tuple-element.93.u_ref, bf16[2,128,512]{2,1,0:T(8,128)(2,1)S(1)} %get-tuple-element.92.spread_ref, bf16[2,2,256,256]{3,2,1,0:T(8,128)(2,1)S(1)} %get-tuple-element.76.kq_ref.refs_0_, ...), custom_call_target="tpu_custom_call" | custom-call | flops 100000000 | bytes 300000 | tf_op jit(solution)/shard_map/within_30/pallas_call | solution.py:52
  41.5 0.0 collective-permute-done.9.r1_ref
  41.5 1.5 %collective-permute-done.10.r2_ref = bf16[144,512]{1,0:T(8,128)(2,1)S(1)} collective-permute-done((bf16[144,512]{1,0:T(8,128)(2,1)S(1)}, bf16[144,512]{1,0:T(8,128)(2,1)S(1)}, u32[]{:S(2)}, u32[]{:S(2)}) %collective-permute-start.10) | collective-permute-done | bytes 147488 | tf_op jit(solution)/shard_map/ppermute | solution.py:595
  43.0 0.0 collective-permute-done.11.r3_ref
  43.0 0.3 entries_b.1
  43.4 1.9 %collective-permute-start.13 = (bf16[2,128,512]{2,1,0:T(8,128)(2,1)S(1)}, bf16[2,128,512]{2,1,0:T(8,128)(2,1)S(1)}, u32[]{:S(2)}, u32[]{:S(2)}) collective-permute-start(bf16[2,128,512]{2,1,0:T(8,128)(2,1)S(1)} %get-tuple-element.108), channel_id=1, source_target_pairs={{0,2},{1,3},{2,0},{3,1},{4,6},{5,7},{6,4},{7,5},{8,10},{9,11},{10,... | collective-permute-start | bytes 786440 | tf_op jit(solution)/shard_map/ppermute | solution.py:595
  45.2 1.1 %finish_30.1 = (f32[256,512]{1,0:T(8,128)S(1)}, bf16[256,512]{1,0:T(8,128)(2,1)S(1)}, f32[2,256,128]{2,1,0:T(8,128)S(1)}) custom-call(bf16[2,128,512]{2,1,0:T(8,128)(2,1)S(1)} %get-tuple-element.90.after_ref.entry_ref, bf16[6,128,512]{2,1,0:T(8,128)(2,1)S(1)} %get-tuple-element.91.saved_ref, bf16[2,128,512]{2,1,0:T(8,128)(2,1)S(1)} %get-tuple-element.92.spread_ref, ...), custom_call_target="tpu_custom_call" | custom-call | flops 100000000 | bytes 300000 | tf_op jit(solution)/shard_map/finish_30/pallas_call | solution.py:52
  46.3 2.6 %collective-permute-start.14 = (bf16[256,512]{1,0:T(8,128)(2,1)S(1)}, bf16[256,512]{1,0:T(8,128)(2,1)S(1)}, u32[]{:S(2)}, u32[]{:S(2)}) collective-permute-start(bf16[256,512]{1,0:T(8,128)(2,1)S(1)} %get-tuple-element.111), channel_id=1, source_target_pairs={{0,1},{1,0},{2,3},{3,2},{4,5},{5,4},{6,7},{7,6},{8,9},{9,8},{10,11... | collective-permute-start | bytes 786440 | tf_op jit(solution)/shard_map/ppermute | solution.py:595
  48.9 1.7 %within_31.1.within_ref = bf16[2,256,512]{2,1,0:T(8,128)(2,1)S(1)} custom-call(bf16[2,2,256,512]{3,2,1,0:T(8,128)(2,1)S(1)} %get-tuple-element.101.u_ref, bf16[2,128,512]{2,1,0:T(8,128)(2,1)S(1)} %get-tuple-element.100.spread_ref, bf16[2,2,256,256]{3,2,1,0:T(8,128)(2,1)S(1)} %get-tuple-element.76.kq_ref.refs_0_, ...), custom_call_target="tpu_custom_call" | custom-call | flops 100000000 | bytes 300000 | tf_op jit(solution)/shard_map/within_31/pallas_call | solution.py:52
  50.6 1.1 %finish_31.1 = (f32[256,512]{1,0:T(8,128)S(1)}, bf16[256,512]{1,0:T(8,128)(2,1)S(1)}, f32[2,256,128]{2,1,0:T(8,128)S(1)}) custom-call(bf16[2,128,512]{2,1,0:T(8,128)(2,1)S(1)} %get-tuple-element.98.after_ref.entry_ref, bf16[6,128,512]{2,1,0:T(8,128)(2,1)S(1)} %get-tuple-element.99.saved_ref, bf16[2,128,512]{2,1,0:T(8,128)(2,1)S(1)} %get-tuple-element.100.spread_ref, ...), custom_call_target="tpu_custom_call" | custom-call | flops 100000000 | bytes 300000 | tf_op jit(solution)/shard_map/finish_31/pallas_call | solution.py:52
  51.7 0.1 collective-permute-start.15
  51.8 0.0 collective-permute-done.12.entry_ref
  51.8 1.1 %finish_20.1 = (f32[256,512]{1,0:T(8,128)S(1)}, bf16[256,512]{1,0:T(8,128)(2,1)S(1)}, f32[2,256,128]{2,1,0:T(8,128)S(1)}) custom-call(bf16[2,128,512]{2,1,0:T(8,128)(2,1)S(1)} %collective-permute-done.12.entry_ref, bf16[6,128,512]{2,1,0:T(8,128)(2,1)S(1)} %get-tuple-element.105.saved_ref, bf16[2,128,512]{2,1,0:T(8,128)(2,1)S(1)} %get-tuple-element.75.spread_ref, ...), custom_call_target="tpu_custom_call" | custom-call | flops 100000000 | bytes 300000 | tf_op jit(solution)/shard_map/finish_20/pallas_call | solution.py:52
  53.0 0.4 collective-permute-done.15.refs_5_
  53.3 0.7 %finish_other.1.refs_4_ = bf16[256,640]{1,0:T(8,128)(2,1)S(1)} custom-call(bf16[2,128,512]{2,1,0:T(8,128)(2,1)S(1)} %collective-permute-done.13.entry_ref, bf16[6,128,512]{2,1,0:T(8,128)(2,1)S(1)} %get-tuple-element.109.saved_ref, bf16[2,128,512]{2,1,0:T(8,128)(2,1)S(1)} %get-tuple-element.87.spread_ref, ...), custom_call_target="tpu_custom_call" | custom-call | flops 100000000 | bytes 300000 | tf_op jit(solution)/shard_map/finish_other/pallas_call | solution.py:52
  54.0 0.4 collective-permute-start.17
  54.4 0.2 collective-permute-start.16
  54.6 0.6 %finish_own.1 = (f32[256,512]{1,0:T(8,128)S(1)}, f32[256,128]{1,0:T(8,128)S(1)}) custom-call(bf16[2,128,512]{2,1,0:T(8,128)(2,1)S(1)} %collective-permute-done.13.entry_ref, bf16[6,128,512]{2,1,0:T(8,128)(2,1)S(1)} %get-tuple-element.109.saved_ref, bf16[2,128,512]{2,1,0:T(8,128)(2,1)S(1)} %get-tuple-element.87.spread_ref, ...), custom_call_target="tpu_custom_call" | custom-call | flops 100000000 | bytes 300000 | tf_op jit(solution)/shard_map/finish_own/pallas_call | solution.py:52
  55.2 0.9 %collective-permute-done.16.refs_6_ = bf16[256,512]{1,0:T(8,128)(2,1)S(1)} collective-permute-done((bf16[256,512]{1,0:T(8,128)(2,1)S(1)}, bf16[256,512]{1,0:T(8,128)(2,1)S(1)}, u32[]{:S(2)}, u32[]{:S(2)}) %collective-permute-start.16) | collective-permute-done | bytes 262176 | tf_op jit(solution)/shard_map/ppermute | solution.py:595
  56.1 1.5 %norm.1 = bf16[256,4096]{1,0:T(8,128)(2,1)} custom-call(f32[256,512]{1,0:T(8,128)S(1)} %get-tuple-element.95.refs_0_, f32[256,512]{1,0:T(8,128)S(1)} %get-tuple-element.103.refs_1_, f32[256,512]{1,0:T(8,128)S(1)} %get-tuple-element.107.refs_2_, f32[256,512]{1,0:T(8,128)S(1)} %get-tuple-element.113.refs_3_, ...), custom_call_target="tpu_custom_call" | custom-call | flops 100000000 | bytes 300000 | tf_op jit(solution)/shard_map/norm/pallas_call | solution.py:52
  (10 shorter events, 0.0 us)
Async XLA Ops:
  1.4 7.0 %collective-permute-start = (bf16[256,2560]{1,0:T(8,128)(2,1)S(1)}, bf16[256,2560]{1,0:T(8,128)(2,1)S(1)}, u32[]{:S(2)}, u32[]{:S(2)}) collective-permute-start(bf16[256,2560]{1,0:T(8,128)(2,1)S(1)} %get-tuple-element.61), channel_id=1, source_target_pairs={{0,1},{1,0},{2,3},{3,2},{4,5},{5,4},{6,7},{7,6},{8,9},{9,8},{10,11... | collective-permute-start | bytes 3932168 | tf_op jit(solution)/shard_map/ppermute | solution.py:595
  2.9 9.0 %collective-permute-start.1 = (bf16[16,4352]{1,0:T(8,128)(2,1)S(1)}, bf16[16,4352]{1,0:T(8,128)(2,1)S(1)}, u32[]{:S(2)}, u32[]{:S(2)}) collective-permute-start(bf16[16,4352]{1,0:T(8,128)(2,1)S(1)} %get-tuple-element.64), channel_id=1, source_target_pairs={{1,2},{3,4},{5,6},{7,8},{9,10},{11,12},{13,14},{2,1},{4,3},{6,5},{... | collective-permute-start | bytes 417800 | tf_op jit(solution)/shard_map/ppermute | solution.py:595
  11.9 1.3 %collective-permute-start.2 = (bf16[16,2304]{1,0:T(8,128)(2,1)S(1)}, bf16[16,2304]{1,0:T(8,128)(2,1)S(1)}, u32[]{:S(2)}, u32[]{:S(2)}) collective-permute-start(bf16[16,2304]{1,0:T(8,128)(2,1)S(1)} %get-tuple-element.67), channel_id=1, source_target_pairs={{0,1},{1,0},{2,3},{3,2},{4,5},{5,4},{6,7},{7,6},{8,9},{9,8},{10,11... | collective-permute-start | bytes 221192 | tf_op jit(solution)/shard_map/ppermute | solution.py:595
  14.5 11.3 %collective-permute-start.4 = (bf16[256,2048]{1,0:T(8,128)(2,1)S(1)}, bf16[256,2048]{1,0:T(8,128)(2,1)S(1)}, u32[]{:S(2)}, u32[]{:S(2)}) collective-permute-start(bf16[256,2048]{1,0:T(8,128)(2,1)S(1)} %get-tuple-element.82), channel_id=1, source_target_pairs={{0,1},{1,0},{2,3},{3,2},{4,5},{5,4},{6,7},{7,6},{8,9},{9,8},{10,11... | collective-permute-start | bytes 3145736 | tf_op jit(solution)/shard_map/ppermute | solution.py:595
  15.0 10.8 %collective-permute-start.3 = (bf16[272,512]{1,0:T(8,128)(2,1)S(1)}, bf16[272,512]{1,0:T(8,128)(2,1)S(1)}, u32[]{:S(2)}, u32[]{:S(2)}) collective-permute-start(bf16[272,512]{1,0:T(8,128)(2,1)S(1)} %get-tuple-element.72.after_ref), channel_id=1, source_target_pairs={{0,2},{1,3},{2,0},{3,1},{4,6},{5,7},{6,4},{7,5},{8,10},{9,11},{10,... | collective-permute-start | bytes 835592 | tf_op jit(solution)/shard_map/ppermute | solution.py:595
  21.7 11.1 %collective-permute-start.8 = (bf16[272,512]{1,0:T(8,128)(2,1)S(1)}, bf16[272,512]{1,0:T(8,128)(2,1)S(1)}, u32[]{:S(2)}, u32[]{:S(2)}) collective-permute-start(bf16[272,512]{1,0:T(8,128)(2,1)S(1)} %get-tuple-element.79.after_ref), channel_id=1, source_target_pairs={{0,2},{1,3},{2,0},{3,1},{4,6},{5,7},{6,4},{7,5},{8,10},{9,11},{10,... | collective-permute-start | bytes 835592 | tf_op jit(solution)/shard_map/ppermute | solution.py:595
  25.9 9.4 %collective-permute-start.5 = (bf16[144,512]{1,0:T(8,128)(2,1)S(1)}, bf16[144,512]{1,0:T(8,128)(2,1)S(1)}, u32[]{:S(2)}, u32[]{:S(2)}) collective-permute-start(bf16[144,512]{1,0:T(8,128)(2,1)S(1)} %get-tuple-element.83.after_ref), channel_id=1, source_target_pairs={{0,4},{1,5},{2,6},{3,7},{4,8},{5,9},{6,10},{7,11},{8,12},{9,13},{1... | collective-permute-start | bytes 442376 | tf_op jit(solution)/shard_map/ppermute | solution.py:595
  27.5 8.9 %collective-permute-start.6 = (bf16[144,512]{1,0:T(8,128)(2,1)S(1)}, bf16[144,512]{1,0:T(8,128)(2,1)S(1)}, u32[]{:S(2)}, u32[]{:S(2)}) collective-permute-start(bf16[144,512]{1,0:T(8,128)(2,1)S(1)} %get-tuple-element.84), channel_id=1, source_target_pairs={{0,8},{1,9},{2,10},{3,11},{4,12},{5,13},{6,14},{7,15},{8,0},{9,1},... | collective-permute-start | bytes 442376 | tf_op jit(solution)/shard_map/ppermute | solution.py:595
  30.1 6.2 %collective-permute-start.7 = (bf16[144,512]{1,0:T(8,128)(2,1)S(1)}, bf16[144,512]{1,0:T(8,128)(2,1)S(1)}, u32[]{:S(2)}, u32[]{:S(2)}) collective-permute-start(bf16[144,512]{1,0:T(8,128)(2,1)S(1)} %get-tuple-element.85), channel_id=1, source_target_pairs={{0,12},{1,13},{2,14},{3,15},{4,0},{5,1},{6,2},{7,3},{8,4},{9,5},{1... | collective-permute-start | bytes 442376 | tf_op jit(solution)/shard_map/ppermute | solution.py:595
  33.0 8.5 %collective-permute-start.9 = (bf16[144,512]{1,0:T(8,128)(2,1)S(1)}, bf16[144,512]{1,0:T(8,128)(2,1)S(1)}, u32[]{:S(2)}, u32[]{:S(2)}) collective-permute-start(bf16[144,512]{1,0:T(8,128)(2,1)S(1)} %get-tuple-element.89.refs_0_), channel_id=1, source_target_pairs={{0,4},{1,5},{2,6},{3,7},{4,8},{5,9},{6,10},{7,11},{8,12},{9,13},{1... | collective-permute-start | bytes 442376 | tf_op jit(solution)/shard_map/ppermute | solution.py:595
  33.5 9.6 %collective-permute-start.10 = (bf16[144,512]{1,0:T(8,128)(2,1)S(1)}, bf16[144,512]{1,0:T(8,128)(2,1)S(1)}, u32[]{:S(2)}, u32[]{:S(2)}) collective-permute-start(bf16[144,512]{1,0:T(8,128)(2,1)S(1)} %get-tuple-element.96), channel_id=1, source_target_pairs={{0,8},{1,9},{2,10},{3,11},{4,12},{5,13},{6,14},{7,15},{8,0},{9,1},... | collective-permute-start | bytes 442376 | tf_op jit(solution)/shard_map/ppermute | solution.py:595
  35.4 7.7 %collective-permute-start.11 = (bf16[144,512]{1,0:T(8,128)(2,1)S(1)}, bf16[144,512]{1,0:T(8,128)(2,1)S(1)}, u32[]{:S(2)}, u32[]{:S(2)}) collective-permute-start(bf16[144,512]{1,0:T(8,128)(2,1)S(1)} %get-tuple-element.97), channel_id=1, source_target_pairs={{0,12},{1,13},{2,14},{3,15},{4,0},{5,1},{6,2},{7,3},{8,4},{9,5},{1... | collective-permute-start | bytes 442376 | tf_op jit(solution)/shard_map/ppermute | solution.py:595
  36.7 15.1 %collective-permute-start.12 = (bf16[2,128,512]{2,1,0:T(8,128)(2,1)S(1)}, bf16[2,128,512]{2,1,0:T(8,128)(2,1)S(1)}, u32[]{:S(2)}, u32[]{:S(2)}) collective-permute-start(bf16[2,128,512]{2,1,0:T(8,128)(2,1)S(1)} %get-tuple-element.104), channel_id=1, source_target_pairs={{0,2},{1,3},{2,0},{3,1},{4,6},{5,7},{6,4},{7,5},{8,10},{9,11},{10,... | collective-permute-start | bytes 786440 | tf_op jit(solution)/shard_map/ppermute | solution.py:595
  43.4 9.6 %collective-permute-start.13 = (bf16[2,128,512]{2,1,0:T(8,128)(2,1)S(1)}, bf16[2,128,512]{2,1,0:T(8,128)(2,1)S(1)}, u32[]{:S(2)}, u32[]{:S(2)}) collective-permute-start(bf16[2,128,512]{2,1,0:T(8,128)(2,1)S(1)} %get-tuple-element.108), channel_id=1, source_target_pairs={{0,2},{1,3},{2,0},{3,1},{4,6},{5,7},{6,4},{7,5},{8,10},{9,11},{10,... | collective-permute-start | bytes 786440 | tf_op jit(solution)/shard_map/ppermute | solution.py:595
  46.3 6.6 %collective-permute-start.14 = (bf16[256,512]{1,0:T(8,128)(2,1)S(1)}, bf16[256,512]{1,0:T(8,128)(2,1)S(1)}, u32[]{:S(2)}, u32[]{:S(2)}) collective-permute-start(bf16[256,512]{1,0:T(8,128)(2,1)S(1)} %get-tuple-element.111), channel_id=1, source_target_pairs={{0,1},{1,0},{2,3},{3,2},{4,5},{5,4},{6,7},{7,6},{8,9},{9,8},{10,11... | collective-permute-start | bytes 786440 | tf_op jit(solution)/shard_map/ppermute | solution.py:595
  51.7 1.6 %collective-permute-start.15 = (bf16[256,512]{1,0:T(8,128)(2,1)S(1)}, bf16[256,512]{1,0:T(8,128)(2,1)S(1)}, u32[]{:S(2)}, u32[]{:S(2)}) collective-permute-start(bf16[256,512]{1,0:T(8,128)(2,1)S(1)} %get-tuple-element.112), channel_id=1, source_target_pairs={{0,1},{1,0},{2,3},{3,2},{4,5},{5,4},{6,7},{7,6},{8,9},{9,8},{10,11... | collective-permute-start | bytes 786440 | tf_op jit(solution)/shard_map/ppermute | solution.py:595
  54.0 2.1 %collective-permute-start.17 = (bf16[256,640]{1,0:T(8,128)(2,1)S(1)}, bf16[256,640]{1,0:T(8,128)(2,1)S(1)}, u32[]{:S(2)}, u32[]{:S(2)}) collective-permute-start(bf16[256,640]{1,0:T(8,128)(2,1)S(1)} %finish_other.1.refs_4_), channel_id=1, source_target_pairs={{0,1},{1,0},{2,3},{3,2},{4,5},{5,4},{6,7},{7,6},{8,9},{9,8},{10,11... | collective-permute-start | bytes 983048 | tf_op jit(solution)/shard_map/ppermute | solution.py:595
  54.4 1.6 %collective-permute-start.16 = (bf16[256,512]{1,0:T(8,128)(2,1)S(1)}, bf16[256,512]{1,0:T(8,128)(2,1)S(1)}, u32[]{:S(2)}, u32[]{:S(2)}) collective-permute-start(bf16[256,512]{1,0:T(8,128)(2,1)S(1)} %get-tuple-element.114), channel_id=1, source_target_pairs={{0,1},{1,0},{2,3},{3,2},{4,5},{5,4},{6,7},{7,6},{8,9},{9,8},{10,11... | collective-permute-start | bytes 786440 | tf_op jit(solution)/shard_map/ppermute | solution.py:595

commit v8 on v7

--- a/solution.py
+++ b/solution.py
@@ -84,9 +84,10 @@
     return jnp.where((col >= low) & (col < low + HEAD_DIM), 1.0, 0.0).astype(BF16)
 
 
-def expand(table_ref, first, spread):
-    both = dot(table_ref[first : first + 2].reshape(2 * TOK, 2 * HEADS), spread)
-    return both[0:TOK], both[TOK:]
+def expand(table_ref, drow_ref, first, spread):
+    rows = jnp.concatenate([table_ref[first : first + 2].reshape(2 * TOK, 2 * HEADS), drow_ref[...]], axis=0)
+    wide = dot(rows, spread)
+    return wide[0:TOK], wide[TOK : 2 * TOK], wide[2 * TOK :]
 
 
 def read_decay(rows):
@@ -289,10 +290,8 @@
     for b in range(2):
         spread = spread_matrix(b * HALF + start)
         spread_ref[b] = spread
-        drow = dot(drow_ref[...], spread)
+        *weights, drow = expand(table_ref, drow_ref, WF, spread)
         d0, d1 = drow[8:9], drow[9:10]
-
-        weights = expand(table_ref, WF, spread)
 
         def weighted(d, r):
             return (u_ref[b, d, r : r + SUB].astype(F32) * weights[d][r : r + SUB]).astype(BF16)
@@ -430,10 +429,10 @@
         start = b * HALF + start_of(k, p)
         first = start // HEAD_DIM
         spread = spread_ref[b]
-        skip = dot(drow_ref[...], spread)[10:11]
         mcol = pltpu.roll(mcol_ref[...], 2 * HEADS - first, 1)
         mrow = mrow_ref[pl.ds(pl.multiple_of(first, HC), HC), :]
-        wv, gt = expand(table_ref, WV, spread)
+        wv, gt, drow = expand(table_ref, drow_ref, WV, spread)
+        skip = drow[10:11]
         for s in range(2):
             rows = slice(s * SUB, (s + 1) * SUB)
             for two in range(HC // 2):
@@ -475,7 +474,7 @@
     start = start_of(k, p)
     at = columns(start, CW)
     spread = spread_ref[b]
-    drow = dot(drow_ref[...], spread)
+    gf, gr, drow = expand(table_ref, drow_ref, GF, spread)
     d0, d1 = drow[8:9], drow[9:10]
     far = dot(drow_ref[...], spread_ref[1 - b])
     far = far[0:1] + far[1:2]
@@ -488,7 +487,6 @@
         (ef.astype(BF16), (er * d1 + saved_ref[2 * b + 1].astype(F32)).astype(BF16)),
         ((ef * d0 + saved_ref[2 * b].astype(F32)).astype(BF16), er.astype(BF16)),
     ]
-    gf, gr = expand(table_ref, GF, spread)
     for s in range(2):
         rows = slice(s * SUB, (s + 1) * SUB)
         cf = dot(kq_ref[b, 0, rows, STATE : 2 * STATE], inside[s][0])

time: 57.9 us -> 58 us (level)
  transfers between devices with their start and end apart: 18 -> 18, of which waited for: 5 -> 4; matrix products, arithmetic and copies ran while one was open for 0% -> 0% of each run, Pallas kernels for 37% -> 38%
where the time goes in v8:
time: 58 us; the launch traced here: 57.8 us
  starting transfers between devices  28.1 us (48%)
  Pallas kernels  26.8 us (46%)
  waiting for transfers between devices  2.56 us (4%)
    ppermute x18, starting transfers between devices, send(): return lax.ppermute(v, 'seq', perm)  28.1 us
    pallas_call x22, Pallas kernels, call(): pl.pallas_call(kernel, name=name, in_specs=[VMEM] * len(operands) + [HBM]...  26.8 us
    ppermute x18, waiting for transfers between devices, send(): return lax.ppermute(v, 'seq', perm)  2.56 us
  transfers between devices with their start and end apart: 18, of which 4 were waited for; matrix products, arithmetic and copies ran while one was open for 0% of the time, Pallas kernels for 38%

profile of v8, /device:TPU:1, one launch (start us, length us, event | category | flops | bytes accessed | tf_op | source)
XLA Modules:
  0.0 57.8 jit_solution(1858734320036038393)
XLA Ops:
  0.0 1.4 %edges.1 = (bf16[256,2560]{1,0:T(8,128)(2,1)S(1)}, bf16[16,4352]{1,0:T(8,128)(2,1)S(1)}) custom-call(bf16[256,4352]{1,0:T(8,128)(2,1)} %x_hbm.3, f32[64,256]{1,0:T(8,128)} %step_hbm.3), custom_call_target="tpu_custom_call" | custom-call | flops 100000000 | bytes 300000 | tf_op jit(solution)/shard_map/edges/pallas_call | solution.py:52
  1.4 1.5 %collective-permute-start = (bf16[256,2560]{1,0:T(8,128)(2,1)S(1)}, bf16[256,2560]{1,0:T(8,128)(2,1)S(1)}, u32[]{:S(2)}, u32[]{:S(2)}) collective-permute-start(bf16[256,2560]{1,0:T(8,128)(2,1)S(1)} %get-tuple-element.61), channel_id=1, source_target_pairs={{0,1},{1,0},{2,3},{3,2},{4,5},{5,4},{6,7},{7,6},{8,9},{9,8},{10,11... | collective-permute-start | bytes 3932168 | tf_op jit(solution)/shard_map/ppermute | solution.py:593
  2.9 5.5 %collective-permute-start.1 = (bf16[16,4352]{1,0:T(8,128)(2,1)S(1)}, bf16[16,4352]{1,0:T(8,128)(2,1)S(1)}, u32[]{:S(2)}, u32[]{:S(2)}) collective-permute-start(bf16[16,4352]{1,0:T(8,128)(2,1)S(1)} %get-tuple-element.64), channel_id=1, source_target_pairs={{1,2},{3,4},{5,6},{7,8},{9,10},{11,12},{13,14},{2,1},{4,3},{6,5},{... | collective-permute-start | bytes 417800 | tf_op jit(solution)/shard_map/ppermute | solution.py:593
  8.4 0.0 collective-permute-done.other_ref
  8.4 3.5 %front.1 = (bf16[2,256,2304]{2,1,0:T(8,128)(2,1)S(1)}, bf16[6,256,128]{2,1,0:T(8,128)(2,1)S(1)}, f32[256,128]{1,0:T(8,128)S(1)}, f32[64,256]{1,0:T(8,128)S(1)}, ...) custom-call(bf16[256,2560]{1,0:T(8,128)(2,1)S(1)} %collective-permut, ...), custom_call_target="tpu_custom_call" | custom-call | flops 100000000 | bytes 300000 | tf_op jit(solution)/shard_map/front/pallas_call | solution.py:52
  11.9 0.0 collective-permute-done.1.halo_ref
  11.9 0.1 collective-permute-start.2
  12.0 1.1 %conv_21.1.after_ref.outs_0_ = bf16[2,2,256,512]{3,2,1,0:T(8,128)(2,1)S(1)} custom-call(bf16[2,256,2304]{2,1,0:T(8,128)(2,1)S(1)} %get-tuple-element.62.x_ref, f32[8,2304]{1,0:T(8,128)S(1)} %get-tuple-element.63.taps_ref), custom_call_target="tpu_custom_call" | custom-call | flops 100000000 | bytes 300000 | tf_op jit(solution)/shard_map/conv_21/pallas_call | solution.py:52
  13.1 0.1 collective-permute-done.2.core_halo_ref
  13.2 1.2 %states_first.1 = (bf16[2,2,256,256]{3,2,1,0:T(8,128)(2,1)S(1)}, bf16[2,2,256,512]{3,2,1,0:T(8,128)(2,1)S(1)}, bf16[2,2,128,256]{3,2,1,0:T(8,128)(2,1)S(1)}, bf1...) custom-call(bf16[2,2,256,256]{3,2,1,0:T(8,128)(2,1)S(1)} %get-tuple-, ...), custom_call_target="tpu_custom_call", output_to_operand_aliasing={{0}: (0, {}), {1}: (1, {})} | custom-call | flops 100000000 | bytes 300000 | tf_op jit(solution)/shard_map/states_first/pallas_call | solution.py:52
  14.5 0.4 collective-permute-start.4
  14.9 3.5 %collective-permute-start.3 = (bf16[272,512]{1,0:T(8,128)(2,1)S(1)}, bf16[272,512]{1,0:T(8,128)(2,1)S(1)}, u32[]{:S(2)}, u32[]{:S(2)}) collective-permute-start(bf16[272,512]{1,0:T(8,128)(2,1)S(1)} %get-tuple-element.72.after_ref), channel_id=1, source_target_pairs={{0,2},{1,3},{2,0},{3,1},{4,6},{5,7},{6,4},{7,5},{8,10},{9,11},{10,... | collective-permute-start | bytes 835592 | tf_op jit(solution)/shard_map/ppermute | solution.py:593
  18.4 2.0 %states_30.1 = (bf16[2,2,256,512]{3,2,1,0:T(8,128)(2,1)S(1)}, bf16[6,128,512]{2,1,0:T(8,128)(2,1)S(1)}, bf16[2,128,512]{2,1,0:T(8,128)(2,1)S(1)}, bf16[272,512]{1,0:T(8,128)(2,1)S(1)}) custom-call(bf16[2,256,2304]{2,1,0:T(8,128)(2,1)S(1)} %get-tuple-element.62.x_ref, f32[8,2304]{1,0:T(8,128)S(1)} %get-tuple-element.63.taps_ref, ...), custom_call_target="tpu_custom_call" | custom-call | flops 100000000 | bytes 300000 | tf_op jit(solution)/shard_map/states_30/pallas_call | solution.py:52
  20.4 1.0 %states_21.1 = (bf16[2,2,256,512]{3,2,1,0:T(8,128)(2,1)S(1)}, bf16[6,128,512]{2,1,0:T(8,128)(2,1)S(1)}, bf16[2,128,512]{2,1,0:T(8,128)(2,1)S(1)}, bf16[272,512]{1,0:T(8,128)(2,1)S(1)}) custom-call(bf16[2,256,2304]{2,1,0:T(8,128)(2,1)S(1)} %get-tuple-element.62.x_ref, f32[8,2304]{1,0:T(8,128)S(1)} %get-tuple-element.63.taps_ref, ...), custom_call_target="tpu_custom_call", output_to_operand_aliasing={{0}: (8, {})} | custom-call | flops 100000000 | bytes 300000 | tf_op jit(solution)/shard_map/states_21/pallas_call | solution.py:52
  21.4 0.1 collective-permute-start.8
  21.5 2.1 %states_31.1 = (bf16[2,2,256,512]{3,2,1,0:T(8,128)(2,1)S(1)}, bf16[6,128,512]{2,1,0:T(8,128)(2,1)S(1)}, bf16[2,128,512]{2,1,0:T(8,128)(2,1)S(1)}, bf16[272,512]{...) custom-call(bf16[2,256,2304]{2,1,0:T(8,128)(2,1)S(1)} %get-tuple-element.62.x_ref, ...), custom_call_target="tpu_custom_call" | custom-call | flops 100000000 | bytes 300000 | tf_op jit(solution)/shard_map/states_31/pallas_call | solution.py:52
  23.6 1.8 %within_20.1 = (bf16[2,256,512]{2,1,0:T(8,128)(2,1)S(1)}, f32[2,2,2,128,128]{4,3,2,1,0:T(8,128)S(1)}) custom-call(bf16[2,2,256,512]{3,2,1,0:T(8,128)(2,1)S(1)} %get-tuple-element.74.u_ref, bf16[2,128,512]{2,1,0:T(8,128)(2,1)S(1)} %get-tuple-element.75.spread_ref, bf16[2,2,256,256]{3,2,1,0:T(8,128)(2,1)S(1)} %get-tuple-element.76.kq_ref.refs_0_, ...), custom_call_target="tpu_custom_call" | custom-call | flops 100000000 | bytes 300000 | tf_op jit(solution)/shard_map/within_20/pallas_call | solution.py:52
  25.4 0.0 collective-permute-done.4.refs_1_.gate_other_ref.gate_ref
  25.4 0.1 group_a.1
  25.6 1.5 %collective-permute-start.5 = (bf16[144,512]{1,0:T(8,128)(2,1)S(1)}, bf16[144,512]{1,0:T(8,128)(2,1)S(1)}, u32[]{:S(2)}, u32[]{:S(2)}) collective-permute-start(bf16[144,512]{1,0:T(8,128)(2,1)S(1)} %get-tuple-element.83.after_ref), channel_id=1, source_target_pairs={{0,4},{1,5},{2,6},{3,7},{4,8},{5,9},{6,10},{7,11},{8,12},{9,13},{1... | collective-permute-start | bytes 442376 | tf_op jit(solution)/shard_map/ppermute | solution.py:593
  27.1 2.6 %collective-permute-start.6 = (bf16[144,512]{1,0:T(8,128)(2,1)S(1)}, bf16[144,512]{1,0:T(8,128)(2,1)S(1)}, u32[]{:S(2)}, u32[]{:S(2)}) collective-permute-start(bf16[144,512]{1,0:T(8,128)(2,1)S(1)} %get-tuple-element.84), channel_id=1, source_target_pairs={{0,8},{1,9},{2,10},{3,11},{4,12},{5,13},{6,14},{7,15},{8,0},{9,1},... | collective-permute-start | bytes 442376 | tf_op jit(solution)/shard_map/ppermute | solution.py:593
  29.7 1.1 %collective-permute-start.7 = (bf16[144,512]{1,0:T(8,128)(2,1)S(1)}, bf16[144,512]{1,0:T(8,128)(2,1)S(1)}, u32[]{:S(2)}, u32[]{:S(2)}) collective-permute-start(bf16[144,512]{1,0:T(8,128)(2,1)S(1)} %get-tuple-element.85), channel_id=1, source_target_pairs={{0,12},{1,13},{2,14},{3,15},{4,0},{5,1},{6,2},{7,3},{8,4},{9,5},{1... | collective-permute-start | bytes 442376 | tf_op jit(solution)/shard_map/ppermute | solution.py:593
  30.8 1.6 %within_21.1.refs_0_.within_ref = bf16[2,256,512]{2,1,0:T(8,128)(2,1)S(1)} custom-call(bf16[2,2,256,512]{3,2,1,0:T(8,128)(2,1)S(1)} %get-tuple-element.86.u_ref, bf16[2,128,512]{2,1,0:T(8,128)(2,1)S(1)} %get-tuple-element.87.spread_ref, bf16[2,2,256,256]{3,2,1,0:T(8,128)(2,1)S(1)} %get-tuple-element.76.kq_ref.refs_0_, ...), custom_call_target="tpu_custom_call" | custom-call | flops 100000000 | bytes 300000 | tf_op jit(solution)/shard_map/within_21/pallas_call | solution.py:52
  32.4 0.0 collective-permute-done.8.got_ref
  32.4 0.1 group_b.1
  32.6 0.5 collective-permute-start.9
  33.1 2.3 %collective-permute-start.10 = (bf16[144,512]{1,0:T(8,128)(2,1)S(1)}, bf16[144,512]{1,0:T(8,128)(2,1)S(1)}, u32[]{:S(2)}, u32[]{:S(2)}) collective-permute-start(bf16[144,512]{1,0:T(8,128)(2,1)S(1)} %get-tuple-element.96), channel_id=1, source_target_pairs={{0,8},{1,9},{2,10},{3,11},{4,12},{5,13},{6,14},{7,15},{8,0},{9,1},... | collective-permute-start | bytes 442376 | tf_op jit(solution)/shard_map/ppermute | solution.py:593
  35.3 0.0 collective-permute-done.5.r1_ref
  35.3 0.8 %collective-permute-start.11 = (bf16[144,512]{1,0:T(8,128)(2,1)S(1)}, bf16[144,512]{1,0:T(8,128)(2,1)S(1)}, u32[]{:S(2)}, u32[]{:S(2)}) collective-permute-start(bf16[144,512]{1,0:T(8,128)(2,1)S(1)} %get-tuple-element.97), channel_id=1, source_target_pairs={{0,12},{1,13},{2,14},{3,15},{4,0},{5,1},{6,2},{7,3},{8,4},{9,5},{1... | collective-permute-start | bytes 442376 | tf_op jit(solution)/shard_map/ppermute | solution.py:593
  36.2 0.3 entries_a.1
  36.5 3.3 %collective-permute-start.12 = (bf16[2,128,512]{2,1,0:T(8,128)(2,1)S(1)}, bf16[2,128,512]{2,1,0:T(8,128)(2,1)S(1)}, u32[]{:S(2)}, u32[]{:S(2)}) collective-permute-start(bf16[2,128,512]{2,1,0:T(8,128)(2,1)S(1)} %get-tuple-element.104), channel_id=1, source_target_pairs={{0,2},{1,3},{2,0},{3,1},{4,6},{5,7},{6,4},{7,5},{8,10},{9,11},{10,... | collective-permute-start | bytes 786440 | tf_op jit(solution)/shard_map/ppermute | solution.py:593
  39.8 1.6 %within_30.1.within_ref.refs_0_ = bf16[2,256,512]{2,1,0:T(8,128)(2,1)S(1)} custom-call(bf16[2,2,256,512]{3,2,1,0:T(8,128)(2,1)S(1)} %get-tuple-element.93.u_ref, bf16[2,128,512]{2,1,0:T(8,128)(2,1)S(1)} %get-tuple-element.92.spread_ref, bf16[2,2,256,256]{3,2,1,0:T(8,128)(2,1)S(1)} %get-tuple-element.76.kq_ref.refs_0_, ...), custom_call_target="tpu_custom_call" | custom-call | flops 100000000 | bytes 300000 | tf_op jit(solution)/shard_map/within_30/pallas_call | solution.py:52
  41.4 1.4 %collective-permute-done.10.r2_ref = bf16[144,512]{1,0:T(8,128)(2,1)S(1)} collective-permute-done((bf16[144,512]{1,0:T(8,128)(2,1)S(1)}, bf16[144,512]{1,0:T(8,128)(2,1)S(1)}, u32[]{:S(2)}, u32[]{:S(2)}) %collective-permute-start.10) | collective-permute-done | bytes 147488 | tf_op jit(solution)/shard_map/ppermute | solution.py:593
  42.9 0.3 entries_b.1
  43.2 1.6 %collective-permute-start.13 = (bf16[2,128,512]{2,1,0:T(8,128)(2,1)S(1)}, bf16[2,128,512]{2,1,0:T(8,128)(2,1)S(1)}, u32[]{:S(2)}, u32[]{:S(2)}) collective-permute-start(bf16[2,128,512]{2,1,0:T(8,128)(2,1)S(1)} %get-tuple-element.108), channel_id=1, source_target_pairs={{0,2},{1,3},{2,0},{3,1},{4,6},{5,7},{6,4},{7,5},{8,10},{9,11},{10,... | collective-permute-start | bytes 786440 | tf_op jit(solution)/shard_map/ppermute | solution.py:593
  44.8 1.2 %finish_30.1 = (f32[256,512]{1,0:T(8,128)S(1)}, bf16[256,512]{1,0:T(8,128)(2,1)S(1)}, f32[2,256,128]{2,1,0:T(8,128)S(1)}) custom-call(bf16[2,128,512]{2,1,0:T(8,128)(2,1)S(1)} %get-tuple-element.90.after_ref.entry_ref, bf16[6,128,512]{2,1,0:T(8,128)(2,1)S(1)} %get-tuple-element.91.saved_ref, bf16[2,128,512]{2,1,0:T(8,128)(2,1)S(1)} %get-tuple-element.92.spread_ref, ...), custom_call_target="tpu_custom_call" | custom-call | flops 100000000 | bytes 300000 | tf_op jit(solution)/shard_map/finish_30/pallas_call | solution.py:52
  46.1 2.6 %collective-permute-start.14 = (bf16[256,512]{1,0:T(8,128)(2,1)S(1)}, bf16[256,512]{1,0:T(8,128)(2,1)S(1)}, u32[]{:S(2)}, u32[]{:S(2)}) collective-permute-start(bf16[256,512]{1,0:T(8,128)(2,1)S(1)} %get-tuple-element.111), channel_id=1, source_target_pairs={{0,1},{1,0},{2,3},{3,2},{4,5},{5,4},{6,7},{7,6},{8,9},{9,8},{10,11... | collective-permute-start | bytes 786440 | tf_op jit(solution)/shard_map/ppermute | solution.py:593
  48.7 1.6 %within_31.1.within_ref = bf16[2,256,512]{2,1,0:T(8,128)(2,1)S(1)} custom-call(bf16[2,2,256,512]{3,2,1,0:T(8,128)(2,1)S(1)} %get-tuple-element.101.u_ref, bf16[2,128,512]{2,1,0:T(8,128)(2,1)S(1)} %get-tuple-element.100.spread_ref, bf16[2,2,256,256]{3,2,1,0:T(8,128)(2,1)S(1)} %get-tuple-element.76.kq_ref.refs_0_, ...), custom_call_target="tpu_custom_call" | custom-call | flops 100000000 | bytes 300000 | tf_op jit(solution)/shard_map/within_31/pallas_call | solution.py:52
  50.3 1.3 %finish_31.1 = (f32[256,512]{1,0:T(8,128)S(1)}, bf16[256,512]{1,0:T(8,128)(2,1)S(1)}, f32[2,256,128]{2,1,0:T(8,128)S(1)}) custom-call(bf16[2,128,512]{2,1,0:T(8,128)(2,1)S(1)} %get-tuple-element.98.after_ref.entry_ref, bf16[6,128,512]{2,1,0:T(8,128)(2,1)S(1)} %get-tuple-element.99.saved_ref, bf16[2,128,512]{2,1,0:T(8,128)(2,1)S(1)} %get-tuple-element.100.spread_ref, ...), custom_call_target="tpu_custom_call" | custom-call | flops 100000000 | bytes 300000 | tf_op jit(solution)/shard_map/finish_31/pallas_call | solution.py:52
  51.6 0.1 collective-permute-start.15
  51.7 1.3 %finish_20.1 = (f32[256,512]{1,0:T(8,128)S(1)}, bf16[256,512]{1,0:T(8,128)(2,1)S(1)}, f32[2,256,128]{2,1,0:T(8,128)S(1)}) custom-call(bf16[2,128,512]{2,1,0:T(8,128)(2,1)S(1)} %collective-permute-done.12.entry_ref, bf16[6,128,512]{2,1,0:T(8,128)(2,1)S(1)} %get-tuple-element.105.saved_ref, bf16[2,128,512]{2,1,0:T(8,128)(2,1)S(1)} %get-tuple-element.75.spread_ref, ...), custom_call_target="tpu_custom_call" | custom-call | flops 100000000 | bytes 300000 | tf_op jit(solution)/shard_map/finish_20/pallas_call | solution.py:52
  53.1 0.2 collective-permute-done.15.refs_5_
  53.3 0.8 %finish_other.1.refs_4_ = bf16[256,640]{1,0:T(8,128)(2,1)S(1)} custom-call(bf16[2,128,512]{2,1,0:T(8,128)(2,1)S(1)} %collective-permute-done.13.entry_ref, bf16[6,128,512]{2,1,0:T(8,128)(2,1)S(1)} %get-tuple-element.109.saved_ref, bf16[2,128,512]{2,1,0:T(8,128)(2,1)S(1)} %get-tuple-element.87.spread_ref, ...), custom_call_target="tpu_custom_call" | custom-call | flops 100000000 | bytes 300000 | tf_op jit(solution)/shard_map/finish_other/pallas_call | solution.py:52
  54.1 0.4 collective-permute-start.17
  54.5 0.2 collective-permute-start.16
  54.7 0.7 %finish_own.1 = (f32[256,512]{1,0:T(8,128)S(1)}, f32[256,128]{1,0:T(8,128)S(1)}) custom-call(bf16[2,128,512]{2,1,0:T(8,128)(2,1)S(1)} %collective-permute-done.13.entry_ref, bf16[6,128,512]{2,1,0:T(8,128)(2,1)S(1)} %get-tuple-element.109.saved_ref, bf16[2,128,512]{2,1,0:T(8,128)(2,1)S(1)} %get-tuple-element.87.spread_ref, ...), custom_call_target="tpu_custom_call" | custom-call | flops 100000000 | bytes 300000 | tf_op jit(solution)/shard_map/finish_own/pallas_call | solution.py:52
  55.4 0.8 %collective-permute-done.16.refs_6_ = bf16[256,512]{1,0:T(8,128)(2,1)S(1)} collective-permute-done((bf16[256,512]{1,0:T(8,128)(2,1)S(1)}, bf16[256,512]{1,0:T(8,128)(2,1)S(1)}, u32[]{:S(2)}, u32[]{:S(2)}) %collective-permute-start.16) | collective-permute-done | bytes 262176 | tf_op jit(solution)/shard_map/ppermute | solution.py:593
  56.2 1.5 %norm.1 = bf16[256,4096]{1,0:T(8,128)(2,1)} custom-call(f32[256,512]{1,0:T(8,128)S(1)} %get-tuple-element.95.refs_0_, f32[256,512]{1,0:T(8,128)S(1)} %get-tuple-element.103.refs_1_, f32[256,512]{1,0:T(8,128)S(1)} %get-tuple-element.107.refs_2_, f32[256,512]{1,0:T(8,128)S(1)} %get-tuple-element.113.refs_3_, ...), custom_call_target="tpu_custom_call" | custom-call | flops 100000000 | bytes 300000 | tf_op jit(solution)/shard_map/norm/pallas_call | solution.py:52
  (10 shorter events, 0.0 us)
Async XLA Ops:
  1.4 7.0 %collective-permute-start = (bf16[256,2560]{1,0:T(8,128)(2,1)S(1)}, bf16[256,2560]{1,0:T(8,128)(2,1)S(1)}, u32[]{:S(2)}, u32[]{:S(2)}) collective-permute-start(bf16[256,2560]{1,0:T(8,128)(2,1)S(1)} %get-tuple-element.61), channel_id=1, source_target_pairs={{0,1},{1,0},{2,3},{3,2},{4,5},{5,4},{6,7},{7,6},{8,9},{9,8},{10,11... | collective-permute-start | bytes 3932168 | tf_op jit(solution)/shard_map/ppermute | solution.py:593
  2.9 9.0 %collective-permute-start.1 = (bf16[16,4352]{1,0:T(8,128)(2,1)S(1)}, bf16[16,4352]{1,0:T(8,128)(2,1)S(1)}, u32[]{:S(2)}, u32[]{:S(2)}) collective-permute-start(bf16[16,4352]{1,0:T(8,128)(2,1)S(1)} %get-tuple-element.64), channel_id=1, source_target_pairs={{1,2},{3,4},{5,6},{7,8},{9,10},{11,12},{13,14},{2,1},{4,3},{6,5},{... | collective-permute-start | bytes 417800 | tf_op jit(solution)/shard_map/ppermute | solution.py:593
  11.9 1.3 %collective-permute-start.2 = (bf16[16,2304]{1,0:T(8,128)(2,1)S(1)}, bf16[16,2304]{1,0:T(8,128)(2,1)S(1)}, u32[]{:S(2)}, u32[]{:S(2)}) collective-permute-start(bf16[16,2304]{1,0:T(8,128)(2,1)S(1)} %get-tuple-element.67), channel_id=1, source_target_pairs={{0,1},{1,0},{2,3},{3,2},{4,5},{5,4},{6,7},{7,6},{8,9},{9,8},{10,11... | collective-permute-start | bytes 221192 | tf_op jit(solution)/shard_map/ppermute | solution.py:593
  14.5 10.9 %collective-permute-start.4 = (bf16[256,2048]{1,0:T(8,128)(2,1)S(1)}, bf16[256,2048]{1,0:T(8,128)(2,1)S(1)}, u32[]{:S(2)}, u32[]{:S(2)}) collective-permute-start(bf16[256,2048]{1,0:T(8,128)(2,1)S(1)} %get-tuple-element.82), channel_id=1, source_target_pairs={{0,1},{1,0},{2,3},{3,2},{4,5},{5,4},{6,7},{7,6},{8,9},{9,8},{10,11... | collective-permute-start | bytes 3145736 | tf_op jit(solution)/shard_map/ppermute | solution.py:593
  14.9 10.5 %collective-permute-start.3 = (bf16[272,512]{1,0:T(8,128)(2,1)S(1)}, bf16[272,512]{1,0:T(8,128)(2,1)S(1)}, u32[]{:S(2)}, u32[]{:S(2)}) collective-permute-start(bf16[272,512]{1,0:T(8,128)(2,1)S(1)} %get-tuple-element.72.after_ref), channel_id=1, source_target_pairs={{0,2},{1,3},{2,0},{3,1},{4,6},{5,7},{6,4},{7,5},{8,10},{9,11},{10,... | collective-permute-start | bytes 835592 | tf_op jit(solution)/shard_map/ppermute | solution.py:593
  21.4 11.0 %collective-permute-start.8 = (bf16[272,512]{1,0:T(8,128)(2,1)S(1)}, bf16[272,512]{1,0:T(8,128)(2,1)S(1)}, u32[]{:S(2)}, u32[]{:S(2)}) collective-permute-start(bf16[272,512]{1,0:T(8,128)(2,1)S(1)} %get-tuple-element.79.after_ref), channel_id=1, source_target_pairs={{0,2},{1,3},{2,0},{3,1},{4,6},{5,7},{6,4},{7,5},{8,10},{9,11},{10,... | collective-permute-start | bytes 835592 | tf_op jit(solution)/shard_map/ppermute | solution.py:593
  25.6 9.8 %collective-permute-start.5 = (bf16[144,512]{1,0:T(8,128)(2,1)S(1)}, bf16[144,512]{1,0:T(8,128)(2,1)S(1)}, u32[]{:S(2)}, u32[]{:S(2)}) collective-permute-start(bf16[144,512]{1,0:T(8,128)(2,1)S(1)} %get-tuple-element.83.after_ref), channel_id=1, source_target_pairs={{0,4},{1,5},{2,6},{3,7},{4,8},{5,9},{6,10},{7,11},{8,12},{9,13},{1... | collective-permute-start | bytes 442376 | tf_op jit(solution)/shard_map/ppermute | solution.py:593
  27.1 9.0 %collective-permute-start.6 = (bf16[144,512]{1,0:T(8,128)(2,1)S(1)}, bf16[144,512]{1,0:T(8,128)(2,1)S(1)}, u32[]{:S(2)}, u32[]{:S(2)}) collective-permute-start(bf16[144,512]{1,0:T(8,128)(2,1)S(1)} %get-tuple-element.84), channel_id=1, source_target_pairs={{0,8},{1,9},{2,10},{3,11},{4,12},{5,13},{6,14},{7,15},{8,0},{9,1},... | collective-permute-start | bytes 442376 | tf_op jit(solution)/shard_map/ppermute | solution.py:593
  29.7 6.4 %collective-permute-start.7 = (bf16[144,512]{1,0:T(8,128)(2,1)S(1)}, bf16[144,512]{1,0:T(8,128)(2,1)S(1)}, u32[]{:S(2)}, u32[]{:S(2)}) collective-permute-start(bf16[144,512]{1,0:T(8,128)(2,1)S(1)} %get-tuple-element.85), channel_id=1, source_target_pairs={{0,12},{1,13},{2,14},{3,15},{4,0},{5,1},{6,2},{7,3},{8,4},{9,5},{1... | collective-permute-start | bytes 442376 | tf_op jit(solution)/shard_map/ppermute | solution.py:593
  32.6 8.8 %collective-permute-start.9 = (bf16[144,512]{1,0:T(8,128)(2,1)S(1)}, bf16[144,512]{1,0:T(8,128)(2,1)S(1)}, u32[]{:S(2)}, u32[]{:S(2)}) collective-permute-start(bf16[144,512]{1,0:T(8,128)(2,1)S(1)} %get-tuple-element.89.refs_0_), channel_id=1, source_target_pairs={{0,4},{1,5},{2,6},{3,7},{4,8},{5,9},{6,10},{7,11},{8,12},{9,13},{1... | collective-permute-start | bytes 442376 | tf_op jit(solution)/shard_map/ppermute | solution.py:593
  33.1 9.8 %collective-permute-start.10 = (bf16[144,512]{1,0:T(8,128)(2,1)S(1)}, bf16[144,512]{1,0:T(8,128)(2,1)S(1)}, u32[]{:S(2)}, u32[]{:S(2)}) collective-permute-start(bf16[144,512]{1,0:T(8,128)(2,1)S(1)} %get-tuple-element.96), channel_id=1, source_target_pairs={{0,8},{1,9},{2,10},{3,11},{4,12},{5,13},{6,14},{7,15},{8,0},{9,1},... | collective-permute-start | bytes 442376 | tf_op jit(solution)/shard_map/ppermute | solution.py:593
  35.3 7.5 %collective-permute-start.11 = (bf16[144,512]{1,0:T(8,128)(2,1)S(1)}, bf16[144,512]{1,0:T(8,128)(2,1)S(1)}, u32[]{:S(2)}, u32[]{:S(2)}) collective-permute-start(bf16[144,512]{1,0:T(8,128)(2,1)S(1)} %get-tuple-element.97), channel_id=1, source_target_pairs={{0,12},{1,13},{2,14},{3,15},{4,0},{5,1},{6,2},{7,3},{8,4},{9,5},{1... | collective-permute-start | bytes 442376 | tf_op jit(solution)/shard_map/ppermute | solution.py:593
  36.5 15.2 %collective-permute-start.12 = (bf16[2,128,512]{2,1,0:T(8,128)(2,1)S(1)}, bf16[2,128,512]{2,1,0:T(8,128)(2,1)S(1)}, u32[]{:S(2)}, u32[]{:S(2)}) collective-permute-start(bf16[2,128,512]{2,1,0:T(8,128)(2,1)S(1)} %get-tuple-element.104), channel_id=1, source_target_pairs={{0,2},{1,3},{2,0},{3,1},{4,6},{5,7},{6,4},{7,5},{8,10},{9,11},{10,... | collective-permute-start | bytes 786440 | tf_op jit(solution)/shard_map/ppermute | solution.py:593
  43.2 9.8 %collective-permute-start.13 = (bf16[2,128,512]{2,1,0:T(8,128)(2,1)S(1)}, bf16[2,128,512]{2,1,0:T(8,128)(2,1)S(1)}, u32[]{:S(2)}, u32[]{:S(2)}) collective-permute-start(bf16[2,128,512]{2,1,0:T(8,128)(2,1)S(1)} %get-tuple-element.108), channel_id=1, source_target_pairs={{0,2},{1,3},{2,0},{3,1},{4,6},{5,7},{6,4},{7,5},{8,10},{9,11},{10,... | collective-permute-start | bytes 786440 | tf_op jit(solution)/shard_map/ppermute | solution.py:593
  46.1 7.0 %collective-permute-start.14 = (bf16[256,512]{1,0:T(8,128)(2,1)S(1)}, bf16[256,512]{1,0:T(8,128)(2,1)S(1)}, u32[]{:S(2)}, u32[]{:S(2)}) collective-permute-start(bf16[256,512]{1,0:T(8,128)(2,1)S(1)} %get-tuple-element.111), channel_id=1, source_target_pairs={{0,1},{1,0},{2,3},{3,2},{4,5},{5,4},{6,7},{7,6},{8,9},{9,8},{10,11... | collective-permute-start | bytes 786440 | tf_op jit(solution)/shard_map/ppermute | solution.py:593
  51.6 1.6 %collective-permute-start.15 = (bf16[256,512]{1,0:T(8,128)(2,1)S(1)}, bf16[256,512]{1,0:T(8,128)(2,1)S(1)}, u32[]{:S(2)}, u32[]{:S(2)}) collective-permute-start(bf16[256,512]{1,0:T(8,128)(2,1)S(1)} %get-tuple-element.112), channel_id=1, source_target_pairs={{0,1},{1,0},{2,3},{3,2},{4,5},{5,4},{6,7},{7,6},{8,9},{9,8},{10,11... | collective-permute-start | bytes 786440 | tf_op jit(solution)/shard_map/ppermute | solution.py:593
  54.1 2.1 %collective-permute-start.17 = (bf16[256,640]{1,0:T(8,128)(2,1)S(1)}, bf16[256,640]{1,0:T(8,128)(2,1)S(1)}, u32[]{:S(2)}, u32[]{:S(2)}) collective-permute-start(bf16[256,640]{1,0:T(8,128)(2,1)S(1)} %finish_other.1.refs_4_), channel_id=1, source_target_pairs={{0,1},{1,0},{2,3},{3,2},{4,5},{5,4},{6,7},{7,6},{8,9},{9,8},{10,11... | collective-permute-start | bytes 983048 | tf_op jit(solution)/shard_map/ppermute | solution.py:593
  54.5 1.7 %collective-permute-start.16 = (bf16[256,512]{1,0:T(8,128)(2,1)S(1)}, bf16[256,512]{1,0:T(8,128)(2,1)S(1)}, u32[]{:S(2)}, u32[]{:S(2)}) collective-permute-start(bf16[256,512]{1,0:T(8,128)(2,1)S(1)} %get-tuple-element.114), channel_id=1, source_target_pairs={{0,1},{1,0},{2,3},{3,2},{4,5},{5,4},{6,7},{7,6},{8,9},{9,8},{10,11... | collective-permute-start | bytes 786440 | tf_op jit(solution)/shard_map/ppermute | solution.py:593
